TPU v7x, 32 devices: a whole 2x2x4 slice. The times are simulated.
32 devices in a mesh: grp: 2 (over y), seq: 4 (over z), head: 4 (over x, core).
Axes of the slice: x: 2, y: 2, z: 4, core: 2. Of those that a mesh axis runs over, the one named last changes fastest.
Arguments:
- tokens: bfloat16 [1024, 2048], P(('grp', 'seq')), parts along dimension 0, may hold values from -6 to 6
- attn_weight: bfloat16 [4, 2048, 2048], P(None, 'seq', 'head'), may hold values from -0.125 to 0.125
- attn_gain: float32 [2048], replicated, may hold values from 0.25 to 1.75
- moe_gain: float32 [2048], replicated, may hold values from 0.25 to 1.75
- routes: int32 [1024, 8], P(('grp', 'seq')), parts along dimension 0, may hold values from 0 to 63, all different within a row; in each aligned block of 128 rows (0 to 127, 128 to 255, ...) at most 18 rows name the same one
- gates: float32 [1024, 8], P(('grp', 'seq')), parts along dimension 0, may hold values from 0.05 to 0.4
- expert_gate: bfloat16 [64, 2048, 1024], P('seq', None, 'head'), may hold values from -0.125 to 0.125
- expert_up: bfloat16 [64, 2048, 1024], P('seq', None, 'head'), may hold values from -0.125 to 0.125
- expert_down: bfloat16 [64, 1024, 2048], P('seq', 'head'), may hold values from -0.1875 to 0.1875
Outputs:
- mixed: bfloat16 [1024, 2048], P(('grp', 'seq')), parts along dimension 0
There are 2 independent parts, one for each index of `grp`. A program takes and returns all parts, laid end to end along the dimension named above; an argument that names none is the same for every part. Nothing has to cross between parts.
Inputs may be any that keep to these rules, and one draw needn't show every extreme that they name: `routes`: in each aligned block of 128 tokens, no expert is named by more than 18 pairs of a token and a choice, a bound that some block reaches; a token's 8 experts differ.
All inputs are finite; a program needn't handle non-finite values.
Results may differ from a plain program's by a relative error of at most 0.015.
Values may be sent and summed in bfloat16 or wider, within the bound.
No kernel may reach another device: no remote copies, remote signals or barrier semaphores. Data moves between devices by JAX's collectives and lax.ppermute only.
A program may use at most 128 MiB of HBM per device.

v0:
```python
import jax
import jax.numpy as jnp
from jax import lax
from jax.sharding import PartitionSpec as P

HEAD_DIM = 128
EXPERTS = 64
TOPK = 8
CAP = 18


PRECISE = lax.Precision.HIGHEST


def prefix_2(array, axis, combine, identity):
    peers, position = (lax.axis_size(axis), lax.axis_index(axis))
    everything = lax.all_gather(array.astype(jnp.bfloat16), axis)
    start = jnp.broadcast_to(jnp.asarray(identity, array.dtype), array.shape)

    def hop(k, before):
        reached = k < position
        new = combine(before, everything[k].astype(array.dtype))
        return jnp.where(reached, new, before)

    return lax.fori_loop(0, peers, hop, start)


def rms_scale(row_block, gain_vec):
    widened = row_block.astype(jnp.float32)
    factor = lax.rsqrt(jnp.mean(widened * widened, axis=-1, keepdims=True) + 1e-06)
    return widened * factor * gain_vec


def head_norm(outputs):
    return outputs * lax.rsqrt(jnp.mean(outputs * outputs, axis=-1, keepdims=True) + 1e-06)


def add_states(earlier, later):
    return earlier + later


def slot_numbers(route_flat):
    one_hot = (route_flat[:, None] == jnp.arange(EXPERTS, dtype=jnp.int32)[None, :]).astype(
        jnp.int32
    )
    earlier = jnp.cumsum(one_hot, axis=0) - one_hot
    return route_flat * CAP + jnp.sum(earlier * one_hot, axis=1)


def make_runner(expert_gate, expert_up, expert_down):

    def run_experts(received):
        gate_val = jnp.einsum(
            "necd,edf->necf", received, expert_gate, preferred_element_type=jnp.float32
        )
        up_val = jnp.einsum(
            "necd,edf->necf", received, expert_up, preferred_element_type=jnp.float32
        )
        hidden = (jax.nn.silu(gate_val) * up_val).astype(jnp.bfloat16)
        partial_value = jnp.einsum(
            "necf,efd->necd", hidden, expert_down, preferred_element_type=jnp.float32
        ).astype(jnp.bfloat16)
        groups = lax.axis_size("head")
        shape_now = partial_value.shape
        split = partial_value.reshape(
            shape_now[0], shape_now[1], shape_now[2], groups, shape_now[3] // groups
        )
        by_group = lax.all_to_all(split, "head", split_axis=3, concat_axis=3, tiled=True)
        summed = jnp.sum(by_group.astype(jnp.float32), axis=3)
        return lax.all_to_all(
            summed.astype(jnp.bfloat16), "seq", split_axis=0, concat_axis=0, tiled=True
        ).astype(summed.dtype)

    return run_experts


def body(
    tokens, attn_weight, attn_gain, moe_gain, routes, gates, expert_gate, expert_up, expert_down
):
    local_rows = tokens.shape[0]
    normed = rms_scale(tokens, attn_gain).astype(jnp.bfloat16)
    weights = lax.all_gather(attn_weight, "seq", axis=1, tiled=True)
    head_count = weights.shape[2] // HEAD_DIM
    projected = [
        jnp.dot(normed, weights[which], preferred_element_type=jnp.float32)
        .astype(jnp.bfloat16)
        .reshape(local_rows, head_count, HEAD_DIM)
        for which in range(3)
    ]
    query_rows, key_rows, value_rows = projected
    own_state = jnp.einsum("thd,the->hde", key_rows, value_rows, preferred_element_type=jnp.float32)
    prefix = prefix_2(own_state, "seq", add_states, jnp.zeros_like(own_state))
    inter_part = jnp.einsum(
        "thd,hde->the", query_rows.astype(jnp.float32), prefix, precision=PRECISE
    )
    scores = jnp.einsum("thd,shd->hts", query_rows, key_rows, preferred_element_type=jnp.float32)
    lower_mask = jnp.arange(local_rows)[:, None] >= jnp.arange(local_rows)[None, :]
    scores = jnp.where(lower_mask[None], scores, 0.0)
    intra_part = jnp.einsum(
        "hts,she->the", scores, value_rows.astype(jnp.float32), precision=PRECISE
    )
    attended = (
        head_norm(inter_part + intra_part)
        .reshape(local_rows, head_count * HEAD_DIM)
        .astype(jnp.bfloat16)
    )
    out_part = lax.dot_general(
        attended, weights[3], (((1,), (1,)), ((), ())), preferred_element_type=jnp.float32
    )
    residual = (
        tokens.astype(jnp.float32)
        + lax.psum(out_part.astype(jnp.bfloat16), "head").astype(jnp.float32)
    ).astype(jnp.bfloat16)
    moe_in = rms_scale(residual, moe_gain).astype(jnp.bfloat16)
    route_flat = routes.reshape(-1)
    slots = slot_numbers(route_flat)
    owners = lax.axis_size("seq")
    local_experts = expert_gate.shape[0]
    source_row = jnp.arange(route_flat.shape[0], dtype=jnp.int32) // TOPK
    run_experts = make_runner(expert_gate, expert_up, expert_down)
    outbound = (
        jnp.zeros((EXPERTS * CAP, moe_in.shape[1]), jnp.bfloat16).at[slots].set(moe_in[source_row])
    )
    outbound = outbound.reshape(owners, local_experts, CAP, moe_in.shape[1])
    returned = run_experts(lax.all_to_all(outbound, "seq", split_axis=0, concat_axis=0, tiled=True))
    arrived = returned.reshape(EXPERTS * CAP, -1)[slots].reshape(local_rows, TOPK, -1)
    moe_partial = jnp.einsum("tkd,tk->td", arrived, gates, precision=PRECISE)
    column_span = moe_partial.shape[1]
    residual_share = lax.dynamic_slice_in_dim(
        residual, lax.axis_index("head") * column_span, column_span, 1
    )
    mixed_share = (residual_share.astype(jnp.float32) + moe_partial).astype(jnp.bfloat16)
    return lax.all_gather(mixed_share, "head", axis=1, tiled=True)


def solution(mesh):
    return jax.shard_map(
        body,
        mesh=mesh,
        in_specs=(
            P(("grp", "seq"), None),
            P(None, "seq", "head"),
            P(),
            P(),
            P(("grp", "seq"), None),
            P(("grp", "seq"), None),
            P("seq", None, "head"),
            P("seq", None, "head"),
            P("seq", "head", None),
        ),
        out_specs=P(("grp", "seq"), None),
        check_vma=False,
    )
```

profile of v0, /device:TPU:0, one launch (start us, length us, event | category | flops | bytes accessed | tf_op | source)
XLA Modules:
  0.0 538.8 jit_solution(6225158763991145865)
XLA Ops:
  6.5 0.0 copy-start.1
  6.5 0.0 copy-start.4
  6.5 0.0 all-gather.3.cloned.1.call-start
  6.5 0.7 all-gather.3.cloned.1.call-update
  7.3 0.0 all-reduce.2.cloned.1.call-start
  7.3 0.8 copy.35
  8.1 0.1 eq.29
  8.2 0.1 eq.25
  8.3 18.0 %reduce-window.6 = s32[64,8,128]{2,1,0:T(8,128)S(1)} reduce-window(s32[64,8,128]{2,1,0:T(8,128)S(1)} %fusion.48, s32[]{:T(128)} %constant.64.clone.1), window={size=1x1x128 pad=0_0x0_0x127_0}, to_apply=%region_5.6 | reduce-window | flops 8323072 | bytes 524292 | tf_op jit(solution)/shard_map/reduce-window
  26.3 0.1 slice.32
  26.5 0.1 copy.37
  26.7 0.1 copy.38
  26.8 1.2 fusion.37
  28.0 0.7 broadcast_multiply_fusion
  28.7 0.1 broadcast_add_fusion
  28.9 132.5 %all-gather.3.cloned.1.call-done = bf16[4,2048,512]{2,1,0:T(8,128)(2,1)} async-done(((bf16[4,512,512]{2,1,0:T(8,128)(2,1)}), bf16[4,2048,512]{2,1,0:T(8,128)(2,1)}) %all-gather.3.cloned.1.call-update) | async-done | bytes 8388624 | tf_op jit(solution)/shard_map/all_gather | solution.py:82
  161.3 0.0 copy-done.1
  161.3 0.0 copy-done.4
  161.3 2.1 fusion.30
  163.4 0.1 copy.55
  163.6 2.1 fusion.33
  165.7 0.2 convolution_convert_fusion.1
  165.9 16.3 %all-gather = bf16[16,128,128]{2,1,0:T(8,128)(2,1)S(1)} all-gather(bf16[4,128,128]{2,1,0:T(8,128)(2,1)S(1)} %convolution_convert_fusion.1), channel_id=2, replica_groups=mesh['grp'=2,'seq'=4,'head'=4] {'seq'}, dimensions={0}, use_global_device_ids=true | all-gather | bytes 655360 | tf_op jit(solution)/shard_map/all_gather | solution.py:17
  182.2 0.5 while.14
  182.2 0.1 add_select_fusion.2
  182.3 0.1 add_select_fusion.2
  182.5 0.1 add_select_fusion.2
  182.6 0.1 add_select_fusion.2
  182.7 2.1 fusion.32
  184.8 0.0 copy-start.2
  184.8 0.4 fusion.50
  185.2 0.2 convolution_select_fusion
  185.4 0.4 multiply_reduce_fusion
  185.9 3.2 convolution_convert_fusion
  189.1 0.0 all-reduce.2.cloned.1.call-update
  189.1 0.1 fusion.46
  189.2 0.1 copy.34
  189.3 0.1 mul.89
  189.4 31.3 %all-reduce.2.cloned.1.call-done = bf16[128,2048]{1,0:T(8,128)(2,1)} async-done(((bf16[128,2048]{1,0:T(8,128)(2,1)}), bf16[128,2048]{1,0:T(8,128)(2,1)}) %all-reduce.2.cloned.1.call-update) | async-done | bytes 524304 | tf_op jit(solution)/shard_map/psum | solution.py:112
  220.7 1.3 fusion.34
  222.0 0.0 copy-done.2
  222.0 0.2 fusion.36
  222.2 23.3 %scatter_custom_fusion = bf16[1152,2048]{1,0:T(8,128)(2,1)} fusion(s32[1024]{0:T(1024)S(1)} %bitcast.134, bf16[128,2048]{1,0:T(8,128)(2,1)S(1)} %fusion.36, s32[1024]{0:T(1024)S(1)} %broadcast_clamp_fusion.1, bf16[]{:T(256)} %constant.73.clone.1), kind=kCustom, calls=%fused_computation.13 | custom fusion | bytes 4718594 | tf_op jit(solution)/shard_map/scatter | solution.py:122
  245.5 17.8 %reshape.156 = bf16[4,16,18,2048]{3,2,1,0:T(8,128)(2,1)} reshape(bf16[1152,2048]{1,0:T(8,128)(2,1)} %scatter_custom_fusion) | data formatting | bytes 9437184 | tf_op jit(solution)/shard_map/reshape | solution.py:124
  263.3 5.4 copy.39
  268.6 107.8 %all_to_all.15 = bf16[4,16,18,2048]{3,1,2,0:T(8,128)(2,1)S(1)} all-to-all(bf16[4,16,18,2048]{3,1,2,0:T(8,128)(2,1)S(1)} %copy.39), channel_id=1, replica_groups=mesh['grp'=2,'seq'=4,'head'=4] {'seq'}, dimensions={0} | all-to-all | bytes 9437184 | tf_op jit(solution)/shard_map/all_to_all | solution.py:125
  376.5 0.0 copy-start
  376.5 2.2 copy-done
  378.7 10.7 %fusion.4 = f32[16,4,18,256]{3,2,1,0:T(8,128)S(1)} fusion(bf16[16,2048,256]{2,1,0:T(8,128)(2,1)} %param.17, bf16[4,16,18,2048]{3,1,2,0:T(8,128)(2,1)S(1)} %all_to_all.15), kind=kOutput, calls=%fused_computation.8 | convolution fusion | flops 1207959552 | bytes 22675456 | tf_op jit(solution)/shard_map/necd,edf->necf/dot_general | solution.py:53
  389.5 18.6 %convert_bitcast_fusion = bf16[4,16,18,2048]{3,2,0,1:T(8,128)(2,1)} fusion(bf16[16,256,2048]{2,1,0:T(8,128)(2,1)} %param.19, f32[16,4,18,256]{3,2,1,0:T(8,128)S(1)} %fusion.4, bf16[16,2048,256]{2,1,0:T(8,128)(2,1)} %param.18, bf16[4,16,18,2048]{3,1,2,0:T(8,128)(2,1)} %copy-done), kind=kOutput, calls=%fused_computation.12 | convolution fusion | flops 2420047872 | bytes 44171264 | tf_op jit(solution)/shard_map/necf,efd->necd/dot_general | solution.py:60
  408.0 11.3 %reshape.192 = bf16[4,16,18,4,512]{4,3,2,0,1:T(4,128)(2,1)} reshape(bf16[4,16,18,2048]{3,2,0,1:T(8,128)(2,1)} %convert_bitcast_fusion) | data formatting | bytes 9437184 | tf_op jit(solution)/shard_map/reshape | solution.py:65
  419.3 5.0 copy.43
  424.3 57.2 %all_to_all.16 = bf16[4,16,18,4,512]{4,1,2,0,3:T(8,128)(2,1)} all-to-all(bf16[4,16,18,4,512]{4,1,2,0,3:T(8,128)(2,1)S(1)} %copy.43), channel_id=1, replica_groups=mesh['grp'=2,'seq'=4,'head'=4] {'head'}, dimensions={3} | all-to-all | bytes 9437184 | tf_op jit(solution)/shard_map/all_to_all | solution.py:68
  481.5 4.8 reduce_sum.55
  486.3 3.5 all-to-all-start.2
  489.9 0.0 copy-done.3
  489.9 0.1 copy.50
  490.0 28.3 %all-to-all-done.2 = bf16[4,16,18,512]{3,1,2,0:T(8,128)(2,1)S(1)} async-done(((bf16[4,16,18,512]{3,1,2,0:T(8,128)(2,1)}), bf16[4,16,18,512]{3,1,2,0:T(8,128)(2,1)S(1)}, u32[]{:S(2)}, u32[]{:S(2)}) %all-to-all-start.2) | async-done | bytes 1179680 | tf_op jit(solution)/shard_map/all_to_all | solution.py:70
  518.3 0.7 copy.45
  519.0 0.4 reshape.158
  519.4 4.0 gather_fusion
  523.4 1.0 fusion.41
  524.4 6.5 %all_gather.15 = bf16[128,2048]{1,0:T(8,128)(2,1)S(1)} all-gather(bf16[128,512]{1,0:T(8,128)(2,1)S(1)} %fusion.47), channel_id=1, replica_groups=mesh['grp'=2,'seq'=4,'head'=4] {'head'}, dimensions={1}, use_global_device_ids=true | all-gather | bytes 655360 | tf_op jit(solution)/shard_map/all_gather | solution.py:133
  530.9 0.8 copy.93
  (15 shorter events, 0.2 us)
Async XLA Ops:
  6.5 154.8 %copy-start.1 = (bf16[128,2048]{1,0:T(8,128)(2,1)S(1)}, bf16[128,2048]{1,0:T(8,128)(2,1)}, u32[]{:S(2)}) copy-start(bf16[128,2048]{1,0:T(8,128)(2,1)} %param.11) | copy-start | bytes 1572868
  6.5 154.8 %copy-start.4 = (f32[2048]{0:T(1024)S(1)}, f32[2048]{0:T(1024)}, u32[]{:S(2)}) copy-start(f32[2048]{0:T(1024)} %param.13) | copy-start | bytes 24580
  6.5 154.8 %all-gather.3.cloned.1.call-start = ((), (), s32[]{:S(2)}) async-start(), calls=%async_computation.3 | async-start | bytes 10485760 | tf_op jit(solution)/shard_map/all_gather | solution.py:82
  7.3 213.4 %all-reduce.2.cloned.1.call-start = ((), (), s32[]{:S(2)}) async-start(), calls=%async_computation.4 | async-start | bytes 1048576 | tf_op jit(solution)/shard_map/psum | solution.py:112
  184.8 37.2 %copy-start.2 = (f32[2048]{0:T(1024)S(1)}, f32[2048]{0:T(1024)}, u32[]{:S(2)}) copy-start(f32[2048]{0:T(1024)} %param.14) | copy-start | bytes 24580
  376.5 2.2 copy-start
  481.5 8.4 %copy-start.3 = (f32[128,8]{0,1:T(8,128)S(1)}, f32[128,8]{0,1:T(8,128)}, u32[]{:S(2)}) copy-start(f32[128,8]{0,1:T(8,128)} %param.16) | copy-start | bytes 12292
  486.3 31.9 %all-to-all-start.2 = ((bf16[4,16,18,512]{3,1,2,0:T(8,128)(2,1)}), bf16[4,16,18,512]{3,1,2,0:T(8,128)(2,1)S(1)}, u32[]{:S(2)}, u32[]{:S(2)}) async-start(bf16[4,16,18,512]{3,1,2,0:T(8,128)(2,1)} %reduce_sum.55), calls=%async_computation.2 | async-start | bytes 2359296 | tf_op jit(solution)/shard_map/all_to_all | solution.py:70
Sparse Core Ops, SparseCore 0:
  8.9 152.3 all-gather.2
  189.2 31.4 all-reduce.1
where the time goes:
time: 539 us
  waiting for transfers between devices  193 us (36%)
  blocking collectives  188 us (35%)
  local copies, waits for them, and re-layouts  72.5 us (13%)
  matrix products  41 us (8%)
  other arithmetic  27.1 us (5%)
  between operations  13.9 us (3%)
    all_gather x1, waiting for transfers between devices, body(): weights = lax.all_gather(attn_weight, 'seq', axis=1, tiled=True)  132 us
    all_to_all x1, blocking collectives, body(): lax.all_to_all(outbound, 'seq', split_axis=0, concat_axis=0, tiled=True)  108 us
    all_to_all x1, blocking collectives, run_experts(): lax.all_to_all(split, 'head', split_axis=3, concat_axis=3, tiled=True)  57.2 us
    psum x1, waiting for transfers between devices, body(): lax.psum(out_part.astype(jnp.bfloat16), 'head').astype(jnp.float32)  31.3 us
    all_to_all x1, waiting for transfers between devices, run_experts(): lax.all_to_all(summed.astype(jnp.bfloat16), 'seq', split_axis=0, concat_a...  28.3 us
    scatter x1, local copies, waits for them, and re-layouts, body(): jnp.zeros((EXPERTS * CAP, moe_in.shape[1]), jnp.bfloat16).at[slots]  23.3 us
    reshape x2, local copies, waits for them, and re-layouts, body(): outbound = outbound.reshape(owners, local_experts, CAP, moe_in.shape[1])  23.1 us
    dot_general x1, matrix products, run_experts(): jnp.einsum('necf,efd->necd', hidden, expert_down, preferred_element_type=...  18.6 us
  transfers between devices with their start and end apart: 3, of which 3 were waited for; matrix products, arithmetic and copies ran while one was open for 4% of the time, Pallas kernels for 0%

commit v1 on v0

--- a/solution.py
+++ b/solution.py
@@ -1,15 +1,25 @@
+import functools
+
 import jax
 import jax.numpy as jnp
 from jax import lax
+from jax.experimental import pallas as pl
+from jax.experimental.pallas import tpu as pltpu
 from jax.sharding import PartitionSpec as P
 
 HEAD_DIM = 128
 EXPERTS = 64
 TOPK = 8
 CAP = 18
-
+EPS = 1e-06
 
 PRECISE = lax.Precision.HIGHEST
+BF16 = jnp.bfloat16
+F32 = jnp.float32
+ANY = pl.BlockSpec(memory_space=pl.ANY)
+SMEM = pl.BlockSpec(memory_space=pltpu.SMEM)
+VMEM = pl.BlockSpec(memory_space=pltpu.VMEM)
+MIB = 1024 * 1024
 
 
 def prefix_2(array, axis, combine, identity):
@@ -74,7 +84,7 @@
     return run_experts
 
 
-def body(
+def general_body(
     tokens, attn_weight, attn_gain, moe_gain, routes, gates, expert_gate, expert_up, expert_down
 ):
     local_rows = tokens.shape[0]
@@ -133,7 +143,380 @@
     return lax.all_gather(mixed_share, "head", axis=1, tiled=True)
 
 
+def swap(array, axis, distance):
+    size = lax.axis_size(axis)
+    return lax.ppermute(array, axis, [(i, i ^ distance) for i in range(size)])
+
+
+def run_copies(copies):
+    for copy in copies:
+        copy.start()
+    for copy in copies:
+        copy.wait()
+
+
+def prep_kernel(n, pos, tokens, weight, x_send, w_own, *rest):
+    w_sends, sems = rest[:-1], rest[-1]
+    g, s, h = pos[0], pos[1], pos[2]
+    rows, cols = x_send.shape
+    depth, half = w_own.shape[0], w_sends[0].shape[0]
+    copies = [
+        (tokens.at[:, pl.ds(pl.multiple_of(h * cols, cols), cols)], x_send),
+    ]
+    for which in range(3):
+        span = pl.ds(which * HEAD_DIM, HEAD_DIM)
+        for distance, out in enumerate(w_sends, 1):
+            column = pl.multiple_of((s ^ distance) * HEAD_DIM, HEAD_DIM)
+            copies.append(
+                (
+                    weight.at[
+                        which, pl.ds(pl.multiple_of(g * half, half), half), pl.ds(column, HEAD_DIM)
+                    ],
+                    out.at[:, span],
+                )
+            )
+        column = pl.multiple_of(s * HEAD_DIM, HEAD_DIM)
+        copies.append((weight.at[which, :, pl.ds(column, HEAD_DIM)], w_own.at[:, span]))
+    run_copies([pltpu.make_async_copy(a, b, sems.at[i]) for i, (a, b) in enumerate(copies)])
+
+
+def attend_kernel(n, pos, gain, tokens, w_own, *rest):
+    x_pieces, rest = rest[:n], rest[n:]
+    w_near, rest = rest[: n - 1], rest[n - 1 :]
+    w_far, rest = rest[: n - 1], rest[n - 1 :]
+    attended, x_share, x_all, w_all, sems = rest
+    g, s, h = pos[0], pos[1], pos[2]
+    rows, width = tokens.shape
+    cols = width // n
+    depth, half = w_own.shape[0], w_near[0].shape[0]
+    total = n * rows
+
+    def at_rows(block, size):
+        return pl.ds(pl.multiple_of(block * size, size), size)
+
+    copies = [(tokens, x_all.at[at_rows(s, rows)]), (w_own, w_all.at[at_rows(s, depth)])]
+    for e in range(n):
+        for d in range(1, n):
+            copies.append(
+                (x_pieces[e].at[d - 1], x_all.at[at_rows(s ^ d, rows), at_rows(h ^ e, cols)])
+            )
+    for d in range(1, n):
+        copies.append((w_near[d - 1], w_all.at[at_rows((s ^ d) * 2 + g, half)]))
+        copies.append((w_far[d - 1], w_all.at[at_rows((s ^ d) * 2 + (1 - g), half)]))
+    run_copies([pltpu.make_async_copy(a, b, sems.at[i]) for i, (a, b) in enumerate(copies)])
+
+    projected = []
+    for block in range(n):
+        wide = x_all[block * rows : (block + 1) * rows, :].astype(F32)
+        factor = lax.rsqrt(jnp.mean(wide * wide, axis=-1, keepdims=True) + EPS)
+        normed = (wide * factor * gain[...]).astype(BF16)
+        projected.append(
+            jnp.dot(normed, w_all[...], preferred_element_type=F32).astype(BF16)
+        )
+    whole = jnp.concatenate(projected, axis=0)
+    query, key, value = (whole[:, i * HEAD_DIM : (i + 1) * HEAD_DIM] for i in range(3))
+    for block in range(n):
+        upto = (block + 1) * rows
+        scores = lax.dot_general(
+            query[block * rows : upto],
+            key[:upto],
+            (((1,), (1,)), ((), ())),
+            preferred_element_type=F32,
+        )
+        ahead = lax.broadcasted_iota(jnp.int32, scores.shape, 0) + block * rows
+        scores = jnp.where(ahead >= lax.broadcasted_iota(jnp.int32, scores.shape, 1), scores, 0.0)
+        high = scores.astype(BF16)
+        low = (scores - high.astype(F32)).astype(BF16)
+        out = jnp.dot(high, value[:upto], preferred_element_type=F32) + jnp.dot(
+            low, value[:upto], preferred_element_type=F32
+        )
+        out = out * lax.rsqrt(jnp.mean(out * out, axis=-1, keepdims=True) + EPS)
+        attended[block] = out.astype(BF16)
+    x_share[...] = x_all[at_rows(h, rows), at_rows(s, cols)]
+
+
+def project_kernel(n, pos, x_share, w_own, w_others, *rest):
+    pieces, (out, a_all, w_all, sems) = rest[:n], rest[n:]
+    s, h = pos[1], pos[2]
+    cols = w_own.shape[1]
+    copies = []
+    for e in range(n):
+        source = w_own if e == 0 else w_others.at[e - 1]
+        copies.append((source, w_all.at[:, pl.ds(pl.multiple_of((h ^ e) * cols, cols), cols)]))
+        for d in range(n):
+            head = (h ^ e) * n + (s ^ d)
+            span = pl.ds(pl.multiple_of(head * HEAD_DIM, HEAD_DIM), HEAD_DIM)
+            copies.append((pieces[d].at[e], a_all.at[:, span]))
+    run_copies([pltpu.make_async_copy(a, b, sems.at[i]) for i, (a, b) in enumerate(copies)])
+    product = lax.dot_general(
+        a_all[...], w_all[...], (((1,), (1,)), ((), ())), preferred_element_type=F32
+    )
+    out[...] = (x_share[...].astype(F32) + product).astype(BF16)
+
+
+def route_kernel(n, experts, slots, pos, own, *rest):
+    others, (pick, place, weight, table, sems) = rest[: n - 1], rest[n - 1 :]
+    s = pos[1]
+    rows = own.shape[1]
+    total = n * rows
+    copies = []
+    for d, piece in enumerate((own,) + tuple(others)):
+        copies.append((piece, table.at[:, pl.ds(pl.multiple_of((s ^ d) * rows, rows), rows)]))
+    run_copies([pltpu.make_async_copy(a, b, sems.at[i]) for i, (a, b) in enumerate(copies)])
+    first = (s * experts).astype(F32)
+    names = lax.broadcasted_iota(jnp.int32, (experts, total), 0).astype(F32) + first
+    member = jnp.zeros((experts, total), F32)
+    gate = jnp.zeros((experts, total), F32)
+    for k in range(TOPK):
+        hit = table[k : k + 1, :] == names
+        member = jnp.where(hit, 1.0, member)
+        gate = jnp.where(hit, table[TOPK + k : TOPK + k + 1, :], gate)
+    earlier = (
+        lax.broadcasted_iota(jnp.int32, (total, total), 0)
+        < lax.broadcasted_iota(jnp.int32, (total, total), 1)
+    ).astype(F32).astype(BF16)
+    rank = jnp.dot(member.astype(BF16), earlier, preferred_element_type=F32)
+    slot = jnp.where(member > 0.0, rank, -1.0).astype(BF16)
+    pairs = experts * slots
+    expand = (
+        lax.broadcasted_iota(jnp.int32, (experts, pairs), 1) // slots
+        == lax.broadcasted_iota(jnp.int32, (experts, pairs), 0)
+    ).astype(F32).astype(BF16)
+    across = lax.dot_general(
+        slot, expand, (((0,), (0,)), ((), ())), preferred_element_type=F32
+    )
+    number = (lax.broadcasted_iota(jnp.int32, (total, pairs), 1) % slots).astype(F32)
+    place[...] = jnp.where(across == number, 1.0, 0.0).astype(BF16)
+    for e in range(experts):
+        span = pl.ds(e * slots, slots)
+        number = lax.broadcasted_iota(jnp.int32, (slots, total), 0).astype(F32)
+        hit = number == slot[e : e + 1, :].astype(F32)
+        pick[span, :] = jnp.where(hit, 1.0, 0.0).astype(BF16)
+        chosen = jnp.sum(jnp.where(hit, gate[e : e + 1, :], 0.0), axis=1, keepdims=True)
+        weight[span, :] = jnp.broadcast_to(chosen, (slots, weight.shape[1]))
+
+
+def experts_kernel(
+    n, pos, gain, r0, r1, r2, r3, pick, place, weight, w_gate, w_up, w_down,
+    out, share, r_all, x_slots, y_slots, sems,
+):
+    s, h = pos[1], pos[2]
+    step = pl.program_id(0)
+    rows, cols = r0.shape[1:]
+    slots = x_slots.shape[0] // pl.num_programs(0)
+
+    def span(block, size):
+        return pl.ds(pl.multiple_of(block * size, size), size)
+
+    @pl.when(step == 0)
+    def _():
+        copies = []
+        for e, piece in enumerate((r0, r1, r2, r3)):
+            for d in range(n):
+                copies.append((piece.at[d], r_all.at[span(h ^ e, rows), span(s ^ d, cols)]))
+        run_copies([pltpu.make_async_copy(a, b, sems.at[i]) for i, (a, b) in enumerate(copies)])
+        share[...] = r_all[span(s, rows), span(h, cols)]
+        for block in range(n):
+            where = slice(block * rows, (block + 1) * rows)
+            wide = r_all[where, :].astype(F32)
+            factor = lax.rsqrt(jnp.mean(wide * wide, axis=-1, keepdims=True) + EPS)
+            r_all[where, :] = (wide * factor * gain[...]).astype(BF16)
+        for block in range(n):
+            where = slice(block * cols, (block + 1) * cols)
+            x_slots[:, where] = jnp.dot(
+                pick[...], r_all[:, where], preferred_element_type=F32
+            ).astype(BF16)
+
+    mine = span(step, slots)
+    taken = x_slots[mine, :]
+    gate_val = jnp.dot(taken, w_gate[0], preferred_element_type=F32)
+    up_val = jnp.dot(taken, w_up[0], preferred_element_type=F32)
+    scale = weight[mine, :1]
+    hidden = (gate_val * jax.nn.sigmoid(gate_val) * up_val * scale).astype(BF16)
+    y_slots[mine, :] = jnp.dot(hidden, w_down[0], preferred_element_type=F32).astype(BF16)
+
+    @pl.when(step == pl.num_programs(0) - 1)
+    def _():
+        for e in range(n):
+            out[e] = jnp.dot(
+                place[...], y_slots[:, span(h ^ e, cols)], preferred_element_type=F32
+            ).astype(BF16)
+
+
+def square_body(
+    n, tokens, attn_weight, attn_gain, moe_gain, routes, gates, expert_gate, expert_up, expert_down
+):
+    g, s, h = (lax.axis_index(axis) for axis in ("grp", "seq", "head"))
+    pos = jnp.stack([g, s, h]).astype(jnp.int32)
+    rows, width = tokens.shape
+    cols = width // n
+    depth = attn_weight.shape[1]
+    half = depth // 2
+    experts, _, hidden = expert_gate.shape
+    total = n * rows
+    slots = -(-n * CAP // 16) * 16
+    sds = jax.ShapeDtypeStruct
+    dma = pltpu.SemaphoreType.DMA
+
+    with jax.named_scope("route_tables"):
+        table = jnp.concatenate([routes.T.astype(F32), gates.T], axis=0)
+        table_others = [swap(table, "seq", d) for d in range(1, n)]
+
+    with jax.named_scope("cut_pieces"):
+        x_send, w_own, *w_sends = pl.pallas_call(
+            functools.partial(prep_kernel, n),
+            out_shape=[sds((rows, cols), BF16), sds((depth, 3 * HEAD_DIM), BF16)]
+            + [sds((half, 3 * HEAD_DIM), BF16)] * (n - 1),
+            in_specs=[SMEM, ANY, ANY],
+            out_specs=[ANY] * (n + 1),
+            scratch_shapes=[dma((1 + 3 * n,))],
+        )(pos, tokens, attn_weight)
+    with jax.named_scope("gather_tokens"):
+        x_near = jnp.stack([swap(x_send, "seq", d) for d in range(1, n)])
+        x_pieces = {0: x_near}
+        for stride in (2, 1):
+            for e in list(x_pieces):
+                x_pieces[e ^ stride] = swap(x_pieces[e], "head", stride)
+    with jax.named_scope("gather_head_weights"):
+        w_near = [swap(w_sends[d - 1], "seq", d) for d in range(1, n)]
+        w_far = [swap(w, "grp", 1) for w in w_near]
+    with jax.named_scope("gather_out_weights"):
+        o_own = attn_weight[3]
+        o_pieces = {0: o_own}
+        for stride in (2, 1):
+            for e in list(o_pieces):
+                o_pieces[e ^ stride] = swap(o_pieces[e], "head", stride)
+        o_others = jnp.stack([o_pieces[e] for e in range(1, n)])
+
+    with jax.named_scope("routing"):
+        pick, place, weight = pl.pallas_call(
+            functools.partial(route_kernel, n, experts, slots),
+            out_shape=[
+                sds((experts * slots, total), BF16),
+                sds((total, experts * slots), BF16),
+                sds((experts * slots, 128), F32),
+            ],
+            in_specs=[SMEM] + [ANY] * n,
+            out_specs=[VMEM] * 3,
+            scratch_shapes=[pltpu.VMEM((2 * TOPK, total), F32), dma((n,))],
+            compiler_params=pltpu.CompilerParams(vmem_limit_bytes=32 * MIB),
+        )(pos, table, *table_others)
+
+    with jax.named_scope("attention"):
+        attended, x_share = pl.pallas_call(
+            functools.partial(attend_kernel, n),
+            out_shape=[sds((n, rows, HEAD_DIM), BF16), sds((rows, cols), BF16)],
+            in_specs=[SMEM, VMEM] + [ANY] * (2 + n + 2 * (n - 1)),
+            out_specs=[VMEM] * 2,
+            scratch_shapes=[
+                pltpu.VMEM((total, width), BF16),
+                pltpu.VMEM((width, 3 * HEAD_DIM), BF16),
+                dma((2 + n * (n - 1) + 2 * (n - 1),)),
+            ],
+            compiler_params=pltpu.CompilerParams(vmem_limit_bytes=32 * MIB),
+        )(
+            pos, attn_gain.reshape(1, width), tokens, w_own,
+            *[x_pieces[e] for e in range(n)], *w_near, *w_far,
+        )
+
+    with jax.named_scope("heads_to_tokens"):
+        by_block = [
+            lax.dynamic_index_in_dim(attended, h ^ e, 0, keepdims=False) for e in range(n)
+        ]
+        arrived = jnp.stack(
+            [by_block[0]] + [swap(by_block[e], "head", e) for e in range(1, n)]
+        )
+        a_pieces = [arrived] + [swap(arrived, "seq", d) for d in range(1, n)]
+
+    with jax.named_scope("output_projection"):
+        residual = pl.pallas_call(
+            functools.partial(project_kernel, n),
+            out_shape=sds((rows, cols), BF16),
+            in_specs=[SMEM, VMEM] + [ANY] * (2 + n),
+            out_specs=VMEM,
+            scratch_shapes=[
+                pltpu.VMEM((rows, width), BF16),
+                pltpu.VMEM((depth, width), BF16),
+                dma((n + n * n,)),
+            ],
+            compiler_params=pltpu.CompilerParams(vmem_limit_bytes=32 * MIB),
+        )(pos, x_share, o_own, o_others, *a_pieces)
+
+    with jax.named_scope("gather_residual"):
+        r_near = jnp.stack([residual] + [swap(residual, "seq", d) for d in range(1, n)])
+        r_pieces = {0: r_near}
+        for stride in (2, 1):
+            for e in list(r_pieces):
+                r_pieces[e ^ stride] = swap(r_pieces[e], "head", stride)
+
+    with jax.named_scope("experts"):
+        full = lambda *shape: pl.BlockSpec(shape, lambda e: (0,) * len(shape))
+        out, r_share = pl.pallas_call(
+            functools.partial(experts_kernel, n),
+            grid=(experts,),
+            out_shape=[sds((n, total, cols), BF16), sds((rows, cols), BF16)],
+            in_specs=[SMEM, full(1, width)]
+            + [ANY] * n
+            + [
+                full(experts * slots, total),
+                full(total, experts * slots),
+                full(experts * slots, 128),
+                pl.BlockSpec((1, width, hidden), lambda e: (e, 0, 0)),
+                pl.BlockSpec((1, width, hidden), lambda e: (e, 0, 0)),
+                pl.BlockSpec((1, hidden, width), lambda e: (e, 0, 0)),
+            ],
+            out_specs=[full(n, total, cols), full(rows, cols)],
+            scratch_shapes=[
+                pltpu.VMEM((total, width), BF16),
+                pltpu.VMEM((experts * slots, width), BF16),
+                pltpu.VMEM((experts * slots, width), BF16),
+                dma((n * n,)),
+            ],
+            compiler_params=pltpu.CompilerParams(vmem_limit_bytes=52 * MIB),
+        )(
+            pos, moe_gain.reshape(1, width), *[r_pieces[e] for e in range(n)],
+            pick, place, weight, expert_gate, expert_up, expert_down,
+        )
+
+    def plus(a, b):
+        return (a.astype(F32) + b.astype(F32)).astype(BF16)
+
+    with jax.named_scope("sum_over_head"):
+        parts = {e: out[e] for e in range(n)}
+        for stride in (1, 2):
+            parts = {
+                e: plus(parts[e], swap(parts[e ^ stride], "head", stride))
+                for e in parts
+                if not e & stride
+            }
+        summed = parts[0].reshape(n, rows, cols)
+    with jax.named_scope("sum_over_seq"):
+        blocks = [lax.dynamic_index_in_dim(summed, s ^ d, 0, keepdims=False) for d in range(n)]
+        mixed = r_share.astype(F32) + blocks[0].astype(F32)
+        for d in range(1, n):
+            mixed = mixed + swap(blocks[d], "seq", d).astype(F32)
+        mixed = mixed.astype(BF16)
+    with jax.named_scope("gather_columns"):
+        return lax.all_gather(mixed, "head", axis=1, tiled=True)
+
+
 def solution(mesh):
+    sizes = dict(mesh.shape)
+    n = sizes["seq"]
+
+    def body(tokens, attn_weight, *rest):
+        width = tokens.shape[1]
+        square = (
+            n == sizes["head"]
+            and n == 4
+            and sizes["grp"] == 2
+            and width == n * attn_weight.shape[1] == n * attn_weight.shape[2]
+            and width == n * n * HEAD_DIM
+        )
+        if square:
+            return square_body(n, tokens, attn_weight, *rest)
+        return general_body(tokens, attn_weight, *rest)
+
     return jax.shard_map(
         body,
         mesh=mesh,

time: 539 us -> 228 us (0.42)
  blocking collectives: 188 us -> 6.86 us
  waiting for transfers between devices: 193 us -> 85.8 us
  Pallas kernels: 0 us -> 77.6 us
  local copies, waits for them, and re-layouts: 72.5 us -> 11.2 us
  matrix products: 41 us -> 0 us
  starting transfers between devices: 3.57 us -> 42.4 us
  other arithmetic: 27.1 us -> 3.84 us
  between operations: 13.9 us -> 0.26 us
    all_to_all x2 -> x0, blocking collectives: 165 us -> none  [the longest x1 108 us: body(): lax.all_to_all(outbound, 'seq', split_axis=0, concat_axis=0, tiled=True)]
    all_gather x1 -> x0, waiting for transfers between devices: 132 us -> none  [body(): weights = lax.all_gather(attn_weight, 'seq', axis=1, tiled=True)]
    ppermute x0 -> x36, waiting for transfers between devices: none -> 85.8 us  [swap(): return lax.ppermute(array, axis, [(i, i ^ distance) for i in range(size)])]
    pallas_call x0 -> x5, Pallas kernels: none -> 77.6 us  [the longest x1 35.8 us: square_body(): pl.pallas_call(functools.partial(prep_kernel, n), out_shape=[sds((rows, c...]
    ppermute x0 -> x36, starting transfers between devices: none -> 42.4 us  [swap(): return lax.ppermute(array, axis, [(i, i ^ distance) for i in range(size)])]
    dot_general x11 -> x0, matrix products: 41 us -> none  [the longest x1 18.6 us: run_experts(): jnp.einsum('necf,efd->necd', hidden, expert_down, preferred_element_type=...]
    reshape x6 -> x0, local copies, waits for them, and re-layouts: 39.9 us -> none  [the longest x2 23.1 us: body(): outbound = outbound.reshape(owners, local_experts, CAP, moe_in.shape[1])]
    psum x1 -> x0, waiting for transfers between devices: 31.3 us -> none  [body(): lax.psum(out_part.astype(jnp.bfloat16), 'head').astype(jnp.float32)]
  transfers between devices with their start and end apart: 3 -> 36, of which waited for: 3 -> 17; matrix products, arithmetic and copies ran while one was open for 4% -> 1% of each run, Pallas kernels for 0% -> 3%
where the time goes in v1:
time: 228 us
  waiting for transfers between devices  85.8 us (38%)
  Pallas kernels  77.6 us (34%)
  starting transfers between devices  42.4 us (19%)
  local copies, waits for them, and re-layouts  11.2 us (5%)
  blocking collectives  6.86 us (3%)
  other arithmetic  3.84 us (2%)
    ppermute x36, waiting for transfers between devices, swap(): return lax.ppermute(array, axis, [(i, i ^ distance) for i in range(size)])  85.8 us
    ppermute x36, starting transfers between devices, swap(): return lax.ppermute(array, axis, [(i, i ^ distance) for i in range(size)])  42.4 us
    pallas_call x1, Pallas kernels, square_body(): pl.pallas_call(functools.partial(prep_kernel, n), out_shape=[sds((rows, c...  35.8 us
    pallas_call x1, Pallas kernels, square_body(): pl.pallas_call(functools.partial(experts_kernel, n), grid=(experts,), out...  33.6 us
    unnamed x33, local copies, waits for them, and re-layouts  7.84 us
    all_gather x1, blocking collectives, square_body(): return lax.all_gather(mixed, 'head', axis=1, tiled=True)  6.86 us
    pallas_call x1, Pallas kernels, square_body(): pl.pallas_call(functools.partial(attend_kernel, n), out_shape=[sds((n, ro...  4.77 us
  transfers between devices with their start and end apart: 36, of which 17 were waited for; matrix products, arithmetic and copies ran while one was open for 1% of the time, Pallas kernels for 3%

profile of v1, /device:TPU:0, one launch (start us, length us, event | category | flops | bytes accessed | tf_op | source)
XLA Modules:
  0.0 227.9 jit_solution(5760332909613428652)
XLA Ops:
  0.0 0.7 pad_add_fusion.pos
  0.7 35.8 %cut_pieces.1 = (bf16[128,512]{1,0:T(8,128)(2,1)}, bf16[512,384]{1,0:T(8,128)(2,1)}, bf16[256,384]{1,0:T(8,128)(2,1)}, bf16[256,384]{1,0:T(8,128)(2,1)}, bf16[256,384]{1,0:T(8,128)(2,1)}) custom-call(s32[3]{0:T(128)} %pad_add_fusion.pos, bf16[128,2048]{1,0:T(8,128)(2,1)} %tokens.3, bf16[4,512,512]{2,1,0:T(8,128)(2,1)} %weight.1), custom_call_target="tpu_custom_call" | custom-call | tf_op jit(solution)/shard_map/cut_pieces/pallas_call | solution.py:366
  36.4 3.1 %collective-permute-start = (bf16[128,512]{1,0:T(8,128)(2,1)}, bf16[128,512]{1,0:T(8,128)(2,1)S(1)}, u32[]{:S(2)}, u32[]{:S(2)}) collective-permute-start(bf16[128,512]{1,0:T(8,128)(2,1)} %get-tuple-element.18), channel_id=1, source_target_pairs={{0,4},{4,0},{8,12},{12,8},{1,5},{5,1},{9,13},{13,9},{2,6},{6,2},{1... | collective-permute-start | bytes 393224 | tf_op jit(solution)/shard_map/gather_tokens/ppermute | solution.py:148
  39.5 2.6 %collective-permute-start.1 = (bf16[128,512]{1,0:T(8,128)(2,1)}, bf16[128,512]{1,0:T(8,128)(2,1)S(1)}, u32[]{:S(2)}, u32[]{:S(2)}) collective-permute-start(bf16[128,512]{1,0:T(8,128)(2,1)} %get-tuple-element.18), channel_id=1, source_target_pairs={{0,8},{4,12},{8,0},{12,4},{1,9},{5,13},{9,1},{13,5},{2,10},{6,14},... | collective-permute-start | bytes 393224 | tf_op jit(solution)/shard_map/gather_tokens/ppermute | solution.py:148
  42.1 1.1 slice_bitcast_fusion.2.w_own
  43.2 1.8 collective-permute-start.13
  45.0 7.7 %collective-permute-done.1 = bf16[128,512]{1,0:T(8,128)(2,1)S(1)} collective-permute-done((bf16[128,512]{1,0:T(8,128)(2,1)}, bf16[128,512]{1,0:T(8,128)(2,1)S(1)}, u32[]{:S(2)}, u32[]{:S(2)}) %collective-permute-start.1) | collective-permute-done | bytes 131104 | tf_op jit(solution)/shard_map/gather_tokens/ppermute | solution.py:148
  52.7 1.6 collective-permute-start.4
  54.3 3.0 %collective-permute-start.7 = (bf16[256,384]{1,0:T(8,128)(2,1)}, bf16[256,384]{1,0:T(8,128)(2,1)S(1)}, u32[]{:S(2)}, u32[]{:S(2)}) collective-permute-start(bf16[256,384]{1,0:T(8,128)(2,1)} %get-tuple-element.20), channel_id=1, source_target_pairs={{0,8},{4,12},{8,0},{12,4},{1,9},{5,13},{9,1},{13,5},{2,10},{6,14},... | collective-permute-start | bytes 589832 | tf_op jit(solution)/shard_map/gather_head_weights/ppermute | solution.py:148
  57.2 1.4 collective-permute-start.8
  58.6 12.1 %collective-permute-done.7.rest_5_ = bf16[256,384]{1,0:T(8,128)(2,1)S(1)} collective-permute-done((bf16[256,384]{1,0:T(8,128)(2,1)}, bf16[256,384]{1,0:T(8,128)(2,1)S(1)}, u32[]{:S(2)}, u32[]{:S(2)}) %collective-permute-start.7) | collective-permute-done | bytes 196640 | tf_op jit(solution)/shard_map/gather_head_weights/ppermute | solution.py:148
  70.7 1.5 collective-permute-start.10
  72.3 0.5 collective-permute-start.11
  72.8 0.5 collective-permute-start.5
  73.3 4.1 %collective-permute-done.10.rest_8_ = bf16[256,384]{1,0:T(8,128)(2,1)S(1)} collective-permute-done((bf16[256,384]{1,0:T(8,128)(2,1)S(1)}, bf16[256,384]{1,0:T(8,128)(2,1)S(1)}, u32[]{:S(2)}, u32[]{:S(2)}) %collective-permute-start.10) | collective-permute-done | bytes 196640 | tf_op jit(solution)/shard_map/gather_head_weights/ppermute | solution.py:148
  77.4 0.7 copy-done.5
  78.1 0.5 collective-permute-start.14
  78.6 0.9 collective-permute-done.11.rest_9_
  79.5 0.7 copy-done.7
  80.2 1.5 collective-permute-start.9
  81.7 4.7 %collective-permute-done.9.rest_7_ = bf16[256,384]{1,0:T(8,128)(2,1)} collective-permute-done((bf16[256,384]{1,0:T(8,128)(2,1)}, bf16[256,384]{1,0:T(8,128)(2,1)}, u32[]{:S(2)}, u32[]{:S(2)}) %collective-permute-start.9) | collective-permute-done | bytes 196640 | tf_op jit(solution)/shard_map/gather_head_weights/ppermute | solution.py:148
  86.5 0.9 copy-done.6
  87.4 0.9 copy-done.8
  88.3 4.8 %attention.1 = (bf16[4,128,128]{2,1,0:T(8,128)(2,1)S(1)}, bf16[128,512]{1,0:T(8,128)(2,1)S(1)}) custom-call(s32[3]{0:T(128)S(1)} %copy-done.9, f32[1,2048]{1,0:T(1,128)S(1)} %bitcast.50, bf16[128,2048]{1,0:T(8,128)(2,1)S(1)} %copy-done, bf16[512,384]{1,0:T(8,128)(2,1)S(1)} %copy-done.4, bf16[3,128,512]{2,1,0:T(8,128)(2,1)S(1)} %pad_maximum_fusion.2.rest_0_, ...), custom_call_target="tpu_custom_call" | custom-call | tf_op jit(solution)/shard_map/attention/pallas_call | solution.py:406
  93.2 0.6 collective-permute-start.16
  93.8 1.3 collective-permute-start.17
  95.0 2.4 %collective-permute-done.16 = bf16[128,128]{1,0:T(8,128)(2,1)S(1)} collective-permute-done((bf16[128,128]{1,0:T(8,128)(2,1)S(1)}, bf16[128,128]{1,0:T(8,128)(2,1)S(1)}, u32[]{:S(2)}, u32[]{:S(2)}) %collective-permute-start.16) | collective-permute-done | bytes 32800 | tf_op jit(solution)/shard_map/heads_to_tokens/ppermute | solution.py:148
  97.5 0.6 collective-permute-start.18
  98.1 1.3 collective-permute-start.19
  99.4 2.6 %collective-permute-start.20 = (bf16[4,128,128]{2,1,0:T(8,128)(2,1)S(1)}, bf16[4,128,128]{2,1,0:T(8,128)(2,1)S(1)}, u32[]{:S(2)}, u32[]{:S(2)}) collective-permute-start(bf16[4,128,128]{2,1,0:T(8,128)(2,1)S(1)} %pad_maximum_fusion.3.rest_0_), channel_id=1, source_target_pairs={{0,12},{4,8},{8,4},{12,0},{1,13},{5,9},{9,5},{13,1},{2,14},{6,10},... | collective-permute-start | bytes 393224 | tf_op jit(solution)/shard_map/heads_to_tokens/ppermute | solution.py:148
  102.0 1.5 pad_maximum_fusion.w_others
  103.5 1.2 collective-permute-done.18.rest_1_
  104.7 6.2 %collective-permute-done.19.rest_2_ = bf16[4,128,128]{2,1,0:T(8,128)(2,1)S(1)} collective-permute-done((bf16[4,128,128]{2,1,0:T(8,128)(2,1)S(1)}, bf16[4,128,128]{2,1,0:T(8,128)(2,1)S(1)}, u32[]{:S(2)}, u32[]{:S(2)}) %collective-permute-start.19) | collective-permute-done | bytes 131104 | tf_op jit(solution)/shard_map/heads_to_tokens/ppermute | solution.py:148
  111.0 2.1 output_projection.1
  113.1 2.4 %collective-permute-start.21 = (bf16[128,512]{1,0:T(8,128)(2,1)S(1)}, bf16[128,512]{1,0:T(8,128)(2,1)S(1)}, u32[]{:S(2)}, u32[]{:S(2)}) collective-permute-start(bf16[128,512]{1,0:T(8,128)(2,1)S(1)} %output_projection.1), channel_id=1, source_target_pairs={{0,4},{4,0},{8,12},{12,8},{1,5},{5,1},{9,13},{13,9},{2,6},{6,2},{1... | collective-permute-start | bytes 393224 | tf_op jit(solution)/shard_map/gather_residual/ppermute | solution.py:148
  115.4 0.1 collective-permute-start.22
  115.6 2.3 %collective-permute-start.23 = (bf16[128,512]{1,0:T(8,128)(2,1)S(1)}, bf16[128,512]{1,0:T(8,128)(2,1)S(1)}, u32[]{:S(2)}, u32[]{:S(2)}) collective-permute-start(bf16[128,512]{1,0:T(8,128)(2,1)S(1)} %output_projection.1), channel_id=1, source_target_pairs={{0,12},{4,8},{8,4},{12,0},{1,13},{5,9},{9,5},{13,1},{2,14},{6,10},... | collective-permute-start | bytes 393224 | tf_op jit(solution)/shard_map/gather_residual/ppermute | solution.py:148
  117.9 1.5 collective-permute-done.21
  119.4 7.8 %collective-permute-done.22 = bf16[128,512]{1,0:T(8,128)(2,1)S(1)} collective-permute-done((bf16[128,512]{1,0:T(8,128)(2,1)S(1)}, bf16[128,512]{1,0:T(8,128)(2,1)S(1)}, u32[]{:S(2)}, u32[]{:S(2)}) %collective-permute-start.22) | collective-permute-done | bytes 131104 | tf_op jit(solution)/shard_map/gather_residual/ppermute | solution.py:148
  127.2 1.2 collective-permute-start.25
  128.4 10.8 %collective-permute-done.25.r2 = bf16[4,128,512]{2,1,0:T(8,128)(2,1)S(1)} collective-permute-done((bf16[4,128,512]{2,1,0:T(8,128)(2,1)S(1)}, bf16[4,128,512]{2,1,0:T(8,128)(2,1)S(1)}, u32[]{:S(2)}, u32[]{:S(2)}) %collective-permute-start.25) | collective-permute-done | bytes 524320 | tf_op jit(solution)/shard_map/gather_residual/ppermute | solution.py:148
  139.3 3.4 %collective-permute-start.27 = (f32[16,128]{1,0:T(8,128)S(1)}, f32[16,128]{1,0:T(8,128)S(1)}, u32[]{:S(2)}, u32[]{:S(2)}) collective-permute-start(f32[16,128]{1,0:T(8,128)S(1)} %pad_maximum_fusion.4.own), channel_id=1, source_target_pairs={{0,4},{4,0},{8,12},{12,8},{1,5},{5,1},{9,13},{13,9},{2,6},{6,2},{1... | collective-permute-start | bytes 24584 | tf_op jit(solution)/shard_map/route_tables/ppermute | solution.py:148
  142.7 2.4 %collective-permute-start.29 = (f32[16,128]{1,0:T(8,128)S(1)}, f32[16,128]{1,0:T(8,128)S(1)}, u32[]{:S(2)}, u32[]{:S(2)}) collective-permute-start(f32[16,128]{1,0:T(8,128)S(1)} %pad_maximum_fusion.4.own), channel_id=1, source_target_pairs={{0,12},{4,8},{8,4},{12,0},{1,13},{5,9},{9,5},{13,1},{2,14},{6,10},... | collective-permute-start | bytes 24584 | tf_op jit(solution)/shard_map/route_tables/ppermute | solution.py:148
  145.2 2.1 collective-permute-done.28.rest_1_
  147.3 0.9 collective-permute-done.29.rest_2_
  148.2 1.4 routing.1
  149.6 1.1 copy-done.1
  150.7 1.1 copy-done.2
  151.7 0.8 copy-done.3
  152.6 0.8 copy-done.13
  153.4 33.6 %experts.1 = (bf16[4,512,512]{2,1,0:T(8,128)(2,1)}, bf16[128,512]{1,0:T(8,128)(2,1)S(1)}) custom-call(s32[3]{0:T(128)S(1)} %copy-done.9, f32[1,2048]{1,0:T(1,128)S(1)} %bitcast.51, bf16[4,128,512]{2,1,0:T(8,128)(2,1)S(1)} %pad_maximum_fusion.1.r0, bf16[4,128,512]{2,1,0:T(8,128)(2,1)S(1)} %collective-permute-done.24.r1, ...), custom_call_target="tpu_custom_call" | custom-call | tf_op jit(solution)/shard_map/experts/pallas_call | solution.py:454
  187.0 2.2 slice_bitcast_fusion.1
  189.2 0.5 collective-permute-start.30
  189.7 2.1 collective-permute-done.31
  191.9 0.1 fusion
  192.0 1.2 collective-permute-start.32
  193.2 12.9 %collective-permute-done.32 = bf16[512,512]{1,0:T(8,128)(2,1)} collective-permute-done((bf16[512,512]{1,0:T(8,128)(2,1)S(1)}, bf16[512,512]{1,0:T(8,128)(2,1)}, u32[]{:S(2)}, u32[]{:S(2)}) %collective-permute-start.32) | collective-permute-done | bytes 524320 | tf_op jit(solution)/shard_map/sum_over_head/ppermute | solution.py:148
  206.1 1.3 add_convert_fusion
  207.5 3.0 %collective-permute-start.34 = (bf16[128,512]{1,0:T(8,128)(2,1)S(1)}, bf16[128,512]{1,0:T(8,128)(2,1)S(1)}, u32[]{:S(2)}, u32[]{:S(2)}) collective-permute-start(bf16[128,512]{1,0:T(8,128)(2,1)S(1)} %get-tuple-element.33), channel_id=1, source_target_pairs={{0,8},{4,12},{8,0},{12,4},{1,9},{5,13},{9,1},{13,5},{2,10},{6,14},... | collective-permute-start | bytes 393224 | tf_op jit(solution)/shard_map/sum_over_seq/ppermute | solution.py:148
  210.5 1.4 collective-permute-start.35
  211.9 2.2 collective-permute-done.33
  214.1 6.1 %collective-permute-done.34 = bf16[128,512]{1,0:T(8,128)(2,1)S(1)} collective-permute-done((bf16[128,512]{1,0:T(8,128)(2,1)S(1)}, bf16[128,512]{1,0:T(8,128)(2,1)S(1)}, u32[]{:S(2)}, u32[]{:S(2)}) %collective-permute-start.34) | collective-permute-done | bytes 131104 | tf_op jit(solution)/shard_map/sum_over_seq/ppermute | solution.py:148
  220.3 6.9 %all_gather.3 = bf16[128,2048]{1,0:T(8,128)(2,1)S(1)} all-gather(bf16[128,512]{1,0:T(8,128)(2,1)S(1)} %fusion.5), channel_id=1, replica_groups=mesh['grp'=2,'seq'=4,'head'=4] {'head'}, dimensions={1}, use_global_device_ids=true | all-gather | bytes 655360 | tf_op jit(solution)/shard_map/gather_columns/all_gather | solution.py:500
  227.2 0.8 copy.11
  (61 shorter events, 0.6 us)
Async XLA Ops:
  0.7 85.8 %copy-start = (bf16[128,2048]{1,0:T(8,128)(2,1)S(1)}, bf16[128,2048]{1,0:T(8,128)(2,1)}, u32[]{:S(2)}) copy-start(bf16[128,2048]{1,0:T(8,128)(2,1)} %tokens.3) | copy-start | bytes 1572868
  0.7 85.8 %copy-start.9 = (s32[3]{0:T(128)S(1)}, s32[3]{0:T(128)}, u32[]{:S(2)}) copy-start(s32[3]{0:T(128)} %pad_add_fusion.pos) | copy-start | bytes 40
  0.7 85.8 %copy-start.10 = (f32[2048]{0:T(1024)S(1)}, f32[2048]{0:T(1024)}, u32[]{:S(2)}) copy-start(f32[2048]{0:T(1024)} %param.11) | copy-start | bytes 24580
  36.4 50.0 %copy-start.4 = (bf16[512,384]{1,0:T(8,128)(2,1)S(1)}, bf16[512,384]{1,0:T(8,128)(2,1)}, u32[]{:S(2)}) copy-start(bf16[512,384]{1,0:T(8,128)(2,1)} %get-tuple-element.17.w_own) | copy-start | bytes 1179652
  36.4 8.5 %collective-permute-start = (bf16[128,512]{1,0:T(8,128)(2,1)}, bf16[128,512]{1,0:T(8,128)(2,1)S(1)}, u32[]{:S(2)}, u32[]{:S(2)}) collective-permute-start(bf16[128,512]{1,0:T(8,128)(2,1)} %get-tuple-element.18), channel_id=1, source_target_pairs={{0,4},{4,0},{8,12},{12,8},{1,5},{5,1},{9,13},{13,9},{2,6},{6,2},{1... | collective-permute-start | bytes 393224 | tf_op jit(solution)/shard_map/gather_tokens/ppermute | solution.py:148
  39.5 13.2 %collective-permute-start.1 = (bf16[128,512]{1,0:T(8,128)(2,1)}, bf16[128,512]{1,0:T(8,128)(2,1)S(1)}, u32[]{:S(2)}, u32[]{:S(2)}) collective-permute-start(bf16[128,512]{1,0:T(8,128)(2,1)} %get-tuple-element.18), channel_id=1, source_target_pairs={{0,8},{4,12},{8,0},{12,4},{1,9},{5,13},{9,1},{13,5},{2,10},{6,14},... | collective-permute-start | bytes 393224 | tf_op jit(solution)/shard_map/gather_tokens/ppermute | solution.py:148
  42.1 10.6 %collective-permute-start.2 = (bf16[128,512]{1,0:T(8,128)(2,1)}, bf16[128,512]{1,0:T(8,128)(2,1)S(1)}, u32[]{:S(2)}, u32[]{:S(2)}) collective-permute-start(bf16[128,512]{1,0:T(8,128)(2,1)} %get-tuple-element.18), channel_id=1, source_target_pairs={{0,12},{4,8},{8,4},{12,0},{1,13},{5,9},{9,5},{13,1},{2,14},{6,10},... | collective-permute-start | bytes 393224 | tf_op jit(solution)/shard_map/gather_tokens/ppermute | solution.py:148
  43.2 34.9 %collective-permute-start.13 = (bf16[512,512]{1,0:T(8,128)(2,1)S(1)}, bf16[512,512]{1,0:T(8,128)(2,1)}, u32[]{:S(2)}, u32[]{:S(2)}) collective-permute-start(bf16[512,512]{1,0:T(8,128)(2,1)S(1)} %slice_bitcast_fusion.2.w_own), channel_id=1, source_target_pairs={{0,2},{1,3},{2,0},{3,1},{4,6},{5,7},{6,4},{7,5},{8,10},{9,11},{10,... | collective-permute-start | bytes 1572872 | tf_op jit(solution)/shard_map/gather_out_weights/ppermute | solution.py:148
  52.7 20.0 %collective-permute-start.4 = (bf16[3,128,512]{2,1,0:T(8,128)(2,1)S(1)}, bf16[3,128,512]{2,1,0:T(8,128)(2,1)S(1)}, u32[]{:S(2)}, u32[]{:S(2)}) collective-permute-start(bf16[3,128,512]{2,1,0:T(8,128)(2,1)S(1)} %pad_maximum_fusion.2.rest_0_), channel_id=1, source_target_pairs={{0,2},{1,3},{2,0},{3,1},{4,6},{5,7},{6,4},{7,5},{8,10},{9,11},{10,... | collective-permute-start | bytes 1179656 | tf_op jit(solution)/shard_map/gather_tokens/ppermute | solution.py:148
  54.3 16.4 %collective-permute-start.7 = (bf16[256,384]{1,0:T(8,128)(2,1)}, bf16[256,384]{1,0:T(8,128)(2,1)S(1)}, u32[]{:S(2)}, u32[]{:S(2)}) collective-permute-start(bf16[256,384]{1,0:T(8,128)(2,1)} %get-tuple-element.20), channel_id=1, source_target_pairs={{0,8},{4,12},{8,0},{12,4},{1,9},{5,13},{9,1},{13,5},{2,10},{6,14},... | collective-permute-start | bytes 589832 | tf_op jit(solution)/shard_map/gather_head_weights/ppermute | solution.py:148
  57.2 15.0 %collective-permute-start.8 = (bf16[256,384]{1,0:T(8,128)(2,1)}, bf16[256,384]{1,0:T(8,128)(2,1)S(1)}, u32[]{:S(2)}, u32[]{:S(2)}) collective-permute-start(bf16[256,384]{1,0:T(8,128)(2,1)} %get-tuple-element.21), channel_id=1, source_target_pairs={{0,12},{4,8},{8,4},{12,0},{1,13},{5,9},{9,5},{13,1},{2,14},{6,10},... | collective-permute-start | bytes 589832 | tf_op jit(solution)/shard_map/gather_head_weights/ppermute | solution.py:148
  58.6 14.1 %collective-permute-start.6 = (bf16[256,384]{1,0:T(8,128)(2,1)}, bf16[256,384]{1,0:T(8,128)(2,1)}, u32[]{:S(2)}, u32[]{:S(2)}) collective-permute-start(bf16[256,384]{1,0:T(8,128)(2,1)} %get-tuple-element.19), channel_id=1, source_target_pairs={{0,4},{4,0},{8,12},{12,8},{1,5},{5,1},{9,13},{13,9},{2,6},{6,2},{1... | collective-permute-start | bytes 589832 | tf_op jit(solution)/shard_map/gather_head_weights/ppermute | solution.py:148
  70.7 6.7 %collective-permute-start.10 = (bf16[256,384]{1,0:T(8,128)(2,1)S(1)}, bf16[256,384]{1,0:T(8,128)(2,1)S(1)}, u32[]{:S(2)}, u32[]{:S(2)}) collective-permute-start(bf16[256,384]{1,0:T(8,128)(2,1)S(1)} %collective-permute-done.7.rest_5_), channel_id=1, source_target_pairs={{0,16},{16,0},{1,17},{17,1},{2,18},{18,2},{3,19},{19,3},{4,20},{20... | collective-permute-start | bytes 589832 | tf_op jit(solution)/shard_map/gather_head_weights/ppermute | solution.py:148
  72.3 7.2 %collective-permute-start.11 = (bf16[256,384]{1,0:T(8,128)(2,1)S(1)}, bf16[256,384]{1,0:T(8,128)(2,1)S(1)}, u32[]{:S(2)}, u32[]{:S(2)}) collective-permute-start(bf16[256,384]{1,0:T(8,128)(2,1)S(1)} %collective-permute-done.8.rest_6_), channel_id=1, source_target_pairs={{0,16},{16,0},{1,17},{17,1},{2,18},{18,2},{3,19},{19,3},{4,20},{20... | collective-permute-start | bytes 589832 | tf_op jit(solution)/shard_map/gather_head_weights/ppermute | solution.py:148
  72.8 13.6 %collective-permute-start.3 = (bf16[3,128,512]{2,1,0:T(8,128)(2,1)S(1)}, bf16[3,128,512]{2,1,0:T(8,128)(2,1)S(1)}, u32[]{:S(2)}, u32[]{:S(2)}) collective-permute-start(bf16[3,128,512]{2,1,0:T(8,128)(2,1)S(1)} %pad_maximum_fusion.2.rest_0_), channel_id=1, source_target_pairs={{0,1},{1,0},{2,3},{3,2},{4,5},{5,4},{6,7},{7,6},{8,9},{9,8},{10,11... | collective-permute-start | bytes 1179656 | tf_op jit(solution)/shard_map/gather_tokens/ppermute | solution.py:148
  72.8 13.6 %collective-permute-start.5 = (bf16[3,128,512]{2,1,0:T(8,128)(2,1)S(1)}, bf16[3,128,512]{2,1,0:T(8,128)(2,1)S(1)}, u32[]{:S(2)}, u32[]{:S(2)}) collective-permute-start(bf16[3,128,512]{2,1,0:T(8,128)(2,1)S(1)} %collective-permute-done.4.rest_2_), channel_id=1, source_target_pairs={{0,1},{1,0},{2,3},{3,2},{4,5},{5,4},{6,7},{7,6},{8,9},{9,8},{10,11... | collective-permute-start | bytes 1179656 | tf_op jit(solution)/shard_map/gather_tokens/ppermute | solution.py:148
  77.4 0.7 copy-start.5
  78.1 23.9 %collective-permute-start.12 = (bf16[512,512]{1,0:T(8,128)(2,1)S(1)}, bf16[512,512]{1,0:T(8,128)(2,1)}, u32[]{:S(2)}, u32[]{:S(2)}) collective-permute-start(bf16[512,512]{1,0:T(8,128)(2,1)S(1)} %slice_bitcast_fusion.2.w_own), channel_id=1, source_target_pairs={{0,1},{1,0},{2,3},{3,2},{4,5},{5,4},{6,7},{7,6},{8,9},{9,8},{10,11... | collective-permute-start | bytes 1572872 | tf_op jit(solution)/shard_map/gather_out_weights/ppermute | solution.py:148
  78.1 23.9 %collective-permute-start.14 = (bf16[512,512]{1,0:T(8,128)(2,1)}, bf16[512,512]{1,0:T(8,128)(2,1)}, u32[]{:S(2)}, u32[]{:S(2)}) collective-permute-start(bf16[512,512]{1,0:T(8,128)(2,1)} %collective-permute-done.13), channel_id=1, source_target_pairs={{0,1},{1,0},{2,3},{3,2},{4,5},{5,4},{6,7},{7,6},{8,9},{9,8},{10,11... | collective-permute-start | bytes 1572872 | tf_op jit(solution)/shard_map/gather_out_weights/ppermute | solution.py:148
  79.5 0.7 copy-start.7
  80.2 6.2 %collective-permute-start.9 = (bf16[256,384]{1,0:T(8,128)(2,1)}, bf16[256,384]{1,0:T(8,128)(2,1)}, u32[]{:S(2)}, u32[]{:S(2)}) collective-permute-start(bf16[256,384]{1,0:T(8,128)(2,1)} %collective-permute-done.6.rest_4_), channel_id=1, source_target_pairs={{0,16},{16,0},{1,17},{17,1},{2,18},{18,2},{3,19},{19,3},{4,20},{20... | collective-permute-start | bytes 589832 | tf_op jit(solution)/shard_map/gather_head_weights/ppermute | solution.py:148
  86.4 0.9 copy-start.6
  87.4 0.9 copy-start.8
  93.1 1.9 collective-permute-start.15
  93.2 4.3 %collective-permute-start.16 = (bf16[128,128]{1,0:T(8,128)(2,1)S(1)}, bf16[128,128]{1,0:T(8,128)(2,1)S(1)}, u32[]{:S(2)}, u32[]{:S(2)}) collective-permute-start(bf16[128,128]{1,0:T(8,128)(2,1)S(1)} %get-tuple-element.36), channel_id=1, source_target_pairs={{0,2},{1,3},{2,0},{3,1},{4,6},{5,7},{6,4},{7,5},{8,10},{9,11},{10,... | collective-permute-start | bytes 98312 | tf_op jit(solution)/shard_map/heads_to_tokens/ppermute | solution.py:148
  93.8 3.7 %collective-permute-start.17 = (bf16[128,128]{1,0:T(8,128)(2,1)S(1)}, bf16[128,128]{1,0:T(8,128)(2,1)S(1)}, u32[]{:S(2)}, u32[]{:S(2)}) collective-permute-start(bf16[128,128]{1,0:T(8,128)(2,1)S(1)} %get-tuple-element.35), channel_id=1, source_target_pairs={{0,3},{1,2},{2,1},{3,0},{4,7},{5,6},{6,5},{7,4},{8,11},{9,10},{10,... | collective-permute-start | bytes 98312 | tf_op jit(solution)/shard_map/heads_to_tokens/ppermute | solution.py:148
  97.5 7.2 %collective-permute-start.18 = (bf16[4,128,128]{2,1,0:T(8,128)(2,1)S(1)}, bf16[4,128,128]{2,1,0:T(8,128)(2,1)S(1)}, u32[]{:S(2)}, u32[]{:S(2)}) collective-permute-start(bf16[4,128,128]{2,1,0:T(8,128)(2,1)S(1)} %pad_maximum_fusion.3.rest_0_), channel_id=1, source_target_pairs={{0,4},{4,0},{8,12},{12,8},{1,5},{5,1},{9,13},{13,9},{2,6},{6,2},{1... | collective-permute-start | bytes 393224 | tf_op jit(solution)/shard_map/heads_to_tokens/ppermute | solution.py:148
  98.1 12.9 %collective-permute-start.19 = (bf16[4,128,128]{2,1,0:T(8,128)(2,1)S(1)}, bf16[4,128,128]{2,1,0:T(8,128)(2,1)S(1)}, u32[]{:S(2)}, u32[]{:S(2)}) collective-permute-start(bf16[4,128,128]{2,1,0:T(8,128)(2,1)S(1)} %pad_maximum_fusion.3.rest_0_), channel_id=1, source_target_pairs={{0,8},{4,12},{8,0},{12,4},{1,9},{5,13},{9,1},{13,5},{2,10},{6,14},... | collective-permute-start | bytes 393224 | tf_op jit(solution)/shard_map/heads_to_tokens/ppermute | solution.py:148
  99.4 11.6 %collective-permute-start.20 = (bf16[4,128,128]{2,1,0:T(8,128)(2,1)S(1)}, bf16[4,128,128]{2,1,0:T(8,128)(2,1)S(1)}, u32[]{:S(2)}, u32[]{:S(2)}) collective-permute-start(bf16[4,128,128]{2,1,0:T(8,128)(2,1)S(1)} %pad_maximum_fusion.3.rest_0_), channel_id=1, source_target_pairs={{0,12},{4,8},{8,4},{12,0},{1,13},{5,9},{9,5},{13,1},{2,14},{6,10},... | collective-permute-start | bytes 393224 | tf_op jit(solution)/shard_map/heads_to_tokens/ppermute | solution.py:148
  103.5 35.7 %copy-start.14 = (s32[128,8]{0,1:T(8,128)S(1)}, s32[128,8]{0,1:T(8,128)}, u32[]{:S(2)}) copy-start(s32[128,8]{0,1:T(8,128)} %param.13) | copy-start | bytes 12292
  103.5 35.7 %copy-start.15 = (f32[128,8]{0,1:T(8,128)S(1)}, f32[128,8]{0,1:T(8,128)}, u32[]{:S(2)}) copy-start(f32[128,8]{0,1:T(8,128)} %param.14) | copy-start | bytes 12292
  103.5 49.9 %copy-start.11 = (f32[2048]{0:T(1024)S(1)}, f32[2048]{0:T(1024)}, u32[]{:S(2)}) copy-start(f32[2048]{0:T(1024)} %param.12) | copy-start | bytes 24580
  113.1 6.3 %collective-permute-start.21 = (bf16[128,512]{1,0:T(8,128)(2,1)S(1)}, bf16[128,512]{1,0:T(8,128)(2,1)S(1)}, u32[]{:S(2)}, u32[]{:S(2)}) collective-permute-start(bf16[128,512]{1,0:T(8,128)(2,1)S(1)} %output_projection.1), channel_id=1, source_target_pairs={{0,4},{4,0},{8,12},{12,8},{1,5},{5,1},{9,13},{13,9},{2,6},{6,2},{1... | collective-permute-start | bytes 393224 | tf_op jit(solution)/shard_map/gather_residual/ppermute | solution.py:148
  115.4 11.7 %collective-permute-start.22 = (bf16[128,512]{1,0:T(8,128)(2,1)S(1)}, bf16[128,512]{1,0:T(8,128)(2,1)S(1)}, u32[]{:S(2)}, u32[]{:S(2)}) collective-permute-start(bf16[128,512]{1,0:T(8,128)(2,1)S(1)} %output_projection.1), channel_id=1, source_target_pairs={{0,8},{4,12},{8,0},{12,4},{1,9},{5,13},{9,1},{13,5},{2,10},{6,14},... | collective-permute-start | bytes 393224 | tf_op jit(solution)/shard_map/gather_residual/ppermute | solution.py:148
  115.6 11.6 %collective-permute-start.23 = (bf16[128,512]{1,0:T(8,128)(2,1)S(1)}, bf16[128,512]{1,0:T(8,128)(2,1)S(1)}, u32[]{:S(2)}, u32[]{:S(2)}) collective-permute-start(bf16[128,512]{1,0:T(8,128)(2,1)S(1)} %output_projection.1), channel_id=1, source_target_pairs={{0,12},{4,8},{8,4},{12,0},{1,13},{5,9},{9,5},{13,1},{2,14},{6,10},... | collective-permute-start | bytes 393224 | tf_op jit(solution)/shard_map/gather_residual/ppermute | solution.py:148
  127.2 12.0 %collective-permute-start.25 = (bf16[4,128,512]{2,1,0:T(8,128)(2,1)S(1)}, bf16[4,128,512]{2,1,0:T(8,128)(2,1)S(1)}, u32[]{:S(2)}, u32[]{:S(2)}) collective-permute-start(bf16[4,128,512]{2,1,0:T(8,128)(2,1)S(1)} %pad_maximum_fusion.1.r0), channel_id=1, source_target_pairs={{0,2},{1,3},{2,0},{3,1},{4,6},{5,7},{6,4},{7,5},{8,10},{9,11},{10,... | collective-permute-start | bytes 1572872 | tf_op jit(solution)/shard_map/gather_residual/ppermute | solution.py:148
  128.4 24.2 %collective-permute-start.24 = (bf16[4,128,512]{2,1,0:T(8,128)(2,1)S(1)}, bf16[4,128,512]{2,1,0:T(8,128)(2,1)S(1)}, u32[]{:S(2)}, u32[]{:S(2)}) collective-permute-start(bf16[4,128,512]{2,1,0:T(8,128)(2,1)S(1)} %pad_maximum_fusion.1.r0), channel_id=1, source_target_pairs={{0,1},{1,0},{2,3},{3,2},{4,5},{5,4},{6,7},{7,6},{8,9},{9,8},{10,11... | collective-permute-start | bytes 1572872 | tf_op jit(solution)/shard_map/gather_residual/ppermute | solution.py:148
  139.2 13.4 %collective-permute-start.26 = (bf16[4,128,512]{2,1,0:T(8,128)(2,1)S(1)}, bf16[4,128,512]{2,1,0:T(8,128)(2,1)S(1)}, u32[]{:S(2)}, u32[]{:S(2)}) collective-permute-start(bf16[4,128,512]{2,1,0:T(8,128)(2,1)S(1)} %collective-permute-done.25.r2), channel_id=1, source_target_pairs={{0,1},{1,0},{2,3},{3,2},{4,5},{5,4},{6,7},{7,6},{8,9},{9,8},{10,11... | collective-permute-start | bytes 1572872 | tf_op jit(solution)/shard_map/gather_residual/ppermute | solution.py:148
  139.3 5.9 %collective-permute-start.27 = (f32[16,128]{1,0:T(8,128)S(1)}, f32[16,128]{1,0:T(8,128)S(1)}, u32[]{:S(2)}, u32[]{:S(2)}) collective-permute-start(f32[16,128]{1,0:T(8,128)S(1)} %pad_maximum_fusion.4.own), channel_id=1, source_target_pairs={{0,4},{4,0},{8,12},{12,8},{1,5},{5,1},{9,13},{13,9},{2,6},{6,2},{1... | collective-permute-start | bytes 24584 | tf_op jit(solution)/shard_map/route_tables/ppermute | solution.py:148
  142.7 4.5 %collective-permute-start.28 = (f32[16,128]{1,0:T(8,128)S(1)}, f32[16,128]{1,0:T(8,128)S(1)}, u32[]{:S(2)}, u32[]{:S(2)}) collective-permute-start(f32[16,128]{1,0:T(8,128)S(1)} %pad_maximum_fusion.4.own), channel_id=1, source_target_pairs={{0,8},{4,12},{8,0},{12,4},{1,9},{5,13},{9,1},{13,5},{2,10},{6,14},... | collective-permute-start | bytes 24584 | tf_op jit(solution)/shard_map/route_tables/ppermute | solution.py:148
  142.7 5.4 %collective-permute-start.29 = (f32[16,128]{1,0:T(8,128)S(1)}, f32[16,128]{1,0:T(8,128)S(1)}, u32[]{:S(2)}, u32[]{:S(2)}) collective-permute-start(f32[16,128]{1,0:T(8,128)S(1)} %pad_maximum_fusion.4.own), channel_id=1, source_target_pairs={{0,12},{4,8},{8,4},{12,0},{1,13},{5,9},{9,5},{13,1},{2,14},{6,10},... | collective-permute-start | bytes 24584 | tf_op jit(solution)/shard_map/route_tables/ppermute | solution.py:148
  149.6 1.1 copy-start.1
  150.7 1.1 copy-start.2
  151.7 0.8 copy-start.3
  152.6 0.8 copy-start.13
  187.0 4.9 %copy-start.12 = (bf16[4,512,512]{2,1,0:T(8,128)(2,1)S(1)}, bf16[4,512,512]{2,1,0:T(8,128)(2,1)}, u32[]{:S(2)}) copy-start(bf16[4,512,512]{2,1,0:T(8,128)(2,1)} %get-tuple-element.28) | copy-start | bytes 6291460
  189.2 2.6 %collective-permute-start.31 = (bf16[512,512]{1,0:T(8,128)(2,1)S(1)}, bf16[512,512]{1,0:T(8,128)(2,1)S(1)}, u32[]{:S(2)}, u32[]{:S(2)}) collective-permute-start(bf16[512,512]{1,0:T(8,128)(2,1)S(1)} %get-tuple-element.30), channel_id=1, source_target_pairs={{0,1},{1,0},{2,3},{3,2},{4,5},{5,4},{6,7},{7,6},{8,9},{9,8},{10,11... | collective-permute-start | bytes 1572872 | tf_op jit(solution)/shard_map/sum_over_head/ppermute | solution.py:148
  189.2 4.0 %collective-permute-start.30 = (bf16[512,512]{1,0:T(8,128)(2,1)}, bf16[512,512]{1,0:T(8,128)(2,1)S(1)}, u32[]{:S(2)}, u32[]{:S(2)}) collective-permute-start(bf16[512,512]{1,0:T(8,128)(2,1)} %get-tuple-element.29), channel_id=1, source_target_pairs={{0,1},{1,0},{2,3},{3,2},{4,5},{5,4},{6,7},{7,6},{8,9},{9,8},{10,11... | collective-permute-start | bytes 1572872 | tf_op jit(solution)/shard_map/sum_over_head/ppermute | solution.py:148
  192.0 14.1 %collective-permute-start.32 = (bf16[512,512]{1,0:T(8,128)(2,1)S(1)}, bf16[512,512]{1,0:T(8,128)(2,1)}, u32[]{:S(2)}, u32[]{:S(2)}) collective-permute-start(bf16[512,512]{1,0:T(8,128)(2,1)S(1)} %fusion), channel_id=1, source_target_pairs={{0,2},{1,3},{2,0},{3,1},{4,6},{5,7},{6,4},{7,5},{8,10},{9,11},{10,... | collective-permute-start | bytes 1572872 | tf_op jit(solution)/shard_map/sum_over_head/ppermute | solution.py:148
  207.5 6.7 %collective-permute-start.33 = (bf16[128,512]{1,0:T(8,128)(2,1)S(1)}, bf16[128,512]{1,0:T(8,128)(2,1)S(1)}, u32[]{:S(2)}, u32[]{:S(2)}) collective-permute-start(bf16[128,512]{1,0:T(8,128)(2,1)S(1)} %get-tuple-element.31), channel_id=1, source_target_pairs={{0,4},{4,0},{8,12},{12,8},{1,5},{5,1},{9,13},{13,9},{2,6},{6,2},{1... | collective-permute-start | bytes 393224 | tf_op jit(solution)/shard_map/sum_over_seq/ppermute | solution.py:148
  207.5 12.7 %collective-permute-start.34 = (bf16[128,512]{1,0:T(8,128)(2,1)S(1)}, bf16[128,512]{1,0:T(8,128)(2,1)S(1)}, u32[]{:S(2)}, u32[]{:S(2)}) collective-permute-start(bf16[128,512]{1,0:T(8,128)(2,1)S(1)} %get-tuple-element.33), channel_id=1, source_target_pairs={{0,8},{4,12},{8,0},{12,4},{1,9},{5,13},{9,1},{13,5},{2,10},{6,14},... | collective-permute-start | bytes 393224 | tf_op jit(solution)/shard_map/sum_over_seq/ppermute | solution.py:148
  210.5 9.7 %collective-permute-start.35 = (bf16[128,512]{1,0:T(8,128)(2,1)S(1)}, bf16[128,512]{1,0:T(8,128)(2,1)S(1)}, u32[]{:S(2)}, u32[]{:S(2)}) collective-permute-start(bf16[128,512]{1,0:T(8,128)(2,1)S(1)} %get-tuple-element.32), channel_id=1, source_target_pairs={{0,12},{4,8},{8,4},{12,0},{1,13},{5,9},{9,5},{13,1},{2,14},{6,10},... | collective-permute-start | bytes 393224 | tf_op jit(solution)/shard_map/sum_over_seq/ppermute | solution.py:148

commit v2 on v1

--- a/solution.py
+++ b/solution.py
@@ -155,11 +155,14 @@
         copy.wait()
 
 
-def prep_kernel(n, pos, tokens, weight, x_send, w_own, *rest):
+def after(array, *earlier):
+    return lax.optimization_barrier((array,) + earlier)[0]
+
+
+def cut_kernel(pos, tokens, weight, x_send, w_own, *rest):
     w_sends, sems = rest[:-1], rest[-1]
     g, s, h = pos[0], pos[1], pos[2]
-    rows, cols = x_send.shape
-    depth, half = w_own.shape[0], w_sends[0].shape[0]
+    cols, half = x_send.shape[1], w_sends[0].shape[0]
     copies = [
         (tokens.at[:, pl.ds(pl.multiple_of(h * cols, cols), cols)], x_send),
     ]
@@ -167,13 +170,9 @@
         span = pl.ds(which * HEAD_DIM, HEAD_DIM)
         for distance, out in enumerate(w_sends, 1):
             column = pl.multiple_of((s ^ distance) * HEAD_DIM, HEAD_DIM)
+            own_half = pl.ds(pl.multiple_of(g * half, half), half)
             copies.append(
-                (
-                    weight.at[
-                        which, pl.ds(pl.multiple_of(g * half, half), half), pl.ds(column, HEAD_DIM)
-                    ],
-                    out.at[:, span],
-                )
+                (weight.at[which, own_half, pl.ds(column, HEAD_DIM)], out.at[:, span])
             )
         column = pl.multiple_of(s * HEAD_DIM, HEAD_DIM)
         copies.append((weight.at[which, :, pl.ds(column, HEAD_DIM)], w_own.at[:, span]))
@@ -235,14 +234,13 @@
     x_share[...] = x_all[at_rows(h, rows), at_rows(s, cols)]
 
 
-def project_kernel(n, pos, x_share, w_own, w_others, *rest):
-    pieces, (out, a_all, w_all, sems) = rest[:n], rest[n:]
+def project_kernel(n, pos, x_share, *rest):
+    weights, pieces, (out, a_all, w_all, sems) = rest[:n], rest[n : 2 * n], rest[2 * n :]
     s, h = pos[1], pos[2]
-    cols = w_own.shape[1]
+    cols = weights[0].shape[1]
     copies = []
     for e in range(n):
-        source = w_own if e == 0 else w_others.at[e - 1]
-        copies.append((source, w_all.at[:, pl.ds(pl.multiple_of((h ^ e) * cols, cols), cols)]))
+        copies.append((weights[e], w_all.at[:, pl.ds(pl.multiple_of((h ^ e) * cols, cols), cols)]))
         for d in range(n):
             head = (h ^ e) * n + (s ^ d)
             span = pl.ds(pl.multiple_of(head * HEAD_DIM, HEAD_DIM), HEAD_DIM)
@@ -296,51 +294,63 @@
         weight[span, :] = jnp.broadcast_to(chosen, (slots, weight.shape[1]))
 
 
-def experts_kernel(
-    n, pos, gain, r0, r1, r2, r3, pick, place, weight, w_gate, w_up, w_down,
-    out, share, r_all, x_slots, y_slots, sems,
-):
-    s, h = pos[1], pos[2]
+def hidden_kernel(n, slots, group, first, last, pos, *refs):
+    refs = list(refs)
+    gain = refs.pop(0)
+    pieces = [refs.pop(0) for _ in range(n)]
+    pick, w_gate, w_up = (refs.pop(0) for _ in range(3))
+    if not first:
+        total_in, square_in = refs.pop(0), refs.pop(0)
+    if last:
+        weight, hidden_out, r_all = refs
+    else:
+        total_out, square_out, r_all = refs
+    h = pos[2]
+    rows = pieces[0].shape[0]
+    hidden = w_gate.shape[2]
+
+    @pl.when(pl.program_id(0) == 0)
+    def _():
+        for e in range(n):
+            r_all[pl.ds(pl.multiple_of((h ^ e) * rows, rows), rows), :] = pieces[e][...]
+
+    taken = jnp.dot(pick[...], r_all[...], preferred_element_type=F32)
+    square = jnp.sum(taken * taken, axis=1, keepdims=True)
+    if not first:
+        square = square + square_in[:, :1]
+    scaled = (taken * gain[...]).astype(BF16)
+    for e in range(group):
+        span = slice(e * slots, (e + 1) * slots)
+        gate_val = jnp.dot(scaled[span], w_gate[e], preferred_element_type=F32)
+        up_val = jnp.dot(scaled[span], w_up[e], preferred_element_type=F32)
+        if not first:
+            gate_val = gate_val + total_in[span, :hidden]
+            up_val = up_val + total_in[span, hidden:]
+        if last:
+            width = n * r_all.shape[1]
+            factor = lax.rsqrt(square[span] / width + EPS)
+            gate_val, up_val = gate_val * factor, up_val * factor
+            value = gate_val * jax.nn.sigmoid(gate_val) * (up_val * weight[span, :1])
+            hidden_out[span, :] = value.astype(BF16)
+        else:
+            total_out[span, :hidden] = gate_val
+            total_out[span, hidden:] = up_val
+    if not last:
+        square_out[...] = jnp.broadcast_to(square, square_out.shape)
+
+
+def down_kernel(n, slots, group, pos, hidden, place, w_down, out, y_slots):
     step = pl.program_id(0)
-    rows, cols = r0.shape[1:]
-    slots = x_slots.shape[0] // pl.num_programs(0)
-
-    def span(block, size):
-        return pl.ds(pl.multiple_of(block * size, size), size)
-
-    @pl.when(step == 0)
-    def _():
-        copies = []
-        for e, piece in enumerate((r0, r1, r2, r3)):
-            for d in range(n):
-                copies.append((piece.at[d], r_all.at[span(h ^ e, rows), span(s ^ d, cols)]))
-        run_copies([pltpu.make_async_copy(a, b, sems.at[i]) for i, (a, b) in enumerate(copies)])
-        share[...] = r_all[span(s, rows), span(h, cols)]
-        for block in range(n):
-            where = slice(block * rows, (block + 1) * rows)
-            wide = r_all[where, :].astype(F32)
-            factor = lax.rsqrt(jnp.mean(wide * wide, axis=-1, keepdims=True) + EPS)
-            r_all[where, :] = (wide * factor * gain[...]).astype(BF16)
-        for block in range(n):
-            where = slice(block * cols, (block + 1) * cols)
-            x_slots[:, where] = jnp.dot(
-                pick[...], r_all[:, where], preferred_element_type=F32
-            ).astype(BF16)
-
-    mine = span(step, slots)
-    taken = x_slots[mine, :]
-    gate_val = jnp.dot(taken, w_gate[0], preferred_element_type=F32)
-    up_val = jnp.dot(taken, w_up[0], preferred_element_type=F32)
-    scale = weight[mine, :1]
-    hidden = (gate_val * jax.nn.sigmoid(gate_val) * up_val * scale).astype(BF16)
-    y_slots[mine, :] = jnp.dot(hidden, w_down[0], preferred_element_type=F32).astype(BF16)
+    for e in range(group):
+        product = jnp.dot(
+            hidden[e * slots : (e + 1) * slots, :], w_down[e], preferred_element_type=F32
+        )
+        row = pl.multiple_of(step * group * slots, group * slots) + e * slots
+        y_slots[pl.ds(pl.multiple_of(row, slots), slots), :] = product.astype(BF16)
 
     @pl.when(step == pl.num_programs(0) - 1)
     def _():
-        for e in range(n):
-            out[e] = jnp.dot(
-                place[...], y_slots[:, span(h ^ e, cols)], preferred_element_type=F32
-            ).astype(BF16)
+        out[...] = jnp.dot(place[...], y_slots[...], preferred_element_type=F32).astype(BF16)
 
 
 def square_body(
@@ -355,52 +365,61 @@
     experts, _, hidden = expert_gate.shape
     total = n * rows
     slots = -(-n * CAP // 16) * 16
+    pairs = experts * slots
     sds = jax.ShapeDtypeStruct
     dma = pltpu.SemaphoreType.DMA
-
+    grid_spec = functools.partial(pltpu.PrefetchScalarGridSpec, num_scalar_prefetch=1)
+
+    def room(mib):
+        return pltpu.CompilerParams(vmem_limit_bytes=mib * MIB)
+
+    def whole(*shape):
+        return pl.BlockSpec(shape, lambda step, pos: (0,) * len(shape))
+
+    def plus(*terms):
+        total_value = terms[0].astype(F32)
+        for term in terms[1:]:
+            total_value = total_value + term.astype(F32)
+        return total_value
+
+    with jax.named_scope("cut_pieces"):
+        x_send, w_own, *w_sends = pl.pallas_call(
+            cut_kernel,
+            out_shape=[sds((rows, cols), BF16), sds((depth, 3 * HEAD_DIM), BF16)]
+            + [sds((half, 3 * HEAD_DIM), BF16)] * (n - 1),
+            in_specs=[SMEM, ANY, ANY],
+            out_specs=[VMEM] * (n + 1),
+            scratch_shapes=[dma((1 + 3 * n,))],
+            compiler_params=room(8),
+        )(pos, tokens, attn_weight)
+    with jax.named_scope("gather_tokens"):
+        x_far = [swap(x_send, "seq", d) for d in range(1, n)]
+        x_pieces = {0: jnp.stack(x_far)}
+        x_pieces[2] = swap(x_pieces[0], "head", 2)
+        for e in (0, 2):
+            x_pieces[e ^ 1] = swap(x_pieces[e], "head", 1)
+    with jax.named_scope("gather_head_weights"):
+        w_near = [swap(w_sends[0], "seq", 1)]
+        w_near += [swap(after(w_sends[d - 1], *x_far), "seq", d) for d in range(2, n)]
+        w_far = [swap(w, "grp", 1) for w in w_near]
     with jax.named_scope("route_tables"):
         table = jnp.concatenate([routes.T.astype(F32), gates.T], axis=0)
         table_others = [swap(table, "seq", d) for d in range(1, n)]
-
-    with jax.named_scope("cut_pieces"):
-        x_send, w_own, *w_sends = pl.pallas_call(
-            functools.partial(prep_kernel, n),
-            out_shape=[sds((rows, cols), BF16), sds((depth, 3 * HEAD_DIM), BF16)]
-            + [sds((half, 3 * HEAD_DIM), BF16)] * (n - 1),
-            in_specs=[SMEM, ANY, ANY],
-            out_specs=[ANY] * (n + 1),
-            scratch_shapes=[dma((1 + 3 * n,))],
-        )(pos, tokens, attn_weight)
-    with jax.named_scope("gather_tokens"):
-        x_near = jnp.stack([swap(x_send, "seq", d) for d in range(1, n)])
-        x_pieces = {0: x_near}
-        for stride in (2, 1):
-            for e in list(x_pieces):
-                x_pieces[e ^ stride] = swap(x_pieces[e], "head", stride)
-    with jax.named_scope("gather_head_weights"):
-        w_near = [swap(w_sends[d - 1], "seq", d) for d in range(1, n)]
-        w_far = [swap(w, "grp", 1) for w in w_near]
-    with jax.named_scope("gather_out_weights"):
-        o_own = attn_weight[3]
-        o_pieces = {0: o_own}
-        for stride in (2, 1):
-            for e in list(o_pieces):
-                o_pieces[e ^ stride] = swap(o_pieces[e], "head", stride)
-        o_others = jnp.stack([o_pieces[e] for e in range(1, n)])
-
     with jax.named_scope("routing"):
         pick, place, weight = pl.pallas_call(
             functools.partial(route_kernel, n, experts, slots),
-            out_shape=[
-                sds((experts * slots, total), BF16),
-                sds((total, experts * slots), BF16),
-                sds((experts * slots, 128), F32),
-            ],
+            out_shape=[sds((pairs, total), BF16), sds((total, pairs), BF16), sds((pairs, 128), F32)],
             in_specs=[SMEM] + [ANY] * n,
             out_specs=[VMEM] * 3,
             scratch_shapes=[pltpu.VMEM((2 * TOPK, total), F32), dma((n,))],
-            compiler_params=pltpu.CompilerParams(vmem_limit_bytes=32 * MIB),
+            compiler_params=room(16),
         )(pos, table, *table_others)
+        w_near[0] = after(w_near[0], pick)
+    with jax.named_scope("gather_out_weights"):
+        o_pieces = {0: after(attn_weight, x_far[0])[3]}
+        o_pieces[2] = swap(after(o_pieces[0], x_pieces[2]), "head", 2)
+        for e in (0, 2):
+            o_pieces[e ^ 1] = swap(o_pieces[e], "head", 1)
 
     with jax.named_scope("attention"):
         attended, x_share = pl.pallas_call(
@@ -413,7 +432,7 @@
                 pltpu.VMEM((width, 3 * HEAD_DIM), BF16),
                 dma((2 + n * (n - 1) + 2 * (n - 1),)),
             ],
-            compiler_params=pltpu.CompilerParams(vmem_limit_bytes=32 * MIB),
+            compiler_params=room(20),
         )(
             pos, attn_gain.reshape(1, width), tokens, w_own,
             *[x_pieces[e] for e in range(n)], *w_near, *w_far,
@@ -423,78 +442,104 @@
         by_block = [
             lax.dynamic_index_in_dim(attended, h ^ e, 0, keepdims=False) for e in range(n)
         ]
-        arrived = jnp.stack(
-            [by_block[0]] + [swap(by_block[e], "head", e) for e in range(1, n)]
-        )
+        arrived = jnp.stack([by_block[0]] + [swap(by_block[e], "head", e) for e in range(1, n)])
         a_pieces = [arrived] + [swap(arrived, "seq", d) for d in range(1, n)]
 
     with jax.named_scope("output_projection"):
         residual = pl.pallas_call(
             functools.partial(project_kernel, n),
             out_shape=sds((rows, cols), BF16),
-            in_specs=[SMEM, VMEM] + [ANY] * (2 + n),
+            in_specs=[SMEM, VMEM] + [ANY] * (2 * n),
             out_specs=VMEM,
             scratch_shapes=[
                 pltpu.VMEM((rows, width), BF16),
                 pltpu.VMEM((depth, width), BF16),
                 dma((n + n * n,)),
             ],
-            compiler_params=pltpu.CompilerParams(vmem_limit_bytes=32 * MIB),
-        )(pos, x_share, o_own, o_others, *a_pieces)
+            compiler_params=room(12),
+        )(pos, x_share, *[o_pieces[e] for e in range(n)], *a_pieces)
 
     with jax.named_scope("gather_residual"):
-        r_near = jnp.stack([residual] + [swap(residual, "seq", d) for d in range(1, n)])
-        r_pieces = {0: r_near}
-        for stride in (2, 1):
-            for e in list(r_pieces):
-                r_pieces[e ^ stride] = swap(r_pieces[e], "head", stride)
-
-    with jax.named_scope("experts"):
-        full = lambda *shape: pl.BlockSpec(shape, lambda e: (0,) * len(shape))
-        out, r_share = pl.pallas_call(
-            functools.partial(experts_kernel, n),
-            grid=(experts,),
-            out_shape=[sds((n, total, cols), BF16), sds((rows, cols), BF16)],
-            in_specs=[SMEM, full(1, width)]
-            + [ANY] * n
-            + [
-                full(experts * slots, total),
-                full(total, experts * slots),
-                full(experts * slots, 128),
-                pl.BlockSpec((1, width, hidden), lambda e: (e, 0, 0)),
-                pl.BlockSpec((1, width, hidden), lambda e: (e, 0, 0)),
-                pl.BlockSpec((1, hidden, width), lambda e: (e, 0, 0)),
-            ],
-            out_specs=[full(n, total, cols), full(rows, cols)],
-            scratch_shapes=[
-                pltpu.VMEM((total, width), BF16),
-                pltpu.VMEM((experts * slots, width), BF16),
-                pltpu.VMEM((experts * slots, width), BF16),
-                dma((n * n,)),
-            ],
-            compiler_params=pltpu.CompilerParams(vmem_limit_bytes=52 * MIB),
-        )(
-            pos, moe_gain.reshape(1, width), *[r_pieces[e] for e in range(n)],
-            pick, place, weight, expert_gate, expert_up, expert_down,
-        )
-
-    def plus(a, b):
-        return (a.astype(F32) + b.astype(F32)).astype(BF16)
-
-    with jax.named_scope("sum_over_head"):
-        parts = {e: out[e] for e in range(n)}
-        for stride in (1, 2):
-            parts = {
-                e: plus(parts[e], swap(parts[e ^ stride], "head", stride))
-                for e in parts
-                if not e & stride
-            }
-        summed = parts[0].reshape(n, rows, cols)
-    with jax.named_scope("sum_over_seq"):
-        blocks = [lax.dynamic_index_in_dim(summed, s ^ d, 0, keepdims=False) for d in range(n)]
-        mixed = r_share.astype(F32) + blocks[0].astype(F32)
-        for d in range(1, n):
-            mixed = mixed + swap(blocks[d], "seq", d).astype(F32)
+        r_pieces = []
+        for d in range(n):
+            r = {0: residual if d == 0 else swap(residual, "seq", d)}
+            r[2] = swap(r[0], "head", 2)
+            for e in (0, 2):
+                r[e ^ 1] = swap(r[e], "head", 1)
+            r_pieces.append(r)
+
+    group = 4
+    block = group * slots
+    state = ()
+    for d in range(n):
+        first, last = d == 0, d == n - 1
+        by_step = lambda size: pl.BlockSpec((block, size), lambda step, pos: (step, 0))
+
+        def columns(step, pos, d=d):
+            return (step, pos[1] ^ d, 0)
+
+        totals = [by_step(2 * hidden), by_step(128)]
+        with jax.named_scope(f"hidden_units_{d}"):
+            state = pl.pallas_call(
+                functools.partial(hidden_kernel, n, slots, group, first, last),
+                out_shape=[sds((pairs, hidden), BF16)]
+                if last
+                else [sds((pairs, 2 * hidden), F32), sds((pairs, 128), F32)],
+                grid_spec=grid_spec(
+                    grid=(experts // group,),
+                    in_specs=[pl.BlockSpec((1, cols), lambda step, pos, d=d: (0, pos[1] ^ d))]
+                    + [whole(rows, cols)] * n
+                    + [by_step(total)]
+                    + [pl.BlockSpec((group, cols, hidden), columns)] * 2
+                    + ([] if first else totals)
+                    + ([by_step(128)] if last else []),
+                    out_specs=[by_step(hidden)] if last else totals,
+                    scratch_shapes=[pltpu.VMEM((total, cols), BF16)],
+                ),
+                compiler_params=room(16),
+            )(
+                pos, moe_gain.reshape(1, width), *[r_pieces[d][e] for e in range(n)],
+                pick, expert_gate, expert_up, *state, *([weight] if last else []),
+            )
+    (units,) = state
+
+    group_down = 8
+    out = {}
+    for e in (3, 2, 1, 0):
+        with jax.named_scope(f"down_quarter_{e}"):
+            out[e] = pl.pallas_call(
+                functools.partial(down_kernel, n, slots, group_down),
+                out_shape=sds((total, cols), BF16),
+                grid_spec=grid_spec(
+                    grid=(experts // group_down,),
+                    in_specs=[
+                        pl.BlockSpec((group_down * slots, hidden), lambda step, pos: (step, 0)),
+                        whole(total, pairs),
+                        pl.BlockSpec(
+                            (group_down, hidden, cols),
+                            lambda step, pos, e=e: (step, 0, pos[2] ^ e),
+                        ),
+                    ],
+                    out_specs=whole(total, cols),
+                    scratch_shapes=[pltpu.VMEM((pairs, cols), BF16)],
+                ),
+                compiler_params=room(16),
+            )(pos, units, place, expert_down)
+
+    def rows_of(array, d):
+        return lax.dynamic_slice_in_dim(array, (s ^ d) * rows, rows, 0)
+
+    with jax.named_scope("sum_over_devices"):
+        from_core = {e: swap(out[e ^ 1], "head", 1) for e in (2, 0)}
+        mixed = lax.select_n(s ^ h, *[r_pieces[d][d] for d in range(n)]).astype(F32)
+        for d in (3, 2, 1, 0):
+            near = plus(rows_of(out[2], d), rows_of(from_core[2], d)).astype(BF16)
+            summed = plus(
+                rows_of(out[0], d), rows_of(from_core[0], d), swap(near, "head", 2)
+            )
+            if d:
+                summed = swap(summed.astype(BF16), "seq", d)
+            mixed = mixed + summed
         mixed = mixed.astype(BF16)
     with jax.named_scope("gather_columns"):
         return lax.all_gather(mixed, "head", axis=1, tiled=True)

time: 228 us -> 212 us (0.930)
  Pallas kernels: 77.6 us -> 44 us
  local copies, waits for them, and re-layouts: 11.2 us -> 41.6 us
  waiting for transfers between devices: 85.8 us -> 61.8 us
  starting transfers between devices: 42.4 us -> 51.7 us
    pallas_call x2 -> x9, Pallas kernels: 69.4 us -> 33.9 us  [the longest x4 21.8 us: square_body(): pl.pallas_call(functools.partial(hidden_kernel, n, slots, group, first, l...]
    unnamed x33 -> x57, local copies, waits for them, and re-layouts: 7.84 us -> 40.5 us
    ppermute x36 -> x48, waiting for transfers between devices: 85.8 us -> 61.8 us  [swap(): return lax.ppermute(array, axis, [(i, i ^ distance) for i in range(size)])]
    ppermute x36 -> x48, starting transfers between devices: 42.4 us -> 51.7 us  [swap(): return lax.ppermute(array, axis, [(i, i ^ distance) for i in range(size)])]
  transfers between devices with their start and end apart: 36 -> 48, of which waited for: 17 -> 18; matrix products, arithmetic and copies ran while one was open for 1% -> 2% of each run, Pallas kernels for 3% -> 15%
where the time goes in v2:
time: 212 us; the launch traced here: 211 us
  waiting for transfers between devices  61.8 us (29%)
  starting transfers between devices  51.7 us (24%)
  Pallas kernels  44 us (21%)
  local copies, waits for them, and re-layouts  41.6 us (20%)
  blocking collectives  6.8 us (3%)
  other arithmetic  4.31 us (2%)
    ppermute x48, waiting for transfers between devices, swap(): return lax.ppermute(array, axis, [(i, i ^ distance) for i in range(size)])  61.8 us
    ppermute x48, starting transfers between devices, swap(): return lax.ppermute(array, axis, [(i, i ^ distance) for i in range(size)])  51.7 us
    unnamed x57, local copies, waits for them, and re-layouts  40.5 us
    pallas_call x4, Pallas kernels, square_body(): pl.pallas_call(functools.partial(hidden_kernel, n, slots, group, first, l...  21.8 us
    pallas_call x4, Pallas kernels, square_body(): pl.pallas_call(functools.partial(down_kernel, n, slots, group_down), out_...  11.1 us
    all_gather x1, blocking collectives, square_body(): return lax.all_gather(mixed, 'head', axis=1, tiled=True)  6.8 us
    pallas_call x1, Pallas kernels, square_body(): pl.pallas_call(functools.partial(attend_kernel, n), out_shape=[sds((n, ro...  5.65 us
  transfers between devices with their start and end apart: 48, of which 18 were waited for; matrix products, arithmetic and copies ran while one was open for 2% of the time, Pallas kernels for 15%

profile of v2, /device:TPU:0, one launch (start us, length us, event | category | flops | bytes accessed | tf_op | source)
XLA Modules:
  0.0 210.7 jit_solution(11745361962313637113)
XLA Ops:
  0.1 1.6 copy-done.5
  1.7 1.0 copy-done.6
  4.4 3.0 %collective-permute-start = (bf16[128,512]{1,0:T(8,128)(2,1)S(1)}, bf16[128,512]{1,0:T(8,128)(2,1)S(1)}, u32[]{:S(2)}, u32[]{:S(2)}) collective-permute-start(bf16[128,512]{1,0:T(8,128)(2,1)S(1)} %get-tuple-element.27), channel_id=1, source_target_pairs={{0,4},{4,0},{8,12},{12,8},{1,5},{5,1},{9,13},{13,9},{2,6},{6,2},{1... | collective-permute-start | bytes 393224 | tf_op jit(solution)/shard_map/gather_tokens/ppermute | solution.py:148
  7.4 2.6 %collective-permute-start.1 = (bf16[128,512]{1,0:T(8,128)(2,1)S(1)}, bf16[128,512]{1,0:T(8,128)(2,1)S(1)}, u32[]{:S(2)}, u32[]{:S(2)}) collective-permute-start(bf16[128,512]{1,0:T(8,128)(2,1)S(1)} %get-tuple-element.27), channel_id=1, source_target_pairs={{0,8},{4,12},{8,0},{12,4},{1,9},{5,13},{9,1},{13,5},{2,10},{6,14},... | collective-permute-start | bytes 393224 | tf_op jit(solution)/shard_map/gather_tokens/ppermute | solution.py:148
  10.0 2.4 %collective-permute-done = bf16[128,512]{1,0:T(8,128)(2,1)S(1)} collective-permute-done((bf16[128,512]{1,0:T(8,128)(2,1)S(1)}, bf16[128,512]{1,0:T(8,128)(2,1)S(1)}, u32[]{:S(2)}, u32[]{:S(2)}) %collective-permute-start) | collective-permute-done | bytes 131104 | tf_op jit(solution)/shard_map/gather_tokens/ppermute | solution.py:148
  12.4 7.9 %collective-permute-done.1 = bf16[128,512]{1,0:T(8,128)(2,1)S(1)} collective-permute-done((bf16[128,512]{1,0:T(8,128)(2,1)S(1)}, bf16[128,512]{1,0:T(8,128)(2,1)S(1)}, u32[]{:S(2)}, u32[]{:S(2)}) %collective-permute-start.1) | collective-permute-done | bytes 131104 | tf_op jit(solution)/shard_map/gather_tokens/ppermute | solution.py:148
  20.4 1.6 collective-permute-start.4
  21.9 2.0 collective-permute-start.6
  24.9 1.1 slice_bitcast_fusion.rest_0_
  26.0 3.7 %collective-permute-done.4.rest_2_ = bf16[3,128,512]{2,1,0:T(8,128)(2,1)} collective-permute-done((bf16[3,128,512]{2,1,0:T(8,128)(2,1)S(1)}, bf16[3,128,512]{2,1,0:T(8,128)(2,1)}, u32[]{:S(2)}, u32[]{:S(2)}) %collective-permute-start.4) | collective-permute-done | bytes 393248 | tf_op jit(solution)/shard_map/gather_tokens/ppermute | solution.py:148
  29.7 1.5 collective-permute-start.16
  31.2 2.3 %collective-permute-start.11 = (bf16[256,384]{1,0:T(8,128)(2,1)S(1)}, bf16[256,384]{1,0:T(8,128)(2,1)}, u32[]{:S(2)}, u32[]{:S(2)}) collective-permute-start(bf16[256,384]{1,0:T(8,128)(2,1)S(1)} %get-tuple-element.34), channel_id=1, source_target_pairs={{0,12},{4,8},{8,4},{12,0},{1,13},{5,9},{9,5},{13,1},{2,14},{6,10},... | collective-permute-start | bytes 589832 | tf_op jit(solution)/shard_map/gather_head_weights/ppermute | solution.py:148
  33.5 2.0 collective-permute-start.7
  35.5 2.5 %collective-permute-done.7.rest_0_ = f32[16,128]{1,0:T(8,128)S(1)} collective-permute-done((f32[16,128]{1,0:T(8,128)S(1)}, f32[16,128]{1,0:T(8,128)S(1)}, u32[]{:S(2)}, u32[]{:S(2)}) %collective-permute-start.7) | collective-permute-done | bytes 8224 | tf_op jit(solution)/shard_map/route_tables/ppermute | solution.py:148
  38.0 1.4 collective-permute-start.8
  39.3 3.5 %collective-permute-done.8.rest_1_ = f32[16,128]{1,0:T(8,128)S(1)} collective-permute-done((f32[16,128]{1,0:T(8,128)S(1)}, f32[16,128]{1,0:T(8,128)S(1)}, u32[]{:S(2)}, u32[]{:S(2)}) %collective-permute-start.8) | collective-permute-done | bytes 8224 | tf_op jit(solution)/shard_map/route_tables/ppermute | solution.py:148
  42.8 2.5 %collective-permute-start.9 = (f32[16,128]{1,0:T(8,128)S(1)}, f32[16,128]{1,0:T(8,128)S(1)}, u32[]{:S(2)}, u32[]{:S(2)}) collective-permute-start(f32[16,128]{1,0:T(8,128)S(1)} %pad_maximum_fusion.2.own), channel_id=1, source_target_pairs={{0,12},{4,8},{8,4},{12,0},{1,13},{5,9},{9,5},{13,1},{2,14},{6,10},... | collective-permute-start | bytes 24584 | tf_op jit(solution)/shard_map/route_tables/ppermute | solution.py:148
  45.4 1.5 collective-permute-start.12
  48.8 1.5 collective-permute-start.13
  51.8 1.5 collective-permute-start.14
  53.3 3.3 %collective-permute-done.13.rest_8_ = bf16[256,384]{1,0:T(8,128)(2,1)S(1)} collective-permute-done((bf16[256,384]{1,0:T(8,128)(2,1)S(1)}, bf16[256,384]{1,0:T(8,128)(2,1)S(1)}, u32[]{:S(2)}, u32[]{:S(2)}) %collective-permute-start.13) | collective-permute-done | bytes 196640 | tf_op jit(solution)/shard_map/gather_head_weights/ppermute | solution.py:148
  57.8 1.4 routing.1
  64.7 5.7 %attention.1 = (bf16[4,128,128]{2,1,0:T(8,128)(2,1)S(1)}, bf16[128,512]{1,0:T(8,128)(2,1)S(1)}) custom-call(s32[3]{0:T(128)S(1)} %pad_add_fusion.pos, f32[1,2048]{1,0:T(1,128)S(1)} %bitcast.28, bf16[128,2048]{1,0:T(8,128)(2,1)S(1)} %copy-done.7, bf16[512,384]{1,0:T(8,128)(2,1)S(1)} %copy-done.11, bf16[3,128,512]{2,1,0:T(8,128)(2,1)S(1)} %pad_maximum_fusion.rest_0_, ...), custom_call_target="tpu_custom_call" | custom-call | tf_op jit(solution)/shard_map/attention/pallas_call | solution.py:425
  71.1 1.3 collective-permute-start.20
  72.4 2.4 %collective-permute-done.19 = bf16[128,128]{1,0:T(8,128)(2,1)S(1)} collective-permute-done((bf16[128,128]{1,0:T(8,128)(2,1)S(1)}, bf16[128,128]{1,0:T(8,128)(2,1)S(1)}, u32[]{:S(2)}, u32[]{:S(2)}) %collective-permute-start.19) | collective-permute-done | bytes 32800 | tf_op jit(solution)/shard_map/heads_to_tokens/ppermute | solution.py:148
  74.9 3.1 %collective-permute-start.22 = (bf16[4,128,128]{2,1,0:T(8,128)(2,1)S(1)}, bf16[4,128,128]{2,1,0:T(8,128)(2,1)S(1)}, u32[]{:S(2)}, u32[]{:S(2)}) collective-permute-start(bf16[4,128,128]{2,1,0:T(8,128)(2,1)S(1)} %pad_maximum_fusion.1.rest_4_), channel_id=1, source_target_pairs={{0,8},{4,12},{8,0},{12,4},{1,9},{5,13},{9,1},{13,5},{2,10},{6,14},... | collective-permute-start | bytes 393224 | tf_op jit(solution)/shard_map/heads_to_tokens/ppermute | solution.py:148
  78.0 1.3 collective-permute-start.23
  79.3 3.5 %collective-permute-done.21.rest_5_ = bf16[4,128,128]{2,1,0:T(8,128)(2,1)S(1)} collective-permute-done((bf16[4,128,128]{2,1,0:T(8,128)(2,1)S(1)}, bf16[4,128,128]{2,1,0:T(8,128)(2,1)S(1)}, u32[]{:S(2)}, u32[]{:S(2)}) %collective-permute-start.21) | collective-permute-done | bytes 131104 | tf_op jit(solution)/shard_map/heads_to_tokens/ppermute | solution.py:148
  82.8 5.2 %collective-permute-done.22.rest_6_ = bf16[4,128,128]{2,1,0:T(8,128)(2,1)S(1)} collective-permute-done((bf16[4,128,128]{2,1,0:T(8,128)(2,1)S(1)}, bf16[4,128,128]{2,1,0:T(8,128)(2,1)S(1)}, u32[]{:S(2)}, u32[]{:S(2)}) %collective-permute-start.22) | collective-permute-done | bytes 131104 | tf_op jit(solution)/shard_map/heads_to_tokens/ppermute | solution.py:148
  88.0 3.1 %output_projection.1.refs_1_ = bf16[128,512]{1,0:T(8,128)(2,1)S(1)} custom-call(s32[3]{0:T(128)S(1)} %pad_add_fusion.pos, bf16[128,512]{1,0:T(8,128)(2,1)S(1)} %get-tuple-element.35.x_share, bf16[512,512]{1,0:T(8,128)(2,1)S(1)} %slice_bitcast_fusion.rest_0_, bf16[512,512]{1,0:T(8,128)(2,1)} %collective-permute-done.15.rest_1_, ...), custom_call_target="tpu_custom_call" | custom-call | tf_op jit(solution)/shard_map/output_projection/pallas_call | solution.py:449
  91.1 2.7 %collective-permute-start.24 = (bf16[128,512]{1,0:T(8,128)(2,1)S(1)}, bf16[128,512]{1,0:T(8,128)(2,1)S(1)}, u32[]{:S(2)}, u32[]{:S(2)}) collective-permute-start(bf16[128,512]{1,0:T(8,128)(2,1)S(1)} %output_projection.1.refs_1_), channel_id=1, source_target_pairs={{0,4},{4,0},{8,12},{12,8},{1,5},{5,1},{9,13},{13,9},{2,6},{6,2},{1... | collective-permute-start | bytes 393224 | tf_op jit(solution)/shard_map/gather_residual/ppermute | solution.py:148
  93.7 1.1 collective-permute-start.37
  94.9 1.1 collective-permute-start.26
  95.9 1.4 collective-permute-start.28
  97.4 1.4 collective-permute-start.34
  98.7 7.9 %collective-permute-done.26.refs_1_ = bf16[128,512]{1,0:T(8,128)(2,1)S(1)} collective-permute-done((bf16[128,512]{1,0:T(8,128)(2,1)S(1)}, bf16[128,512]{1,0:T(8,128)(2,1)S(1)}, u32[]{:S(2)}, u32[]{:S(2)}) %collective-permute-start.26) | collective-permute-done | bytes 131104 | tf_op jit(solution)/shard_map/gather_residual/ppermute | solution.py:148
  107.4 1.3 collective-permute-start.29
  109.3 3.4 %collective-permute-done.27.refs_3_ = bf16[128,512]{1,0:T(8,128)(2,1)S(1)} collective-permute-done((bf16[128,512]{1,0:T(8,128)(2,1)S(1)}, bf16[128,512]{1,0:T(8,128)(2,1)S(1)}, u32[]{:S(2)}, u32[]{:S(2)}) %collective-permute-start.27) | collective-permute-done | bytes 131104 | tf_op jit(solution)/shard_map/gather_residual/ppermute | solution.py:148
  113.2 1.2 collective-permute-done.29.refs_3_
  114.4 5.8 %copy-done.1 = bf16[16,2048,256]{2,1,0:T(8,128)(2,1)S(1)} copy-done((bf16[16,2048,256]{2,1,0:T(8,128)(2,1)S(1)}, bf16[16,2048,256]{2,1,0:T(8,128)(2,1)}, u32[]{:S(2)}) %copy-start.1) | copy-done | bytes 16777240
  120.2 5.8 %copy-done.4 = bf16[16,2048,256]{2,1,0:T(8,128)(2,1)S(1)} copy-done((bf16[16,2048,256]{2,1,0:T(8,128)(2,1)S(1)}, bf16[16,2048,256]{2,1,0:T(8,128)(2,1)}, u32[]{:S(2)}) %copy-start.4) | copy-done | bytes 16777240
  126.0 4.1 %hidden_units_0.1 = (f32[1280,512]{1,0:T(8,128)S(1)}, f32[1280,128]{1,0:T(8,128)S(1)}) custom-call(s32[3]{0:T(128)S(1)} %pad_add_fusion.pos, f32[1,2048]{1,0:T(1,128)S(1)} %bitcast.24, bf16[128,512]{1,0:T(8,128)(2,1)S(1)} %output_projection.1.refs_1_, bf16[128,512]{1,0:T(8,128)(2,1)S(1)} %collective-permute-done.36.refs_2_, ...), custom_call_target="tpu_custom_call" | custom-call | tf_op jit(solution)/shard_map/hidden_units_0/pallas_call | solution.py:483
  130.1 5.8 %copy-done.2 = bf16[16,2048,256]{2,1,0:T(8,128)(2,1)S(1)} copy-done((bf16[16,2048,256]{2,1,0:T(8,128)(2,1)S(1)}, bf16[16,2048,256]{2,1,0:T(8,128)(2,1)}, u32[]{:S(2)}) %copy-start.2) | copy-done | bytes 16777240
  135.9 5.7 %hidden_units_1.1 = (f32[1280,512]{1,0:T(8,128)S(1)}, f32[1280,128]{1,0:T(8,128)S(1)}) custom-call(s32[3]{0:T(128)S(1)} %pad_add_fusion.pos, f32[1,2048]{1,0:T(1,128)S(1)} %bitcast.25, bf16[128,512]{1,0:T(8,128)(2,1)S(1)} %collective-permute-done.24.refs_1_, bf16[128,512]{1,0:T(8,128)(2,1)S(1)} %collective-permute-done.25.refs_2_, ...), custom_call_target="tpu_custom_call" | custom-call | tf_op jit(solution)/shard_map/hidden_units_1/pallas_call | solution.py:483
  141.7 6.0 %hidden_units_2.1 = (f32[1280,512]{1,0:T(8,128)S(1)}, f32[1280,128]{1,0:T(8,128)S(1)}) custom-call(s32[3]{0:T(128)S(1)} %pad_add_fusion.pos, f32[1,2048]{1,0:T(1,128)S(1)} %bitcast.26, bf16[128,512]{1,0:T(8,128)(2,1)S(1)} %collective-permute-done.26.refs_1_, bf16[128,512]{1,0:T(8,128)(2,1)S(1)} %collective-permute-done.32.refs_2_, ...), custom_call_target="tpu_custom_call" | custom-call | tf_op jit(solution)/shard_map/hidden_units_2/pallas_call | solution.py:483
  147.7 5.8 %copy-done.3 = bf16[16,2048,256]{2,1,0:T(8,128)(2,1)S(1)} copy-done((bf16[16,2048,256]{2,1,0:T(8,128)(2,1)S(1)}, bf16[16,2048,256]{2,1,0:T(8,128)(2,1)}, u32[]{:S(2)}) %copy-start.3) | copy-done | bytes 16777240
  153.6 6.0 %hidden_units_3.1.hidden = bf16[1280,256]{1,0:T(8,128)(2,1)S(1)} custom-call(s32[3]{0:T(128)S(1)} %pad_add_fusion.pos, f32[1,2048]{1,0:T(1,128)S(1)} %bitcast.27, bf16[128,512]{1,0:T(8,128)(2,1)S(1)} %collective-permute-done.28.refs_1_, bf16[128,512]{1,0:T(8,128)(2,1)S(1)} %collective-permute-done.31.refs_2_, ...), custom_call_target="tpu_custom_call" | custom-call | tf_op jit(solution)/shard_map/hidden_units_3/pallas_call | solution.py:483
  159.6 2.7 %down_quarter_3.1 = bf16[512,512]{1,0:T(8,128)(2,1)S(1)} custom-call(s32[3]{0:T(128)S(1)} %pad_add_fusion.pos, bf16[1280,256]{1,0:T(8,128)(2,1)S(1)} %hidden_units_3.1.hidden, bf16[512,1280]{1,0:T(8,128)(2,1)S(1)} %get-tuple-element.46.place, bf16[16,256,2048]{2,1,0:T(8,128)(2,1)S(1)} %bitcast.23), custom_call_target="tpu_custom_call" | custom-call | tf_op jit(solution)/shard_map/down_quarter_3/pallas_call | solution.py:510
  162.9 2.7 %down_quarter_1.1 = bf16[512,512]{1,0:T(8,128)(2,1)S(1)} custom-call(s32[3]{0:T(128)S(1)} %pad_add_fusion.pos, bf16[1280,256]{1,0:T(8,128)(2,1)S(1)} %hidden_units_3.1.hidden, bf16[512,1280]{1,0:T(8,128)(2,1)S(1)} %get-tuple-element.46.place, bf16[16,256,2048]{2,1,0:T(8,128)(2,1)S(1)} %bitcast.23), custom_call_target="tpu_custom_call" | custom-call | tf_op jit(solution)/shard_map/down_quarter_1/pallas_call | solution.py:510
  165.8 5.8 %copy-done = bf16[16,256,2048]{2,1,0:T(8,128)(2,1)S(1)} copy-done((bf16[16,256,2048]{2,1,0:T(8,128)(2,1)S(1)}, bf16[16,256,2048]{2,1,0:T(8,128)(2,1)}, u32[]{:S(2)}) %copy-start) | copy-done | bytes 16777240
  171.5 2.9 %down_quarter_2.1 = bf16[512,512]{1,0:T(8,128)(2,1)S(1)} custom-call(s32[3]{0:T(128)S(1)} %pad_add_fusion.pos, bf16[1280,256]{1,0:T(8,128)(2,1)S(1)} %hidden_units_3.1.hidden, bf16[512,1280]{1,0:T(8,128)(2,1)S(1)} %get-tuple-element.46.place, bf16[16,256,2048]{2,1,0:T(8,128)(2,1)S(1)} %copy-done), custom_call_target="tpu_custom_call" | custom-call | tf_op jit(solution)/shard_map/down_quarter_2/pallas_call | solution.py:510
  174.5 1.9 add_convert_fusion.7
  177.1 1.3 collective-permute-start.43
  179.2 2.7 %down_quarter_0.1 = bf16[512,512]{1,0:T(8,128)(2,1)S(1)} custom-call(s32[3]{0:T(128)S(1)} %pad_add_fusion.pos, bf16[1280,256]{1,0:T(8,128)(2,1)S(1)} %hidden_units_3.1.hidden, bf16[512,1280]{1,0:T(8,128)(2,1)S(1)} %get-tuple-element.46.place, bf16[16,256,2048]{2,1,0:T(8,128)(2,1)S(1)} %copy-done), custom_call_target="tpu_custom_call" | custom-call | tf_op jit(solution)/shard_map/down_quarter_0/pallas_call | solution.py:510
  181.9 1.3 collective-permute-start.47
  183.2 2.2 %collective-permute-done.43 = bf16[128,512]{1,0:T(8,128)(2,1)S(1)} collective-permute-done((bf16[128,512]{1,0:T(8,128)(2,1)S(1)}, bf16[128,512]{1,0:T(8,128)(2,1)S(1)}, u32[]{:S(2)}, u32[]{:S(2)}) %collective-permute-start.43) | collective-permute-done | bytes 131104 | tf_op jit(solution)/shard_map/sum_over_devices/ppermute | solution.py:148
  185.5 2.8 %collective-permute-done.45 = bf16[128,512]{1,0:T(8,128)(2,1)S(1)} collective-permute-done((bf16[128,512]{1,0:T(8,128)(2,1)S(1)}, bf16[128,512]{1,0:T(8,128)(2,1)S(1)}, u32[]{:S(2)}, u32[]{:S(2)}) %collective-permute-start.45) | collective-permute-done | bytes 131104 | tf_op jit(solution)/shard_map/sum_over_devices/ppermute | solution.py:148
  188.3 1.2 add_convert_fusion.6
  189.5 2.5 %collective-permute-start.42 = (bf16[128,512]{1,0:T(8,128)(2,1)S(1)}, bf16[128,512]{1,0:T(8,128)(2,1)S(1)}, u32[]{:S(2)}, u32[]{:S(2)}) collective-permute-start(bf16[128,512]{1,0:T(8,128)(2,1)S(1)} %get-tuple-element.47), channel_id=1, source_target_pairs={{0,12},{4,8},{8,4},{12,0},{1,13},{5,9},{9,5},{13,1},{2,14},{6,10},... | collective-permute-start | bytes 393224 | tf_op jit(solution)/shard_map/sum_over_devices/ppermute | solution.py:148
  192.0 1.9 collective-permute-start.46
  193.9 3.8 %collective-permute-done.42 = bf16[128,512]{1,0:T(8,128)(2,1)S(1)} collective-permute-done((bf16[128,512]{1,0:T(8,128)(2,1)S(1)}, bf16[128,512]{1,0:T(8,128)(2,1)S(1)}, u32[]{:S(2)}, u32[]{:S(2)}) %collective-permute-start.42) | collective-permute-done | bytes 131104 | tf_op jit(solution)/shard_map/sum_over_devices/ppermute | solution.py:148
  197.8 4.3 %collective-permute-done.44 = bf16[128,512]{1,0:T(8,128)(2,1)S(1)} collective-permute-done((bf16[128,512]{1,0:T(8,128)(2,1)S(1)}, bf16[128,512]{1,0:T(8,128)(2,1)S(1)}, u32[]{:S(2)}, u32[]{:S(2)}) %collective-permute-start.44) | collective-permute-done | bytes 131104 | tf_op jit(solution)/shard_map/sum_over_devices/ppermute | solution.py:148
  202.0 1.1 add_convert_fusion
  203.1 6.8 %all_gather.3 = bf16[128,2048]{1,0:T(8,128)(2,1)S(1)} all-gather(bf16[128,512]{1,0:T(8,128)(2,1)S(1)} %add_convert_fusion), channel_id=1, replica_groups=mesh['grp'=2,'seq'=4,'head'=4] {'head'}, dimensions={1}, use_global_device_ids=true | all-gather | bytes 655360 | tf_op jit(solution)/shard_map/gather_columns/all_gather | solution.py:545
  (113 shorter events, 18.5 us)
Async XLA Ops:
  0.0 31.2 %copy-start.22 = (s32[128,8]{0,1:T(8,128)S(1)}, s32[128,8]{0,1:T(8,128)}, u32[]{:S(2)}) copy-start(s32[128,8]{0,1:T(8,128)} %param.13) | copy-start | bytes 12292
  0.0 33.5 %copy-start.23 = (f32[128,8]{0,1:T(8,128)S(1)}, f32[128,8]{0,1:T(8,128)}, u32[]{:S(2)}) copy-start(f32[128,8]{0,1:T(8,128)} %param.14) | copy-start | bytes 12292
  0.0 60.0 %copy-start.21 = (f32[2048]{0:T(1024)S(1)}, f32[2048]{0:T(1024)}, u32[]{:S(2)}) copy-start(f32[2048]{0:T(1024)} %param.11) | copy-start | bytes 24580
  2.7 57.3 %copy-start.7 = (bf16[128,2048]{1,0:T(8,128)(2,1)S(1)}, bf16[128,2048]{1,0:T(8,128)(2,1)}, u32[]{:S(2)}) copy-start(bf16[128,2048]{1,0:T(8,128)(2,1)} %tokens.3) | copy-start | bytes 1572868
  4.4 8.1 %collective-permute-start = (bf16[128,512]{1,0:T(8,128)(2,1)S(1)}, bf16[128,512]{1,0:T(8,128)(2,1)S(1)}, u32[]{:S(2)}, u32[]{:S(2)}) collective-permute-start(bf16[128,512]{1,0:T(8,128)(2,1)S(1)} %get-tuple-element.27), channel_id=1, source_target_pairs={{0,4},{4,0},{8,12},{12,8},{1,5},{5,1},{9,13},{13,9},{2,6},{6,2},{1... | collective-permute-start | bytes 393224 | tf_op jit(solution)/shard_map/gather_tokens/ppermute | solution.py:148
  7.4 12.9 %collective-permute-start.1 = (bf16[128,512]{1,0:T(8,128)(2,1)S(1)}, bf16[128,512]{1,0:T(8,128)(2,1)S(1)}, u32[]{:S(2)}, u32[]{:S(2)}) collective-permute-start(bf16[128,512]{1,0:T(8,128)(2,1)S(1)} %get-tuple-element.27), channel_id=1, source_target_pairs={{0,8},{4,12},{8,0},{12,4},{1,9},{5,13},{9,1},{13,5},{2,10},{6,14},... | collective-permute-start | bytes 393224 | tf_op jit(solution)/shard_map/gather_tokens/ppermute | solution.py:148
  10.0 10.3 %collective-permute-start.2 = (bf16[128,512]{1,0:T(8,128)(2,1)S(1)}, bf16[128,512]{1,0:T(8,128)(2,1)S(1)}, u32[]{:S(2)}, u32[]{:S(2)}) collective-permute-start(bf16[128,512]{1,0:T(8,128)(2,1)S(1)} %get-tuple-element.27), channel_id=1, source_target_pairs={{0,12},{4,8},{8,4},{12,0},{1,13},{5,9},{9,5},{13,1},{2,14},{6,10},... | collective-permute-start | bytes 393224 | tf_op jit(solution)/shard_map/gather_tokens/ppermute | solution.py:148
  20.4 9.3 %collective-permute-start.4 = (bf16[3,128,512]{2,1,0:T(8,128)(2,1)S(1)}, bf16[3,128,512]{2,1,0:T(8,128)(2,1)}, u32[]{:S(2)}, u32[]{:S(2)}) collective-permute-start(bf16[3,128,512]{2,1,0:T(8,128)(2,1)S(1)} %pad_maximum_fusion.rest_0_), channel_id=1, source_target_pairs={{0,2},{1,3},{2,0},{3,1},{4,6},{5,7},{6,4},{7,5},{8,10},{9,11},{10,... | collective-permute-start | bytes 1179656 | tf_op jit(solution)/shard_map/gather_tokens/ppermute | solution.py:148
  21.9 23.5 %collective-permute-start.6 = (bf16[256,384]{1,0:T(8,128)(2,1)S(1)}, bf16[256,384]{1,0:T(8,128)(2,1)S(1)}, u32[]{:S(2)}, u32[]{:S(2)}) collective-permute-start(bf16[256,384]{1,0:T(8,128)(2,1)S(1)} %get-tuple-element.28), channel_id=1, source_target_pairs={{0,4},{4,0},{8,12},{12,8},{1,5},{5,1},{9,13},{13,9},{2,6},{6,2},{1... | collective-permute-start | bytes 589832 | tf_op jit(solution)/shard_map/gather_head_weights/ppermute | solution.py:148
  23.9 24.4 %collective-permute-start.10 = (bf16[256,384]{1,0:T(8,128)(2,1)S(1)}, bf16[256,384]{1,0:T(8,128)(2,1)S(1)}, u32[]{:S(2)}, u32[]{:S(2)}) collective-permute-start(bf16[256,384]{1,0:T(8,128)(2,1)S(1)} %get-tuple-element.32), channel_id=1, source_target_pairs={{0,8},{4,12},{8,0},{12,4},{1,9},{5,13},{9,1},{13,5},{2,10},{6,14},... | collective-permute-start | bytes 589832 | tf_op jit(solution)/shard_map/gather_head_weights/ppermute | solution.py:148
  29.7 27.5 %collective-permute-start.16 = (bf16[512,512]{1,0:T(8,128)(2,1)S(1)}, bf16[512,512]{1,0:T(8,128)(2,1)}, u32[]{:S(2)}, u32[]{:S(2)}) collective-permute-start(bf16[512,512]{1,0:T(8,128)(2,1)S(1)} %slice_bitcast_fusion.rest_0_), channel_id=1, source_target_pairs={{0,2},{1,3},{2,0},{3,1},{4,6},{5,7},{6,4},{7,5},{8,10},{9,11},{10,... | collective-permute-start | bytes 1572872 | tf_op jit(solution)/shard_map/gather_out_weights/ppermute | solution.py:148
  31.2 17.6 %collective-permute-start.11 = (bf16[256,384]{1,0:T(8,128)(2,1)S(1)}, bf16[256,384]{1,0:T(8,128)(2,1)}, u32[]{:S(2)}, u32[]{:S(2)}) collective-permute-start(bf16[256,384]{1,0:T(8,128)(2,1)S(1)} %get-tuple-element.34), channel_id=1, source_target_pairs={{0,12},{4,8},{8,4},{12,0},{1,13},{5,9},{9,5},{13,1},{2,14},{6,10},... | collective-permute-start | bytes 589832 | tf_op jit(solution)/shard_map/gather_head_weights/ppermute | solution.py:148
  33.5 4.4 %collective-permute-start.7 = (f32[16,128]{1,0:T(8,128)S(1)}, f32[16,128]{1,0:T(8,128)S(1)}, u32[]{:S(2)}, u32[]{:S(2)}) collective-permute-start(f32[16,128]{1,0:T(8,128)S(1)} %pad_maximum_fusion.2.own), channel_id=1, source_target_pairs={{0,4},{4,0},{8,12},{12,8},{1,5},{5,1},{9,13},{13,9},{2,6},{6,2},{1... | collective-permute-start | bytes 24584 | tf_op jit(solution)/shard_map/route_tables/ppermute | solution.py:148
  38.0 4.9 %collective-permute-start.8 = (f32[16,128]{1,0:T(8,128)S(1)}, f32[16,128]{1,0:T(8,128)S(1)}, u32[]{:S(2)}, u32[]{:S(2)}) collective-permute-start(f32[16,128]{1,0:T(8,128)S(1)} %pad_maximum_fusion.2.own), channel_id=1, source_target_pairs={{0,8},{4,12},{8,0},{12,4},{1,9},{5,13},{9,1},{13,5},{2,10},{6,14},... | collective-permute-start | bytes 24584 | tf_op jit(solution)/shard_map/route_tables/ppermute | solution.py:148
  42.8 5.4 %collective-permute-start.9 = (f32[16,128]{1,0:T(8,128)S(1)}, f32[16,128]{1,0:T(8,128)S(1)}, u32[]{:S(2)}, u32[]{:S(2)}) collective-permute-start(f32[16,128]{1,0:T(8,128)S(1)} %pad_maximum_fusion.2.own), channel_id=1, source_target_pairs={{0,12},{4,8},{8,4},{12,0},{1,13},{5,9},{9,5},{13,1},{2,14},{6,10},... | collective-permute-start | bytes 24584 | tf_op jit(solution)/shard_map/route_tables/ppermute | solution.py:148
  45.4 5.7 %collective-permute-start.12 = (bf16[256,384]{1,0:T(8,128)(2,1)S(1)}, bf16[256,384]{1,0:T(8,128)(2,1)S(1)}, u32[]{:S(2)}, u32[]{:S(2)}) collective-permute-start(bf16[256,384]{1,0:T(8,128)(2,1)S(1)} %collective-permute-done.6.rest_4_), channel_id=1, source_target_pairs={{0,16},{16,0},{1,17},{17,1},{2,18},{18,2},{3,19},{19,3},{4,20},{20... | collective-permute-start | bytes 589832 | tf_op jit(solution)/shard_map/gather_head_weights/ppermute | solution.py:148
  48.3 11.7 %collective-permute-start.3 = (bf16[3,128,512]{2,1,0:T(8,128)(2,1)S(1)}, bf16[3,128,512]{2,1,0:T(8,128)(2,1)}, u32[]{:S(2)}, u32[]{:S(2)}) collective-permute-start(bf16[3,128,512]{2,1,0:T(8,128)(2,1)S(1)} %pad_maximum_fusion.rest_0_), channel_id=1, source_target_pairs={{0,1},{1,0},{2,3},{3,2},{4,5},{5,4},{6,7},{7,6},{8,9},{9,8},{10,11... | collective-permute-start | bytes 1179656 | tf_op jit(solution)/shard_map/gather_tokens/ppermute | solution.py:148
  48.3 11.7 %collective-permute-start.5 = (bf16[3,128,512]{2,1,0:T(8,128)(2,1)}, bf16[3,128,512]{2,1,0:T(8,128)(2,1)}, u32[]{:S(2)}, u32[]{:S(2)}) collective-permute-start(bf16[3,128,512]{2,1,0:T(8,128)(2,1)} %collective-permute-done.4.rest_2_), channel_id=1, source_target_pairs={{0,1},{1,0},{2,3},{3,2},{4,5},{5,4},{6,7},{7,6},{8,9},{9,8},{10,11... | collective-permute-start | bytes 1179656 | tf_op jit(solution)/shard_map/gather_tokens/ppermute | solution.py:148
  48.8 7.8 %collective-permute-start.13 = (bf16[256,384]{1,0:T(8,128)(2,1)S(1)}, bf16[256,384]{1,0:T(8,128)(2,1)S(1)}, u32[]{:S(2)}, u32[]{:S(2)}) collective-permute-start(bf16[256,384]{1,0:T(8,128)(2,1)S(1)} %collective-permute-done.10.rest_5_), channel_id=1, source_target_pairs={{0,16},{16,0},{1,17},{17,1},{2,18},{18,2},{3,19},{19,3},{4,20},{20... | collective-permute-start | bytes 589832 | tf_op jit(solution)/shard_map/gather_head_weights/ppermute | solution.py:148
  51.8 8.3 %collective-permute-start.14 = (bf16[256,384]{1,0:T(8,128)(2,1)}, bf16[256,384]{1,0:T(8,128)(2,1)}, u32[]{:S(2)}, u32[]{:S(2)}) collective-permute-start(bf16[256,384]{1,0:T(8,128)(2,1)} %collective-permute-done.11.rest_6_), channel_id=1, source_target_pairs={{0,16},{16,0},{1,17},{17,1},{2,18},{18,2},{3,19},{19,3},{4,20},{20... | collective-permute-start | bytes 589832 | tf_op jit(solution)/shard_map/gather_head_weights/ppermute | solution.py:148
  57.3 22.0 %collective-permute-start.15 = (bf16[512,512]{1,0:T(8,128)(2,1)S(1)}, bf16[512,512]{1,0:T(8,128)(2,1)}, u32[]{:S(2)}, u32[]{:S(2)}) collective-permute-start(bf16[512,512]{1,0:T(8,128)(2,1)S(1)} %slice_bitcast_fusion.rest_0_), channel_id=1, source_target_pairs={{0,1},{1,0},{2,3},{3,2},{4,5},{5,4},{6,7},{7,6},{8,9},{9,8},{10,11... | collective-permute-start | bytes 1572872 | tf_op jit(solution)/shard_map/gather_out_weights/ppermute | solution.py:148
  57.3 30.7 %collective-permute-start.17 = (bf16[512,512]{1,0:T(8,128)(2,1)}, bf16[512,512]{1,0:T(8,128)(2,1)}, u32[]{:S(2)}, u32[]{:S(2)}) collective-permute-start(bf16[512,512]{1,0:T(8,128)(2,1)} %collective-permute-done.16.rest_2_), channel_id=1, source_target_pairs={{0,1},{1,0},{2,3},{3,2},{4,5},{5,4},{6,7},{7,6},{8,9},{9,8},{10,11... | collective-permute-start | bytes 1572872 | tf_op jit(solution)/shard_map/gather_out_weights/ppermute | solution.py:148
  70.4 44.0 %copy-start.20 = (f32[2048]{0:T(1024)S(1)}, f32[2048]{0:T(1024)}, u32[]{:S(2)}) copy-start(f32[2048]{0:T(1024)} %param.12) | copy-start | bytes 24580
  70.4 1.9 collective-permute-start.18
  70.5 4.3 %collective-permute-start.19 = (bf16[128,128]{1,0:T(8,128)(2,1)S(1)}, bf16[128,128]{1,0:T(8,128)(2,1)S(1)}, u32[]{:S(2)}, u32[]{:S(2)}) collective-permute-start(bf16[128,128]{1,0:T(8,128)(2,1)S(1)} %get-tuple-element.56), channel_id=1, source_target_pairs={{0,2},{1,3},{2,0},{3,1},{4,6},{5,7},{6,4},{7,5},{8,10},{9,11},{10,... | collective-permute-start | bytes 98312 | tf_op jit(solution)/shard_map/heads_to_tokens/ppermute | solution.py:148
  71.1 3.7 %collective-permute-start.20 = (bf16[128,128]{1,0:T(8,128)(2,1)S(1)}, bf16[128,128]{1,0:T(8,128)(2,1)S(1)}, u32[]{:S(2)}, u32[]{:S(2)}) collective-permute-start(bf16[128,128]{1,0:T(8,128)(2,1)S(1)} %get-tuple-element.55), channel_id=1, source_target_pairs={{0,3},{1,2},{2,1},{3,0},{4,7},{5,6},{6,5},{7,4},{8,11},{9,10},{10,... | collective-permute-start | bytes 98312 | tf_op jit(solution)/shard_map/heads_to_tokens/ppermute | solution.py:148
  74.8 7.9 %collective-permute-start.21 = (bf16[4,128,128]{2,1,0:T(8,128)(2,1)S(1)}, bf16[4,128,128]{2,1,0:T(8,128)(2,1)S(1)}, u32[]{:S(2)}, u32[]{:S(2)}) collective-permute-start(bf16[4,128,128]{2,1,0:T(8,128)(2,1)S(1)} %pad_maximum_fusion.1.rest_4_), channel_id=1, source_target_pairs={{0,4},{4,0},{8,12},{12,8},{1,5},{5,1},{9,13},{13,9},{2,6},{6,2},{1... | collective-permute-start | bytes 393224 | tf_op jit(solution)/shard_map/heads_to_tokens/ppermute | solution.py:148
  74.9 13.1 %collective-permute-start.22 = (bf16[4,128,128]{2,1,0:T(8,128)(2,1)S(1)}, bf16[4,128,128]{2,1,0:T(8,128)(2,1)S(1)}, u32[]{:S(2)}, u32[]{:S(2)}) collective-permute-start(bf16[4,128,128]{2,1,0:T(8,128)(2,1)S(1)} %pad_maximum_fusion.1.rest_4_), channel_id=1, source_target_pairs={{0,8},{4,12},{8,0},{12,4},{1,9},{5,13},{9,1},{13,5},{2,10},{6,14},... | collective-permute-start | bytes 393224 | tf_op jit(solution)/shard_map/heads_to_tokens/ppermute | solution.py:148
  78.0 10.0 %collective-permute-start.23 = (bf16[4,128,128]{2,1,0:T(8,128)(2,1)S(1)}, bf16[4,128,128]{2,1,0:T(8,128)(2,1)S(1)}, u32[]{:S(2)}, u32[]{:S(2)}) collective-permute-start(bf16[4,128,128]{2,1,0:T(8,128)(2,1)S(1)} %pad_maximum_fusion.1.rest_4_), channel_id=1, source_target_pairs={{0,12},{4,8},{8,4},{12,0},{1,13},{5,9},{9,5},{13,1},{2,14},{6,10},... | collective-permute-start | bytes 393224 | tf_op jit(solution)/shard_map/heads_to_tokens/ppermute | solution.py:148
  91.1 6.3 %collective-permute-start.24 = (bf16[128,512]{1,0:T(8,128)(2,1)S(1)}, bf16[128,512]{1,0:T(8,128)(2,1)S(1)}, u32[]{:S(2)}, u32[]{:S(2)}) collective-permute-start(bf16[128,512]{1,0:T(8,128)(2,1)S(1)} %output_projection.1.refs_1_), channel_id=1, source_target_pairs={{0,4},{4,0},{8,12},{12,8},{1,5},{5,1},{9,13},{13,9},{2,6},{6,2},{1... | collective-permute-start | bytes 393224 | tf_op jit(solution)/shard_map/gather_residual/ppermute | solution.py:148
  93.7 5.0 %collective-permute-start.37 = (bf16[128,512]{1,0:T(8,128)(2,1)S(1)}, bf16[128,512]{1,0:T(8,128)(2,1)S(1)}, u32[]{:S(2)}, u32[]{:S(2)}) collective-permute-start(bf16[128,512]{1,0:T(8,128)(2,1)S(1)} %output_projection.1.refs_1_), channel_id=1, source_target_pairs={{0,2},{1,3},{2,0},{3,1},{4,6},{5,7},{6,4},{7,5},{8,10},{9,11},{10,... | collective-permute-start | bytes 393224 | tf_op jit(solution)/shard_map/gather_residual/ppermute | solution.py:148
  94.9 11.8 %collective-permute-start.26 = (bf16[128,512]{1,0:T(8,128)(2,1)S(1)}, bf16[128,512]{1,0:T(8,128)(2,1)S(1)}, u32[]{:S(2)}, u32[]{:S(2)}) collective-permute-start(bf16[128,512]{1,0:T(8,128)(2,1)S(1)} %output_projection.1.refs_1_), channel_id=1, source_target_pairs={{0,8},{4,12},{8,0},{12,4},{1,9},{5,13},{9,1},{13,5},{2,10},{6,14},... | collective-permute-start | bytes 393224 | tf_op jit(solution)/shard_map/gather_residual/ppermute | solution.py:148
  95.9 11.5 %collective-permute-start.36 = (bf16[128,512]{1,0:T(8,128)(2,1)S(1)}, bf16[128,512]{1,0:T(8,128)(2,1)S(1)}, u32[]{:S(2)}, u32[]{:S(2)}) collective-permute-start(bf16[128,512]{1,0:T(8,128)(2,1)S(1)} %output_projection.1.refs_1_), channel_id=1, source_target_pairs={{0,1},{1,0},{2,3},{3,2},{4,5},{5,4},{6,7},{7,6},{8,9},{9,8},{10,11... | collective-permute-start | bytes 393224 | tf_op jit(solution)/shard_map/gather_residual/ppermute | solution.py:148
  95.9 11.5 %collective-permute-start.28 = (bf16[128,512]{1,0:T(8,128)(2,1)S(1)}, bf16[128,512]{1,0:T(8,128)(2,1)S(1)}, u32[]{:S(2)}, u32[]{:S(2)}) collective-permute-start(bf16[128,512]{1,0:T(8,128)(2,1)S(1)} %output_projection.1.refs_1_), channel_id=1, source_target_pairs={{0,12},{4,8},{8,4},{12,0},{1,13},{5,9},{9,5},{13,1},{2,14},{6,10},... | collective-permute-start | bytes 393224 | tf_op jit(solution)/shard_map/gather_residual/ppermute | solution.py:148
  97.4 11.4 %collective-permute-start.34 = (bf16[128,512]{1,0:T(8,128)(2,1)S(1)}, bf16[128,512]{1,0:T(8,128)(2,1)S(1)}, u32[]{:S(2)}, u32[]{:S(2)}) collective-permute-start(bf16[128,512]{1,0:T(8,128)(2,1)S(1)} %collective-permute-done.24.refs_1_), channel_id=1, source_target_pairs={{0,2},{1,3},{2,0},{3,1},{4,6},{5,7},{6,4},{7,5},{8,10},{9,11},{10,... | collective-permute-start | bytes 393224 | tf_op jit(solution)/shard_map/gather_residual/ppermute | solution.py:148
  98.7 10.2 %collective-permute-start.38 = (bf16[128,512]{1,0:T(8,128)(2,1)S(1)}, bf16[128,512]{1,0:T(8,128)(2,1)S(1)}, u32[]{:S(2)}, u32[]{:S(2)}) collective-permute-start(bf16[128,512]{1,0:T(8,128)(2,1)S(1)} %collective-permute-done.37.refs_3_), channel_id=1, source_target_pairs={{0,1},{1,0},{2,3},{3,2},{4,5},{5,4},{6,7},{7,6},{8,9},{9,8},{10,11... | collective-permute-start | bytes 393224 | tf_op jit(solution)/shard_map/gather_residual/ppermute | solution.py:148
  106.6 6.1 %collective-permute-start.27 = (bf16[128,512]{1,0:T(8,128)(2,1)S(1)}, bf16[128,512]{1,0:T(8,128)(2,1)S(1)}, u32[]{:S(2)}, u32[]{:S(2)}) collective-permute-start(bf16[128,512]{1,0:T(8,128)(2,1)S(1)} %collective-permute-done.26.refs_1_), channel_id=1, source_target_pairs={{0,2},{1,3},{2,0},{3,1},{4,6},{5,7},{6,4},{7,5},{8,10},{9,11},{10,... | collective-permute-start | bytes 393224 | tf_op jit(solution)/shard_map/gather_residual/ppermute | solution.py:148
  107.4 5.3 %collective-permute-start.25 = (bf16[128,512]{1,0:T(8,128)(2,1)S(1)}, bf16[128,512]{1,0:T(8,128)(2,1)S(1)}, u32[]{:S(2)}, u32[]{:S(2)}) collective-permute-start(bf16[128,512]{1,0:T(8,128)(2,1)S(1)} %collective-permute-done.24.refs_1_), channel_id=1, source_target_pairs={{0,1},{1,0},{2,3},{3,2},{4,5},{5,4},{6,7},{7,6},{8,9},{9,8},{10,11... | collective-permute-start | bytes 393224 | tf_op jit(solution)/shard_map/gather_residual/ppermute | solution.py:148
  107.4 7.0 %collective-permute-start.29 = (bf16[128,512]{1,0:T(8,128)(2,1)S(1)}, bf16[128,512]{1,0:T(8,128)(2,1)S(1)}, u32[]{:S(2)}, u32[]{:S(2)}) collective-permute-start(bf16[128,512]{1,0:T(8,128)(2,1)S(1)} %collective-permute-done.28.refs_1_), channel_id=1, source_target_pairs={{0,2},{1,3},{2,0},{3,1},{4,6},{5,7},{6,4},{7,5},{8,10},{9,11},{10,... | collective-permute-start | bytes 393224 | tf_op jit(solution)/shard_map/gather_residual/ppermute | solution.py:148
  108.8 21.3 %collective-permute-start.35 = (bf16[128,512]{1,0:T(8,128)(2,1)S(1)}, bf16[128,512]{1,0:T(8,128)(2,1)S(1)}, u32[]{:S(2)}, u32[]{:S(2)}) collective-permute-start(bf16[128,512]{1,0:T(8,128)(2,1)S(1)} %collective-permute-done.34.refs_3_), channel_id=1, source_target_pairs={{0,1},{1,0},{2,3},{3,2},{4,5},{5,4},{6,7},{7,6},{8,9},{9,8},{10,11... | collective-permute-start | bytes 393224 | tf_op jit(solution)/shard_map/gather_residual/ppermute | solution.py:148
  108.9 32.7 %collective-permute-start.32 = (bf16[128,512]{1,0:T(8,128)(2,1)S(1)}, bf16[128,512]{1,0:T(8,128)(2,1)S(1)}, u32[]{:S(2)}, u32[]{:S(2)}) collective-permute-start(bf16[128,512]{1,0:T(8,128)(2,1)S(1)} %collective-permute-done.26.refs_1_), channel_id=1, source_target_pairs={{0,1},{1,0},{2,3},{3,2},{4,5},{5,4},{6,7},{7,6},{8,9},{9,8},{10,11... | collective-permute-start | bytes 393224 | tf_op jit(solution)/shard_map/gather_residual/ppermute | solution.py:148
  112.7 28.9 %collective-permute-start.33 = (bf16[128,512]{1,0:T(8,128)(2,1)S(1)}, bf16[128,512]{1,0:T(8,128)(2,1)S(1)}, u32[]{:S(2)}, u32[]{:S(2)}) collective-permute-start(bf16[128,512]{1,0:T(8,128)(2,1)S(1)} %collective-permute-done.27.refs_3_), channel_id=1, source_target_pairs={{0,1},{1,0},{2,3},{3,2},{4,5},{5,4},{6,7},{7,6},{8,9},{9,8},{10,11... | collective-permute-start | bytes 393224 | tf_op jit(solution)/shard_map/gather_residual/ppermute | solution.py:148
  112.7 35.0 %collective-permute-start.31 = (bf16[128,512]{1,0:T(8,128)(2,1)S(1)}, bf16[128,512]{1,0:T(8,128)(2,1)S(1)}, u32[]{:S(2)}, u32[]{:S(2)}) collective-permute-start(bf16[128,512]{1,0:T(8,128)(2,1)S(1)} %collective-permute-done.28.refs_1_), channel_id=1, source_target_pairs={{0,1},{1,0},{2,3},{3,2},{4,5},{5,4},{6,7},{7,6},{8,9},{9,8},{10,11... | collective-permute-start | bytes 393224 | tf_op jit(solution)/shard_map/gather_residual/ppermute | solution.py:148
  114.4 33.3 %collective-permute-start.30 = (bf16[128,512]{1,0:T(8,128)(2,1)S(1)}, bf16[128,512]{1,0:T(8,128)(2,1)S(1)}, u32[]{:S(2)}, u32[]{:S(2)}) collective-permute-start(bf16[128,512]{1,0:T(8,128)(2,1)S(1)} %collective-permute-done.29.refs_3_), channel_id=1, source_target_pairs={{0,1},{1,0},{2,3},{3,2},{4,5},{5,4},{6,7},{7,6},{8,9},{9,8},{10,11... | collective-permute-start | bytes 393224 | tf_op jit(solution)/shard_map/gather_residual/ppermute | solution.py:148
  114.4 5.8 %copy-start.1 = (bf16[16,2048,256]{2,1,0:T(8,128)(2,1)S(1)}, bf16[16,2048,256]{2,1,0:T(8,128)(2,1)}, u32[]{:S(2)}) copy-start(bf16[16,2048,256]{2,1,0:T(8,128)(2,1)} %refs_6_.7) | copy-start | bytes 50331652
  120.2 5.8 %copy-start.4 = (bf16[16,2048,256]{2,1,0:T(8,128)(2,1)S(1)}, bf16[16,2048,256]{2,1,0:T(8,128)(2,1)}, u32[]{:S(2)}) copy-start(bf16[16,2048,256]{2,1,0:T(8,128)(2,1)} %refs_7_.7) | copy-start | bytes 50331652
  130.1 5.8 %copy-start.2 = (bf16[16,2048,256]{2,1,0:T(8,128)(2,1)S(1)}, bf16[16,2048,256]{2,1,0:T(8,128)(2,1)}, u32[]{:S(2)}) copy-start(bf16[16,2048,256]{2,1,0:T(8,128)(2,1)} %refs_6_.7) | copy-start | bytes 50331652
  141.6 17.9 %slice-start = ((s8[16777216]{0:T(1024)(128)(4,1)}), s8[4194304]{0:T(1024)(128)(4,1)S(1)}, s32[]{:S(2)}) async-start(s8[16777216]{0:T(1024)(128)(4,1)} %bitcast.22), calls=%async_computation | async-start | bytes 8388608
  141.7 17.9 %slice-start.1 = ((s8[16777216]{0:T(1024)(128)(4,1)}), s8[4194304]{0:T(1024)(128)(4,1)S(1)}, s32[]{:S(2)}) async-start(s8[16777216]{0:T(1024)(128)(4,1)} %bitcast.22), calls=%async_computation.1 | async-start | bytes 8388608
  147.7 11.8 %copy-start.8 = (bf16[128,512]{1,0:T(8,128)(2,1)}, bf16[128,512]{1,0:T(8,128)(2,1)S(1)}, u32[]{:S(2)}) copy-start(bf16[128,512]{1,0:T(8,128)(2,1)S(1)} %collective-permute-done.30.refs_4_) | copy-start | bytes 393220
  147.7 5.8 %copy-start.3 = (bf16[16,2048,256]{2,1,0:T(8,128)(2,1)S(1)}, bf16[16,2048,256]{2,1,0:T(8,128)(2,1)}, u32[]{:S(2)}) copy-start(bf16[16,2048,256]{2,1,0:T(8,128)(2,1)} %refs_6_.7) | copy-start | bytes 50331652
  153.6 6.0 %slice-start.2 = ((s8[16777216]{0:T(1024)(128)(4,1)}), s8[4194304]{0:T(1024)(128)(4,1)S(1)}, s32[]{:S(2)}) async-start(s8[16777216]{0:T(1024)(128)(4,1)} %bitcast.22), calls=%async_computation.2 | async-start | bytes 8388608
  153.6 6.0 %slice-start.3 = ((s8[16777216]{0:T(1024)(128)(4,1)}), s8[4194304]{0:T(1024)(128)(4,1)S(1)}, s32[]{:S(2)}) async-start(s8[16777216]{0:T(1024)(128)(4,1)} %bitcast.22), calls=%async_computation.3 | async-start | bytes 8388608
  162.3 12.1 %collective-permute-start.40 = (bf16[512,512]{1,0:T(8,128)(2,1)S(1)}, bf16[512,512]{1,0:T(8,128)(2,1)}, u32[]{:S(2)}, u32[]{:S(2)}) collective-permute-start(bf16[512,512]{1,0:T(8,128)(2,1)S(1)} %down_quarter_3.1), channel_id=1, source_target_pairs={{0,1},{1,0},{2,3},{3,2},{4,5},{5,4},{6,7},{7,6},{8,9},{9,8},{10,11... | collective-permute-start | bytes 1572872 | tf_op jit(solution)/shard_map/sum_over_devices/ppermute | solution.py:148
  165.6 17.6 %collective-permute-start.39 = (bf16[512,512]{1,0:T(8,128)(2,1)S(1)}, bf16[512,512]{1,0:T(8,128)(2,1)}, u32[]{:S(2)}, u32[]{:S(2)}) collective-permute-start(bf16[512,512]{1,0:T(8,128)(2,1)S(1)} %down_quarter_1.1), channel_id=1, source_target_pairs={{0,1},{1,0},{2,3},{3,2},{4,5},{5,4},{6,7},{7,6},{8,9},{9,8},{10,11... | collective-permute-start | bytes 1572872 | tf_op jit(solution)/shard_map/sum_over_devices/ppermute | solution.py:148
  165.7 5.8 %copy-start = (bf16[16,256,2048]{2,1,0:T(8,128)(2,1)S(1)}, bf16[16,256,2048]{2,1,0:T(8,128)(2,1)}, u32[]{:S(2)}) copy-start(bf16[16,256,2048]{2,1,0:T(8,128)(2,1)} %w_down.7) | copy-start | bytes 50331652
  176.4 6.9 %collective-permute-start.41 = (bf16[128,512]{1,0:T(8,128)(2,1)S(1)}, bf16[128,512]{1,0:T(8,128)(2,1)S(1)}, u32[]{:S(2)}, u32[]{:S(2)}) collective-permute-start(bf16[128,512]{1,0:T(8,128)(2,1)S(1)} %get-tuple-element.50), channel_id=1, source_target_pairs={{0,2},{1,3},{2,0},{3,1},{4,6},{5,7},{6,4},{7,5},{8,10},{9,11},{10,... | collective-permute-start | bytes 393224 | tf_op jit(solution)/shard_map/sum_over_devices/ppermute | solution.py:148
  177.1 8.3 %collective-permute-start.43 = (bf16[128,512]{1,0:T(8,128)(2,1)S(1)}, bf16[128,512]{1,0:T(8,128)(2,1)S(1)}, u32[]{:S(2)}, u32[]{:S(2)}) collective-permute-start(bf16[128,512]{1,0:T(8,128)(2,1)S(1)} %get-tuple-element.53), channel_id=1, source_target_pairs={{0,2},{1,3},{2,0},{3,1},{4,6},{5,7},{6,4},{7,5},{8,10},{9,11},{10,... | collective-permute-start | bytes 393224 | tf_op jit(solution)/shard_map/sum_over_devices/ppermute | solution.py:148
  178.4 23.6 %copy-start.9 = (bf16[128,512]{1,0:T(8,128)(2,1)S(1)}, bf16[128,512]{1,0:T(8,128)(2,1)}, u32[]{:S(2)}) copy-start(bf16[128,512]{1,0:T(8,128)(2,1)} %copy-done.8) | copy-start | bytes 393220
  178.4 9.9 %collective-permute-start.45 = (bf16[128,512]{1,0:T(8,128)(2,1)S(1)}, bf16[128,512]{1,0:T(8,128)(2,1)S(1)}, u32[]{:S(2)}, u32[]{:S(2)}) collective-permute-start(bf16[128,512]{1,0:T(8,128)(2,1)S(1)} %get-tuple-element.52), channel_id=1, source_target_pairs={{0,2},{1,3},{2,0},{3,1},{4,6},{5,7},{6,4},{7,5},{8,10},{9,11},{10,... | collective-permute-start | bytes 393224 | tf_op jit(solution)/shard_map/sum_over_devices/ppermute | solution.py:148
  181.9 12.0 %collective-permute-start.47 = (bf16[128,512]{1,0:T(8,128)(2,1)}, bf16[128,512]{1,0:T(8,128)(2,1)S(1)}, u32[]{:S(2)}, u32[]{:S(2)}) collective-permute-start(bf16[128,512]{1,0:T(8,128)(2,1)} %get-tuple-element.51), channel_id=1, source_target_pairs={{0,2},{1,3},{2,0},{3,1},{4,6},{5,7},{6,4},{7,5},{8,10},{9,11},{10,... | collective-permute-start | bytes 393224 | tf_op jit(solution)/shard_map/sum_over_devices/ppermute | solution.py:148
  189.5 8.3 %collective-permute-start.42 = (bf16[128,512]{1,0:T(8,128)(2,1)S(1)}, bf16[128,512]{1,0:T(8,128)(2,1)S(1)}, u32[]{:S(2)}, u32[]{:S(2)}) collective-permute-start(bf16[128,512]{1,0:T(8,128)(2,1)S(1)} %get-tuple-element.47), channel_id=1, source_target_pairs={{0,12},{4,8},{8,4},{12,0},{1,13},{5,9},{9,5},{13,1},{2,14},{6,10},... | collective-permute-start | bytes 393224 | tf_op jit(solution)/shard_map/sum_over_devices/ppermute | solution.py:148
  192.0 10.0 %collective-permute-start.44 = (bf16[128,512]{1,0:T(8,128)(2,1)S(1)}, bf16[128,512]{1,0:T(8,128)(2,1)S(1)}, u32[]{:S(2)}, u32[]{:S(2)}) collective-permute-start(bf16[128,512]{1,0:T(8,128)(2,1)S(1)} %get-tuple-element.49), channel_id=1, source_target_pairs={{0,8},{4,12},{8,0},{12,4},{1,9},{5,13},{9,1},{13,5},{2,10},{6,14},... | collective-permute-start | bytes 393224 | tf_op jit(solution)/shard_map/sum_over_devices/ppermute | solution.py:148
  192.0 10.0 %collective-permute-start.46 = (bf16[128,512]{1,0:T(8,128)(2,1)S(1)}, bf16[128,512]{1,0:T(8,128)(2,1)S(1)}, u32[]{:S(2)}, u32[]{:S(2)}) collective-permute-start(bf16[128,512]{1,0:T(8,128)(2,1)S(1)} %get-tuple-element.48), channel_id=1, source_target_pairs={{0,4},{4,0},{8,12},{12,8},{1,5},{5,1},{9,13},{13,9},{2,6},{6,2},{1... | collective-permute-start | bytes 393224 | tf_op jit(solution)/shard_map/sum_over_devices/ppermute | solution.py:148
  (12 other events, 10.8 us)

commit v3 on v2

--- a/solution.py
+++ b/solution.py
@@ -159,12 +159,20 @@
     return lax.optimization_barrier((array,) + earlier)[0]
 
 
-def cut_kernel(pos, tokens, weight, x_send, w_own, *rest):
+def held(array):
+    return pltpu.with_memory_space_constraint(array, pltpu.HBM)
+
+
+def cut_kernel(pos, routes, gates, tokens, weight, x_send, w_own, o_own, *rest):
     w_sends, sems = rest[:-1], rest[-1]
     g, s, h = pos[0], pos[1], pos[2]
-    cols, half = x_send.shape[1], w_sends[0].shape[0]
+    rows, cols, half = tokens.shape[0], x_send.shape[1], w_sends[0].shape[0]
     copies = [
-        (tokens.at[:, pl.ds(pl.multiple_of(h * cols, cols), cols)], x_send),
+        (
+            tokens.at[:, pl.ds(pl.multiple_of(h * cols, cols), cols)],
+            x_send.at[pl.ds(0, rows)],
+        ),
+        (weight.at[3], o_own),
     ]
     for which in range(3):
         span = pl.ds(which * HEAD_DIM, HEAD_DIM)
@@ -176,7 +184,21 @@
             )
         column = pl.multiple_of(s * HEAD_DIM, HEAD_DIM)
         copies.append((weight.at[which, :, pl.ds(column, HEAD_DIM)], w_own.at[:, span]))
-    run_copies([pltpu.make_async_copy(a, b, sems.at[i]) for i, (a, b) in enumerate(copies)])
+    copies = [pltpu.make_async_copy(a, b, sems.at[i]) for i, (a, b) in enumerate(copies)]
+    for copy in copies:
+        copy.start()
+    parts, left = [routes[...].astype(F32)], gates[...]
+    for _ in range(3):
+        parts.append(left.astype(BF16).astype(F32))
+        left = left - parts[-1]
+    lines = jnp.concatenate(parts, axis=1)
+    lines = jnp.concatenate([lines, jnp.zeros_like(lines)], axis=0)
+    blank = jnp.zeros((lines.shape[0], cols - lines.shape[1]), F32)
+    if blank.shape[1]:
+        lines = jnp.concatenate([lines, blank], axis=1)
+    x_send[rows:, :] = lines.astype(BF16)
+    for copy in copies:
+        copy.wait()
 
 
 def attend_kernel(n, pos, gain, tokens, w_own, *rest):
@@ -252,15 +274,16 @@
     out[...] = (x_share[...].astype(F32) + product).astype(BF16)
 
 
-def route_kernel(n, experts, slots, pos, own, *rest):
-    others, (pick, place, weight, table, sems) = rest[: n - 1], rest[n - 1 :]
+def route_kernel(n, experts, slots, pos, *refs):
+    pieces, (pick, place, weight, table) = refs[:n], refs[n:]
     s = pos[1]
-    rows = own.shape[1]
+    rows = pieces[0].shape[0] - 2 * TOPK
     total = n * rows
-    copies = []
-    for d, piece in enumerate((own,) + tuple(others)):
-        copies.append((piece, table.at[:, pl.ds(pl.multiple_of((s ^ d) * rows, rows), rows)]))
-    run_copies([pltpu.make_async_copy(a, b, sems.at[i]) for i, (a, b) in enumerate(copies)])
+    for d in range(n):
+        lines = pieces[d][rows:, :].astype(F32)[:TOPK]
+        gate = sum(lines[:, (1 + i) * rows : (2 + i) * rows] for i in range(3))
+        span = pl.ds(pl.multiple_of((s ^ d) * rows, rows), rows)
+        table[:, span] = jnp.concatenate([lines[:, :rows], gate], axis=0)
     first = (s * experts).astype(F32)
     names = lax.broadcasted_iota(jnp.int32, (experts, total), 0).astype(F32) + first
     member = jnp.zeros((experts, total), F32)
@@ -294,63 +317,100 @@
         weight[span, :] = jnp.broadcast_to(chosen, (slots, weight.shape[1]))
 
 
-def hidden_kernel(n, slots, group, first, last, pos, *refs):
+def stream(n_parts, moves):
+    parts = [
+        [pltpu.make_async_copy(*refs, sem) for refs, sem in moves(i)] for i in range(n_parts)
+    ]
+    for part in parts:
+        for copy in part:
+            copy.start()
+
+    def wait(i):
+        for copy in parts[i]:
+            copy.wait()
+
+    return wait
+
+
+def hidden_kernel(n, slots, group, distance, last, pos, gain, *refs):
+    first = distance == 0
     refs = list(refs)
-    gain = refs.pop(0)
     pieces = [refs.pop(0) for _ in range(n)]
     pick, w_gate, w_up = (refs.pop(0) for _ in range(3))
     if not first:
         total_in, square_in = refs.pop(0), refs.pop(0)
     if last:
-        weight, hidden_out, r_all = refs
+        weight, hidden_out, r_all, scaled, g_all, u_all, sems = refs
     else:
-        total_out, square_out, r_all = refs
+        total_out, square_out, r_all, scaled, g_all, u_all, sems = refs
+    s, h = pos[1], pos[2]
+    rows, cols = pieces[0].shape
+    experts, _, hidden = g_all.shape
+    column = pl.ds(pl.multiple_of((s ^ distance) * cols, cols), cols)
+
+    def moves(i):
+        part = pl.ds(i * group, group)
+        return [
+            ((w_gate.at[part, column, :], g_all.at[part]), sems.at[2 * i]),
+            ((w_up.at[part, column, :], u_all.at[part]), sems.at[2 * i + 1]),
+        ]
+
+    wait = stream(experts // group, moves)
+    for e in range(n):
+        r_all[pl.ds(pl.multiple_of((h ^ e) * rows, rows), rows), :] = pieces[e][...]
+    width = n * cols
+    factor = []
+    for i in range(experts // group):
+        part = slice(i * group * slots, (i + 1) * group * slots)
+        taken = jnp.dot(pick[part, :], r_all[...], preferred_element_type=F32)
+        square = jnp.sum(taken * taken, axis=1, keepdims=True)
+        if not first:
+            square = square + square_in[part, :1]
+        if last:
+            factor.append(lax.rsqrt(square / width + EPS))
+        else:
+            square_out[part, :] = jnp.broadcast_to(square, (group * slots, square_out.shape[1]))
+        scaled[part, :] = (taken * gain[:, column]).astype(BF16)
+    for i in range(experts // group):
+        wait(i)
+        for e in range(i * group, (i + 1) * group):
+            span = slice(e * slots, (e + 1) * slots)
+            gate_val = jnp.dot(scaled[span, :], g_all[e], preferred_element_type=F32)
+            up_val = jnp.dot(scaled[span, :], u_all[e], preferred_element_type=F32)
+            if not first:
+                gate_val = gate_val + total_in[span, :hidden]
+                up_val = up_val + total_in[span, hidden:]
+            if last:
+                inner = (e - i * group) * slots
+                scale = factor[i][inner : inner + slots]
+                gate_val, up_val = gate_val * scale, up_val * scale
+                value = gate_val * jax.nn.sigmoid(gate_val) * (up_val * weight[span, :1])
+                hidden_out[span, :] = value.astype(BF16)
+            else:
+                total_out[span, :hidden] = gate_val
+                total_out[span, hidden:] = up_val
+
+
+def down_kernel(n, slots, group, distances, pos, hidden, place, w_down, *refs):
+    outs, (d_all, y_slots, sems) = refs[: len(distances)], refs[len(distances) :]
     h = pos[2]
-    rows = pieces[0].shape[0]
-    hidden = w_gate.shape[2]
-
-    @pl.when(pl.program_id(0) == 0)
-    def _():
-        for e in range(n):
-            r_all[pl.ds(pl.multiple_of((h ^ e) * rows, rows), rows), :] = pieces[e][...]
-
-    taken = jnp.dot(pick[...], r_all[...], preferred_element_type=F32)
-    square = jnp.sum(taken * taken, axis=1, keepdims=True)
-    if not first:
-        square = square + square_in[:, :1]
-    scaled = (taken * gain[...]).astype(BF16)
-    for e in range(group):
-        span = slice(e * slots, (e + 1) * slots)
-        gate_val = jnp.dot(scaled[span], w_gate[e], preferred_element_type=F32)
-        up_val = jnp.dot(scaled[span], w_up[e], preferred_element_type=F32)
-        if not first:
-            gate_val = gate_val + total_in[span, :hidden]
-            up_val = up_val + total_in[span, hidden:]
-        if last:
-            width = n * r_all.shape[1]
-            factor = lax.rsqrt(square[span] / width + EPS)
-            gate_val, up_val = gate_val * factor, up_val * factor
-            value = gate_val * jax.nn.sigmoid(gate_val) * (up_val * weight[span, :1])
-            hidden_out[span, :] = value.astype(BF16)
-        else:
-            total_out[span, :hidden] = gate_val
-            total_out[span, hidden:] = up_val
-    if not last:
-        square_out[...] = jnp.broadcast_to(square, square_out.shape)
-
-
-def down_kernel(n, slots, group, pos, hidden, place, w_down, out, y_slots):
-    step = pl.program_id(0)
-    for e in range(group):
-        product = jnp.dot(
-            hidden[e * slots : (e + 1) * slots, :], w_down[e], preferred_element_type=F32
-        )
-        row = pl.multiple_of(step * group * slots, group * slots) + e * slots
-        y_slots[pl.ds(pl.multiple_of(row, slots), slots), :] = product.astype(BF16)
-
-    @pl.when(step == pl.num_programs(0) - 1)
-    def _():
-        out[...] = jnp.dot(place[...], y_slots[...], preferred_element_type=F32).astype(BF16)
+    _, experts, _, cols = d_all.shape
+    parts = experts // group
+
+    def moves(i):
+        k, part = i // parts, pl.ds(i % parts * group, group)
+        column = pl.ds(pl.multiple_of((h ^ distances[k]) * cols, cols), cols)
+        return [((w_down.at[part, :, column], d_all.at[k, part]), sems.at[i])]
+
+    wait = stream(len(distances) * parts, moves)
+    for k in range(len(distances)):
+        for i in range(parts):
+            wait(k * parts + i)
+            for e in range(i * group, (i + 1) * group):
+                span = slice(e * slots, (e + 1) * slots)
+                product = jnp.dot(hidden[span, :], d_all[k, e], preferred_element_type=F32)
+                y_slots[span, :] = product.astype(BF16)
+        outs[k][...] = jnp.dot(place[...], y_slots[...], preferred_element_type=F32).astype(BF16)
 
 
 def square_body(
@@ -368,13 +428,12 @@
     pairs = experts * slots
     sds = jax.ShapeDtypeStruct
     dma = pltpu.SemaphoreType.DMA
-    grid_spec = functools.partial(pltpu.PrefetchScalarGridSpec, num_scalar_prefetch=1)
 
     def room(mib):
         return pltpu.CompilerParams(vmem_limit_bytes=mib * MIB)
 
-    def whole(*shape):
-        return pl.BlockSpec(shape, lambda step, pos: (0,) * len(shape))
+    def cost(macs, size):
+        return pl.CostEstimate(flops=2 * macs, bytes_accessed=size, transcendentals=0)
 
     def plus(*terms):
         total_value = terms[0].astype(F32)
@@ -382,44 +441,42 @@
             total_value = total_value + term.astype(F32)
         return total_value
 
+    lines = 2 * TOPK
     with jax.named_scope("cut_pieces"):
-        x_send, w_own, *w_sends = pl.pallas_call(
+        x_send, w_own, o_own, *w_sends = pl.pallas_call(
             cut_kernel,
-            out_shape=[sds((rows, cols), BF16), sds((depth, 3 * HEAD_DIM), BF16)]
+            out_shape=[
+                sds((rows + lines, cols), BF16),
+                sds((depth, 3 * HEAD_DIM), BF16),
+                sds((depth, cols), BF16),
+            ]
             + [sds((half, 3 * HEAD_DIM), BF16)] * (n - 1),
-            in_specs=[SMEM, ANY, ANY],
-            out_specs=[VMEM] * (n + 1),
-            scratch_shapes=[dma((1 + 3 * n,))],
+            in_specs=[SMEM, VMEM, VMEM, ANY, ANY],
+            out_specs=[VMEM] * (n + 2),
+            scratch_shapes=[dma((2 + 3 * n,))],
             compiler_params=room(8),
-        )(pos, tokens, attn_weight)
-    with jax.named_scope("gather_tokens"):
+        )(pos, routes.T, gates.T, tokens, attn_weight)
+    with jax.named_scope("gather_tokens_and_weights"):
         x_far = [swap(x_send, "seq", d) for d in range(1, n)]
-        x_pieces = {0: jnp.stack(x_far)}
+        w_near = [swap(w_sends[d - 1], "seq", d) for d in range(1, n - 1)]
+        o_pieces = {0: o_own, 2: swap(o_own, "head", 2)}
+        w_near.append(swap(after(w_sends[-1], *x_far, *w_near), "seq", n - 1))
+        w_far = [swap(w, "grp", 1) for w in w_near]
+        x_pieces = {0: after(jnp.stack([x[:rows] for x in x_far]), o_pieces[2])}
         x_pieces[2] = swap(x_pieces[0], "head", 2)
-        for e in (0, 2):
-            x_pieces[e ^ 1] = swap(x_pieces[e], "head", 1)
-    with jax.named_scope("gather_head_weights"):
-        w_near = [swap(w_sends[0], "seq", 1)]
-        w_near += [swap(after(w_sends[d - 1], *x_far), "seq", d) for d in range(2, n)]
-        w_far = [swap(w, "grp", 1) for w in w_near]
-    with jax.named_scope("route_tables"):
-        table = jnp.concatenate([routes.T.astype(F32), gates.T], axis=0)
-        table_others = [swap(table, "seq", d) for d in range(1, n)]
+        for pieces in (o_pieces, x_pieces):
+            for e in (0, 2):
+                pieces[e ^ 1] = swap(pieces[e], "head", 1)
     with jax.named_scope("routing"):
         pick, place, weight = pl.pallas_call(
             functools.partial(route_kernel, n, experts, slots),
             out_shape=[sds((pairs, total), BF16), sds((total, pairs), BF16), sds((pairs, 128), F32)],
-            in_specs=[SMEM] + [ANY] * n,
+            in_specs=[SMEM] + [VMEM] * n,
             out_specs=[VMEM] * 3,
-            scratch_shapes=[pltpu.VMEM((2 * TOPK, total), F32), dma((n,))],
+            scratch_shapes=[pltpu.VMEM((2 * TOPK, total), F32)],
             compiler_params=room(16),
-        )(pos, table, *table_others)
-        w_near[0] = after(w_near[0], pick)
-    with jax.named_scope("gather_out_weights"):
-        o_pieces = {0: after(attn_weight, x_far[0])[3]}
-        o_pieces[2] = swap(after(o_pieces[0], x_pieces[2]), "head", 2)
-        for e in (0, 2):
-            o_pieces[e ^ 1] = swap(o_pieces[e], "head", 1)
+        )(pos, x_send, *x_far)
+        w_near[-1] = after(w_near[-1], pick)
 
     with jax.named_scope("attention"):
         attended, x_share = pl.pallas_call(
@@ -468,63 +525,56 @@
                 r[e ^ 1] = swap(r[e], "head", 1)
             r_pieces.append(r)
 
-    group = 4
-    block = group * slots
+    group = experts // 4
     state = ()
     for d in range(n):
-        first, last = d == 0, d == n - 1
-        by_step = lambda size: pl.BlockSpec((block, size), lambda step, pos: (step, 0))
-
-        def columns(step, pos, d=d):
-            return (step, pos[1] ^ d, 0)
-
-        totals = [by_step(2 * hidden), by_step(128)]
+        last = d == n - 1
         with jax.named_scope(f"hidden_units_{d}"):
             state = pl.pallas_call(
-                functools.partial(hidden_kernel, n, slots, group, first, last),
+                functools.partial(hidden_kernel, n, slots, group, d, last),
                 out_shape=[sds((pairs, hidden), BF16)]
                 if last
                 else [sds((pairs, 2 * hidden), F32), sds((pairs, 128), F32)],
-                grid_spec=grid_spec(
-                    grid=(experts // group,),
-                    in_specs=[pl.BlockSpec((1, cols), lambda step, pos, d=d: (0, pos[1] ^ d))]
-                    + [whole(rows, cols)] * n
-                    + [by_step(total)]
-                    + [pl.BlockSpec((group, cols, hidden), columns)] * 2
-                    + ([] if first else totals)
-                    + ([by_step(128)] if last else []),
-                    out_specs=[by_step(hidden)] if last else totals,
-                    scratch_shapes=[pltpu.VMEM((total, cols), BF16)],
-                ),
-                compiler_params=room(16),
+                in_specs=[SMEM]
+                + [VMEM] * (n + 2)
+                + [ANY] * 2
+                + [VMEM] * (len(state) + last),
+                out_specs=[VMEM] * (2 - last),
+                scratch_shapes=[
+                    pltpu.VMEM((total, cols), BF16),
+                    pltpu.VMEM((pairs, cols), BF16),
+                    pltpu.VMEM((experts, cols, hidden), BF16),
+                    pltpu.VMEM((experts, cols, hidden), BF16),
+                    dma((2 * (experts // group),)),
+                ],
+                compiler_params=room(28),
+                cost_estimate=cost(pairs * cols * (total + 2 * hidden), 4 * experts * cols * hidden),
             )(
                 pos, moe_gain.reshape(1, width), *[r_pieces[d][e] for e in range(n)],
-                pick, expert_gate, expert_up, *state, *([weight] if last else []),
+                pick, held(expert_gate), held(expert_up), *state, *([weight] if last else []),
             )
     (units,) = state
 
-    group_down = 8
     out = {}
-    for e in (3, 2, 1, 0):
-        with jax.named_scope(f"down_quarter_{e}"):
-            out[e] = pl.pallas_call(
-                functools.partial(down_kernel, n, slots, group_down),
-                out_shape=sds((total, cols), BF16),
-                grid_spec=grid_spec(
-                    grid=(experts // group_down,),
-                    in_specs=[
-                        pl.BlockSpec((group_down * slots, hidden), lambda step, pos: (step, 0)),
-                        whole(total, pairs),
-                        pl.BlockSpec(
-                            (group_down, hidden, cols),
-                            lambda step, pos, e=e: (step, 0, pos[2] ^ e),
-                        ),
-                    ],
-                    out_specs=whole(total, cols),
-                    scratch_shapes=[pltpu.VMEM((pairs, cols), BF16)],
+    for distances in ((3,), (2,), (1, 0)):
+        with jax.named_scope("down_quarters_" + "_".join(map(str, distances))):
+            outs = pl.pallas_call(
+                functools.partial(down_kernel, n, slots, group, distances),
+                out_shape=[sds((total, cols), BF16)] * len(distances),
+                in_specs=[SMEM, VMEM, VMEM, ANY],
+                out_specs=[VMEM] * len(distances),
+                scratch_shapes=[
+                    pltpu.VMEM((len(distances), experts, hidden, cols), BF16),
+                    pltpu.VMEM((pairs, cols), BF16),
+                    dma((len(distances) * (experts // group),)),
+                ],
+                compiler_params=room(24),
+                cost_estimate=cost(
+                    len(distances) * pairs * cols * (total + hidden),
+                    2 * len(distances) * experts * cols * hidden,
                 ),
-                compiler_params=room(16),
-            )(pos, units, place, expert_down)
+            )(pos, units, place, held(expert_down))
+            out.update(zip(distances, outs))
 
     def rows_of(array, d):
         return lax.dynamic_slice_in_dim(array, (s ^ d) * rows, rows, 0)

time: 212 us -> 181 us (0.85)
  local copies, waits for them, and re-layouts: 41.6 us -> 10.7 us
  waiting for transfers between devices: 61.8 us -> 67.3 us
  starting transfers between devices: 51.7 us -> 46.5 us
    unnamed x57 -> x31, local copies, waits for them, and re-layouts: 40.5 us -> 10.6 us
    ppermute x48 -> x45, waiting for transfers between devices: 61.8 us -> 67.3 us  [swap(): return lax.ppermute(array, axis, [(i, i ^ distance) for i in range(size)])]
    ppermute x48 -> x45, starting transfers between devices: 51.7 us -> 46.5 us  [swap(): return lax.ppermute(array, axis, [(i, i ^ distance) for i in range(size)])]
    pallas_call x9 -> x8, Pallas kernels: 33.9 us -> 34.9 us  [the longest x4 20.5 us: square_body(): pl.pallas_call(functools.partial(hidden_kernel, n, slots, group, d, last)...]
  transfers between devices with their start and end apart: 48 -> 45, of which waited for: 18 -> 21; matrix products, arithmetic and copies ran while one was open for 2% -> 1% of each run, Pallas kernels for 15% -> 18%
where the time goes in v3:
time: 181 us; the launch traced here: 180 us
  waiting for transfers between devices  67.3 us (37%)
  starting transfers between devices  46.5 us (26%)
  Pallas kernels  45.1 us (25%)
  local copies, waits for them, and re-layouts  10.7 us (6%)
  blocking collectives  6.96 us (4%)
  other arithmetic  3.65 us (2%)
    ppermute x45, waiting for transfers between devices, swap(): return lax.ppermute(array, axis, [(i, i ^ distance) for i in range(size)])  67.3 us
    ppermute x45, starting transfers between devices, swap(): return lax.ppermute(array, axis, [(i, i ^ distance) for i in range(size)])  46.5 us
    pallas_call x4, Pallas kernels, square_body(): pl.pallas_call(functools.partial(hidden_kernel, n, slots, group, d, last)...  20.5 us
    pallas_call x3, Pallas kernels, square_body(): pl.pallas_call(functools.partial(down_kernel, n, slots, group, distances)...  13.5 us
    unnamed x31, local copies, waits for them, and re-layouts  10.6 us
    all_gather x1, blocking collectives, square_body(): return lax.all_gather(mixed, 'head', axis=1, tiled=True)  6.96 us
    pallas_call x1, Pallas kernels, square_body(): pl.pallas_call(functools.partial(attend_kernel, n), out_shape=[sds((n, ro...  5.67 us
  transfers between devices with their start and end apart: 45, of which 21 were waited for; matrix products, arithmetic and copies ran while one was open for 1% of the time, Pallas kernels for 18%

profile of v3, /device:TPU:0, one launch (start us, length us, event | category | flops | bytes accessed | tf_op | source)
XLA Modules:
  0.0 180.5 jit_solution(20384289227104130)
XLA Ops:
  0.1 1.6 copy-done
  1.7 1.0 copy-done.1
  2.7 0.7 copy-done.13
  3.4 0.7 copy-done.14
  4.1 0.9 cut_pieces.1
  5.0 5.1 %collective-permute-start.2 = (bf16[144,512]{1,0:T(8,128)(2,1)S(1)}, bf16[144,512]{1,0:T(8,128)(2,1)S(1)}, u32[]{:S(2)}, u32[]{:S(2)}) collective-permute-start(bf16[144,512]{1,0:T(8,128)(2,1)S(1)} %get-tuple-element.28.refs_0_), channel_id=1, source_target_pairs={{0,12},{4,8},{8,4},{12,0},{1,13},{5,9},{9,5},{13,1},{2,14},{6,10},... | collective-permute-start | bytes 442376 | tf_op jit(solution)/shard_map/gather_tokens_and_weights/ppermute | solution.py:148
  10.8 1.6 collective-permute-start.3
  12.4 2.4 %collective-permute-done.2.refs_3_ = bf16[144,512]{1,0:T(8,128)(2,1)S(1)} collective-permute-done((bf16[144,512]{1,0:T(8,128)(2,1)S(1)}, bf16[144,512]{1,0:T(8,128)(2,1)S(1)}, u32[]{:S(2)}, u32[]{:S(2)}) %collective-permute-start.2) | collective-permute-done | bytes 147488 | tf_op jit(solution)/shard_map/gather_tokens_and_weights/ppermute | solution.py:148
  14.9 7.7 %collective-permute-done.1.refs_2_ = bf16[144,512]{1,0:T(8,128)(2,1)S(1)} collective-permute-done((bf16[144,512]{1,0:T(8,128)(2,1)S(1)}, bf16[144,512]{1,0:T(8,128)(2,1)S(1)}, u32[]{:S(2)}, u32[]{:S(2)}) %collective-permute-start.1) | collective-permute-done | bytes 147488 | tf_op jit(solution)/shard_map/gather_tokens_and_weights/ppermute | solution.py:148
  22.8 1.3 collective-permute-done.3.rest_2_
  24.0 1.5 collective-permute-start.5
  25.5 1.4 collective-permute-start.7
  26.9 2.6 %collective-permute-start.8 = (bf16[256,384]{1,0:T(8,128)(2,1)S(1)}, bf16[256,384]{1,0:T(8,128)(2,1)S(1)}, u32[]{:S(2)}, u32[]{:S(2)}) collective-permute-start(bf16[256,384]{1,0:T(8,128)(2,1)S(1)} %get-tuple-element.32), channel_id=1, source_target_pairs={{0,8},{4,12},{8,0},{12,4},{1,9},{5,13},{9,1},{13,5},{2,10},{6,14},... | collective-permute-start | bytes 589832 | tf_op jit(solution)/shard_map/gather_tokens_and_weights/ppermute | solution.py:148
  29.5 3.8 %collective-permute-done.7.rest_4_ = bf16[256,384]{1,0:T(8,128)(2,1)S(1)} collective-permute-done((bf16[256,384]{1,0:T(8,128)(2,1)S(1)}, bf16[256,384]{1,0:T(8,128)(2,1)S(1)}, u32[]{:S(2)}, u32[]{:S(2)}) %collective-permute-start.7) | collective-permute-done | bytes 196640 | tf_op jit(solution)/shard_map/gather_tokens_and_weights/ppermute | solution.py:148
  33.4 5.5 %collective-permute-done.8.rest_5_ = bf16[256,384]{1,0:T(8,128)(2,1)S(1)} collective-permute-done((bf16[256,384]{1,0:T(8,128)(2,1)S(1)}, bf16[256,384]{1,0:T(8,128)(2,1)S(1)}, u32[]{:S(2)}, u32[]{:S(2)}) %collective-permute-start.8) | collective-permute-done | bytes 196640 | tf_op jit(solution)/shard_map/gather_tokens_and_weights/ppermute | solution.py:148
  38.8 3.3 %collective-permute-start.9 = (bf16[256,384]{1,0:T(8,128)(2,1)S(1)}, bf16[256,384]{1,0:T(8,128)(2,1)}, u32[]{:S(2)}, u32[]{:S(2)}) collective-permute-start(bf16[256,384]{1,0:T(8,128)(2,1)S(1)} %get-tuple-element.34), channel_id=1, source_target_pairs={{0,12},{4,8},{8,4},{12,0},{1,13},{5,9},{9,5},{13,1},{2,14},{6,10},... | collective-permute-start | bytes 589832 | tf_op jit(solution)/shard_map/gather_tokens_and_weights/ppermute | solution.py:148
  42.6 1.5 collective-permute-start.10
  45.3 1.1 collective-permute-done.9.rest_6_
  46.4 1.5 collective-permute-start.12
  47.9 2.5 %collective-permute-done.10.rest_7_ = bf16[256,384]{1,0:T(8,128)(2,1)S(1)} collective-permute-done((bf16[256,384]{1,0:T(8,128)(2,1)S(1)}, bf16[256,384]{1,0:T(8,128)(2,1)S(1)}, u32[]{:S(2)}, u32[]{:S(2)}) %collective-permute-start.10) | collective-permute-done | bytes 196640 | tf_op jit(solution)/shard_map/gather_tokens_and_weights/ppermute | solution.py:148
  51.0 3.5 %collective-permute-done.11.rest_8_ = bf16[256,384]{1,0:T(8,128)(2,1)S(1)} collective-permute-done((bf16[256,384]{1,0:T(8,128)(2,1)S(1)}, bf16[256,384]{1,0:T(8,128)(2,1)S(1)}, u32[]{:S(2)}, u32[]{:S(2)}) %collective-permute-start.11) | collective-permute-done | bytes 196640 | tf_op jit(solution)/shard_map/gather_tokens_and_weights/ppermute | solution.py:148
  55.3 1.3 routing.1
  56.6 1.3 collective-permute-done.12.rest_9_
  58.0 1.0 copy-done.4
  59.0 0.9 copy-done.6
  59.9 0.9 copy-done.8
  60.8 0.9 copy-done.10
  61.7 5.7 %attention.1 = (bf16[4,128,128]{2,1,0:T(8,128)(2,1)S(1)}, bf16[128,512]{1,0:T(8,128)(2,1)S(1)}) custom-call(s32[3]{0:T(128)S(1)} %pad_add_fusion.pos, f32[1,2048]{1,0:T(1,128)S(1)} %bitcast.26, bf16[128,2048]{1,0:T(8,128)(2,1)S(1)} %copy-done.2, bf16[512,384]{1,0:T(8,128)(2,1)S(1)} %copy-done.4, bf16[3,128,512]{2,1,0:T(8,128)(2,1)S(1)} %pad_maximum_fusion.rest_0_, ...), custom_call_target="tpu_custom_call" | custom-call | tf_op jit(solution)/shard_map/attention/pallas_call | solution.py:482
  68.1 1.3 collective-permute-start.17
  69.4 2.4 %collective-permute-done.16 = bf16[128,128]{1,0:T(8,128)(2,1)S(1)} collective-permute-done((bf16[128,128]{1,0:T(8,128)(2,1)S(1)}, bf16[128,128]{1,0:T(8,128)(2,1)S(1)}, u32[]{:S(2)}, u32[]{:S(2)}) %collective-permute-start.16) | collective-permute-done | bytes 32800 | tf_op jit(solution)/shard_map/heads_to_tokens/ppermute | solution.py:148
  71.9 1.2 collective-permute-start.19
  73.1 3.2 %collective-permute-start.20 = (bf16[4,128,128]{2,1,0:T(8,128)(2,1)S(1)}, bf16[4,128,128]{2,1,0:T(8,128)(2,1)S(1)}, u32[]{:S(2)}, u32[]{:S(2)}) collective-permute-start(bf16[4,128,128]{2,1,0:T(8,128)(2,1)S(1)} %pad_maximum_fusion.1.rest_4_), channel_id=1, source_target_pairs={{0,12},{4,8},{8,4},{12,0},{1,13},{5,9},{9,5},{13,1},{2,14},{6,10},... | collective-permute-start | bytes 393224 | tf_op jit(solution)/shard_map/heads_to_tokens/ppermute | solution.py:148
  76.3 2.4 %collective-permute-done.18.rest_5_ = bf16[4,128,128]{2,1,0:T(8,128)(2,1)S(1)} collective-permute-done((bf16[4,128,128]{2,1,0:T(8,128)(2,1)S(1)}, bf16[4,128,128]{2,1,0:T(8,128)(2,1)S(1)}, u32[]{:S(2)}, u32[]{:S(2)}) %collective-permute-start.18) | collective-permute-done | bytes 131104 | tf_op jit(solution)/shard_map/heads_to_tokens/ppermute | solution.py:148
  78.7 6.2 %collective-permute-done.19.rest_6_ = bf16[4,128,128]{2,1,0:T(8,128)(2,1)S(1)} collective-permute-done((bf16[4,128,128]{2,1,0:T(8,128)(2,1)S(1)}, bf16[4,128,128]{2,1,0:T(8,128)(2,1)S(1)}, u32[]{:S(2)}, u32[]{:S(2)}) %collective-permute-start.19) | collective-permute-done | bytes 131104 | tf_op jit(solution)/shard_map/heads_to_tokens/ppermute | solution.py:148
  84.9 3.2 %output_projection.1.refs_0_ = bf16[128,512]{1,0:T(8,128)(2,1)S(1)} custom-call(s32[3]{0:T(128)S(1)} %pad_add_fusion.pos, bf16[128,512]{1,0:T(8,128)(2,1)S(1)} %get-tuple-element.37.x_share, bf16[512,512]{1,0:T(8,128)(2,1)S(1)} %get-tuple-element.29.rest_0_, bf16[512,512]{1,0:T(8,128)(2,1)} %collective-permute-done.13.rest_1_, ...), custom_call_target="tpu_custom_call" | custom-call | tf_op jit(solution)/shard_map/output_projection/pallas_call | solution.py:506
  88.1 2.7 %collective-permute-start.21 = (bf16[128,512]{1,0:T(8,128)(2,1)S(1)}, bf16[128,512]{1,0:T(8,128)(2,1)S(1)}, u32[]{:S(2)}, u32[]{:S(2)}) collective-permute-start(bf16[128,512]{1,0:T(8,128)(2,1)S(1)} %output_projection.1.refs_0_), channel_id=1, source_target_pairs={{0,4},{4,0},{8,12},{12,8},{1,5},{5,1},{9,13},{13,9},{2,6},{6,2},{1... | collective-permute-start | bytes 393224 | tf_op jit(solution)/shard_map/gather_residual/ppermute | solution.py:148
  90.8 1.2 collective-permute-start.34
  92.0 2.4 %collective-permute-start.25 = (bf16[128,512]{1,0:T(8,128)(2,1)S(1)}, bf16[128,512]{1,0:T(8,128)(2,1)S(1)}, u32[]{:S(2)}, u32[]{:S(2)}) collective-permute-start(bf16[128,512]{1,0:T(8,128)(2,1)S(1)} %output_projection.1.refs_0_), channel_id=1, source_target_pairs={{0,12},{4,8},{8,4},{12,0},{1,13},{5,9},{9,5},{13,1},{2,14},{6,10},... | collective-permute-start | bytes 393224 | tf_op jit(solution)/shard_map/gather_residual/ppermute | solution.py:148
  94.5 1.1 collective-permute-start.31
  95.8 7.9 %collective-permute-done.23.refs_0_ = bf16[128,512]{1,0:T(8,128)(2,1)S(1)} collective-permute-done((bf16[128,512]{1,0:T(8,128)(2,1)S(1)}, bf16[128,512]{1,0:T(8,128)(2,1)S(1)}, u32[]{:S(2)}, u32[]{:S(2)}) %collective-permute-start.23) | collective-permute-done | bytes 131104 | tf_op jit(solution)/shard_map/gather_residual/ppermute | solution.py:148
  103.7 0.9 collective-permute-start.24
  104.6 1.2 collective-permute-start.26
  106.3 3.4 %collective-permute-done.24.refs_2_ = bf16[128,512]{1,0:T(8,128)(2,1)S(1)} collective-permute-done((bf16[128,512]{1,0:T(8,128)(2,1)S(1)}, bf16[128,512]{1,0:T(8,128)(2,1)S(1)}, u32[]{:S(2)}, u32[]{:S(2)}) %collective-permute-start.24) | collective-permute-done | bytes 131104 | tf_op jit(solution)/shard_map/gather_residual/ppermute | solution.py:148
  109.8 4.8 %hidden_units_0.1 = (f32[1280,512]{1,0:T(8,128)S(1)}, f32[1280,128]{1,0:T(8,128)S(1)}) custom-call(s32[3]{0:T(128)S(1)} %pad_add_fusion.pos, f32[1,2048]{1,0:T(1,128)S(1)} %bitcast.22, bf16[128,512]{1,0:T(8,128)(2,1)S(1)} %output_projection.1.refs_0_, bf16[128,512]{1,0:T(8,128)(2,1)S(1)} %collective-permute-done.33.refs_1_, ...), custom_call_target="tpu_custom_call" | custom-call | flops 1342177280 | bytes 8388608 | tf_op jit(solution)/shard_map/hidden_units_0/pallas_call | solution.py:533
  115.2 5.2 %hidden_units_1.1 = (f32[1280,512]{1,0:T(8,128)S(1)}, f32[1280,128]{1,0:T(8,128)S(1)}) custom-call(s32[3]{0:T(128)S(1)} %pad_add_fusion.pos, f32[1,2048]{1,0:T(1,128)S(1)} %bitcast.23, bf16[128,512]{1,0:T(8,128)(2,1)S(1)} %collective-permute-done.21.refs_0_, bf16[128,512]{1,0:T(8,128)(2,1)S(1)} %collective-permute-done.22.refs_1_, ...), custom_call_target="tpu_custom_call" | custom-call | flops 1342177280 | bytes 8388608 | tf_op jit(solution)/shard_map/hidden_units_1/pallas_call | solution.py:533
  120.4 5.2 %hidden_units_2.1 = (f32[1280,512]{1,0:T(8,128)S(1)}, f32[1280,128]{1,0:T(8,128)S(1)}) custom-call(s32[3]{0:T(128)S(1)} %pad_add_fusion.pos, f32[1,2048]{1,0:T(1,128)S(1)} %bitcast.24, bf16[128,512]{1,0:T(8,128)(2,1)S(1)} %collective-permute-done.23.refs_0_, bf16[128,512]{1,0:T(8,128)(2,1)S(1)} %collective-permute-done.29.refs_1_, ...), custom_call_target="tpu_custom_call" | custom-call | flops 1342177280 | bytes 8388608 | tf_op jit(solution)/shard_map/hidden_units_2/pallas_call | solution.py:533
  125.7 5.3 %hidden_units_3.1.hidden = bf16[1280,256]{1,0:T(8,128)(2,1)S(1)} custom-call(s32[3]{0:T(128)S(1)} %pad_add_fusion.pos, f32[1,2048]{1,0:T(1,128)S(1)} %bitcast.25, bf16[128,512]{1,0:T(8,128)(2,1)S(1)} %collective-permute-done.25.refs_0_, bf16[128,512]{1,0:T(8,128)(2,1)S(1)} %collective-permute-done.28.refs_1_, ...), custom_call_target="tpu_custom_call" | custom-call | flops 1342177280 | bytes 8388608 | tf_op jit(solution)/shard_map/hidden_units_3/pallas_call | solution.py:533
  131.0 3.8 %down_quarters_3.1 = bf16[512,512]{1,0:T(8,128)(2,1)S(1)} custom-call(s32[3]{0:T(128)S(1)} %pad_add_fusion.pos, bf16[1280,256]{1,0:T(8,128)(2,1)S(1)} %hidden_units_3.1.hidden, bf16[512,1280]{1,0:T(8,128)(2,1)S(1)} %get-tuple-element.46.place, bf16[16,256,2048]{2,1,0:T(8,128)(2,1)} %w_down.5), custom_call_target="tpu_custom_call" | custom-call | flops 1006632960 | bytes 4194304 | tf_op jit(solution)/shard_map/down_quarters_3/pallas_call | solution.py:561
  135.3 5.9 %down_quarters_1_0.1 = (bf16[512,512]{1,0:T(8,128)(2,1)}, bf16[512,512]{1,0:T(8,128)(2,1)S(1)}) custom-call(s32[3]{0:T(128)S(1)} %pad_add_fusion.pos, bf16[1280,256]{1,0:T(8,128)(2,1)S(1)} %hidden_units_3.1.hidden, bf16[512,1280]{1,0:T(8,128)(2,1)S(1)} %get-tuple-element.46.place, bf16[16,256,2048]{2,1,0:T(8,128)(2,1)} %w_down.5), custom_call_target="tpu_custom_call" | custom-call | flops 2013265920 | bytes 8388608 | tf_op jit(solution)/shard_map/down_quarters_1_0/pallas_call | solution.py:561
  141.3 3.8 %down_quarters_2.1 = bf16[512,512]{1,0:T(8,128)(2,1)S(1)} custom-call(s32[3]{0:T(128)S(1)} %pad_add_fusion.pos, bf16[1280,256]{1,0:T(8,128)(2,1)S(1)} %hidden_units_3.1.hidden, bf16[512,1280]{1,0:T(8,128)(2,1)S(1)} %get-tuple-element.46.place, bf16[16,256,2048]{2,1,0:T(8,128)(2,1)} %w_down.5), custom_call_target="tpu_custom_call" | custom-call | flops 1006632960 | bytes 4194304 | tf_op jit(solution)/shard_map/down_quarters_2/pallas_call | solution.py:561
  145.1 1.2 add_convert_fusion.7
  147.0 1.5 collective-permute-start.40
  149.0 1.5 collective-permute-start.44
  150.5 2.2 %collective-permute-done.38 = bf16[128,512]{1,0:T(8,128)(2,1)S(1)} collective-permute-done((bf16[128,512]{1,0:T(8,128)(2,1)S(1)}, bf16[128,512]{1,0:T(8,128)(2,1)S(1)}, u32[]{:S(2)}, u32[]{:S(2)}) %collective-permute-start.38) | collective-permute-done | bytes 131104 | tf_op jit(solution)/shard_map/sum_over_devices/ppermute | solution.py:148
  152.8 2.8 %collective-permute-done.40 = bf16[128,512]{1,0:T(8,128)(2,1)S(1)} collective-permute-done((bf16[128,512]{1,0:T(8,128)(2,1)S(1)}, bf16[128,512]{1,0:T(8,128)(2,1)S(1)}, u32[]{:S(2)}, u32[]{:S(2)}) %collective-permute-start.40) | collective-permute-done | bytes 131104 | tf_op jit(solution)/shard_map/sum_over_devices/ppermute | solution.py:148
  155.6 2.8 %collective-permute-done.42 = bf16[128,512]{1,0:T(8,128)(2,1)S(1)} collective-permute-done((bf16[128,512]{1,0:T(8,128)(2,1)S(1)}, bf16[128,512]{1,0:T(8,128)(2,1)S(1)}, u32[]{:S(2)}, u32[]{:S(2)}) %collective-permute-start.42) | collective-permute-done | bytes 131104 | tf_op jit(solution)/shard_map/sum_over_devices/ppermute | solution.py:148
  158.4 1.2 add_convert_fusion.6
  159.6 1.5 collective-permute-start.39
  161.1 2.9 %collective-permute-start.43 = (bf16[128,512]{1,0:T(8,128)(2,1)S(1)}, bf16[128,512]{1,0:T(8,128)(2,1)S(1)}, u32[]{:S(2)}, u32[]{:S(2)}) collective-permute-start(bf16[128,512]{1,0:T(8,128)(2,1)S(1)} %get-tuple-element.50), channel_id=1, source_target_pairs={{0,4},{4,0},{8,12},{12,8},{1,5},{5,1},{9,13},{13,9},{2,6},{6,2},{1... | collective-permute-start | bytes 393224 | tf_op jit(solution)/shard_map/sum_over_devices/ppermute | solution.py:148
  164.0 3.9 %collective-permute-done.39 = bf16[128,512]{1,0:T(8,128)(2,1)S(1)} collective-permute-done((bf16[128,512]{1,0:T(8,128)(2,1)S(1)}, bf16[128,512]{1,0:T(8,128)(2,1)S(1)}, u32[]{:S(2)}, u32[]{:S(2)}) %collective-permute-start.39) | collective-permute-done | bytes 131104 | tf_op jit(solution)/shard_map/sum_over_devices/ppermute | solution.py:148
  167.9 3.7 %collective-permute-done.41 = bf16[128,512]{1,0:T(8,128)(2,1)S(1)} collective-permute-done((bf16[128,512]{1,0:T(8,128)(2,1)S(1)}, bf16[128,512]{1,0:T(8,128)(2,1)S(1)}, u32[]{:S(2)}, u32[]{:S(2)}) %collective-permute-start.41) | collective-permute-done | bytes 131104 | tf_op jit(solution)/shard_map/sum_over_devices/ppermute | solution.py:148
  171.6 1.1 add_convert_fusion
  172.7 7.0 %all_gather.3 = bf16[128,2048]{1,0:T(8,128)(2,1)S(1)} all-gather(bf16[128,512]{1,0:T(8,128)(2,1)S(1)} %add_convert_fusion), channel_id=1, replica_groups=mesh['grp'=2,'seq'=4,'head'=4] {'head'}, dimensions={1}, use_global_device_ids=true | all-gather | bytes 655360 | tf_op jit(solution)/shard_map/gather_columns/all_gather | solution.py:595
  179.7 0.8 copy.11
  (79 shorter events, 7.9 us)
Async XLA Ops:
  0.0 58.0 %copy-start.12 = (f32[2048]{0:T(1024)S(1)}, f32[2048]{0:T(1024)}, u32[]{:S(2)}) copy-start(f32[2048]{0:T(1024)} %param.11) | copy-start | bytes 24580
  0.1 1.6 copy-start
  1.7 1.0 copy-start.1
  2.7 0.7 copy-start.13
  3.4 0.7 copy-start.14
  4.1 53.9 %copy-start.2 = (bf16[128,2048]{1,0:T(8,128)(2,1)S(1)}, bf16[128,2048]{1,0:T(8,128)(2,1)}, u32[]{:S(2)}) copy-start(bf16[128,2048]{1,0:T(8,128)(2,1)} %tokens.3) | copy-start | bytes 1572868
  5.0 17.6 %copy-start.3 = (bf16[512,384]{1,0:T(8,128)(2,1)}, bf16[512,384]{1,0:T(8,128)(2,1)S(1)}, u32[]{:S(2)}) copy-start(bf16[512,384]{1,0:T(8,128)(2,1)S(1)} %get-tuple-element.27.w_own) | copy-start | bytes 1179652
  5.0 9.8 %collective-permute-start.2 = (bf16[144,512]{1,0:T(8,128)(2,1)S(1)}, bf16[144,512]{1,0:T(8,128)(2,1)S(1)}, u32[]{:S(2)}, u32[]{:S(2)}) collective-permute-start(bf16[144,512]{1,0:T(8,128)(2,1)S(1)} %get-tuple-element.28.refs_0_), channel_id=1, source_target_pairs={{0,12},{4,8},{8,4},{12,0},{1,13},{5,9},{9,5},{13,1},{2,14},{6,10},... | collective-permute-start | bytes 442376 | tf_op jit(solution)/shard_map/gather_tokens_and_weights/ppermute | solution.py:148
  10.2 12.5 %collective-permute-start = (bf16[144,512]{1,0:T(8,128)(2,1)S(1)}, bf16[144,512]{1,0:T(8,128)(2,1)S(1)}, u32[]{:S(2)}, u32[]{:S(2)}) collective-permute-start(bf16[144,512]{1,0:T(8,128)(2,1)S(1)} %get-tuple-element.28.refs_0_), channel_id=1, source_target_pairs={{0,4},{4,0},{8,12},{12,8},{1,5},{5,1},{9,13},{13,9},{2,6},{6,2},{1... | collective-permute-start | bytes 442376 | tf_op jit(solution)/shard_map/gather_tokens_and_weights/ppermute | solution.py:148
  10.2 12.5 %collective-permute-start.1 = (bf16[144,512]{1,0:T(8,128)(2,1)S(1)}, bf16[144,512]{1,0:T(8,128)(2,1)S(1)}, u32[]{:S(2)}, u32[]{:S(2)}) collective-permute-start(bf16[144,512]{1,0:T(8,128)(2,1)S(1)} %get-tuple-element.28.refs_0_), channel_id=1, source_target_pairs={{0,8},{4,12},{8,0},{12,4},{1,9},{5,13},{9,1},{13,5},{2,10},{6,14},... | collective-permute-start | bytes 442376 | tf_op jit(solution)/shard_map/gather_tokens_and_weights/ppermute | solution.py:148
  10.8 13.2 %collective-permute-start.3 = (bf16[512,512]{1,0:T(8,128)(2,1)S(1)}, bf16[512,512]{1,0:T(8,128)(2,1)}, u32[]{:S(2)}, u32[]{:S(2)}) collective-permute-start(bf16[512,512]{1,0:T(8,128)(2,1)S(1)} %get-tuple-element.29.rest_0_), channel_id=1, source_target_pairs={{0,2},{1,3},{2,0},{3,1},{4,6},{5,7},{6,4},{7,5},{8,10},{9,11},{10,... | collective-permute-start | bytes 1572872 | tf_op jit(solution)/shard_map/gather_tokens_and_weights/ppermute | solution.py:148
  24.0 18.1 %collective-permute-start.5 = (bf16[3,128,512]{2,1,0:T(8,128)(2,1)S(1)}, bf16[3,128,512]{2,1,0:T(8,128)(2,1)}, u32[]{:S(2)}, u32[]{:S(2)}) collective-permute-start(bf16[3,128,512]{2,1,0:T(8,128)(2,1)S(1)} %pad_maximum_fusion.rest_0_), channel_id=1, source_target_pairs={{0,2},{1,3},{2,0},{3,1},{4,6},{5,7},{6,4},{7,5},{8,10},{9,11},{10,... | collective-permute-start | bytes 1179656 | tf_op jit(solution)/shard_map/gather_tokens_and_weights/ppermute | solution.py:148
  25.5 7.8 %collective-permute-start.7 = (bf16[256,384]{1,0:T(8,128)(2,1)S(1)}, bf16[256,384]{1,0:T(8,128)(2,1)S(1)}, u32[]{:S(2)}, u32[]{:S(2)}) collective-permute-start(bf16[256,384]{1,0:T(8,128)(2,1)S(1)} %get-tuple-element.31), channel_id=1, source_target_pairs={{0,4},{4,0},{8,12},{12,8},{1,5},{5,1},{9,13},{13,9},{2,6},{6,2},{1... | collective-permute-start | bytes 589832 | tf_op jit(solution)/shard_map/gather_tokens_and_weights/ppermute | solution.py:148
  26.9 11.9 %collective-permute-start.8 = (bf16[256,384]{1,0:T(8,128)(2,1)S(1)}, bf16[256,384]{1,0:T(8,128)(2,1)S(1)}, u32[]{:S(2)}, u32[]{:S(2)}) collective-permute-start(bf16[256,384]{1,0:T(8,128)(2,1)S(1)} %get-tuple-element.32), channel_id=1, source_target_pairs={{0,8},{4,12},{8,0},{12,4},{1,9},{5,13},{9,1},{13,5},{2,10},{6,14},... | collective-permute-start | bytes 589832 | tf_op jit(solution)/shard_map/gather_tokens_and_weights/ppermute | solution.py:148
  38.8 7.6 %collective-permute-start.9 = (bf16[256,384]{1,0:T(8,128)(2,1)S(1)}, bf16[256,384]{1,0:T(8,128)(2,1)}, u32[]{:S(2)}, u32[]{:S(2)}) collective-permute-start(bf16[256,384]{1,0:T(8,128)(2,1)S(1)} %get-tuple-element.34), channel_id=1, source_target_pairs={{0,12},{4,8},{8,4},{12,0},{1,13},{5,9},{9,5},{13,1},{2,14},{6,10},... | collective-permute-start | bytes 589832 | tf_op jit(solution)/shard_map/gather_tokens_and_weights/ppermute | solution.py:148
  42.1 15.9 %collective-permute-start.4 = (bf16[3,128,512]{2,1,0:T(8,128)(2,1)S(1)}, bf16[3,128,512]{2,1,0:T(8,128)(2,1)}, u32[]{:S(2)}, u32[]{:S(2)}) collective-permute-start(bf16[3,128,512]{2,1,0:T(8,128)(2,1)S(1)} %pad_maximum_fusion.rest_0_), channel_id=1, source_target_pairs={{0,1},{1,0},{2,3},{3,2},{4,5},{5,4},{6,7},{7,6},{8,9},{9,8},{10,11... | collective-permute-start | bytes 1179656 | tf_op jit(solution)/shard_map/gather_tokens_and_weights/ppermute | solution.py:148
  42.1 15.9 %collective-permute-start.6 = (bf16[3,128,512]{2,1,0:T(8,128)(2,1)}, bf16[3,128,512]{2,1,0:T(8,128)(2,1)}, u32[]{:S(2)}, u32[]{:S(2)}) collective-permute-start(bf16[3,128,512]{2,1,0:T(8,128)(2,1)} %collective-permute-done.5.rest_2_), channel_id=1, source_target_pairs={{0,1},{1,0},{2,3},{3,2},{4,5},{5,4},{6,7},{7,6},{8,9},{9,8},{10,11... | collective-permute-start | bytes 1179656 | tf_op jit(solution)/shard_map/gather_tokens_and_weights/ppermute | solution.py:148
  42.6 7.8 %collective-permute-start.10 = (bf16[256,384]{1,0:T(8,128)(2,1)S(1)}, bf16[256,384]{1,0:T(8,128)(2,1)S(1)}, u32[]{:S(2)}, u32[]{:S(2)}) collective-permute-start(bf16[256,384]{1,0:T(8,128)(2,1)S(1)} %collective-permute-done.7.rest_4_), channel_id=1, source_target_pairs={{0,16},{16,0},{1,17},{17,1},{2,18},{18,2},{3,19},{19,3},{4,20},{20... | collective-permute-start | bytes 589832 | tf_op jit(solution)/shard_map/gather_tokens_and_weights/ppermute | solution.py:148
  44.1 10.5 %collective-permute-start.11 = (bf16[256,384]{1,0:T(8,128)(2,1)S(1)}, bf16[256,384]{1,0:T(8,128)(2,1)S(1)}, u32[]{:S(2)}, u32[]{:S(2)}) collective-permute-start(bf16[256,384]{1,0:T(8,128)(2,1)S(1)} %collective-permute-done.8.rest_5_), channel_id=1, source_target_pairs={{0,16},{16,0},{1,17},{17,1},{2,18},{18,2},{3,19},{19,3},{4,20},{20... | collective-permute-start | bytes 589832 | tf_op jit(solution)/shard_map/gather_tokens_and_weights/ppermute | solution.py:148
  44.6 0.7 copy-start.5
  46.4 11.5 %collective-permute-start.12 = (bf16[256,384]{1,0:T(8,128)(2,1)}, bf16[256,384]{1,0:T(8,128)(2,1)}, u32[]{:S(2)}, u32[]{:S(2)}) collective-permute-start(bf16[256,384]{1,0:T(8,128)(2,1)} %collective-permute-done.9.rest_6_), channel_id=1, source_target_pairs={{0,16},{16,0},{1,17},{17,1},{2,18},{18,2},{3,19},{19,3},{4,20},{20... | collective-permute-start | bytes 589832 | tf_op jit(solution)/shard_map/gather_tokens_and_weights/ppermute | solution.py:148
  50.4 0.7 copy-start.7
  51.0 25.3 %collective-permute-start.13 = (bf16[512,512]{1,0:T(8,128)(2,1)S(1)}, bf16[512,512]{1,0:T(8,128)(2,1)}, u32[]{:S(2)}, u32[]{:S(2)}) collective-permute-start(bf16[512,512]{1,0:T(8,128)(2,1)S(1)} %get-tuple-element.29.rest_0_), channel_id=1, source_target_pairs={{0,1},{1,0},{2,3},{3,2},{4,5},{5,4},{6,7},{7,6},{8,9},{9,8},{10,11... | collective-permute-start | bytes 1572872 | tf_op jit(solution)/shard_map/gather_tokens_and_weights/ppermute | solution.py:148
  54.6 0.7 copy-start.9
  55.3 21.0 %collective-permute-start.14 = (bf16[512,512]{1,0:T(8,128)(2,1)}, bf16[512,512]{1,0:T(8,128)(2,1)}, u32[]{:S(2)}, u32[]{:S(2)}) collective-permute-start(bf16[512,512]{1,0:T(8,128)(2,1)} %collective-permute-done.3.rest_2_), channel_id=1, source_target_pairs={{0,1},{1,0},{2,3},{3,2},{4,5},{5,4},{6,7},{7,6},{8,9},{9,8},{10,11... | collective-permute-start | bytes 1572872 | tf_op jit(solution)/shard_map/gather_tokens_and_weights/ppermute | solution.py:148
  58.0 1.0 copy-start.4
  59.0 0.9 copy-start.6
  59.9 0.9 copy-start.8
  60.8 0.9 copy-start.10
  67.4 42.3 %copy-start.11 = (f32[2048]{0:T(1024)S(1)}, f32[2048]{0:T(1024)}, u32[]{:S(2)}) copy-start(f32[2048]{0:T(1024)} %param.12) | copy-start | bytes 24580
  67.5 1.9 %collective-permute-start.15 = (bf16[128,128]{1,0:T(8,128)(2,1)S(1)}, bf16[128,128]{1,0:T(8,128)(2,1)S(1)}, u32[]{:S(2)}, u32[]{:S(2)}) collective-permute-start(bf16[128,128]{1,0:T(8,128)(2,1)S(1)} %get-tuple-element.59), channel_id=1, source_target_pairs={{0,1},{1,0},{2,3},{3,2},{4,5},{5,4},{6,7},{7,6},{8,9},{9,8},{10,11... | collective-permute-start | bytes 98312 | tf_op jit(solution)/shard_map/heads_to_tokens/ppermute | solution.py:148
  67.5 4.3 %collective-permute-start.16 = (bf16[128,128]{1,0:T(8,128)(2,1)S(1)}, bf16[128,128]{1,0:T(8,128)(2,1)S(1)}, u32[]{:S(2)}, u32[]{:S(2)}) collective-permute-start(bf16[128,128]{1,0:T(8,128)(2,1)S(1)} %get-tuple-element.58), channel_id=1, source_target_pairs={{0,2},{1,3},{2,0},{3,1},{4,6},{5,7},{6,4},{7,5},{8,10},{9,11},{10,... | collective-permute-start | bytes 98312 | tf_op jit(solution)/shard_map/heads_to_tokens/ppermute | solution.py:148
  68.1 3.7 %collective-permute-start.17 = (bf16[128,128]{1,0:T(8,128)(2,1)S(1)}, bf16[128,128]{1,0:T(8,128)(2,1)S(1)}, u32[]{:S(2)}, u32[]{:S(2)}) collective-permute-start(bf16[128,128]{1,0:T(8,128)(2,1)S(1)} %get-tuple-element.57), channel_id=1, source_target_pairs={{0,3},{1,2},{2,1},{3,0},{4,7},{5,6},{6,5},{7,4},{8,11},{9,10},{10,... | collective-permute-start | bytes 98312 | tf_op jit(solution)/shard_map/heads_to_tokens/ppermute | solution.py:148
  71.9 6.8 %collective-permute-start.18 = (bf16[4,128,128]{2,1,0:T(8,128)(2,1)S(1)}, bf16[4,128,128]{2,1,0:T(8,128)(2,1)S(1)}, u32[]{:S(2)}, u32[]{:S(2)}) collective-permute-start(bf16[4,128,128]{2,1,0:T(8,128)(2,1)S(1)} %pad_maximum_fusion.1.rest_4_), channel_id=1, source_target_pairs={{0,4},{4,0},{8,12},{12,8},{1,5},{5,1},{9,13},{13,9},{2,6},{6,2},{1... | collective-permute-start | bytes 393224 | tf_op jit(solution)/shard_map/heads_to_tokens/ppermute | solution.py:148
  71.9 13.0 %collective-permute-start.19 = (bf16[4,128,128]{2,1,0:T(8,128)(2,1)S(1)}, bf16[4,128,128]{2,1,0:T(8,128)(2,1)S(1)}, u32[]{:S(2)}, u32[]{:S(2)}) collective-permute-start(bf16[4,128,128]{2,1,0:T(8,128)(2,1)S(1)} %pad_maximum_fusion.1.rest_4_), channel_id=1, source_target_pairs={{0,8},{4,12},{8,0},{12,4},{1,9},{5,13},{9,1},{13,5},{2,10},{6,14},... | collective-permute-start | bytes 393224 | tf_op jit(solution)/shard_map/heads_to_tokens/ppermute | solution.py:148
  73.1 11.8 %collective-permute-start.20 = (bf16[4,128,128]{2,1,0:T(8,128)(2,1)S(1)}, bf16[4,128,128]{2,1,0:T(8,128)(2,1)S(1)}, u32[]{:S(2)}, u32[]{:S(2)}) collective-permute-start(bf16[4,128,128]{2,1,0:T(8,128)(2,1)S(1)} %pad_maximum_fusion.1.rest_4_), channel_id=1, source_target_pairs={{0,12},{4,8},{8,4},{12,0},{1,13},{5,9},{9,5},{13,1},{2,14},{6,10},... | collective-permute-start | bytes 393224 | tf_op jit(solution)/shard_map/heads_to_tokens/ppermute | solution.py:148
  88.1 6.3 %collective-permute-start.21 = (bf16[128,512]{1,0:T(8,128)(2,1)S(1)}, bf16[128,512]{1,0:T(8,128)(2,1)S(1)}, u32[]{:S(2)}, u32[]{:S(2)}) collective-permute-start(bf16[128,512]{1,0:T(8,128)(2,1)S(1)} %output_projection.1.refs_0_), channel_id=1, source_target_pairs={{0,4},{4,0},{8,12},{12,8},{1,5},{5,1},{9,13},{13,9},{2,6},{6,2},{1... | collective-permute-start | bytes 393224 | tf_op jit(solution)/shard_map/gather_residual/ppermute | solution.py:148
  90.8 5.0 %collective-permute-start.34 = (bf16[128,512]{1,0:T(8,128)(2,1)S(1)}, bf16[128,512]{1,0:T(8,128)(2,1)S(1)}, u32[]{:S(2)}, u32[]{:S(2)}) collective-permute-start(bf16[128,512]{1,0:T(8,128)(2,1)S(1)} %output_projection.1.refs_0_), channel_id=1, source_target_pairs={{0,2},{1,3},{2,0},{3,1},{4,6},{5,7},{6,4},{7,5},{8,10},{9,11},{10,... | collective-permute-start | bytes 393224 | tf_op jit(solution)/shard_map/gather_residual/ppermute | solution.py:148
  92.0 11.8 %collective-permute-start.23 = (bf16[128,512]{1,0:T(8,128)(2,1)S(1)}, bf16[128,512]{1,0:T(8,128)(2,1)S(1)}, u32[]{:S(2)}, u32[]{:S(2)}) collective-permute-start(bf16[128,512]{1,0:T(8,128)(2,1)S(1)} %output_projection.1.refs_0_), channel_id=1, source_target_pairs={{0,8},{4,12},{8,0},{12,4},{1,9},{5,13},{9,1},{13,5},{2,10},{6,14},... | collective-permute-start | bytes 393224 | tf_op jit(solution)/shard_map/gather_residual/ppermute | solution.py:148
  92.0 12.6 %collective-permute-start.33 = (bf16[128,512]{1,0:T(8,128)(2,1)S(1)}, bf16[128,512]{1,0:T(8,128)(2,1)S(1)}, u32[]{:S(2)}, u32[]{:S(2)}) collective-permute-start(bf16[128,512]{1,0:T(8,128)(2,1)S(1)} %output_projection.1.refs_0_), channel_id=1, source_target_pairs={{0,1},{1,0},{2,3},{3,2},{4,5},{5,4},{6,7},{7,6},{8,9},{9,8},{10,11... | collective-permute-start | bytes 393224 | tf_op jit(solution)/shard_map/gather_residual/ppermute | solution.py:148
  92.0 12.6 %collective-permute-start.25 = (bf16[128,512]{1,0:T(8,128)(2,1)S(1)}, bf16[128,512]{1,0:T(8,128)(2,1)S(1)}, u32[]{:S(2)}, u32[]{:S(2)}) collective-permute-start(bf16[128,512]{1,0:T(8,128)(2,1)S(1)} %output_projection.1.refs_0_), channel_id=1, source_target_pairs={{0,12},{4,8},{8,4},{12,0},{1,13},{5,9},{9,5},{13,1},{2,14},{6,10},... | collective-permute-start | bytes 393224 | tf_op jit(solution)/shard_map/gather_residual/ppermute | solution.py:148
  94.5 11.4 %collective-permute-start.31 = (bf16[128,512]{1,0:T(8,128)(2,1)S(1)}, bf16[128,512]{1,0:T(8,128)(2,1)S(1)}, u32[]{:S(2)}, u32[]{:S(2)}) collective-permute-start(bf16[128,512]{1,0:T(8,128)(2,1)S(1)} %collective-permute-done.21.refs_0_), channel_id=1, source_target_pairs={{0,2},{1,3},{2,0},{3,1},{4,6},{5,7},{6,4},{7,5},{8,10},{9,11},{10,... | collective-permute-start | bytes 393224 | tf_op jit(solution)/shard_map/gather_residual/ppermute | solution.py:148
  95.8 10.2 %collective-permute-start.35 = (bf16[128,512]{1,0:T(8,128)(2,1)S(1)}, bf16[128,512]{1,0:T(8,128)(2,1)S(1)}, u32[]{:S(2)}, u32[]{:S(2)}) collective-permute-start(bf16[128,512]{1,0:T(8,128)(2,1)S(1)} %collective-permute-done.34.refs_2_), channel_id=1, source_target_pairs={{0,1},{1,0},{2,3},{3,2},{4,5},{5,4},{6,7},{7,6},{8,9},{9,8},{10,11... | collective-permute-start | bytes 393224 | tf_op jit(solution)/shard_map/gather_residual/ppermute | solution.py:148
  103.7 6.0 %collective-permute-start.24 = (bf16[128,512]{1,0:T(8,128)(2,1)S(1)}, bf16[128,512]{1,0:T(8,128)(2,1)S(1)}, u32[]{:S(2)}, u32[]{:S(2)}) collective-permute-start(bf16[128,512]{1,0:T(8,128)(2,1)S(1)} %collective-permute-done.23.refs_0_), channel_id=1, source_target_pairs={{0,2},{1,3},{2,0},{3,1},{4,6},{5,7},{6,4},{7,5},{8,10},{9,11},{10,... | collective-permute-start | bytes 393224 | tf_op jit(solution)/shard_map/gather_residual/ppermute | solution.py:148
  104.6 9.9 %collective-permute-start.22 = (bf16[128,512]{1,0:T(8,128)(2,1)S(1)}, bf16[128,512]{1,0:T(8,128)(2,1)S(1)}, u32[]{:S(2)}, u32[]{:S(2)}) collective-permute-start(bf16[128,512]{1,0:T(8,128)(2,1)S(1)} %collective-permute-done.21.refs_0_), channel_id=1, source_target_pairs={{0,1},{1,0},{2,3},{3,2},{4,5},{5,4},{6,7},{7,6},{8,9},{9,8},{10,11... | collective-permute-start | bytes 393224 | tf_op jit(solution)/shard_map/gather_residual/ppermute | solution.py:148
  104.6 10.5 %collective-permute-start.26 = (bf16[128,512]{1,0:T(8,128)(2,1)S(1)}, bf16[128,512]{1,0:T(8,128)(2,1)S(1)}, u32[]{:S(2)}, u32[]{:S(2)}) collective-permute-start(bf16[128,512]{1,0:T(8,128)(2,1)S(1)} %collective-permute-done.25.refs_0_), channel_id=1, source_target_pairs={{0,2},{1,3},{2,0},{3,1},{4,6},{5,7},{6,4},{7,5},{8,10},{9,11},{10,... | collective-permute-start | bytes 393224 | tf_op jit(solution)/shard_map/gather_residual/ppermute | solution.py:148
  105.8 9.4 %collective-permute-start.32 = (bf16[128,512]{1,0:T(8,128)(2,1)S(1)}, bf16[128,512]{1,0:T(8,128)(2,1)S(1)}, u32[]{:S(2)}, u32[]{:S(2)}) collective-permute-start(bf16[128,512]{1,0:T(8,128)(2,1)S(1)} %collective-permute-done.31.refs_2_), channel_id=1, source_target_pairs={{0,1},{1,0},{2,3},{3,2},{4,5},{5,4},{6,7},{7,6},{8,9},{9,8},{10,11... | collective-permute-start | bytes 393224 | tf_op jit(solution)/shard_map/gather_residual/ppermute | solution.py:148
  106.0 14.4 %collective-permute-start.29 = (bf16[128,512]{1,0:T(8,128)(2,1)S(1)}, bf16[128,512]{1,0:T(8,128)(2,1)S(1)}, u32[]{:S(2)}, u32[]{:S(2)}) collective-permute-start(bf16[128,512]{1,0:T(8,128)(2,1)S(1)} %collective-permute-done.23.refs_0_), channel_id=1, source_target_pairs={{0,1},{1,0},{2,3},{3,2},{4,5},{5,4},{6,7},{7,6},{8,9},{9,8},{10,11... | collective-permute-start | bytes 393224 | tf_op jit(solution)/shard_map/gather_residual/ppermute | solution.py:148
  109.8 10.7 %collective-permute-start.30 = (bf16[128,512]{1,0:T(8,128)(2,1)S(1)}, bf16[128,512]{1,0:T(8,128)(2,1)S(1)}, u32[]{:S(2)}, u32[]{:S(2)}) collective-permute-start(bf16[128,512]{1,0:T(8,128)(2,1)S(1)} %collective-permute-done.24.refs_2_), channel_id=1, source_target_pairs={{0,1},{1,0},{2,3},{3,2},{4,5},{5,4},{6,7},{7,6},{8,9},{9,8},{10,11... | collective-permute-start | bytes 393224 | tf_op jit(solution)/shard_map/gather_residual/ppermute | solution.py:148
  114.5 11.1 %collective-permute-start.28 = (bf16[128,512]{1,0:T(8,128)(2,1)S(1)}, bf16[128,512]{1,0:T(8,128)(2,1)S(1)}, u32[]{:S(2)}, u32[]{:S(2)}) collective-permute-start(bf16[128,512]{1,0:T(8,128)(2,1)S(1)} %collective-permute-done.25.refs_0_), channel_id=1, source_target_pairs={{0,1},{1,0},{2,3},{3,2},{4,5},{5,4},{6,7},{7,6},{8,9},{9,8},{10,11... | collective-permute-start | bytes 393224 | tf_op jit(solution)/shard_map/gather_residual/ppermute | solution.py:148
  115.1 10.6 %collective-permute-start.27 = (bf16[128,512]{1,0:T(8,128)(2,1)S(1)}, bf16[128,512]{1,0:T(8,128)(2,1)S(1)}, u32[]{:S(2)}, u32[]{:S(2)}) collective-permute-start(bf16[128,512]{1,0:T(8,128)(2,1)S(1)} %collective-permute-done.26.refs_2_), channel_id=1, source_target_pairs={{0,1},{1,0},{2,3},{3,2},{4,5},{5,4},{6,7},{7,6},{8,9},{9,8},{10,11... | collective-permute-start | bytes 393224 | tf_op jit(solution)/shard_map/gather_residual/ppermute | solution.py:148
  134.8 10.3 %collective-permute-start.37 = (bf16[512,512]{1,0:T(8,128)(2,1)S(1)}, bf16[512,512]{1,0:T(8,128)(2,1)}, u32[]{:S(2)}, u32[]{:S(2)}) collective-permute-start(bf16[512,512]{1,0:T(8,128)(2,1)S(1)} %down_quarters_3.1), channel_id=1, source_target_pairs={{0,1},{1,0},{2,3},{3,2},{4,5},{5,4},{6,7},{7,6},{8,9},{9,8},{10,11... | collective-permute-start | bytes 1572872 | tf_op jit(solution)/shard_map/sum_over_devices/ppermute | solution.py:148
  141.2 9.3 %collective-permute-start.36 = (bf16[512,512]{1,0:T(8,128)(2,1)}, bf16[512,512]{1,0:T(8,128)(2,1)}, u32[]{:S(2)}, u32[]{:S(2)}) collective-permute-start(bf16[512,512]{1,0:T(8,128)(2,1)} %get-tuple-element.48), channel_id=1, source_target_pairs={{0,1},{1,0},{2,3},{3,2},{4,5},{5,4},{6,7},{7,6},{8,9},{9,8},{10,11... | collective-permute-start | bytes 1572872 | tf_op jit(solution)/shard_map/sum_over_devices/ppermute | solution.py:148
  146.4 6.4 %collective-permute-start.38 = (bf16[128,512]{1,0:T(8,128)(2,1)S(1)}, bf16[128,512]{1,0:T(8,128)(2,1)S(1)}, u32[]{:S(2)}, u32[]{:S(2)}) collective-permute-start(bf16[128,512]{1,0:T(8,128)(2,1)S(1)} %get-tuple-element.52), channel_id=1, source_target_pairs={{0,2},{1,3},{2,0},{3,1},{4,6},{5,7},{6,4},{7,5},{8,10},{9,11},{10,... | collective-permute-start | bytes 393224 | tf_op jit(solution)/shard_map/sum_over_devices/ppermute | solution.py:148
  147.0 8.6 %collective-permute-start.40 = (bf16[128,512]{1,0:T(8,128)(2,1)S(1)}, bf16[128,512]{1,0:T(8,128)(2,1)S(1)}, u32[]{:S(2)}, u32[]{:S(2)}) collective-permute-start(bf16[128,512]{1,0:T(8,128)(2,1)S(1)} %get-tuple-element.55), channel_id=1, source_target_pairs={{0,2},{1,3},{2,0},{3,1},{4,6},{5,7},{6,4},{7,5},{8,10},{9,11},{10,... | collective-permute-start | bytes 393224 | tf_op jit(solution)/shard_map/sum_over_devices/ppermute | solution.py:148
  148.5 9.9 %collective-permute-start.42 = (bf16[128,512]{1,0:T(8,128)(2,1)S(1)}, bf16[128,512]{1,0:T(8,128)(2,1)S(1)}, u32[]{:S(2)}, u32[]{:S(2)}) collective-permute-start(bf16[128,512]{1,0:T(8,128)(2,1)S(1)} %get-tuple-element.54), channel_id=1, source_target_pairs={{0,2},{1,3},{2,0},{3,1},{4,6},{5,7},{6,4},{7,5},{8,10},{9,11},{10,... | collective-permute-start | bytes 393224 | tf_op jit(solution)/shard_map/sum_over_devices/ppermute | solution.py:148
  149.0 15.0 %collective-permute-start.44 = (bf16[128,512]{1,0:T(8,128)(2,1)S(1)}, bf16[128,512]{1,0:T(8,128)(2,1)S(1)}, u32[]{:S(2)}, u32[]{:S(2)}) collective-permute-start(bf16[128,512]{1,0:T(8,128)(2,1)S(1)} %get-tuple-element.53), channel_id=1, source_target_pairs={{0,2},{1,3},{2,0},{3,1},{4,6},{5,7},{6,4},{7,5},{8,10},{9,11},{10,... | collective-permute-start | bytes 393224 | tf_op jit(solution)/shard_map/sum_over_devices/ppermute | solution.py:148
  159.6 8.4 %collective-permute-start.39 = (bf16[128,512]{1,0:T(8,128)(2,1)S(1)}, bf16[128,512]{1,0:T(8,128)(2,1)S(1)}, u32[]{:S(2)}, u32[]{:S(2)}) collective-permute-start(bf16[128,512]{1,0:T(8,128)(2,1)S(1)} %get-tuple-element.49), channel_id=1, source_target_pairs={{0,12},{4,8},{8,4},{12,0},{1,13},{5,9},{9,5},{13,1},{2,14},{6,10},... | collective-permute-start | bytes 393224 | tf_op jit(solution)/shard_map/sum_over_devices/ppermute | solution.py:148
  161.1 10.5 %collective-permute-start.41 = (bf16[128,512]{1,0:T(8,128)(2,1)S(1)}, bf16[128,512]{1,0:T(8,128)(2,1)S(1)}, u32[]{:S(2)}, u32[]{:S(2)}) collective-permute-start(bf16[128,512]{1,0:T(8,128)(2,1)S(1)} %get-tuple-element.51), channel_id=1, source_target_pairs={{0,8},{4,12},{8,0},{12,4},{1,9},{5,13},{9,1},{13,5},{2,10},{6,14},... | collective-permute-start | bytes 393224 | tf_op jit(solution)/shard_map/sum_over_devices/ppermute | solution.py:148
  161.1 10.5 %collective-permute-start.43 = (bf16[128,512]{1,0:T(8,128)(2,1)S(1)}, bf16[128,512]{1,0:T(8,128)(2,1)S(1)}, u32[]{:S(2)}, u32[]{:S(2)}) collective-permute-start(bf16[128,512]{1,0:T(8,128)(2,1)S(1)} %get-tuple-element.50), channel_id=1, source_target_pairs={{0,4},{4,0},{8,12},{12,8},{1,5},{5,1},{9,13},{13,9},{2,6},{6,2},{1... | collective-permute-start | bytes 393224 | tf_op jit(solution)/shard_map/sum_over_devices/ppermute | solution.py:148

commit v4 on v3

--- a/solution.py
+++ b/solution.py
@@ -20,6 +20,7 @@
 SMEM = pl.BlockSpec(memory_space=pltpu.SMEM)
 VMEM = pl.BlockSpec(memory_space=pltpu.VMEM)
 MIB = 1024 * 1024
+SLOW = 10**10
 
 
 def prefix_2(array, axis, combine, identity):
@@ -163,8 +164,12 @@
     return pltpu.with_memory_space_constraint(array, pltpu.HBM)
 
 
+def in_step(*arrays):
+    return lax.optimization_barrier(arrays)
+
+
 def cut_kernel(pos, routes, gates, tokens, weight, x_send, w_own, o_own, *rest):
-    w_sends, sems = rest[:-1], rest[-1]
+    w_sends, (r_here, g_here, sems) = rest[:-3], rest[-3:]
     g, s, h = pos[0], pos[1], pos[2]
     rows, cols, half = tokens.shape[0], x_send.shape[1], w_sends[0].shape[0]
     copies = [
@@ -173,6 +178,8 @@
             x_send.at[pl.ds(0, rows)],
         ),
         (weight.at[3], o_own),
+        (routes, r_here),
+        (gates, g_here),
     ]
     for which in range(3):
         span = pl.ds(which * HEAD_DIM, HEAD_DIM)
@@ -187,7 +194,9 @@
     copies = [pltpu.make_async_copy(a, b, sems.at[i]) for i, (a, b) in enumerate(copies)]
     for copy in copies:
         copy.start()
-    parts, left = [routes[...].astype(F32)], gates[...]
+    for copy in copies[2:4]:
+        copy.wait()
+    parts, left = [r_here[...].astype(F32)], g_here[...]
     for _ in range(3):
         parts.append(left.astype(BF16).astype(F32))
         left = left - parts[-1]
@@ -197,7 +206,7 @@
     if blank.shape[1]:
         lines = jnp.concatenate([lines, blank], axis=1)
     x_send[rows:, :] = lines.astype(BF16)
-    for copy in copies:
+    for copy in copies[:2] + copies[4:]:
         copy.wait()
 
 
@@ -215,25 +224,36 @@
     def at_rows(block, size):
         return pl.ds(pl.multiple_of(block * size, size), size)
 
-    copies = [(tokens, x_all.at[at_rows(s, rows)]), (w_own, w_all.at[at_rows(s, depth)])]
-    for e in range(n):
-        for d in range(1, n):
+    copies = [(tokens, x_all.at[at_rows(s, rows)])]
+    for d in range(1, n):
+        for e in range(n):
             copies.append(
                 (x_pieces[e].at[d - 1], x_all.at[at_rows(s ^ d, rows), at_rows(h ^ e, cols)])
             )
+    n_rows = len(copies)
+    copies.append((w_own, w_all.at[at_rows(s, depth)]))
     for d in range(1, n):
         copies.append((w_near[d - 1], w_all.at[at_rows((s ^ d) * 2 + g, half)]))
         copies.append((w_far[d - 1], w_all.at[at_rows((s ^ d) * 2 + (1 - g), half)]))
-    run_copies([pltpu.make_async_copy(a, b, sems.at[i]) for i, (a, b) in enumerate(copies)])
-
-    projected = []
+    copies = [pltpu.make_async_copy(a, b, sems.at[i]) for i, (a, b) in enumerate(copies)]
+    for copy in copies:
+        copy.start()
+    for copy in copies[:n_rows]:
+        copy.wait()
+    x_share[...] = x_all[at_rows(h, rows), at_rows(s, cols)]
+
     for block in range(n):
         wide = x_all[block * rows : (block + 1) * rows, :].astype(F32)
         factor = lax.rsqrt(jnp.mean(wide * wide, axis=-1, keepdims=True) + EPS)
-        normed = (wide * factor * gain[...]).astype(BF16)
-        projected.append(
-            jnp.dot(normed, w_all[...], preferred_element_type=F32).astype(BF16)
-        )
+        x_all[block * rows : (block + 1) * rows, :] = (wide * factor * gain[...]).astype(BF16)
+    for copy in copies[n_rows:]:
+        copy.wait()
+    projected = [
+        jnp.dot(
+            x_all[block * rows : (block + 1) * rows, :], w_all[...], preferred_element_type=F32
+        ).astype(BF16)
+        for block in range(n)
+    ]
     whole = jnp.concatenate(projected, axis=0)
     query, key, value = (whole[:, i * HEAD_DIM : (i + 1) * HEAD_DIM] for i in range(3))
     for block in range(n):
@@ -253,25 +273,19 @@
         )
         out = out * lax.rsqrt(jnp.mean(out * out, axis=-1, keepdims=True) + EPS)
         attended[block] = out.astype(BF16)
-    x_share[...] = x_all[at_rows(h, rows), at_rows(s, cols)]
-
 
 def project_kernel(n, pos, x_share, *rest):
-    weights, pieces, (out, a_all, w_all, sems) = rest[:n], rest[n : 2 * n], rest[2 * n :]
-    s, h = pos[1], pos[2]
-    cols = weights[0].shape[1]
-    copies = []
+    weights, pieces, (out, a_all) = rest[:n], rest[n : 2 * n], rest[2 * n :]
+    s = pos[1]
+    total = x_share[...].astype(F32)
     for e in range(n):
-        copies.append((weights[e], w_all.at[:, pl.ds(pl.multiple_of((h ^ e) * cols, cols), cols)]))
         for d in range(n):
-            head = (h ^ e) * n + (s ^ d)
-            span = pl.ds(pl.multiple_of(head * HEAD_DIM, HEAD_DIM), HEAD_DIM)
-            copies.append((pieces[d].at[e], a_all.at[:, span]))
-    run_copies([pltpu.make_async_copy(a, b, sems.at[i]) for i, (a, b) in enumerate(copies)])
-    product = lax.dot_general(
-        a_all[...], w_all[...], (((1,), (1,)), ((), ())), preferred_element_type=F32
-    )
-    out[...] = (x_share[...].astype(F32) + product).astype(BF16)
+            span = pl.ds(pl.multiple_of((s ^ d) * HEAD_DIM, HEAD_DIM), HEAD_DIM)
+            a_all[e, :, span] = pieces[d][e]
+        total = total + lax.dot_general(
+            a_all[e], weights[e][...], (((1,), (1,)), ((), ())), preferred_element_type=F32
+        )
+    out[...] = total.astype(BF16)
 
 
 def route_kernel(n, experts, slots, pos, *refs):
@@ -332,11 +346,11 @@
     return wait
 
 
-def hidden_kernel(n, slots, group, distance, last, pos, gain, *refs):
-    first = distance == 0
+def hidden_kernel(n, slots, group, distances, last, pos, gain, pick, w_gate, w_up, *refs):
+    first = 0 in distances
     refs = list(refs)
-    pieces = [refs.pop(0) for _ in range(n)]
-    pick, w_gate, w_up = (refs.pop(0) for _ in range(3))
+    n_blocks = len(distances)
+    pieces = [[refs.pop(0) for _ in range(n)] for _ in range(n_blocks)]
     if not first:
         total_in, square_in = refs.pop(0), refs.pop(0)
     if last:
@@ -344,51 +358,61 @@
     else:
         total_out, square_out, r_all, scaled, g_all, u_all, sems = refs
     s, h = pos[1], pos[2]
-    rows, cols = pieces[0].shape
+    rows, cols = pieces[0][0].shape
     experts, _, hidden = g_all.shape
-    column = pl.ds(pl.multiple_of((s ^ distance) * cols, cols), cols)
+
+    def span(block, size):
+        return pl.ds(pl.multiple_of(block * size, size), size)
 
     def moves(i):
         part = pl.ds(i * group, group)
-        return [
-            ((w_gate.at[part, column, :], g_all.at[part]), sems.at[2 * i]),
-            ((w_up.at[part, column, :], u_all.at[part]), sems.at[2 * i + 1]),
-        ]
+        out = []
+        for k, distance in enumerate(distances):
+            column, here = span(s ^ distance, cols), pl.ds(k * cols, cols)
+            for which, (w, kept) in enumerate(((w_gate, g_all), (w_up, u_all))):
+                sem = sems.at[(i * n_blocks + k) * 2 + which]
+                out.append(((w.at[part, column, :], kept.at[part, here, :]), sem))
+        return out
 
     wait = stream(experts // group, moves)
-    for e in range(n):
-        r_all[pl.ds(pl.multiple_of((h ^ e) * rows, rows), rows), :] = pieces[e][...]
+    gains = []
+    for k, distance in enumerate(distances):
+        here = slice(k * cols, (k + 1) * cols)
+        for e in range(n):
+            r_all[span(h ^ e, rows), here] = pieces[k][e][...]
+        gains.append(gain[:, span(s ^ distance, cols)])
     width = n * cols
     factor = []
     for i in range(experts // group):
         part = slice(i * group * slots, (i + 1) * group * slots)
-        taken = jnp.dot(pick[part, :], r_all[...], preferred_element_type=F32)
-        square = jnp.sum(taken * taken, axis=1, keepdims=True)
-        if not first:
-            square = square + square_in[part, :1]
+        square = 0.0 if first else square_in[part, :1]
+        for k in range(n_blocks):
+            here = slice(k * cols, (k + 1) * cols)
+            taken = jnp.dot(pick[part, :], r_all[:, here], preferred_element_type=F32)
+            square = square + jnp.sum(taken * taken, axis=1, keepdims=True)
+            scaled[part, here] = (taken * gains[k]).astype(BF16)
         if last:
             factor.append(lax.rsqrt(square / width + EPS))
         else:
             square_out[part, :] = jnp.broadcast_to(square, (group * slots, square_out.shape[1]))
-        scaled[part, :] = (taken * gain[:, column]).astype(BF16)
     for i in range(experts // group):
         wait(i)
         for e in range(i * group, (i + 1) * group):
-            span = slice(e * slots, (e + 1) * slots)
-            gate_val = jnp.dot(scaled[span, :], g_all[e], preferred_element_type=F32)
-            up_val = jnp.dot(scaled[span, :], u_all[e], preferred_element_type=F32)
+            mine = slice(e * slots, (e + 1) * slots)
+            gate_val = jnp.dot(scaled[mine, :], g_all[e], preferred_element_type=F32)
+            up_val = jnp.dot(scaled[mine, :], u_all[e], preferred_element_type=F32)
             if not first:
-                gate_val = gate_val + total_in[span, :hidden]
-                up_val = up_val + total_in[span, hidden:]
+                gate_val = gate_val + total_in[mine, :hidden]
+                up_val = up_val + total_in[mine, hidden:]
             if last:
                 inner = (e - i * group) * slots
                 scale = factor[i][inner : inner + slots]
                 gate_val, up_val = gate_val * scale, up_val * scale
-                value = gate_val * jax.nn.sigmoid(gate_val) * (up_val * weight[span, :1])
-                hidden_out[span, :] = value.astype(BF16)
+                value = gate_val * jax.nn.sigmoid(gate_val) * (up_val * weight[mine, :1])
+                hidden_out[mine, :] = value.astype(BF16)
             else:
-                total_out[span, :hidden] = gate_val
-                total_out[span, hidden:] = up_val
+                total_out[mine, :hidden] = gate_val
+                total_out[mine, hidden:] = up_val
 
 
 def down_kernel(n, slots, group, distances, pos, hidden, place, w_down, *refs):
@@ -411,6 +435,18 @@
                 product = jnp.dot(hidden[span, :], d_all[k, e], preferred_element_type=F32)
                 y_slots[span, :] = product.astype(BF16)
         outs[k][...] = jnp.dot(place[...], y_slots[...], preferred_element_type=F32).astype(BF16)
+
+
+def add_kernel(distances, pos, base, core, part, *outs):
+    s = pos[1]
+    rows = outs[0].shape[0]
+    in_half = part.shape[0] // rows
+    for d, out in zip(distances, outs):
+        block = s ^ d
+        everywhere = pl.ds(pl.multiple_of(block * rows, rows), rows)
+        inside = pl.ds(pl.multiple_of(block % in_half * rows, rows), rows)
+        value = base[everywhere, :].astype(F32) + core[everywhere, :].astype(F32)
+        out[...] = (value + part[inside, :].astype(F32)).astype(out.dtype)
 
 
 def square_body(
@@ -451,22 +487,29 @@
                 sds((depth, cols), BF16),
             ]
             + [sds((half, 3 * HEAD_DIM), BF16)] * (n - 1),
-            in_specs=[SMEM, VMEM, VMEM, ANY, ANY],
+            in_specs=[SMEM] + [ANY] * 4,
             out_specs=[VMEM] * (n + 2),
-            scratch_shapes=[dma((2 + 3 * n,))],
+            scratch_shapes=[
+                pltpu.VMEM((TOPK, rows), jnp.int32),
+                pltpu.VMEM((TOPK, rows), F32),
+                dma((4 + 3 * n,)),
+            ],
             compiler_params=room(8),
-        )(pos, routes.T, gates.T, tokens, attn_weight)
+        )(pos, *map(held, (routes.T, gates.T, tokens, attn_weight)))
     with jax.named_scope("gather_tokens_and_weights"):
         x_far = [swap(x_send, "seq", d) for d in range(1, n)]
         w_near = [swap(w_sends[d - 1], "seq", d) for d in range(1, n - 1)]
+        step = in_step(*x_far, *w_near, w_sends[-1])
+        x_far, w_near, w_last = step[: n - 1], list(step[n - 1 : -1]), step[-1]
+        x_pieces = {0: jnp.stack([x[:rows] for x in x_far])}
+        x_pieces[2] = swap(x_pieces[0], "head", 2)
+        w_far = [swap(w, "grp", 1) for w in w_near]
+        w_near.append(swap(w_last, "seq", n - 1))
+        x_pieces[2], w_near[-1], o_own, *w_far = in_step(x_pieces[2], w_near[-1], o_own, *w_far)
+        w_far.append(swap(w_near[-1], "grp", 1))
         o_pieces = {0: o_own, 2: swap(o_own, "head", 2)}
-        w_near.append(swap(after(w_sends[-1], *x_far, *w_near), "seq", n - 1))
-        w_far = [swap(w, "grp", 1) for w in w_near]
-        x_pieces = {0: after(jnp.stack([x[:rows] for x in x_far]), o_pieces[2])}
-        x_pieces[2] = swap(x_pieces[0], "head", 2)
-        for pieces in (o_pieces, x_pieces):
-            for e in (0, 2):
-                pieces[e ^ 1] = swap(pieces[e], "head", 1)
+        for e in (0, 2):
+            x_pieces[e ^ 1] = swap(x_pieces[e], "head", 1)
     with jax.named_scope("routing"):
         pick, place, weight = pl.pallas_call(
             functools.partial(route_kernel, n, experts, slots),
@@ -482,83 +525,90 @@
         attended, x_share = pl.pallas_call(
             functools.partial(attend_kernel, n),
             out_shape=[sds((n, rows, HEAD_DIM), BF16), sds((rows, cols), BF16)],
-            in_specs=[SMEM, VMEM] + [ANY] * (2 + n + 2 * (n - 1)),
+            in_specs=[SMEM, VMEM] + [ANY] * (2 + n + 2 * (n - 1) - 1) + [VMEM],
             out_specs=[VMEM] * 2,
             scratch_shapes=[
                 pltpu.VMEM((total, width), BF16),
                 pltpu.VMEM((width, 3 * HEAD_DIM), BF16),
                 dma((2 + n * (n - 1) + 2 * (n - 1),)),
             ],
-            compiler_params=room(20),
+            compiler_params=room(14),
         )(
-            pos, attn_gain.reshape(1, width), tokens, w_own,
-            *[x_pieces[e] for e in range(n)], *w_near, *w_far,
+            pos, attn_gain.reshape(1, width), held(tokens), held(w_own),
+            *[held(x_pieces[e]) for e in range(n)], *map(held, w_near), *map(held, w_far[:-1]), w_far[-1],
         )
 
     with jax.named_scope("heads_to_tokens"):
+        for e in (0, 2):
+            o_pieces[e ^ 1] = swap(after(o_pieces[e], attended), "head", 1)
         by_block = [
             lax.dynamic_index_in_dim(attended, h ^ e, 0, keepdims=False) for e in range(n)
         ]
         arrived = jnp.stack([by_block[0]] + [swap(by_block[e], "head", e) for e in range(1, n)])
-        a_pieces = [arrived] + [swap(arrived, "seq", d) for d in range(1, n)]
+        a_pieces = [arrived, swap(arrived, "seq", 1), swap(arrived, "seq", 2)]
+        a_pieces.append(swap(a_pieces[2], "seq", 1))
 
     with jax.named_scope("output_projection"):
         residual = pl.pallas_call(
             functools.partial(project_kernel, n),
             out_shape=sds((rows, cols), BF16),
-            in_specs=[SMEM, VMEM] + [ANY] * (2 * n),
+            in_specs=[SMEM] + [VMEM] * (1 + 2 * n),
             out_specs=VMEM,
-            scratch_shapes=[
-                pltpu.VMEM((rows, width), BF16),
-                pltpu.VMEM((depth, width), BF16),
-                dma((n + n * n,)),
-            ],
+            scratch_shapes=[pltpu.VMEM((n, rows, n * HEAD_DIM), BF16)],
             compiler_params=room(12),
         )(pos, x_share, *[o_pieces[e] for e in range(n)], *a_pieces)
 
-    with jax.named_scope("gather_residual"):
-        r_pieces = []
-        for d in range(n):
-            r = {0: residual if d == 0 else swap(residual, "seq", d)}
-            r[2] = swap(r[0], "head", 2)
-            for e in (0, 2):
-                r[e ^ 1] = swap(r[e], "head", 1)
-            r_pieces.append(r)
-
     group = experts // 4
-    state = ()
-    for d in range(n):
-        last = d == n - 1
-        with jax.named_scope(f"hidden_units_{d}"):
-            state = pl.pallas_call(
-                functools.partial(hidden_kernel, n, slots, group, d, last),
+
+    def add_blocks(distances, pieces, state):
+        last = n - 1 in distances
+        wide = len(distances) * cols
+        with jax.named_scope("hidden_units_" + "_".join(map(str, distances))):
+            return pl.pallas_call(
+                functools.partial(hidden_kernel, n, slots, group, distances, last),
                 out_shape=[sds((pairs, hidden), BF16)]
                 if last
                 else [sds((pairs, 2 * hidden), F32), sds((pairs, 128), F32)],
-                in_specs=[SMEM]
-                + [VMEM] * (n + 2)
-                + [ANY] * 2
-                + [VMEM] * (len(state) + last),
+                in_specs=[SMEM] + [VMEM] * 2 + [ANY] * 2
+                + [VMEM] * (n * len(distances) + len(state) + last),
                 out_specs=[VMEM] * (2 - last),
                 scratch_shapes=[
-                    pltpu.VMEM((total, cols), BF16),
-                    pltpu.VMEM((pairs, cols), BF16),
-                    pltpu.VMEM((experts, cols, hidden), BF16),
-                    pltpu.VMEM((experts, cols, hidden), BF16),
-                    dma((2 * (experts // group),)),
+                    pltpu.VMEM((total, wide), BF16),
+                    pltpu.VMEM((pairs, wide), BF16),
+                    pltpu.VMEM((experts, wide, hidden), BF16),
+                    pltpu.VMEM((experts, wide, hidden), BF16),
+                    dma((2 * len(distances) * (experts // group),)),
                 ],
-                compiler_params=room(28),
-                cost_estimate=cost(pairs * cols * (total + 2 * hidden), 4 * experts * cols * hidden),
+                compiler_params=room(6 + 11 * len(distances)),
+                cost_estimate=cost(pairs * wide * (total + 2 * hidden), 4 * experts * wide * hidden),
             )(
-                pos, moe_gain.reshape(1, width), *[r_pieces[d][e] for e in range(n)],
-                pick, held(expert_gate), held(expert_up), *state, *([weight] if last else []),
+                pos, moe_gain.reshape(1, width), pick, held(expert_gate), held(expert_up),
+                *[pieces[d][e] for d in distances for e in range(n)],
+                *state, *([weight] if last else []),
             )
+
+    with jax.named_scope("gather_residual"):
+        early, late = tuple(range(n // 2)), tuple(range(n // 2, n))
+        r_pieces = {0: {0: residual}}
+        for d in (1, 2):
+            r_pieces[d] = {0: swap(residual, "seq", d)}
+        r_pieces[3] = {0: swap(r_pieces[2][0], "seq", 1)}
+        for d in range(n):
+            r_pieces[d][2] = swap(r_pieces[d][0], "head", 2)
+            r_pieces[d][1] = swap(r_pieces[d][0], "head", 1)
+        for d in early:
+            r_pieces[d][3] = swap(r_pieces[d][2], "head", 1)
+        r_pieces[0][0] = after(residual, *[r_pieces[d][0] for d in late])
+        state = add_blocks(early, r_pieces, ())
+        for d in late:
+            r_pieces[d][3] = swap(after(r_pieces[d][2], state[1]), "head", 1)
+        state = add_blocks(late, r_pieces, state)
+        r_choices = [r_pieces[d][d] for d in range(n)]
     (units,) = state
 
-    out = {}
-    for distances in ((3,), (2,), (1, 0)):
+    def down(distances, units):
         with jax.named_scope("down_quarters_" + "_".join(map(str, distances))):
-            outs = pl.pallas_call(
+            return pl.pallas_call(
                 functools.partial(down_kernel, n, slots, group, distances),
                 out_shape=[sds((total, cols), BF16)] * len(distances),
                 in_specs=[SMEM, VMEM, VMEM, ANY],
@@ -568,28 +618,49 @@
                     pltpu.VMEM((pairs, cols), BF16),
                     dma((len(distances) * (experts // group),)),
                 ],
-                compiler_params=room(24),
+                compiler_params=room(4 + 5 * len(distances)),
                 cost_estimate=cost(
                     len(distances) * pairs * cols * (total + hidden),
                     2 * len(distances) * experts * cols * hidden,
                 ),
             )(pos, units, place, held(expert_down))
-            out.update(zip(distances, outs))
-
-    def rows_of(array, d):
-        return lax.dynamic_slice_in_dim(array, (s ^ d) * rows, rows, 0)
+
+    def rows_of(array, block, count=1):
+        return lax.dynamic_slice_in_dim(array, block * rows, count * rows, 0)
 
     with jax.named_scope("sum_over_devices"):
-        from_core = {e: swap(out[e ^ 1], "head", 1) for e in (2, 0)}
-        mixed = lax.select_n(s ^ h, *[r_pieces[d][d] for d in range(n)]).astype(F32)
-        for d in (3, 2, 1, 0):
-            near = plus(rows_of(out[2], d), rows_of(from_core[2], d)).astype(BF16)
-            summed = plus(
-                rows_of(out[0], d), rows_of(from_core[0], d), swap(near, "head", 2)
-            )
-            if d:
-                summed = swap(summed.astype(BF16), "seq", d)
-            mixed = mixed + summed
+        half_line = n // 2
+        here = s // half_line * half_line
+        there = half_line - here
+        out_3, out_1 = down((3, 1), units)
+        core_2, core_0 = swap(out_3, "head", 1), swap(out_1, "head", 1)
+        (out_2,) = down((2,), after(units, out_3))
+        near = [
+            plus(rows_of(out_2, b, half_line), rows_of(core_2, b, half_line)).astype(BF16)
+            for b in (there, here)
+        ]
+        far = [swap(part, "head", 2) for part in near]
+        (out_0,) = down((0,), after(units, *near))
+
+        def add_parts(scope, distances, part, macs):
+            with jax.named_scope(scope):
+                return pl.pallas_call(
+                    functools.partial(add_kernel, distances),
+                    out_shape=[sds((rows, cols), BF16 if d else F32) for d in distances],
+                    in_specs=[SMEM] + [VMEM] * 3,
+                    out_specs=[VMEM] * len(distances),
+                    compiler_params=room(4),
+                    cost_estimate=cost(macs, 4 * part.size),
+                )(pos, out_0, core_0, part)
+
+        far_line = tuple(range(half_line, n))
+        near_line = tuple(range(half_line))
+        far_sums = add_parts("far_half_rows", far_line, far[0], 0)
+        from_far = [swap(part, "seq", d) for d, part in zip(far_line, far_sums)]
+        own_sum, *near_sums = add_parts("near_half_rows", near_line, far[1], SLOW)
+        from_near = [swap(part, "seq", d) for d, part in zip(near_line[1:], near_sums)]
+        mixed = plus(lax.select_n(s ^ h, *in_step(*r_choices, own_sum)[:n]), own_sum, *from_far)
+        mixed = plus(*in_step(mixed, *from_near))
         mixed = mixed.astype(BF16)
     with jax.named_scope("gather_columns"):
         return lax.all_gather(mixed, "head", axis=1, tiled=True)
@@ -607,6 +678,7 @@
             and sizes["grp"] == 2
             and width == n * attn_weight.shape[1] == n * attn_weight.shape[2]
             and width == n * n * HEAD_DIM
+            and n * tokens.shape[0] <= width // n
         )
         if square:
             return square_body(n, tokens, attn_weight, *rest)

time: 181 us -> 157 us (0.87)
  starting transfers between devices: 46.5 us -> 36.9 us
  waiting for transfers between devices: 67.3 us -> 58.8 us
  local copies, waits for them, and re-layouts: 10.7 us -> 5.65 us
    ppermute x45 -> x43, starting transfers between devices: 46.5 us -> 36.9 us  [swap(): return lax.ppermute(array, axis, [(i, i ^ distance) for i in range(size)])]
    ppermute x45 -> x43, waiting for transfers between devices: 67.3 us -> 58.8 us  [swap(): return lax.ppermute(array, axis, [(i, i ^ distance) for i in range(size)])]
    unnamed x31 -> x39, local copies, waits for them, and re-layouts: 10.6 us -> 5.61 us
    pallas_call x1, Pallas kernels: 0.94 us -> 2.93 us  [square_body(): pl.pallas_call(cut_kernel, out_shape=[sds((rows + lines, cols), BF16), sd...]
  transfers between devices with their start and end apart: 45 -> 43, of which waited for: 21 -> 21; matrix products, arithmetic and copies ran while one was open for 1% -> 1% of each run, Pallas kernels for 18% -> 16%
where the time goes in v4:
time: 157 us
  waiting for transfers between devices  58.8 us (37%)
  Pallas kernels  45 us (29%)
  starting transfers between devices  36.9 us (24%)
  blocking collectives  6.96 us (4%)
  local copies, waits for them, and re-layouts  5.65 us (4%)
  other arithmetic  3 us (2%)
    ppermute x43, waiting for transfers between devices, swap(): return lax.ppermute(array, axis, [(i, i ^ distance) for i in range(size)])  58.8 us
    ppermute x43, starting transfers between devices, swap(): return lax.ppermute(array, axis, [(i, i ^ distance) for i in range(size)])  36.9 us
    pallas_call x2, Pallas kernels, add_blocks(): pl.pallas_call(functools.partial(hidden_kernel, n, slots, group, distance...  17.8 us
    pallas_call x3, Pallas kernels, down(): pl.pallas_call(functools.partial(down_kernel, n, slots, group, distances)...  13.4 us
    all_gather x1, blocking collectives, square_body(): return lax.all_gather(mixed, 'head', axis=1, tiled=True)  6.96 us
    unnamed x39, local copies, waits for them, and re-layouts  5.61 us
    pallas_call x1, Pallas kernels, square_body(): pl.pallas_call(functools.partial(attend_kernel, n), out_shape=[sds((n, ro...  5.52 us
  transfers between devices with their start and end apart: 43, of which 21 were waited for; matrix products, arithmetic and copies ran while one was open for 1% of the time, Pallas kernels for 16%

profile of v4, /device:TPU:0, one launch (start us, length us, event | category | flops | bytes accessed | tf_op | source)
XLA Modules:
  0.0 156.6 jit_solution(15188033802973333124)
XLA Ops:
  0.1 2.9 %cut_pieces.1 = (bf16[144,512]{1,0:T(8,128)(2,1)S(1)}, bf16[512,384]{1,0:T(8,128)(2,1)S(1)}, bf16[512,512]{1,0:T(8,128)(2,1)}, bf16[256,384]{1,0:T(8,128)(2,1)S(...) custom-call(s32[3]{0:T(128)S(1)} %pad_add_fusion.pos, s32[8,128]{1,0:T(8,128)} %bitcast.28, ...), custom_call_target="tpu_custom_call" | custom-call | tf_op jit(solution)/shard_map/cut_pieces/pallas_call | solution.py:482
  3.0 0.7 copy-done.10
  3.8 3.0 %collective-permute-start.3 = (bf16[256,384]{1,0:T(8,128)(2,1)S(1)}, bf16[256,384]{1,0:T(8,128)(2,1)S(1)}, u32[]{:S(2)}, u32[]{:S(2)}) collective-permute-start(bf16[256,384]{1,0:T(8,128)(2,1)S(1)} %get-tuple-element.51), channel_id=1, source_target_pairs={{0,4},{4,0},{8,12},{12,8},{1,5},{5,1},{9,13},{13,9},{2,6},{6,2},{1... | collective-permute-start | bytes 589832 | tf_op jit(solution)/shard_map/gather_tokens_and_weights/ppermute | solution.py:149
  6.8 2.6 %collective-permute-start.4 = (bf16[256,384]{1,0:T(8,128)(2,1)S(1)}, bf16[256,384]{1,0:T(8,128)(2,1)S(1)}, u32[]{:S(2)}, u32[]{:S(2)}) collective-permute-start(bf16[256,384]{1,0:T(8,128)(2,1)S(1)} %get-tuple-element.52), channel_id=1, source_target_pairs={{0,8},{4,12},{8,0},{12,4},{1,9},{5,13},{9,1},{13,5},{2,10},{6,14},... | collective-permute-start | bytes 589832 | tf_op jit(solution)/shard_map/gather_tokens_and_weights/ppermute | solution.py:149
  9.4 0.4 collective-permute-start
  9.8 3.9 %collective-permute-start.2 = (bf16[144,512]{1,0:T(8,128)(2,1)S(1)}, bf16[144,512]{1,0:T(8,128)(2,1)S(1)}, u32[]{:S(2)}, u32[]{:S(2)}) collective-permute-start(bf16[144,512]{1,0:T(8,128)(2,1)S(1)} %get-tuple-element.50.refs_0_), channel_id=1, source_target_pairs={{0,12},{4,8},{8,4},{12,0},{1,13},{5,9},{9,5},{13,1},{2,14},{6,10},... | collective-permute-start | bytes 442376 | tf_op jit(solution)/shard_map/gather_tokens_and_weights/ppermute | solution.py:149
  13.8 0.7 copy-done.11
  14.4 6.6 %collective-permute-done.refs_1_ = bf16[144,512]{1,0:T(8,128)(2,1)S(1)} collective-permute-done((bf16[144,512]{1,0:T(8,128)(2,1)S(1)}, bf16[144,512]{1,0:T(8,128)(2,1)S(1)}, u32[]{:S(2)}, u32[]{:S(2)}) %collective-permute-start) | collective-permute-done | bytes 147488 | tf_op jit(solution)/shard_map/gather_tokens_and_weights/ppermute | solution.py:149
  21.1 8.1 %collective-permute-done.1.refs_2_ = bf16[144,512]{1,0:T(8,128)(2,1)S(1)} collective-permute-done((bf16[144,512]{1,0:T(8,128)(2,1)S(1)}, bf16[144,512]{1,0:T(8,128)(2,1)S(1)}, u32[]{:S(2)}, u32[]{:S(2)}) %collective-permute-start.1) | collective-permute-done | bytes 147488 | tf_op jit(solution)/shard_map/gather_tokens_and_weights/ppermute | solution.py:149
  29.3 0.6 copy-done.2
  29.9 0.8 pad_maximum_fusion.rest_0_
  30.7 1.5 collective-permute-start.6
  32.2 1.5 collective-permute-start.8
  33.7 0.5 collective-permute-start.9
  34.2 2.5 %collective-permute-start.7 = (bf16[256,384]{1,0:T(8,128)(2,1)S(1)}, bf16[256,384]{1,0:T(8,128)(2,1)}, u32[]{:S(2)}, u32[]{:S(2)}) collective-permute-start(bf16[256,384]{1,0:T(8,128)(2,1)S(1)} %get-tuple-element.57), channel_id=1, source_target_pairs={{0,12},{4,8},{8,4},{12,0},{1,13},{5,9},{9,5},{13,1},{2,14},{6,10},... | collective-permute-start | bytes 589832 | tf_op jit(solution)/shard_map/gather_tokens_and_weights/ppermute | solution.py:149
  36.7 1.5 collective-permute-done.8.rest_7_
  38.2 2.1 %collective-permute-done.9.rest_8_ = bf16[256,384]{1,0:T(8,128)(2,1)S(1)} collective-permute-done((bf16[256,384]{1,0:T(8,128)(2,1)S(1)}, bf16[256,384]{1,0:T(8,128)(2,1)S(1)}, u32[]{:S(2)}, u32[]{:S(2)}) %collective-permute-start.9) | collective-permute-done | bytes 196640 | tf_op jit(solution)/shard_map/gather_tokens_and_weights/ppermute | solution.py:149
  40.3 1.6 %collective-permute-done.7.rest_6_ = bf16[256,384]{1,0:T(8,128)(2,1)} collective-permute-done((bf16[256,384]{1,0:T(8,128)(2,1)S(1)}, bf16[256,384]{1,0:T(8,128)(2,1)}, u32[]{:S(2)}, u32[]{:S(2)}) %collective-permute-start.7) | collective-permute-done | bytes 196640 | tf_op jit(solution)/shard_map/gather_tokens_and_weights/ppermute | solution.py:149
  42.0 0.6 collective-permute-start.13
  42.6 0.5 collective-permute-start.10
  43.1 1.5 collective-permute-start.11
  44.6 0.9 copy-done.3
  45.5 0.9 copy-done.5
  46.4 0.9 copy-done.12
  47.3 1.3 routing.1
  48.7 1.5 collective-permute-done.11.rest_9_
  50.2 5.5 %attention.1 = (bf16[4,128,128]{2,1,0:T(8,128)(2,1)S(1)}, bf16[128,512]{1,0:T(8,128)(2,1)S(1)}) custom-call(s32[3]{0:T(128)S(1)} %pad_add_fusion.pos, f32[1,2048]{1,0:T(1,128)S(1)} %bitcast.24, bf16[128,2048]{1,0:T(8,128)(2,1)} %tokens.3, bf16[512,384]{1,0:T(8,128)(2,1)} %copy-done.10, bf16[3,128,512]{2,1,0:T(8,128)(2,1)} %pad_maximum_fusion.rest_0_, ...), custom_call_target="tpu_custom_call" | custom-call | tf_op jit(solution)/shard_map/attention/pallas_call | solution.py:525
  55.8 0.5 collective-permute-start.14
  56.5 1.5 collective-permute-start.16
  58.3 2.1 %collective-permute-done.16 = bf16[128,128]{1,0:T(8,128)(2,1)S(1)} collective-permute-done((bf16[128,128]{1,0:T(8,128)(2,1)S(1)}, bf16[128,128]{1,0:T(8,128)(2,1)S(1)}, u32[]{:S(2)}, u32[]{:S(2)}) %collective-permute-start.16) | collective-permute-done | bytes 32800 | tf_op jit(solution)/shard_map/heads_to_tokens/ppermute | solution.py:149
  60.4 0.9 collective-permute-done.17
  61.3 3.5 %collective-permute-start.19 = (bf16[4,128,128]{2,1,0:T(8,128)(2,1)S(1)}, bf16[4,128,128]{2,1,0:T(8,128)(2,1)S(1)}, u32[]{:S(2)}, u32[]{:S(2)}) collective-permute-start(bf16[4,128,128]{2,1,0:T(8,128)(2,1)S(1)} %pad_maximum_fusion.1.rest_4_), channel_id=1, source_target_pairs={{0,8},{4,12},{8,0},{12,4},{1,9},{5,13},{9,1},{13,5},{2,10},{6,14},... | collective-permute-start | bytes 393224 | tf_op jit(solution)/shard_map/heads_to_tokens/ppermute | solution.py:149
  64.9 6.7 %collective-permute-done.19.rest_6_ = bf16[4,128,128]{2,1,0:T(8,128)(2,1)S(1)} collective-permute-done((bf16[4,128,128]{2,1,0:T(8,128)(2,1)S(1)}, bf16[4,128,128]{2,1,0:T(8,128)(2,1)S(1)}, u32[]{:S(2)}, u32[]{:S(2)}) %collective-permute-start.19) | collective-permute-done | bytes 131104 | tf_op jit(solution)/shard_map/heads_to_tokens/ppermute | solution.py:149
  71.8 4.8 %collective-permute-done.20.rest_7_ = bf16[4,128,128]{2,1,0:T(8,128)(2,1)S(1)} collective-permute-done((bf16[4,128,128]{2,1,0:T(8,128)(2,1)S(1)}, bf16[4,128,128]{2,1,0:T(8,128)(2,1)S(1)}, u32[]{:S(2)}, u32[]{:S(2)}) %collective-permute-start.20) | collective-permute-done | bytes 131104 | tf_op jit(solution)/shard_map/heads_to_tokens/ppermute | solution.py:149
  76.6 2.3 %output_projection.1.refs_0_ = bf16[128,512]{1,0:T(8,128)(2,1)S(1)} custom-call(s32[3]{0:T(128)S(1)} %pad_add_fusion.pos, bf16[128,512]{1,0:T(8,128)(2,1)S(1)} %get-tuple-element.67.x_share, bf16[512,512]{1,0:T(8,128)(2,1)} %get-tuple-element.70.rest_0_, bf16[512,512]{1,0:T(8,128)(2,1)} %collective-permute-done.12.rest_1_, ...), custom_call_target="tpu_custom_call" | custom-call | tf_op jit(solution)/shard_map/output_projection/pallas_call | solution.py:552
  79.2 1.9 %collective-permute-start.21 = (bf16[128,512]{1,0:T(8,128)(2,1)S(1)}, bf16[128,512]{1,0:T(8,128)(2,1)S(1)}, u32[]{:S(2)}, u32[]{:S(2)}) collective-permute-start(bf16[128,512]{1,0:T(8,128)(2,1)S(1)} %output_projection.1.refs_0_), channel_id=1, source_target_pairs={{0,8},{4,12},{8,0},{12,4},{1,9},{5,13},{9,1},{13,5},{2,10},{6,14},... | collective-permute-start | bytes 393224 | tf_op jit(solution)/shard_map/gather_residual/ppermute | solution.py:149
  81.1 0.9 collective-permute-start.28
  82.0 3.4 %collective-permute-done.23.refs_4_ = bf16[128,512]{1,0:T(8,128)(2,1)S(1)} collective-permute-done((bf16[128,512]{1,0:T(8,128)(2,1)S(1)}, bf16[128,512]{1,0:T(8,128)(2,1)S(1)}, u32[]{:S(2)}, u32[]{:S(2)}) %collective-permute-start.23) | collective-permute-done | bytes 131104 | tf_op jit(solution)/shard_map/gather_residual/ppermute | solution.py:149
  85.4 0.8 collective-permute-start.30
  86.2 0.9 collective-permute-done.21.refs_0_
  87.1 0.5 collective-permute-start.24
  87.6 2.8 %collective-permute-done.30.refs_6_ = bf16[128,512]{1,0:T(8,128)(2,1)S(1)} collective-permute-done((bf16[128,512]{1,0:T(8,128)(2,1)S(1)}, bf16[128,512]{1,0:T(8,128)(2,1)S(1)}, u32[]{:S(2)}, u32[]{:S(2)}) %collective-permute-start.30) | collective-permute-done | bytes 131104 | tf_op jit(solution)/shard_map/gather_residual/ppermute | solution.py:149
  90.4 1.6 %collective-permute-done.22.refs_4_ = bf16[128,512]{1,0:T(8,128)(2,1)S(1)} collective-permute-done((bf16[128,512]{1,0:T(8,128)(2,1)S(1)}, bf16[128,512]{1,0:T(8,128)(2,1)S(1)}, u32[]{:S(2)}, u32[]{:S(2)}) %collective-permute-start.22) | collective-permute-done | bytes 131104 | tf_op jit(solution)/shard_map/gather_residual/ppermute | solution.py:149
  92.0 0.9 collective-permute-start.25
  92.9 1.2 collective-permute-start.26
  94.3 8.8 %hidden_units_0_1.1 = (f32[1280,512]{1,0:T(8,128)S(1)}, f32[1280,128]{1,0:T(8,128)S(1)}) custom-call(s32[3]{0:T(128)S(1)} %pad_add_fusion.pos, f32[1,2048]{1,0:T(1,128)S(1)} %bitcast.22, bf16[1280,512]{1,0:T(8,128)(2,1)S(1)} %get-tuple-element.63.pick, bf16[16,2048,256]{2,1,0:T(8,128)(2,1)} %w_gate.3, bf16[16,2048,256]{2,1,0:T(8,128)(2,1)} %w_up.3, ...), custom_call_target="tpu_custom_call" | custom-call | flops 2684354560 | bytes 16777216 | tf_op jit(solution)/shard_map/gather_residual/hidden_units_0_1/pallas_call | solution.py:567
  103.7 0.8 collective-permute-done.32.refs_7_
  104.9 9.0 %hidden_units_2_3.1.hidden = bf16[1280,256]{1,0:T(8,128)(2,1)S(1)} custom-call(s32[3]{0:T(128)S(1)} %pad_add_fusion.pos, f32[1,2048]{1,0:T(1,128)S(1)} %bitcast.23, bf16[1280,512]{1,0:T(8,128)(2,1)S(1)} %get-tuple-element.63.pick, bf16[16,2048,256]{2,1,0:T(8,128)(2,1)} %w_gate.3, bf16[16,2048,256]{2,1,0:T(8,128)(2,1)} %w_up.3, ...), custom_call_target="tpu_custom_call" | custom-call | flops 2684354560 | bytes 16777216 | tf_op jit(solution)/shard_map/gather_residual/hidden_units_2_3/pallas_call | solution.py:567
  113.9 5.8 %down_quarters_3_1.1 = (bf16[512,512]{1,0:T(8,128)(2,1)}, bf16[512,512]{1,0:T(8,128)(2,1)S(1)}) custom-call(s32[3]{0:T(128)S(1)} %pad_add_fusion.pos, bf16[1280,256]{1,0:T(8,128)(2,1)S(1)} %hidden_units_2_3.1.hidden, bf16[512,1280]{1,0:T(8,128)(2,1)S(1)} %get-tuple-element.78.place, bf16[16,256,2048]{2,1,0:T(8,128)(2,1)} %w_down.5), custom_call_target="tpu_custom_call" | custom-call | flops 2013265920 | bytes 8388608 | tf_op jit(solution)/shard_map/sum_over_devices/down_quarters_3_1/pallas_call | solution.py:611
  120.3 3.8 %down_quarters_2.1 = bf16[512,512]{1,0:T(8,128)(2,1)S(1)} custom-call(s32[3]{0:T(128)S(1)} %pad_add_fusion.pos, bf16[1280,256]{1,0:T(8,128)(2,1)S(1)} %hidden_units_2_3.1.hidden, bf16[512,1280]{1,0:T(8,128)(2,1)S(1)} %get-tuple-element.78.place, bf16[16,256,2048]{2,1,0:T(8,128)(2,1)} %w_down.5), custom_call_target="tpu_custom_call" | custom-call | flops 1006632960 | bytes 4194304 | tf_op jit(solution)/shard_map/sum_over_devices/down_quarters_2/pallas_call | solution.py:611
  124.1 1.9 %add_convert_fusion = (bf16[256,512]{1,0:T(8,128)(2,1)}, bf16[256,512]{1,0:T(8,128)(2,1)}) fusion(bf16[512,512]{1,0:T(8,128)(2,1)} %collective-permute-done.36, s32[]{:T(128)S(6)} %select_n.63, bf16[512,512]{1,0:T(8,128)(2,1)S(1)} %down_quarters_2.1, s32[]{:T(128)S(6)} %select_n.62), kind=kLoop, calls=%fused_computation | loop fusion | flops 1048576 | bytes 1572872 | tf_op jit(solution)/shard_map/sum_over_devices/convert_element_type | solution.py:639
  126.0 0.9 collective-permute-start.39
  126.9 1.1 collective-permute-start.38
  128.0 3.8 %down_quarters_0.1.base = bf16[512,512]{1,0:T(8,128)(2,1)S(1)} custom-call(s32[3]{0:T(128)S(1)} %pad_add_fusion.pos, bf16[1280,256]{1,0:T(8,128)(2,1)S(1)} %hidden_units_2_3.1.hidden, bf16[512,1280]{1,0:T(8,128)(2,1)S(1)} %get-tuple-element.78.place, bf16[16,256,2048]{2,1,0:T(8,128)(2,1)} %w_down.5), custom_call_target="tpu_custom_call" | custom-call | flops 1006632960 | bytes 4194304 | tf_op jit(solution)/shard_map/sum_over_devices/down_quarters_0/pallas_call | solution.py:611
  131.8 3.5 %collective-permute-done.39.part = bf16[256,512]{1,0:T(8,128)(2,1)S(1)} collective-permute-done((bf16[256,512]{1,0:T(8,128)(2,1)}, bf16[256,512]{1,0:T(8,128)(2,1)S(1)}, u32[]{:S(2)}, u32[]{:S(2)}) %collective-permute-start.39) | collective-permute-done | bytes 262176 | tf_op jit(solution)/shard_map/sum_over_devices/ppermute | solution.py:149
  135.4 0.6 far_half_rows.1
  136.0 0.4 collective-permute-start.40
  136.4 2.0 %collective-permute-start.41 = (bf16[128,512]{1,0:T(8,128)(2,1)S(1)}, bf16[128,512]{1,0:T(8,128)(2,1)S(1)}, u32[]{:S(2)}, u32[]{:S(2)}) collective-permute-start(bf16[128,512]{1,0:T(8,128)(2,1)S(1)} %get-tuple-element.89), channel_id=1, source_target_pairs={{0,12},{4,8},{8,4},{12,0},{1,13},{5,9},{9,5},{13,1},{2,14},{6,10},... | collective-permute-start | bytes 393224 | tf_op jit(solution)/shard_map/sum_over_devices/ppermute | solution.py:149
  138.4 1.9 %collective-permute-done.38.part = bf16[256,512]{1,0:T(8,128)(2,1)} collective-permute-done((bf16[256,512]{1,0:T(8,128)(2,1)}, bf16[256,512]{1,0:T(8,128)(2,1)}, u32[]{:S(2)}, u32[]{:S(2)}) %collective-permute-start.38) | collective-permute-done | bytes 262176 | tf_op jit(solution)/shard_map/sum_over_devices/ppermute | solution.py:149
  140.3 1.1 near_half_rows.1
  141.5 4.8 %collective-permute-done.40 = bf16[128,512]{1,0:T(8,128)(2,1)S(1)} collective-permute-done((bf16[128,512]{1,0:T(8,128)(2,1)S(1)}, bf16[128,512]{1,0:T(8,128)(2,1)S(1)}, u32[]{:S(2)}, u32[]{:S(2)}) %collective-permute-start.40) | collective-permute-done | bytes 131104 | tf_op jit(solution)/shard_map/sum_over_devices/ppermute | solution.py:149
  146.4 2.5 %collective-permute-done.42 = bf16[128,512]{1,0:T(8,128)(2,1)S(1)} collective-permute-done((bf16[128,512]{1,0:T(8,128)(2,1)S(1)}, bf16[128,512]{1,0:T(8,128)(2,1)S(1)}, u32[]{:S(2)}, u32[]{:S(2)}) %collective-permute-start.42) | collective-permute-done | bytes 131104 | tf_op jit(solution)/shard_map/sum_over_devices/ppermute | solution.py:149
  148.9 7.0 %all_gather.3 = bf16[128,2048]{1,0:T(8,128)(2,1)S(1)} all-gather(bf16[128,512]{1,0:T(8,128)(2,1)S(1)} %add_convert_fusion.2), channel_id=1, replica_groups=mesh['grp'=2,'seq'=4,'head'=4] {'head'}, dimensions={1}, use_global_device_ids=true | all-gather | bytes 655360 | tf_op jit(solution)/shard_map/gather_columns/all_gather | solution.py:666
  155.8 0.8 copy.11
  (82 shorter events, 3.2 us)
Async XLA Ops:
  0.0 50.2 %copy-start.14 = (f32[2048]{0:T(1024)S(1)}, f32[2048]{0:T(1024)}, u32[]{:S(2)}) copy-start(f32[2048]{0:T(1024)} %param.11) | copy-start | bytes 24580
  3.0 0.7 copy-start.10
  3.8 25.5 %collective-permute-start.3 = (bf16[256,384]{1,0:T(8,128)(2,1)S(1)}, bf16[256,384]{1,0:T(8,128)(2,1)S(1)}, u32[]{:S(2)}, u32[]{:S(2)}) collective-permute-start(bf16[256,384]{1,0:T(8,128)(2,1)S(1)} %get-tuple-element.51), channel_id=1, source_target_pairs={{0,4},{4,0},{8,12},{12,8},{1,5},{5,1},{9,13},{13,9},{2,6},{6,2},{1... | collective-permute-start | bytes 589832 | tf_op jit(solution)/shard_map/gather_tokens_and_weights/ppermute | solution.py:149
  6.8 22.4 %collective-permute-start.4 = (bf16[256,384]{1,0:T(8,128)(2,1)S(1)}, bf16[256,384]{1,0:T(8,128)(2,1)S(1)}, u32[]{:S(2)}, u32[]{:S(2)}) collective-permute-start(bf16[256,384]{1,0:T(8,128)(2,1)S(1)} %get-tuple-element.52), channel_id=1, source_target_pairs={{0,8},{4,12},{8,0},{12,4},{1,9},{5,13},{9,1},{13,5},{2,10},{6,14},... | collective-permute-start | bytes 589832 | tf_op jit(solution)/shard_map/gather_tokens_and_weights/ppermute | solution.py:149
  9.4 11.7 %collective-permute-start = (bf16[144,512]{1,0:T(8,128)(2,1)S(1)}, bf16[144,512]{1,0:T(8,128)(2,1)S(1)}, u32[]{:S(2)}, u32[]{:S(2)}) collective-permute-start(bf16[144,512]{1,0:T(8,128)(2,1)S(1)} %get-tuple-element.50.refs_0_), channel_id=1, source_target_pairs={{0,4},{4,0},{8,12},{12,8},{1,5},{5,1},{9,13},{13,9},{2,6},{6,2},{1... | collective-permute-start | bytes 442376 | tf_op jit(solution)/shard_map/gather_tokens_and_weights/ppermute | solution.py:149
  9.8 19.4 %collective-permute-start.1 = (bf16[144,512]{1,0:T(8,128)(2,1)S(1)}, bf16[144,512]{1,0:T(8,128)(2,1)S(1)}, u32[]{:S(2)}, u32[]{:S(2)}) collective-permute-start(bf16[144,512]{1,0:T(8,128)(2,1)S(1)} %get-tuple-element.50.refs_0_), channel_id=1, source_target_pairs={{0,8},{4,12},{8,0},{12,4},{1,9},{5,13},{9,1},{13,5},{2,10},{6,14},... | collective-permute-start | bytes 442376 | tf_op jit(solution)/shard_map/gather_tokens_and_weights/ppermute | solution.py:149
  9.8 19.4 %collective-permute-start.2 = (bf16[144,512]{1,0:T(8,128)(2,1)S(1)}, bf16[144,512]{1,0:T(8,128)(2,1)S(1)}, u32[]{:S(2)}, u32[]{:S(2)}) collective-permute-start(bf16[144,512]{1,0:T(8,128)(2,1)S(1)} %get-tuple-element.50.refs_0_), channel_id=1, source_target_pairs={{0,12},{4,8},{8,4},{12,0},{1,13},{5,9},{9,5},{13,1},{2,14},{6,10},... | collective-permute-start | bytes 442376 | tf_op jit(solution)/shard_map/gather_tokens_and_weights/ppermute | solution.py:149
  13.8 0.7 copy-start.11
  29.2 0.7 copy-start.2
  29.2 0.7 copy-start.4
  29.2 12.7 %copy-start.15 = (bf16[256,384]{1,0:T(8,128)(2,1)}, bf16[256,384]{1,0:T(8,128)(2,1)S(1)}, u32[]{:S(2)}) copy-start(bf16[256,384]{1,0:T(8,128)(2,1)S(1)} %collective-permute-done.3.rest_4_) | copy-start | bytes 589828
  29.2 12.7 %copy-start.16 = (bf16[256,384]{1,0:T(8,128)(2,1)}, bf16[256,384]{1,0:T(8,128)(2,1)S(1)}, u32[]{:S(2)}) copy-start(bf16[256,384]{1,0:T(8,128)(2,1)S(1)} %collective-permute-done.4.rest_5_) | copy-start | bytes 589828
  30.7 11.2 %collective-permute-start.6 = (bf16[3,128,512]{2,1,0:T(8,128)(2,1)}, bf16[3,128,512]{2,1,0:T(8,128)(2,1)}, u32[]{:S(2)}, u32[]{:S(2)}) collective-permute-start(bf16[3,128,512]{2,1,0:T(8,128)(2,1)} %pad_maximum_fusion.rest_0_), channel_id=1, source_target_pairs={{0,2},{1,3},{2,0},{3,1},{4,6},{5,7},{6,4},{7,5},{8,10},{9,11},{10,... | collective-permute-start | bytes 1179656 | tf_op jit(solution)/shard_map/gather_tokens_and_weights/ppermute | solution.py:149
  32.2 6.0 %collective-permute-start.8 = (bf16[256,384]{1,0:T(8,128)(2,1)S(1)}, bf16[256,384]{1,0:T(8,128)(2,1)S(1)}, u32[]{:S(2)}, u32[]{:S(2)}) collective-permute-start(bf16[256,384]{1,0:T(8,128)(2,1)S(1)} %collective-permute-done.3.rest_4_), channel_id=1, source_target_pairs={{0,16},{16,0},{1,17},{17,1},{2,18},{18,2},{3,19},{19,3},{4,20},{20... | collective-permute-start | bytes 589832 | tf_op jit(solution)/shard_map/gather_tokens_and_weights/ppermute | solution.py:149
  33.7 6.6 %collective-permute-start.9 = (bf16[256,384]{1,0:T(8,128)(2,1)S(1)}, bf16[256,384]{1,0:T(8,128)(2,1)S(1)}, u32[]{:S(2)}, u32[]{:S(2)}) collective-permute-start(bf16[256,384]{1,0:T(8,128)(2,1)S(1)} %collective-permute-done.4.rest_5_), channel_id=1, source_target_pairs={{0,16},{16,0},{1,17},{17,1},{2,18},{18,2},{3,19},{19,3},{4,20},{20... | collective-permute-start | bytes 589832 | tf_op jit(solution)/shard_map/gather_tokens_and_weights/ppermute | solution.py:149
  34.2 7.7 %collective-permute-start.7 = (bf16[256,384]{1,0:T(8,128)(2,1)S(1)}, bf16[256,384]{1,0:T(8,128)(2,1)}, u32[]{:S(2)}, u32[]{:S(2)}) collective-permute-start(bf16[256,384]{1,0:T(8,128)(2,1)S(1)} %get-tuple-element.57), channel_id=1, source_target_pairs={{0,12},{4,8},{8,4},{12,0},{1,13},{5,9},{9,5},{13,1},{2,14},{6,10},... | collective-permute-start | bytes 589832 | tf_op jit(solution)/shard_map/gather_tokens_and_weights/ppermute | solution.py:149
  38.2 3.7 %copy-start.17 = (bf16[256,384]{1,0:T(8,128)(2,1)}, bf16[256,384]{1,0:T(8,128)(2,1)S(1)}, u32[]{:S(2)}) copy-start(bf16[256,384]{1,0:T(8,128)(2,1)S(1)} %collective-permute-done.8.rest_7_) | copy-start | bytes 589828
  40.3 2.2 %copy-start.18 = (bf16[256,384]{1,0:T(8,128)(2,1)}, bf16[256,384]{1,0:T(8,128)(2,1)S(1)}, u32[]{:S(2)}) copy-start(bf16[256,384]{1,0:T(8,128)(2,1)S(1)} %collective-permute-done.9.rest_8_) | copy-start | bytes 589828
  42.0 13.9 %collective-permute-start.13 = (bf16[512,512]{1,0:T(8,128)(2,1)}, bf16[512,512]{1,0:T(8,128)(2,1)}, u32[]{:S(2)}, u32[]{:S(2)}) collective-permute-start(bf16[512,512]{1,0:T(8,128)(2,1)} %get-tuple-element.70.rest_0_), channel_id=1, source_target_pairs={{0,2},{1,3},{2,0},{3,1},{4,6},{5,7},{6,4},{7,5},{8,10},{9,11},{10,... | collective-permute-start | bytes 1572872 | tf_op jit(solution)/shard_map/gather_tokens_and_weights/ppermute | solution.py:149
  42.6 6.1 %collective-permute-start.5 = (bf16[3,128,512]{2,1,0:T(8,128)(2,1)}, bf16[3,128,512]{2,1,0:T(8,128)(2,1)}, u32[]{:S(2)}, u32[]{:S(2)}) collective-permute-start(bf16[3,128,512]{2,1,0:T(8,128)(2,1)} %pad_maximum_fusion.rest_0_), channel_id=1, source_target_pairs={{0,1},{1,0},{2,3},{3,2},{4,5},{5,4},{6,7},{7,6},{8,9},{9,8},{10,11... | collective-permute-start | bytes 1179656 | tf_op jit(solution)/shard_map/gather_tokens_and_weights/ppermute | solution.py:149
  42.6 7.6 %collective-permute-start.10 = (bf16[3,128,512]{2,1,0:T(8,128)(2,1)}, bf16[3,128,512]{2,1,0:T(8,128)(2,1)}, u32[]{:S(2)}, u32[]{:S(2)}) collective-permute-start(bf16[3,128,512]{2,1,0:T(8,128)(2,1)} %collective-permute-done.6.rest_2_), channel_id=1, source_target_pairs={{0,1},{1,0},{2,3},{3,2},{4,5},{5,4},{6,7},{7,6},{8,9},{9,8},{10,11... | collective-permute-start | bytes 1179656 | tf_op jit(solution)/shard_map/gather_tokens_and_weights/ppermute | solution.py:149
  43.1 7.1 %collective-permute-start.11 = (bf16[256,384]{1,0:T(8,128)(2,1)}, bf16[256,384]{1,0:T(8,128)(2,1)}, u32[]{:S(2)}, u32[]{:S(2)}) collective-permute-start(bf16[256,384]{1,0:T(8,128)(2,1)} %collective-permute-done.7.rest_6_), channel_id=1, source_target_pairs={{0,16},{16,0},{1,17},{17,1},{2,18},{18,2},{3,19},{19,3},{4,20},{20... | collective-permute-start | bytes 589832 | tf_op jit(solution)/shard_map/gather_tokens_and_weights/ppermute | solution.py:149
  44.6 0.9 copy-start.3
  45.5 0.9 copy-start.5
  46.4 0.9 copy-start.12
  48.7 30.3 %copy-start = (f32[1280,128]{1,0:T(8,128)}, f32[1280,128]{1,0:T(8,128)S(1)}, u32[]{:S(2)}) copy-start(f32[1280,128]{1,0:T(8,128)S(1)} %get-tuple-element.77.refs_10_) | copy-start | bytes 1966084
  55.7 38.6 %copy-start.13 = (f32[2048]{0:T(1024)S(1)}, f32[2048]{0:T(1024)}, u32[]{:S(2)}) copy-start(f32[2048]{0:T(1024)} %param.12) | copy-start | bytes 24580
  55.7 20.8 %collective-permute-start.12 = (bf16[512,512]{1,0:T(8,128)(2,1)}, bf16[512,512]{1,0:T(8,128)(2,1)}, u32[]{:S(2)}, u32[]{:S(2)}) collective-permute-start(bf16[512,512]{1,0:T(8,128)(2,1)} %get-tuple-element.70.rest_0_), channel_id=1, source_target_pairs={{0,1},{1,0},{2,3},{3,2},{4,5},{5,4},{6,7},{7,6},{8,9},{9,8},{10,11... | collective-permute-start | bytes 1572872 | tf_op jit(solution)/shard_map/heads_to_tokens/ppermute | solution.py:149
  55.8 20.7 %collective-permute-start.14 = (bf16[512,512]{1,0:T(8,128)(2,1)}, bf16[512,512]{1,0:T(8,128)(2,1)}, u32[]{:S(2)}, u32[]{:S(2)}) collective-permute-start(bf16[512,512]{1,0:T(8,128)(2,1)} %collective-permute-done.13.rest_2_), channel_id=1, source_target_pairs={{0,1},{1,0},{2,3},{3,2},{4,5},{5,4},{6,7},{7,6},{8,9},{9,8},{10,11... | collective-permute-start | bytes 1572872 | tf_op jit(solution)/shard_map/heads_to_tokens/ppermute | solution.py:149
  56.3 1.9 %collective-permute-start.15 = (bf16[128,128]{1,0:T(8,128)(2,1)S(1)}, bf16[128,128]{1,0:T(8,128)(2,1)S(1)}, u32[]{:S(2)}, u32[]{:S(2)}) collective-permute-start(bf16[128,128]{1,0:T(8,128)(2,1)S(1)} %get-tuple-element.98), channel_id=1, source_target_pairs={{0,1},{1,0},{2,3},{3,2},{4,5},{5,4},{6,7},{7,6},{8,9},{9,8},{10,11... | collective-permute-start | bytes 98312 | tf_op jit(solution)/shard_map/heads_to_tokens/ppermute | solution.py:149
  56.5 3.9 %collective-permute-start.16 = (bf16[128,128]{1,0:T(8,128)(2,1)S(1)}, bf16[128,128]{1,0:T(8,128)(2,1)S(1)}, u32[]{:S(2)}, u32[]{:S(2)}) collective-permute-start(bf16[128,128]{1,0:T(8,128)(2,1)S(1)} %get-tuple-element.97), channel_id=1, source_target_pairs={{0,2},{1,3},{2,0},{3,1},{4,6},{5,7},{6,4},{7,5},{8,10},{9,11},{10,... | collective-permute-start | bytes 98312 | tf_op jit(solution)/shard_map/heads_to_tokens/ppermute | solution.py:149
  58.0 3.4 %collective-permute-start.17 = (bf16[128,128]{1,0:T(8,128)(2,1)S(1)}, bf16[128,128]{1,0:T(8,128)(2,1)S(1)}, u32[]{:S(2)}, u32[]{:S(2)}) collective-permute-start(bf16[128,128]{1,0:T(8,128)(2,1)S(1)} %get-tuple-element.96), channel_id=1, source_target_pairs={{0,3},{1,2},{2,1},{3,0},{4,7},{5,6},{6,5},{7,4},{8,11},{9,10},{10,... | collective-permute-start | bytes 98312 | tf_op jit(solution)/shard_map/heads_to_tokens/ppermute | solution.py:149
  61.3 10.2 %collective-permute-start.19 = (bf16[4,128,128]{2,1,0:T(8,128)(2,1)S(1)}, bf16[4,128,128]{2,1,0:T(8,128)(2,1)S(1)}, u32[]{:S(2)}, u32[]{:S(2)}) collective-permute-start(bf16[4,128,128]{2,1,0:T(8,128)(2,1)S(1)} %pad_maximum_fusion.1.rest_4_), channel_id=1, source_target_pairs={{0,8},{4,12},{8,0},{12,4},{1,9},{5,13},{9,1},{13,5},{2,10},{6,14},... | collective-permute-start | bytes 393224 | tf_op jit(solution)/shard_map/heads_to_tokens/ppermute | solution.py:149
  64.8 6.9 %collective-permute-start.18 = (bf16[4,128,128]{2,1,0:T(8,128)(2,1)S(1)}, bf16[4,128,128]{2,1,0:T(8,128)(2,1)S(1)}, u32[]{:S(2)}, u32[]{:S(2)}) collective-permute-start(bf16[4,128,128]{2,1,0:T(8,128)(2,1)S(1)} %pad_maximum_fusion.1.rest_4_), channel_id=1, source_target_pairs={{0,4},{4,0},{8,12},{12,8},{1,5},{5,1},{9,13},{13,9},{2,6},{6,2},{1... | collective-permute-start | bytes 393224 | tf_op jit(solution)/shard_map/heads_to_tokens/ppermute | solution.py:149
  71.6 5.0 %collective-permute-start.20 = (bf16[4,128,128]{2,1,0:T(8,128)(2,1)S(1)}, bf16[4,128,128]{2,1,0:T(8,128)(2,1)S(1)}, u32[]{:S(2)}, u32[]{:S(2)}) collective-permute-start(bf16[4,128,128]{2,1,0:T(8,128)(2,1)S(1)} %collective-permute-done.19.rest_6_), channel_id=1, source_target_pairs={{0,4},{4,0},{8,12},{12,8},{1,5},{5,1},{9,13},{13,9},{2,6},{6,2},{1... | collective-permute-start | bytes 393224 | tf_op jit(solution)/shard_map/heads_to_tokens/ppermute | solution.py:149
  78.9 6.5 %collective-permute-start.23 = (bf16[128,512]{1,0:T(8,128)(2,1)S(1)}, bf16[128,512]{1,0:T(8,128)(2,1)S(1)}, u32[]{:S(2)}, u32[]{:S(2)}) collective-permute-start(bf16[128,512]{1,0:T(8,128)(2,1)S(1)} %output_projection.1.refs_0_), channel_id=1, source_target_pairs={{0,4},{4,0},{8,12},{12,8},{1,5},{5,1},{9,13},{13,9},{2,6},{6,2},{1... | collective-permute-start | bytes 393224 | tf_op jit(solution)/shard_map/gather_residual/ppermute | solution.py:149
  79.2 7.8 %collective-permute-start.21 = (bf16[128,512]{1,0:T(8,128)(2,1)S(1)}, bf16[128,512]{1,0:T(8,128)(2,1)S(1)}, u32[]{:S(2)}, u32[]{:S(2)}) collective-permute-start(bf16[128,512]{1,0:T(8,128)(2,1)S(1)} %output_projection.1.refs_0_), channel_id=1, source_target_pairs={{0,8},{4,12},{8,0},{12,4},{1,9},{5,13},{9,1},{13,5},{2,10},{6,14},... | collective-permute-start | bytes 393224 | tf_op jit(solution)/shard_map/gather_residual/ppermute | solution.py:149
  81.1 6.4 %collective-permute-start.28 = (bf16[128,512]{1,0:T(8,128)(2,1)S(1)}, bf16[128,512]{1,0:T(8,128)(2,1)S(1)}, u32[]{:S(2)}, u32[]{:S(2)}) collective-permute-start(bf16[128,512]{1,0:T(8,128)(2,1)S(1)} %output_projection.1.refs_0_), channel_id=1, source_target_pairs={{0,2},{1,3},{2,0},{3,1},{4,6},{5,7},{6,4},{7,5},{8,10},{9,11},{10,... | collective-permute-start | bytes 393224 | tf_op jit(solution)/shard_map/gather_residual/ppermute | solution.py:149
  85.4 5.0 %collective-permute-start.30 = (bf16[128,512]{1,0:T(8,128)(2,1)S(1)}, bf16[128,512]{1,0:T(8,128)(2,1)S(1)}, u32[]{:S(2)}, u32[]{:S(2)}) collective-permute-start(bf16[128,512]{1,0:T(8,128)(2,1)S(1)} %collective-permute-done.23.refs_4_), channel_id=1, source_target_pairs={{0,2},{1,3},{2,0},{3,1},{4,6},{5,7},{6,4},{7,5},{8,10},{9,11},{10,... | collective-permute-start | bytes 393224 | tf_op jit(solution)/shard_map/gather_residual/ppermute | solution.py:149
  87.0 5.0 %collective-permute-start.22 = (bf16[128,512]{1,0:T(8,128)(2,1)S(1)}, bf16[128,512]{1,0:T(8,128)(2,1)S(1)}, u32[]{:S(2)}, u32[]{:S(2)}) collective-permute-start(bf16[128,512]{1,0:T(8,128)(2,1)S(1)} %collective-permute-done.21.refs_0_), channel_id=1, source_target_pairs={{0,4},{4,0},{8,12},{12,8},{1,5},{5,1},{9,13},{13,9},{2,6},{6,2},{1... | collective-permute-start | bytes 393224 | tf_op jit(solution)/shard_map/gather_residual/ppermute | solution.py:149
  87.0 5.9 %collective-permute-start.27 = (bf16[128,512]{1,0:T(8,128)(2,1)S(1)}, bf16[128,512]{1,0:T(8,128)(2,1)S(1)}, u32[]{:S(2)}, u32[]{:S(2)}) collective-permute-start(bf16[128,512]{1,0:T(8,128)(2,1)S(1)} %output_projection.1.refs_0_), channel_id=1, source_target_pairs={{0,1},{1,0},{2,3},{3,2},{4,5},{5,4},{6,7},{7,6},{8,9},{9,8},{10,11... | collective-permute-start | bytes 393224 | tf_op jit(solution)/shard_map/gather_residual/ppermute | solution.py:149
  87.1 5.9 %collective-permute-start.24 = (bf16[128,512]{1,0:T(8,128)(2,1)S(1)}, bf16[128,512]{1,0:T(8,128)(2,1)S(1)}, u32[]{:S(2)}, u32[]{:S(2)}) collective-permute-start(bf16[128,512]{1,0:T(8,128)(2,1)S(1)} %collective-permute-done.23.refs_4_), channel_id=1, source_target_pairs={{0,1},{1,0},{2,3},{3,2},{4,5},{5,4},{6,7},{7,6},{8,9},{9,8},{10,11... | collective-permute-start | bytes 393224 | tf_op jit(solution)/shard_map/gather_residual/ppermute | solution.py:149
  87.6 6.6 %collective-permute-start.29 = (bf16[128,512]{1,0:T(8,128)(2,1)S(1)}, bf16[128,512]{1,0:T(8,128)(2,1)S(1)}, u32[]{:S(2)}, u32[]{:S(2)}) collective-permute-start(bf16[128,512]{1,0:T(8,128)(2,1)S(1)} %collective-permute-done.28.refs_2_), channel_id=1, source_target_pairs={{0,1},{1,0},{2,3},{3,2},{4,5},{5,4},{6,7},{7,6},{8,9},{9,8},{10,11... | collective-permute-start | bytes 393224 | tf_op jit(solution)/shard_map/gather_residual/ppermute | solution.py:149
  90.4 3.9 %collective-permute-start.31 = (bf16[128,512]{1,0:T(8,128)(2,1)S(1)}, bf16[128,512]{1,0:T(8,128)(2,1)S(1)}, u32[]{:S(2)}, u32[]{:S(2)}) collective-permute-start(bf16[128,512]{1,0:T(8,128)(2,1)S(1)} %collective-permute-done.30.refs_6_), channel_id=1, source_target_pairs={{0,1},{1,0},{2,3},{3,2},{4,5},{5,4},{6,7},{7,6},{8,9},{9,8},{10,11... | collective-permute-start | bytes 393224 | tf_op jit(solution)/shard_map/gather_residual/ppermute | solution.py:149
  92.0 11.5 %collective-permute-start.25 = (bf16[128,512]{1,0:T(8,128)(2,1)S(1)}, bf16[128,512]{1,0:T(8,128)(2,1)S(1)}, u32[]{:S(2)}, u32[]{:S(2)}) collective-permute-start(bf16[128,512]{1,0:T(8,128)(2,1)S(1)} %collective-permute-done.21.refs_0_), channel_id=1, source_target_pairs={{0,2},{1,3},{2,0},{3,1},{4,6},{5,7},{6,4},{7,5},{8,10},{9,11},{10,... | collective-permute-start | bytes 393224 | tf_op jit(solution)/shard_map/gather_residual/ppermute | solution.py:149
  92.9 10.8 %collective-permute-start.33 = (bf16[128,512]{1,0:T(8,128)(2,1)S(1)}, bf16[128,512]{1,0:T(8,128)(2,1)S(1)}, u32[]{:S(2)}, u32[]{:S(2)}) collective-permute-start(bf16[128,512]{1,0:T(8,128)(2,1)S(1)} %collective-permute-done.21.refs_0_), channel_id=1, source_target_pairs={{0,1},{1,0},{2,3},{3,2},{4,5},{5,4},{6,7},{7,6},{8,9},{9,8},{10,11... | collective-permute-start | bytes 393224 | tf_op jit(solution)/shard_map/gather_residual/ppermute | solution.py:149
  92.9 10.2 %collective-permute-start.26 = (bf16[128,512]{1,0:T(8,128)(2,1)S(1)}, bf16[128,512]{1,0:T(8,128)(2,1)S(1)}, u32[]{:S(2)}, u32[]{:S(2)}) collective-permute-start(bf16[128,512]{1,0:T(8,128)(2,1)S(1)} %collective-permute-done.22.refs_4_), channel_id=1, source_target_pairs={{0,2},{1,3},{2,0},{3,1},{4,6},{5,7},{6,4},{7,5},{8,10},{9,11},{10,... | collective-permute-start | bytes 393224 | tf_op jit(solution)/shard_map/gather_residual/ppermute | solution.py:149
  94.1 9.6 %collective-permute-start.35 = (bf16[128,512]{1,0:T(8,128)(2,1)S(1)}, bf16[128,512]{1,0:T(8,128)(2,1)S(1)}, u32[]{:S(2)}, u32[]{:S(2)}) collective-permute-start(bf16[128,512]{1,0:T(8,128)(2,1)S(1)} %collective-permute-done.22.refs_4_), channel_id=1, source_target_pairs={{0,1},{1,0},{2,3},{3,2},{4,5},{5,4},{6,7},{7,6},{8,9},{9,8},{10,11... | collective-permute-start | bytes 393224 | tf_op jit(solution)/shard_map/gather_residual/ppermute | solution.py:149
  94.3 10.6 %copy-start.1 = (f32[1280,128]{1,0:T(8,128)S(1)}, f32[1280,128]{1,0:T(8,128)}, u32[]{:S(2)}) copy-start(f32[1280,128]{1,0:T(8,128)} %copy-done) | copy-start | bytes 1966084
  103.1 1.4 collective-permute-start.32
  103.5 10.3 %copy-start.6 = (bf16[128,512]{1,0:T(8,128)(2,1)}, bf16[128,512]{1,0:T(8,128)(2,1)S(1)}, u32[]{:S(2)}) copy-start(bf16[128,512]{1,0:T(8,128)(2,1)S(1)} %collective-permute-done.25.refs_2_) | copy-start | bytes 393220
  103.5 1.3 collective-permute-start.34
  104.5 9.4 %copy-start.8 = (bf16[128,512]{1,0:T(8,128)(2,1)}, bf16[128,512]{1,0:T(8,128)(2,1)S(1)}, u32[]{:S(2)}) copy-start(bf16[128,512]{1,0:T(8,128)(2,1)S(1)} %collective-permute-done.32.refs_7_) | copy-start | bytes 393220
  119.7 4.4 %collective-permute-start.36 = (bf16[512,512]{1,0:T(8,128)(2,1)}, bf16[512,512]{1,0:T(8,128)(2,1)}, u32[]{:S(2)}, u32[]{:S(2)}) collective-permute-start(bf16[512,512]{1,0:T(8,128)(2,1)} %get-tuple-element.79), channel_id=1, source_target_pairs={{0,1},{1,0},{2,3},{3,2},{4,5},{5,4},{6,7},{7,6},{8,9},{9,8},{10,11... | collective-permute-start | bytes 1572872 | tf_op jit(solution)/shard_map/sum_over_devices/ppermute | solution.py:149
  119.9 11.9 %collective-permute-start.37 = (bf16[512,512]{1,0:T(8,128)(2,1)S(1)}, bf16[512,512]{1,0:T(8,128)(2,1)S(1)}, u32[]{:S(2)}, u32[]{:S(2)}) collective-permute-start(bf16[512,512]{1,0:T(8,128)(2,1)S(1)} %get-tuple-element.82), channel_id=1, source_target_pairs={{0,1},{1,0},{2,3},{3,2},{4,5},{5,4},{6,7},{7,6},{8,9},{9,8},{10,11... | collective-permute-start | bytes 1572872 | tf_op jit(solution)/shard_map/sum_over_devices/ppermute | solution.py:149
  126.0 9.4 %collective-permute-start.39 = (bf16[256,512]{1,0:T(8,128)(2,1)}, bf16[256,512]{1,0:T(8,128)(2,1)S(1)}, u32[]{:S(2)}, u32[]{:S(2)}) collective-permute-start(bf16[256,512]{1,0:T(8,128)(2,1)} %get-tuple-element.94), channel_id=1, source_target_pairs={{0,2},{1,3},{2,0},{3,1},{4,6},{5,7},{6,4},{7,5},{8,10},{9,11},{10,... | collective-permute-start | bytes 786440 | tf_op jit(solution)/shard_map/sum_over_devices/ppermute | solution.py:149
  126.9 13.4 %collective-permute-start.38 = (bf16[256,512]{1,0:T(8,128)(2,1)}, bf16[256,512]{1,0:T(8,128)(2,1)}, u32[]{:S(2)}, u32[]{:S(2)}) collective-permute-start(bf16[256,512]{1,0:T(8,128)(2,1)} %get-tuple-element.93), channel_id=1, source_target_pairs={{0,2},{1,3},{2,0},{3,1},{4,6},{5,7},{6,4},{7,5},{8,10},{9,11},{10,... | collective-permute-start | bytes 786440 | tf_op jit(solution)/shard_map/sum_over_devices/ppermute | solution.py:149
  136.0 10.2 %collective-permute-start.40 = (bf16[128,512]{1,0:T(8,128)(2,1)S(1)}, bf16[128,512]{1,0:T(8,128)(2,1)S(1)}, u32[]{:S(2)}, u32[]{:S(2)}) collective-permute-start(bf16[128,512]{1,0:T(8,128)(2,1)S(1)} %get-tuple-element.88), channel_id=1, source_target_pairs={{0,8},{4,12},{8,0},{12,4},{1,9},{5,13},{9,1},{13,5},{2,10},{6,14},... | collective-permute-start | bytes 393224 | tf_op jit(solution)/shard_map/sum_over_devices/ppermute | solution.py:149
  136.4 9.8 %copy-start.7 = (bf16[128,512]{1,0:T(8,128)(2,1)S(1)}, bf16[128,512]{1,0:T(8,128)(2,1)}, u32[]{:S(2)}) copy-start(bf16[128,512]{1,0:T(8,128)(2,1)} %copy-done.6) | copy-start | bytes 393220
  136.4 9.8 %copy-start.9 = (bf16[128,512]{1,0:T(8,128)(2,1)S(1)}, bf16[128,512]{1,0:T(8,128)(2,1)}, u32[]{:S(2)}) copy-start(bf16[128,512]{1,0:T(8,128)(2,1)} %copy-done.8) | copy-start | bytes 393220
  136.4 9.8 %collective-permute-start.41 = (bf16[128,512]{1,0:T(8,128)(2,1)S(1)}, bf16[128,512]{1,0:T(8,128)(2,1)S(1)}, u32[]{:S(2)}, u32[]{:S(2)}) collective-permute-start(bf16[128,512]{1,0:T(8,128)(2,1)S(1)} %get-tuple-element.89), channel_id=1, source_target_pairs={{0,12},{4,8},{8,4},{12,0},{1,13},{5,9},{9,5},{13,1},{2,14},{6,10},... | collective-permute-start | bytes 393224 | tf_op jit(solution)/shard_map/sum_over_devices/ppermute | solution.py:149
  141.4 7.5 %collective-permute-start.42 = (bf16[128,512]{1,0:T(8,128)(2,1)S(1)}, bf16[128,512]{1,0:T(8,128)(2,1)S(1)}, u32[]{:S(2)}, u32[]{:S(2)}) collective-permute-start(bf16[128,512]{1,0:T(8,128)(2,1)S(1)} %get-tuple-element.90), channel_id=1, source_target_pairs={{0,4},{4,0},{8,12},{12,8},{1,5},{5,1},{9,13},{13,9},{2,6},{6,2},{1... | collective-permute-start | bytes 393224 | tf_op jit(solution)/shard_map/sum_over_devices/ppermute | solution.py:149

commit v5 on v4

--- a/solution.py
+++ b/solution.py
@@ -164,6 +164,10 @@
     return pltpu.with_memory_space_constraint(array, pltpu.HBM)
 
 
+def here(array):
+    return pltpu.with_memory_space_constraint(array, pltpu.VMEM)
+
+
 def in_step(*arrays):
     return lax.optimization_barrier(arrays)
 
@@ -242,10 +246,14 @@
         copy.wait()
     x_share[...] = x_all[at_rows(h, rows), at_rows(s, cols)]
 
-    for block in range(n):
-        wide = x_all[block * rows : (block + 1) * rows, :].astype(F32)
+    def normalise(block, carry):
+        mine = at_rows(block, rows)
+        wide = x_all[mine, :].astype(F32)
         factor = lax.rsqrt(jnp.mean(wide * wide, axis=-1, keepdims=True) + EPS)
-        x_all[block * rows : (block + 1) * rows, :] = (wide * factor * gain[...]).astype(BF16)
+        x_all[mine, :] = (wide * factor * gain[...]).astype(BF16)
+        return carry
+
+    lax.fori_loop(0, n, normalise, 0)
     for copy in copies[n_rows:]:
         copy.wait()
     projected = [
@@ -273,6 +281,16 @@
         )
         out = out * lax.rsqrt(jnp.mean(out * out, axis=-1, keepdims=True) + EPS)
         attended[block] = out.astype(BF16)
+
+def bring_kernel(*refs):
+    count = len(refs) // 2
+    sems = refs[-1]
+    copies = [pltpu.make_async_copy(refs[i], refs[count + i], sems.at[i]) for i in range(count)]
+    for copy in copies:
+        copy.start()
+    for copy in copies:
+        copy.wait()
+
 
 def project_kernel(n, pos, x_share, *rest):
     weights, pieces, (out, a_all) = rest[:n], rest[n : 2 * n], rest[2 * n :]
@@ -331,110 +349,168 @@
         weight[span, :] = jnp.broadcast_to(chosen, (slots, weight.shape[1]))
 
 
-def stream(n_parts, moves):
-    parts = [
-        [pltpu.make_async_copy(*refs, sem) for refs, sem in moves(i)] for i in range(n_parts)
-    ]
-    for part in parts:
-        for copy in part:
-            copy.start()
-
-    def wait(i):
-        for copy in parts[i]:
-            copy.wait()
-
-    return wait
-
-
-def hidden_kernel(n, slots, group, distances, last, pos, gain, pick, w_gate, w_up, *refs):
-    first = 0 in distances
-    refs = list(refs)
-    n_blocks = len(distances)
-    pieces = [[refs.pop(0) for _ in range(n)] for _ in range(n_blocks)]
-    if not first:
-        total_in, square_in = refs.pop(0), refs.pop(0)
-    if last:
-        weight, hidden_out, r_all, scaled, g_all, u_all, sems = refs
-    else:
-        total_out, square_out, r_all, scaled, g_all, u_all, sems = refs
-    s, h = pos[1], pos[2]
+def span(block, size):
+    return pl.ds(pl.multiple_of(block * size, size), size)
+
+
+def weight_copies(pos, distances, i, group, ins, outs, sems, first=0):
+    source_part, part = pl.ds(first + i * group, group), pl.ds(i * group, group)
+    cols = outs[0].shape[1] // len(distances)
+    copies = []
+    for k, distance in enumerate(distances):
+        for which, (w, kept) in enumerate(zip(ins, outs)):
+            source = w.at[source_part, span(pos[1] ^ distance, cols), :]
+            target = kept.at[part, pl.ds(k * cols, cols), :]
+            copies.append(pltpu.make_async_copy(source, target, sems.at[i, 2 * k + which]))
+    return copies
+
+
+def down_copies(pos, distances, i, group, w_down, outs, sems):
+    part, cols = pl.ds(i * group, group), outs[0].shape[2]
+    copies = []
+    for k, (distance, kept) in enumerate(zip(distances, outs)):
+        source = w_down.at[part, :, span(pos[2] ^ distance, cols)]
+        copies.append(pltpu.make_async_copy(source, kept.at[part], sems.at[i, k]))
+    return copies
+
+
+def load_kernel(group, distances, pos, w_gate, w_up, g_all, u_all, sems):
+    copies = []
+    for i in range(g_all.shape[0] // group):
+        copies += weight_copies(
+            pos, distances, i, group, (w_gate, w_up), (g_all, u_all), sems
+        )
+    for copy in copies:
+        copy.start()
+    for copy in copies:
+        copy.wait()
+
+
+def place_rows(n, distances, pos, pieces, r_all):
     rows, cols = pieces[0][0].shape
-    experts, _, hidden = g_all.shape
-
-    def span(block, size):
-        return pl.ds(pl.multiple_of(block * size, size), size)
-
-    def moves(i):
-        part = pl.ds(i * group, group)
-        out = []
-        for k, distance in enumerate(distances):
-            column, here = span(s ^ distance, cols), pl.ds(k * cols, cols)
-            for which, (w, kept) in enumerate(((w_gate, g_all), (w_up, u_all))):
-                sem = sems.at[(i * n_blocks + k) * 2 + which]
-                out.append(((w.at[part, column, :], kept.at[part, here, :]), sem))
-        return out
-
-    wait = stream(experts // group, moves)
-    gains = []
+    for k in range(len(distances)):
+        for e in range(n):
+            r_all[span(pos[2] ^ e, rows), k * cols : (k + 1) * cols] = pieces[k][e][...]
+
+
+def gather_rows(distances, pos, gain, picked, r_all, square):
+    cols = r_all.shape[1] // len(distances)
+    scaled = []
     for k, distance in enumerate(distances):
-        here = slice(k * cols, (k + 1) * cols)
-        for e in range(n):
-            r_all[span(h ^ e, rows), here] = pieces[k][e][...]
-        gains.append(gain[:, span(s ^ distance, cols)])
-    width = n * cols
-    factor = []
+        taken = jnp.dot(picked, r_all[:, k * cols : (k + 1) * cols], preferred_element_type=F32)
+        square = square + jnp.sum(taken * taken, axis=1, keepdims=True)
+        scaled.append((taken * gain[:, span(pos[1] ^ distance, cols)]).astype(BF16))
+    return scaled, square
+
+
+def first_hidden_kernel(n, slots, group, distances, pos, gain, pick, g_all, u_all, *refs):
+    pieces = [refs[k * n : (k + 1) * n] for k in range(len(distances))]
+    total_out, square_out, r_all, x_slots = refs[n * len(distances) :]
+    experts, wide, hidden = g_all.shape
+    place_rows(n, distances, pos, pieces, r_all)
     for i in range(experts // group):
         part = slice(i * group * slots, (i + 1) * group * slots)
-        square = 0.0 if first else square_in[part, :1]
-        for k in range(n_blocks):
-            here = slice(k * cols, (k + 1) * cols)
-            taken = jnp.dot(pick[part, :], r_all[:, here], preferred_element_type=F32)
-            square = square + jnp.sum(taken * taken, axis=1, keepdims=True)
-            scaled[part, here] = (taken * gains[k]).astype(BF16)
-        if last:
-            factor.append(lax.rsqrt(square / width + EPS))
-        else:
-            square_out[part, :] = jnp.broadcast_to(square, (group * slots, square_out.shape[1]))
-    for i in range(experts // group):
-        wait(i)
-        for e in range(i * group, (i + 1) * group):
+        scaled, square = gather_rows(distances, pos, gain, pick[part, :], r_all, 0.0)
+        for k, value in enumerate(scaled):
+            x_slots[part, k * value.shape[1] : (k + 1) * value.shape[1]] = value
+        square_out[part, :] = jnp.broadcast_to(square, (group * slots, square_out.shape[1]))
+    for e in range(experts):
+        mine = slice(e * slots, (e + 1) * slots)
+        total_out[mine, :hidden] = jnp.dot(x_slots[mine, :], g_all[e], preferred_element_type=F32)
+        total_out[mine, hidden:] = jnp.dot(x_slots[mine, :], u_all[e], preferred_element_type=F32)
+
+
+def last_hidden_kernel(
+    n, slots, group, distances, downs, pos, gain, pick, w_gate, w_up, w_down, g_some, u_some,
+    total_in, square_in, weight, *refs,
+):
+    pieces = [refs[k * n : (k + 1) * n] for k in range(len(distances))]
+    hidden_out, *refs = refs[n * len(distances) :]
+    d_outs, (r_all, x_slots, g_all, u_all, sems, d_sems) = refs[: len(downs)], refs[len(downs) :]
+    some, wide, hidden = g_some.shape
+    ready, parts = some // group, (some + g_all.shape[0]) // group
+    width = n * wide // len(distances)
+
+    def copies(i):
+        return weight_copies(
+            pos, distances, i, group, (w_gate, w_up), (g_all, u_all), sems, first=some
+        )
+
+    def start(i, carry):
+        for copy in copies(i):
+            copy.start()
+        return carry
+
+    def d_copies(i):
+        return down_copies(pos, downs, i, group, w_down, d_outs, d_sems)
+
+    def start_down(i, carry):
+        for copy in d_copies(i):
+            copy.start()
+        return carry
+
+    def step(g_from, u_from, skipped, i, carry):
+        part = span(i, group * slots)
+        scaled, square = gather_rows(
+            distances, pos, gain, pick[part, :], r_all, square_in[part, :1]
+        )
+        for k, value in enumerate(scaled):
+            x_slots[:, k * value.shape[1] : (k + 1) * value.shape[1]] = value
+        scale = lax.rsqrt(square / width + EPS)
+        if skipped:
+            for copy in copies(i - skipped):
+                copy.wait()
+        for e in range(group):
+            inner = slice(e * slots, (e + 1) * slots)
+            mine = pl.ds(pl.multiple_of(i * group * slots + e * slots, slots), slots)
+            taken = x_slots[inner, :]
+            gate_val = jnp.dot(taken, g_from[(i - skipped) * group + e], preferred_element_type=F32)
+            up_val = jnp.dot(taken, u_from[(i - skipped) * group + e], preferred_element_type=F32)
+            gate_val = (gate_val + total_in[mine, :hidden]) * scale[inner]
+            up_val = (up_val + total_in[mine, hidden:]) * scale[inner]
+            value = gate_val * jax.nn.sigmoid(gate_val) * (up_val * weight[mine, :1])
+            hidden_out[mine, :] = value.astype(BF16)
+        return carry
+
+    lax.fori_loop(0, parts - ready, start, 0)
+    lax.fori_loop(0, parts, start_down, 0)
+    place_rows(n, distances, pos, pieces, r_all)
+    lax.fori_loop(0, ready, functools.partial(step, g_some, u_some, 0), 0)
+    lax.fori_loop(ready, parts, functools.partial(step, g_all, u_all, ready), 0)
+    for i in range(parts):
+        for copy in d_copies(i):
+            copy.wait()
+
+
+def self_down_kernel(slots, group, distances, pos, hidden, place, w_down, out, kept, y_slots, sems):
+    copies = [
+        down_copies(pos, distances, i, group, w_down, (kept,), sems)[0]
+        for i in range(kept.shape[0] // group)
+    ]
+    for copy in copies:
+        copy.start()
+
+    def step(i, carry):
+        down_copies(pos, distances, i, group, w_down, (kept,), sems)[0].wait()
+        for e in range(group):
+            mine = pl.ds(pl.multiple_of(i * group * slots + e * slots, slots), slots)
+            product = jnp.dot(hidden[mine, :], kept[i * group + e], preferred_element_type=F32)
+            y_slots[mine, :] = product.astype(BF16)
+        return carry
+
+    lax.fori_loop(0, len(copies), step, 0)
+    out[...] = jnp.dot(place[...], y_slots[...], preferred_element_type=F32).astype(BF16)
+
+
+def down_kernel(slots, pos, hidden, place, *refs):
+    count = len(refs) // 2
+    for kept, out in zip(refs[:count], refs[count:]):
+        y_slots = refs[-1]
+        for e in range(kept.shape[0]):
             mine = slice(e * slots, (e + 1) * slots)
-            gate_val = jnp.dot(scaled[mine, :], g_all[e], preferred_element_type=F32)
-            up_val = jnp.dot(scaled[mine, :], u_all[e], preferred_element_type=F32)
-            if not first:
-                gate_val = gate_val + total_in[mine, :hidden]
-                up_val = up_val + total_in[mine, hidden:]
-            if last:
-                inner = (e - i * group) * slots
-                scale = factor[i][inner : inner + slots]
-                gate_val, up_val = gate_val * scale, up_val * scale
-                value = gate_val * jax.nn.sigmoid(gate_val) * (up_val * weight[mine, :1])
-                hidden_out[mine, :] = value.astype(BF16)
-            else:
-                total_out[mine, :hidden] = gate_val
-                total_out[mine, hidden:] = up_val
-
-
-def down_kernel(n, slots, group, distances, pos, hidden, place, w_down, *refs):
-    outs, (d_all, y_slots, sems) = refs[: len(distances)], refs[len(distances) :]
-    h = pos[2]
-    _, experts, _, cols = d_all.shape
-    parts = experts // group
-
-    def moves(i):
-        k, part = i // parts, pl.ds(i % parts * group, group)
-        column = pl.ds(pl.multiple_of((h ^ distances[k]) * cols, cols), cols)
-        return [((w_down.at[part, :, column], d_all.at[k, part]), sems.at[i])]
-
-    wait = stream(len(distances) * parts, moves)
-    for k in range(len(distances)):
-        for i in range(parts):
-            wait(k * parts + i)
-            for e in range(i * group, (i + 1) * group):
-                span = slice(e * slots, (e + 1) * slots)
-                product = jnp.dot(hidden[span, :], d_all[k, e], preferred_element_type=F32)
-                y_slots[span, :] = product.astype(BF16)
-        outs[k][...] = jnp.dot(place[...], y_slots[...], preferred_element_type=F32).astype(BF16)
+            product = jnp.dot(hidden[mine, :], kept[e], preferred_element_type=F32)
+            y_slots[mine, :] = product.astype(BF16)
+        out[...] = jnp.dot(place[...], y_slots[...], preferred_element_type=F32).astype(BF16)
 
 
 def add_kernel(distances, pos, base, core, part, *outs):
@@ -447,6 +523,15 @@
         inside = pl.ds(pl.multiple_of(block % in_half * rows, rows), rows)
         value = base[everywhere, :].astype(F32) + core[everywhere, :].astype(F32)
         out[...] = (value + part[inside, :].astype(F32)).astype(out.dtype)
+
+
+def halves_kernel(pos, base, core, far, near):
+    rows = near.shape[0]
+    blocks = base.shape[0] // rows
+    mine = pos[1] // blocks
+    for half, out in ((blocks - 1 - mine, far), (mine, near)):
+        value = base[span(half, rows), :].astype(F32) + core[span(half, rows), :].astype(F32)
+        out[...] = value.astype(out.dtype)
 
 
 def square_body(
@@ -496,6 +581,9 @@
             ],
             compiler_params=room(8),
         )(pos, *map(held, (routes.T, gates.T, tokens, attn_weight)))
+    group = experts // 4
+    w_gate, w_up, w_down = map(held, (expert_gate, expert_up, expert_down))
+
     with jax.named_scope("gather_tokens_and_weights"):
         x_far = [swap(x_send, "seq", d) for d in range(1, n)]
         w_near = [swap(w_sends[d - 1], "seq", d) for d in range(1, n - 1)]
@@ -538,6 +626,51 @@
             *[held(x_pieces[e]) for e in range(n)], *map(held, w_near), *map(held, w_far[:-1]), w_far[-1],
         )
 
+    early, late = tuple(range(n // 2)), tuple(range(n // 2, n))
+    wide = n // 2 * cols
+    gain_row = moe_gain.reshape(1, width)
+    ahead = experts // 2
+    hidden_cost = cost(pairs * wide * (total + 2 * hidden), 4 * experts * wide * hidden)
+
+    def load(distances, amount, *earlier):
+        return pl.pallas_call(
+            functools.partial(load_kernel, group, distances),
+            out_shape=[pltpu.VMEM((amount, wide, hidden), BF16)] * 2,
+            in_specs=[SMEM] + [ANY] * 2,
+            out_specs=[VMEM] * 2,
+            scratch_shapes=[dma((amount // group, 2 * len(distances)))],
+            compiler_params=room(2),
+            cost_estimate=cost(0, 4 * amount * wide * hidden),
+        )(after(pos, *earlier), w_gate, w_up)
+
+    def first_hidden(pieces, weights):
+        return pl.pallas_call(
+            functools.partial(first_hidden_kernel, n, slots, group, early),
+            out_shape=[sds((pairs, 2 * hidden), F32), sds((pairs, 128), F32)],
+            in_specs=[SMEM] + [VMEM] * (4 + n * len(early)),
+            out_specs=[VMEM] * 2,
+            scratch_shapes=[pltpu.VMEM((total, wide), BF16), pltpu.VMEM((pairs, wide), BF16)],
+            compiler_params=room(12),
+            cost_estimate=hidden_cost,
+        )(pos, gain_row, pick, *map(here, weights), *pieces)
+
+    def last_hidden(pieces, weights, state, downs):
+        return pl.pallas_call(
+            functools.partial(last_hidden_kernel, n, slots, group, late, downs),
+            out_shape=[sds((pairs, hidden), BF16)]
+            + [pltpu.VMEM((experts, hidden, cols), BF16)] * len(downs),
+            in_specs=[SMEM] + [VMEM] * 2 + [ANY] * 3 + [VMEM] * (5 + n * len(late)),
+            out_specs=[VMEM] * (1 + len(downs)),
+            scratch_shapes=[pltpu.VMEM((total, wide), BF16), pltpu.VMEM((group * slots, wide), BF16)]
+            + [pltpu.VMEM((experts - ahead, wide, hidden), BF16)] * 2
+            + [dma(((experts - ahead) // group, 2 * len(late)))]
+            + [dma((experts // group, len(downs)))],
+            compiler_params=room(16),
+            cost_estimate=hidden_cost,
+        )(
+            pos, gain_row, pick, w_gate, w_up, w_down, *map(here, weights), *state, weight, *pieces
+        )
+
     with jax.named_scope("heads_to_tokens"):
         for e in (0, 2):
             o_pieces[e ^ 1] = swap(after(o_pieces[e], attended), "head", 1)
@@ -546,8 +679,21 @@
         ]
         arrived = jnp.stack([by_block[0]] + [swap(by_block[e], "head", e) for e in range(1, n)])
         a_pieces = [arrived, swap(arrived, "seq", 1), swap(arrived, "seq", 2)]
+        with jax.named_scope("expert_weights"):
+            early_weights = load(early, experts, arrived)
+        a_pieces[2] = after(a_pieces[2], early_weights[0])
         a_pieces.append(swap(a_pieces[2], "seq", 1))
 
+    with jax.named_scope("bring_out_weights"):
+        o_here = pl.pallas_call(
+            bring_kernel,
+            out_shape=[pltpu.VMEM((depth, cols), BF16)] * n,
+            in_specs=[ANY] * n,
+            out_specs=[VMEM] * n,
+            scratch_shapes=[dma((n,))],
+            compiler_params=room(2),
+            cost_estimate=cost(0, 2 * n * depth * cols),
+        )(*[held(o_pieces[e]) for e in range(n)])
     with jax.named_scope("output_projection"):
         residual = pl.pallas_call(
             functools.partial(project_kernel, n),
@@ -556,40 +702,11 @@
             out_specs=VMEM,
             scratch_shapes=[pltpu.VMEM((n, rows, n * HEAD_DIM), BF16)],
             compiler_params=room(12),
-        )(pos, x_share, *[o_pieces[e] for e in range(n)], *a_pieces)
-
-    group = experts // 4
-
-    def add_blocks(distances, pieces, state):
-        last = n - 1 in distances
-        wide = len(distances) * cols
-        with jax.named_scope("hidden_units_" + "_".join(map(str, distances))):
-            return pl.pallas_call(
-                functools.partial(hidden_kernel, n, slots, group, distances, last),
-                out_shape=[sds((pairs, hidden), BF16)]
-                if last
-                else [sds((pairs, 2 * hidden), F32), sds((pairs, 128), F32)],
-                in_specs=[SMEM] + [VMEM] * 2 + [ANY] * 2
-                + [VMEM] * (n * len(distances) + len(state) + last),
-                out_specs=[VMEM] * (2 - last),
-                scratch_shapes=[
-                    pltpu.VMEM((total, wide), BF16),
-                    pltpu.VMEM((pairs, wide), BF16),
-                    pltpu.VMEM((experts, wide, hidden), BF16),
-                    pltpu.VMEM((experts, wide, hidden), BF16),
-                    dma((2 * len(distances) * (experts // group),)),
-                ],
-                compiler_params=room(6 + 11 * len(distances)),
-                cost_estimate=cost(pairs * wide * (total + 2 * hidden), 4 * experts * wide * hidden),
-            )(
-                pos, moe_gain.reshape(1, width), pick, held(expert_gate), held(expert_up),
-                *[pieces[d][e] for d in distances for e in range(n)],
-                *state, *([weight] if last else []),
-            )
+        )(pos, x_share, *map(here, o_here), *a_pieces)
 
     with jax.named_scope("gather_residual"):
-        early, late = tuple(range(n // 2)), tuple(range(n // 2, n))
         r_pieces = {0: {0: residual}}
+        late_weights = load(late, ahead, residual)
         for d in (1, 2):
             r_pieces[d] = {0: swap(residual, "seq", d)}
         r_pieces[3] = {0: swap(r_pieces[2][0], "seq", 1)}
@@ -598,49 +715,63 @@
             r_pieces[d][1] = swap(r_pieces[d][0], "head", 1)
         for d in early:
             r_pieces[d][3] = swap(r_pieces[d][2], "head", 1)
-        r_pieces[0][0] = after(residual, *[r_pieces[d][0] for d in late])
-        state = add_blocks(early, r_pieces, ())
+        r_pieces[0][0] = after(residual, late_weights[0], *[r_pieces[d][0] for d in late])
+        pieces = [r_pieces[d][e] for d in early for e in range(n)]
+        with jax.named_scope("first_hidden_units"):
+            state = first_hidden(pieces, early_weights)
         for d in late:
             r_pieces[d][3] = swap(after(r_pieces[d][2], state[1]), "head", 1)
-        state = add_blocks(late, r_pieces, state)
+        pieces = [r_pieces[d][e] for d in late for e in range(n)]
+        with jax.named_scope("last_hidden_units"):
+            units, d_3, d_1 = last_hidden(pieces, late_weights, state, (3, 1))
         r_choices = [r_pieces[d][d] for d in range(n)]
-    (units,) = state
-
-    def down(distances, units):
-        with jax.named_scope("down_quarters_" + "_".join(map(str, distances))):
+    def down(units, *weights):
+        count = len(weights)
+        with jax.named_scope("down_products"):
             return pl.pallas_call(
-                functools.partial(down_kernel, n, slots, group, distances),
-                out_shape=[sds((total, cols), BF16)] * len(distances),
-                in_specs=[SMEM, VMEM, VMEM, ANY],
-                out_specs=[VMEM] * len(distances),
+                functools.partial(down_kernel, slots),
+                out_shape=[sds((total, cols), BF16)] * count,
+                in_specs=[SMEM] + [VMEM] * (2 + count),
+                out_specs=[VMEM] * count,
+                scratch_shapes=[pltpu.VMEM((pairs, cols), BF16)],
+                compiler_params=room(6),
+                cost_estimate=cost(
+                    count * pairs * cols * (total + hidden), 2 * count * experts * cols * hidden
+                ),
+            )(pos, units, place, *map(here, weights))
+
+    def self_down(units, distance):
+        with jax.named_scope("down_products_alone"):
+            return pl.pallas_call(
+                functools.partial(self_down_kernel, slots, group, (distance,)),
+                out_shape=sds((total, cols), BF16),
+                in_specs=[SMEM] + [VMEM] * 2 + [ANY],
+                out_specs=VMEM,
                 scratch_shapes=[
-                    pltpu.VMEM((len(distances), experts, hidden, cols), BF16),
+                    pltpu.VMEM((experts, hidden, cols), BF16),
                     pltpu.VMEM((pairs, cols), BF16),
-                    dma((len(distances) * (experts // group),)),
+                    dma((experts // group, 1)),
                 ],
-                compiler_params=room(4 + 5 * len(distances)),
-                cost_estimate=cost(
-                    len(distances) * pairs * cols * (total + hidden),
-                    2 * len(distances) * experts * cols * hidden,
-                ),
-            )(pos, units, place, held(expert_down))
-
-    def rows_of(array, block, count=1):
-        return lax.dynamic_slice_in_dim(array, block * rows, count * rows, 0)
+                compiler_params=room(9),
+                cost_estimate=cost(pairs * cols * (total + hidden), 2 * experts * cols * hidden),
+            )(pos, units, place, w_down)
 
     with jax.named_scope("sum_over_devices"):
         half_line = n // 2
-        here = s // half_line * half_line
-        there = half_line - here
-        out_3, out_1 = down((3, 1), units)
+        out_3, out_1 = down(units, d_3, d_1)
         core_2, core_0 = swap(out_3, "head", 1), swap(out_1, "head", 1)
-        (out_2,) = down((2,), after(units, out_3))
-        near = [
-            plus(rows_of(out_2, b, half_line), rows_of(core_2, b, half_line)).astype(BF16)
-            for b in (there, here)
-        ]
+        out_2 = self_down(after(units, out_3), 2)
+        with jax.named_scope("halves_over_cores"):
+            near = pl.pallas_call(
+                halves_kernel,
+                out_shape=[sds((half_line * rows, cols), BF16)] * 2,
+                in_specs=[SMEM] + [VMEM] * 2,
+                out_specs=[VMEM] * 2,
+                compiler_params=room(4),
+                cost_estimate=cost(0, 4 * total * cols),
+            )(pos, out_2, core_2)
         far = [swap(part, "head", 2) for part in near]
-        (out_0,) = down((0,), after(units, *near))
+        out_0 = self_down(after(units, *near), 0)
 
         def add_parts(scope, distances, part, macs):
             with jax.named_scope(scope):

time: 157 us -> 151 us (0.962)
  waiting for transfers between devices: 58.8 us -> 44.8 us
  starting transfers between devices: 36.9 us -> 42.3 us
  Pallas kernels: 45 us -> 49.8 us
  other arithmetic: 3 us -> 1.07 us
    ppermute x43, waiting for transfers between devices: 58.8 us -> 44.8 us  [swap(): return lax.ppermute(array, axis, [(i, i ^ distance) for i in range(size)])]
    pallas_call x5 -> x9, Pallas kernels: 31.1 us -> 37.3 us  [the longest x2 10.5 us: load(): pl.pallas_call(functools.partial(load_kernel, group, distances), out_shap...]
    ppermute x43, starting transfers between devices: 36.9 us -> 42.3 us  [swap(): return lax.ppermute(array, axis, [(i, i ^ distance) for i in range(size)])]
    convert_element_type x1 -> x0, other arithmetic: 1.94 us -> none  [square_body(): plus(rows_of(out_2, b, half_line), rows_of(core_2, b, half_line))]
  transfers between devices with their start and end apart: 43 -> 43, of which waited for: 21 -> 19; matrix products, arithmetic and copies ran while one was open for 1% -> 0% of each run, Pallas kernels for 16% -> 23%
where the time goes in v5:
time: 151 us
  Pallas kernels  49.8 us (33%)
  waiting for transfers between devices  44.8 us (30%)
  starting transfers between devices  42.3 us (28%)
  blocking collectives  6.51 us (4%)
  local copies, waits for them, and re-layouts  6.31 us (4%)
    ppermute x43, waiting for transfers between devices, swap(): return lax.ppermute(array, axis, [(i, i ^ distance) for i in range(size)])  44.8 us
    ppermute x43, starting transfers between devices, swap(): return lax.ppermute(array, axis, [(i, i ^ distance) for i in range(size)])  42.3 us
    pallas_call x2, Pallas kernels, load(): pl.pallas_call(functools.partial(load_kernel, group, distances), out_shap...  10.5 us
    pallas_call x2, Pallas kernels, self_down(): pl.pallas_call(functools.partial(self_down_kernel, slots, group, (distanc...  7.85 us
    pallas_call x1, Pallas kernels, last_hidden(): pl.pallas_call(functools.partial(last_hidden_kernel, n, slots, group, lat...  6.59 us
    all_gather x1, blocking collectives, square_body(): return lax.all_gather(mixed, 'head', axis=1, tiled=True)  6.51 us
    unnamed x39, local copies, waits for them, and re-layouts  6.27 us
    pallas_call x1, Pallas kernels, square_body(): pl.pallas_call(functools.partial(attend_kernel, n), out_shape=[sds((n, ro...  5.6 us
  transfers between devices with their start and end apart: 43, of which 19 were waited for; matrix products, arithmetic and copies ran while one was open for 0% of the time, Pallas kernels for 23%

profile of v5, /device:TPU:0, one launch (start us, length us, event | category | flops | bytes accessed | tf_op | source)
XLA Modules:
  0.0 151.2 jit_solution(13902149322841993488)
XLA Ops:
  0.1 2.9 %cut_pieces.1 = (bf16[144,512]{1,0:T(8,128)(2,1)S(1)}, bf16[512,384]{1,0:T(8,128)(2,1)S(1)}, bf16[512,512]{1,0:T(8,128)(2,1)}, bf16[256,384]{1,0:T(8,128)(2,1)S(...) custom-call(s32[3]{0:T(128)S(1)} %pad_add_fusion.pos, s32[8,128]{1,0:T(8,128)} %bitcast.28, ...), custom_call_target="tpu_custom_call" | custom-call | tf_op jit(solution)/shard_map/cut_pieces/pallas_call | solution.py:567
  3.0 0.7 copy-done.10
  3.8 3.0 %collective-permute-start.3 = (bf16[256,384]{1,0:T(8,128)(2,1)S(1)}, bf16[256,384]{1,0:T(8,128)(2,1)S(1)}, u32[]{:S(2)}, u32[]{:S(2)}) collective-permute-start(bf16[256,384]{1,0:T(8,128)(2,1)S(1)} %get-tuple-element.67), channel_id=1, source_target_pairs={{0,4},{4,0},{8,12},{12,8},{1,5},{5,1},{9,13},{13,9},{2,6},{6,2},{1... | collective-permute-start | bytes 589832 | tf_op jit(solution)/shard_map/gather_tokens_and_weights/ppermute | solution.py:149
  6.8 2.6 %collective-permute-start.4 = (bf16[256,384]{1,0:T(8,128)(2,1)S(1)}, bf16[256,384]{1,0:T(8,128)(2,1)S(1)}, u32[]{:S(2)}, u32[]{:S(2)}) collective-permute-start(bf16[256,384]{1,0:T(8,128)(2,1)S(1)} %get-tuple-element.68), channel_id=1, source_target_pairs={{0,8},{4,12},{8,0},{12,4},{1,9},{5,13},{9,1},{13,5},{2,10},{6,14},... | collective-permute-start | bytes 589832 | tf_op jit(solution)/shard_map/gather_tokens_and_weights/ppermute | solution.py:149
  9.8 3.9 %collective-permute-start.2 = (bf16[144,512]{1,0:T(8,128)(2,1)S(1)}, bf16[144,512]{1,0:T(8,128)(2,1)S(1)}, u32[]{:S(2)}, u32[]{:S(2)}) collective-permute-start(bf16[144,512]{1,0:T(8,128)(2,1)S(1)} %get-tuple-element.66.refs_0_), channel_id=1, source_target_pairs={{0,12},{4,8},{8,4},{12,0},{1,13},{5,9},{9,5},{13,1},{2,14},{6,10},... | collective-permute-start | bytes 442376 | tf_op jit(solution)/shard_map/gather_tokens_and_weights/ppermute | solution.py:149
  13.8 0.6 copy-done.11
  14.4 6.7 %collective-permute-done.refs_1_ = bf16[144,512]{1,0:T(8,128)(2,1)S(1)} collective-permute-done((bf16[144,512]{1,0:T(8,128)(2,1)S(1)}, bf16[144,512]{1,0:T(8,128)(2,1)S(1)}, u32[]{:S(2)}, u32[]{:S(2)}) %collective-permute-start) | collective-permute-done | bytes 147488 | tf_op jit(solution)/shard_map/gather_tokens_and_weights/ppermute | solution.py:149
  21.1 8.1 %collective-permute-done.1.refs_2_ = bf16[144,512]{1,0:T(8,128)(2,1)S(1)} collective-permute-done((bf16[144,512]{1,0:T(8,128)(2,1)S(1)}, bf16[144,512]{1,0:T(8,128)(2,1)S(1)}, u32[]{:S(2)}, u32[]{:S(2)}) %collective-permute-start.1) | collective-permute-done | bytes 147488 | tf_op jit(solution)/shard_map/gather_tokens_and_weights/ppermute | solution.py:149
  29.3 0.6 copy-done.2
  29.9 0.8 pad_maximum_fusion.rest_0_
  30.7 1.5 collective-permute-start.6
  32.2 2.5 %collective-permute-start.7 = (bf16[256,384]{1,0:T(8,128)(2,1)S(1)}, bf16[256,384]{1,0:T(8,128)(2,1)}, u32[]{:S(2)}, u32[]{:S(2)}) collective-permute-start(bf16[256,384]{1,0:T(8,128)(2,1)S(1)} %get-tuple-element.73), channel_id=1, source_target_pairs={{0,12},{4,8},{8,4},{12,0},{1,13},{5,9},{9,5},{13,1},{2,14},{6,10},... | collective-permute-start | bytes 589832 | tf_op jit(solution)/shard_map/gather_tokens_and_weights/ppermute | solution.py:149
  34.7 1.5 %collective-permute-start.8 = (bf16[256,384]{1,0:T(8,128)(2,1)S(1)}, bf16[256,384]{1,0:T(8,128)(2,1)S(1)}, u32[]{:S(2)}, u32[]{:S(2)}) collective-permute-start(bf16[256,384]{1,0:T(8,128)(2,1)S(1)} %collective-permute-done.3.rest_4_), channel_id=1, source_target_pairs={{0,16},{16,0},{1,17},{17,1},{2,18},{18,2},{3,19},{19,3},{4,20},{20... | collective-permute-start | bytes 589832 | tf_op jit(solution)/shard_map/gather_tokens_and_weights/ppermute | solution.py:149
  36.7 3.2 %collective-permute-done.7.rest_6_ = bf16[256,384]{1,0:T(8,128)(2,1)} collective-permute-done((bf16[256,384]{1,0:T(8,128)(2,1)S(1)}, bf16[256,384]{1,0:T(8,128)(2,1)}, u32[]{:S(2)}, u32[]{:S(2)}) %collective-permute-start.7) | collective-permute-done | bytes 196640 | tf_op jit(solution)/shard_map/gather_tokens_and_weights/ppermute | solution.py:149
  40.4 2.1 %collective-permute-done.9.rest_8_ = bf16[256,384]{1,0:T(8,128)(2,1)S(1)} collective-permute-done((bf16[256,384]{1,0:T(8,128)(2,1)S(1)}, bf16[256,384]{1,0:T(8,128)(2,1)S(1)}, u32[]{:S(2)}, u32[]{:S(2)}) %collective-permute-start.9) | collective-permute-done | bytes 196640 | tf_op jit(solution)/shard_map/gather_tokens_and_weights/ppermute | solution.py:149
  42.5 0.7 copy-done.18
  43.2 0.5 collective-permute-start.13
  44.2 1.5 %collective-permute-start.11 = (bf16[256,384]{1,0:T(8,128)(2,1)}, bf16[256,384]{1,0:T(8,128)(2,1)}, u32[]{:S(2)}, u32[]{:S(2)}) collective-permute-start(bf16[256,384]{1,0:T(8,128)(2,1)} %collective-permute-done.7.rest_6_), channel_id=1, source_target_pairs={{0,16},{16,0},{1,17},{17,1},{2,18},{18,2},{3,19},{19,3},{4,20},{20... | collective-permute-start | bytes 589832 | tf_op jit(solution)/shard_map/gather_tokens_and_weights/ppermute | solution.py:149
  45.7 0.9 copy-done.3
  46.6 0.9 copy-done.5
  47.6 0.9 copy-done.12
  48.5 1.3 routing.1
  49.8 1.5 collective-permute-done.11.rest_9_
  51.3 5.6 %attention.1 = (bf16[4,128,128]{2,1,0:T(8,128)(2,1)S(1)}, bf16[128,512]{1,0:T(8,128)(2,1)S(1)}) custom-call(s32[3]{0:T(128)S(1)} %pad_add_fusion.pos, f32[1,2048]{1,0:T(1,128)S(1)} %bitcast.24, bf16[128,2048]{1,0:T(8,128)(2,1)} %tokens.3, bf16[512,384]{1,0:T(8,128)(2,1)} %copy-done.10, bf16[3,128,512]{2,1,0:T(8,128)(2,1)} %pad_maximum_fusion.rest_0_, ...), custom_call_target="tpu_custom_call" | custom-call | tf_op jit(solution)/shard_map/attention/pallas_call | solution.py:613
  57.6 1.2 collective-permute-start.17
  58.8 0.5 collective-permute-start.16
  59.5 1.5 %collective-permute-done.17 = bf16[128,128]{1,0:T(8,128)(2,1)S(1)} collective-permute-done((bf16[128,128]{1,0:T(8,128)(2,1)S(1)}, bf16[128,128]{1,0:T(8,128)(2,1)S(1)}, u32[]{:S(2)}, u32[]{:S(2)}) %collective-permute-start.17) | collective-permute-done | bytes 32800 | tf_op jit(solution)/shard_map/heads_to_tokens/ppermute | solution.py:149
  61.0 1.7 %collective-permute-done.16 = bf16[128,128]{1,0:T(8,128)(2,1)S(1)} collective-permute-done((bf16[128,128]{1,0:T(8,128)(2,1)S(1)}, bf16[128,128]{1,0:T(8,128)(2,1)S(1)}, u32[]{:S(2)}, u32[]{:S(2)}) %collective-permute-start.16) | collective-permute-done | bytes 32800 | tf_op jit(solution)/shard_map/heads_to_tokens/ppermute | solution.py:149
  62.7 2.7 %collective-permute-start.19 = (bf16[4,128,128]{2,1,0:T(8,128)(2,1)S(1)}, bf16[4,128,128]{2,1,0:T(8,128)(2,1)S(1)}, u32[]{:S(2)}, u32[]{:S(2)}) collective-permute-start(bf16[4,128,128]{2,1,0:T(8,128)(2,1)S(1)} %pad_maximum_fusion.1.rest_4_), channel_id=1, source_target_pairs={{0,8},{4,12},{8,0},{12,4},{1,9},{5,13},{9,1},{13,5},{2,10},{6,14},... | collective-permute-start | bytes 393224 | tf_op jit(solution)/shard_map/heads_to_tokens/ppermute | solution.py:149
  65.6 6.5 %expert_weights.1 = (bf16[16,1024,256]{2,1,0:T(8,128)(2,1)S(1)}, bf16[16,1024,256]{2,1,0:T(8,128)(2,1)S(1)}) custom-call(s32[3]{0:T(128)S(1)} %pad_add_fusion.pos, bf16[16,2048,256]{2,1,0:T(8,128)(2,1)} %w_gate.5, bf16[16,2048,256]{2,1,0:T(8,128)(2,1)} %w_up.5), custom_call_target="tpu_custom_call" | custom-call | bytes 16777216 | tf_op jit(solution)/shard_map/heads_to_tokens/expert_weights/pallas_call | solution.py:636
  72.1 1.9 %collective-permute-start.20 = (bf16[4,128,128]{2,1,0:T(8,128)(2,1)S(1)}, bf16[4,128,128]{2,1,0:T(8,128)(2,1)S(1)}, u32[]{:S(2)}, u32[]{:S(2)}) collective-permute-start(bf16[4,128,128]{2,1,0:T(8,128)(2,1)S(1)} %collective-permute-done.19.rest_6_), channel_id=1, source_target_pairs={{0,4},{4,0},{8,12},{12,8},{1,5},{5,1},{9,13},{13,9},{2,6},{6,2},{1... | collective-permute-start | bytes 393224 | tf_op jit(solution)/shard_map/heads_to_tokens/ppermute | solution.py:149
  74.0 1.6 %bring_out_weights.1 = (bf16[512,512]{1,0:T(8,128)(2,1)S(1)}, bf16[512,512]{1,0:T(8,128)(2,1)S(1)}, bf16[512,512]{1,0:T(8,128)(2,1)S(1)}, bf16[512,512]{1,0:T(8,128)(2,1)S(1)}) custom-call(bf16[512,512]{1,0:T(8,128)(2,1)} %get-tuple-element.86.refs_0_, bf16[512,512]{1,0:T(8,128)(2,1)} %collective-permute-done.12.refs_1_, ...), custom_call_target="tpu_custom_call" | custom-call | bytes 2097152 | tf_op jit(solution)/shard_map/bring_out_weights/pallas_call | solution.py:688
  75.6 1.6 %collective-permute-done.20.rest_7_ = bf16[4,128,128]{2,1,0:T(8,128)(2,1)S(1)} collective-permute-done((bf16[4,128,128]{2,1,0:T(8,128)(2,1)S(1)}, bf16[4,128,128]{2,1,0:T(8,128)(2,1)S(1)}, u32[]{:S(2)}, u32[]{:S(2)}) %collective-permute-start.20) | collective-permute-done | bytes 131104 | tf_op jit(solution)/shard_map/heads_to_tokens/ppermute | solution.py:149
  77.1 1.3 output_projection.1.refs_0_
  78.5 1.9 %collective-permute-start.23 = (bf16[128,512]{1,0:T(8,128)(2,1)S(1)}, bf16[128,512]{1,0:T(8,128)(2,1)S(1)}, u32[]{:S(2)}, u32[]{:S(2)}) collective-permute-start(bf16[128,512]{1,0:T(8,128)(2,1)S(1)} %output_projection.1.refs_0_), channel_id=1, source_target_pairs={{0,4},{4,0},{8,12},{12,8},{1,5},{5,1},{9,13},{13,9},{2,6},{6,2},{1... | collective-permute-start | bytes 393224 | tf_op jit(solution)/shard_map/gather_residual/ppermute | solution.py:149
  80.4 1.1 collective-permute-start.21
  81.5 0.8 collective-permute-start.28
  82.3 1.6 %collective-permute-done.23.refs_4_ = bf16[128,512]{1,0:T(8,128)(2,1)S(1)} collective-permute-done((bf16[128,512]{1,0:T(8,128)(2,1)S(1)}, bf16[128,512]{1,0:T(8,128)(2,1)S(1)}, u32[]{:S(2)}, u32[]{:S(2)}) %collective-permute-start.23) | collective-permute-done | bytes 131104 | tf_op jit(solution)/shard_map/gather_residual/ppermute | solution.py:149
  83.9 1.3 collective-permute-start.30
  85.3 2.5 %collective-permute-done.21.refs_0_ = bf16[128,512]{1,0:T(8,128)(2,1)S(1)} collective-permute-done((bf16[128,512]{1,0:T(8,128)(2,1)S(1)}, bf16[128,512]{1,0:T(8,128)(2,1)S(1)}, u32[]{:S(2)}, u32[]{:S(2)}) %collective-permute-start.21) | collective-permute-done | bytes 131104 | tf_op jit(solution)/shard_map/gather_residual/ppermute | solution.py:149
  88.9 4.0 %gather_residual.1 = (bf16[8,1024,256]{2,1,0:T(8,128)(2,1)S(1)}, bf16[8,1024,256]{2,1,0:T(8,128)(2,1)S(1)}) custom-call(s32[3]{0:T(128)S(1)} %pad_add_fusion.pos, bf16[16,2048,256]{2,1,0:T(8,128)(2,1)} %w_gate.5, bf16[16,2048,256]{2,1,0:T(8,128)(2,1)} %w_up.5), custom_call_target="tpu_custom_call" | custom-call | bytes 8388608 | tf_op jit(solution)/shard_map/gather_residual/pallas_call | solution.py:636
  92.9 0.6 collective-permute-start.33
  93.5 1.4 collective-permute-start.25
  94.9 0.7 collective-permute-start.26
  95.6 5.2 %first_hidden_units.1 = (f32[1280,512]{1,0:T(8,128)S(1)}, f32[1280,128]{1,0:T(8,128)S(1)}) custom-call(s32[3]{0:T(128)S(1)} %pad_add_fusion.pos, f32[1,2048]{1,0:T(1,128)S(1)} %bitcast.22, bf16[1280,512]{1,0:T(8,128)(2,1)S(1)} %get-tuple-element.79.pick, bf16[16,1024,256]{2,1,0:T(8,128)(2,1)S(1)} %get-tuple-element.93.g_all, ...), custom_call_target="tpu_custom_call" | custom-call | flops 2684354560 | bytes 16777216 | tf_op jit(solution)/shard_map/gather_residual/first_hidden_units/pallas_call | solution.py:647
  101.0 0.8 collective-permute-done.26.refs_6_
  102.2 0.9 collective-permute-done.32.refs_7_
  103.2 6.6 %last_hidden_units.1 = (bf16[1280,256]{1,0:T(8,128)(2,1)S(1)}, bf16[16,256,512]{2,1,0:T(8,128)(2,1)S(1)}, bf16[16,256,512]{2,1,0:T(8,128)(2,1)S(1)}) custom-call(s32[3]{0:T(128)S(1)} %pad_add_fusion.pos, f32[1,2048]{1,0:T(1,128)S(1)} %bitcast.23, bf16[1280,512]{1,0:T(8,128)(2,1)S(1)} %get-tuple-element.79.pick, bf16[16,2048,256]{2,1,0:T(8,128)(2,1)} %w_gate.5, ...), custom_call_target="tpu_custom_call" | custom-call | flops 2684354560 | bytes 16777216 | tf_op jit(solution)/shard_map/gather_residual/last_hidden_units/pallas_call | solution.py:658
  109.8 4.3 %down_products.1 = (bf16[512,512]{1,0:T(8,128)(2,1)S(1)}, bf16[512,512]{1,0:T(8,128)(2,1)}) custom-call(s32[3]{0:T(128)S(1)} %pad_add_fusion.pos, bf16[1280,256]{1,0:T(8,128)(2,1)S(1)} %get-tuple-element.113.hidden, bf16[512,1280]{1,0:T(8,128)(2,1)S(1)} %get-tuple-element.106.place, bf16[16,256,512]{2,1,0:T(8,128)(2,1)S(1)} %get-tuple-element.107.refs_0_, ...), custom_call_target="tpu_custom_call" | custom-call | flops 2013265920 | bytes 8388608 | tf_op jit(solution)/shard_map/sum_over_devices/down_products/pallas_call | solution.py:731
  114.6 3.9 %down_products_alone.2.base = bf16[512,512]{1,0:T(8,128)(2,1)S(1)} custom-call(s32[3]{0:T(128)S(1)} %pad_add_fusion.pos, bf16[1280,256]{1,0:T(8,128)(2,1)S(1)} %get-tuple-element.113.hidden, bf16[512,1280]{1,0:T(8,128)(2,1)S(1)} %get-tuple-element.106.place, bf16[16,256,2048]{2,1,0:T(8,128)(2,1)} %w_down.5), custom_call_target="tpu_custom_call" | custom-call | flops 1006632960 | bytes 4194304 | tf_op jit(solution)/shard_map/sum_over_devices/down_products_alone/pallas_call | solution.py:745
  118.5 1.3 halves_over_cores.1
  119.9 1.3 collective-permute-start.39
  121.2 0.7 collective-permute-start.38
  121.9 3.9 %down_products_alone.3.base = bf16[512,512]{1,0:T(8,128)(2,1)S(1)} custom-call(s32[3]{0:T(128)S(1)} %pad_add_fusion.pos, bf16[1280,256]{1,0:T(8,128)(2,1)S(1)} %get-tuple-element.113.hidden, bf16[512,1280]{1,0:T(8,128)(2,1)S(1)} %get-tuple-element.106.place, bf16[16,256,2048]{2,1,0:T(8,128)(2,1)} %w_down.5), custom_call_target="tpu_custom_call" | custom-call | flops 1006632960 | bytes 4194304 | tf_op jit(solution)/shard_map/sum_over_devices/down_products_alone/pallas_call | solution.py:745
  125.8 3.4 %collective-permute-done.39.part = bf16[256,512]{1,0:T(8,128)(2,1)S(1)} collective-permute-done((bf16[256,512]{1,0:T(8,128)(2,1)}, bf16[256,512]{1,0:T(8,128)(2,1)S(1)}, u32[]{:S(2)}, u32[]{:S(2)}) %collective-permute-start.39) | collective-permute-done | bytes 262176 | tf_op jit(solution)/shard_map/sum_over_devices/ppermute | solution.py:149
  129.2 0.6 far_half_rows.1
  129.9 3.2 %collective-permute-start.41 = (bf16[128,512]{1,0:T(8,128)(2,1)S(1)}, bf16[128,512]{1,0:T(8,128)(2,1)S(1)}, u32[]{:S(2)}, u32[]{:S(2)}) collective-permute-start(bf16[128,512]{1,0:T(8,128)(2,1)S(1)} %get-tuple-element.121), channel_id=1, source_target_pairs={{0,12},{4,8},{8,4},{12,0},{1,13},{5,9},{9,5},{13,1},{2,14},{6,10},... | collective-permute-start | bytes 393224 | tf_op jit(solution)/shard_map/sum_over_devices/ppermute | solution.py:149
  133.3 0.8 collective-permute-done.38.part
  134.1 0.6 near_half_rows.1
  134.7 1.9 %collective-permute-start.42 = (bf16[128,512]{1,0:T(8,128)(2,1)S(1)}, bf16[128,512]{1,0:T(8,128)(2,1)S(1)}, u32[]{:S(2)}, u32[]{:S(2)}) collective-permute-start(bf16[128,512]{1,0:T(8,128)(2,1)S(1)} %get-tuple-element.122), channel_id=1, source_target_pairs={{0,4},{4,0},{8,12},{12,8},{1,5},{5,1},{9,13},{13,9},{2,6},{6,2},{1... | collective-permute-start | bytes 393224 | tf_op jit(solution)/shard_map/sum_over_devices/ppermute | solution.py:149
  136.7 0.7 collective-permute-done.41
  137.4 6.3 %collective-permute-done.40 = bf16[128,512]{1,0:T(8,128)(2,1)S(1)} collective-permute-done((bf16[128,512]{1,0:T(8,128)(2,1)S(1)}, bf16[128,512]{1,0:T(8,128)(2,1)S(1)}, u32[]{:S(2)}, u32[]{:S(2)}) %collective-permute-start.40) | collective-permute-done | bytes 131104 | tf_op jit(solution)/shard_map/sum_over_devices/ppermute | solution.py:149
  143.8 6.5 %all_gather.3 = bf16[128,2048]{1,0:T(8,128)(2,1)S(1)} all-gather(bf16[128,512]{1,0:T(8,128)(2,1)S(1)} %add_convert_fusion), channel_id=1, replica_groups=mesh['grp'=2,'seq'=4,'head'=4] {'head'}, dimensions={1}, use_global_device_ids=true | all-gather | bytes 655360 | tf_op jit(solution)/shard_map/gather_columns/all_gather | solution.py:797
  150.4 0.8 copy.11
  (85 shorter events, 5.7 us)
Async XLA Ops:
  0.0 51.3 %copy-start.14 = (f32[2048]{0:T(1024)S(1)}, f32[2048]{0:T(1024)}, u32[]{:S(2)}) copy-start(f32[2048]{0:T(1024)} %param.11) | copy-start | bytes 24580
  3.0 0.7 copy-start.10
  3.8 25.5 %collective-permute-start.3 = (bf16[256,384]{1,0:T(8,128)(2,1)S(1)}, bf16[256,384]{1,0:T(8,128)(2,1)S(1)}, u32[]{:S(2)}, u32[]{:S(2)}) collective-permute-start(bf16[256,384]{1,0:T(8,128)(2,1)S(1)} %get-tuple-element.67), channel_id=1, source_target_pairs={{0,4},{4,0},{8,12},{12,8},{1,5},{5,1},{9,13},{13,9},{2,6},{6,2},{1... | collective-permute-start | bytes 589832 | tf_op jit(solution)/shard_map/gather_tokens_and_weights/ppermute | solution.py:149
  6.8 22.4 %collective-permute-start.4 = (bf16[256,384]{1,0:T(8,128)(2,1)S(1)}, bf16[256,384]{1,0:T(8,128)(2,1)S(1)}, u32[]{:S(2)}, u32[]{:S(2)}) collective-permute-start(bf16[256,384]{1,0:T(8,128)(2,1)S(1)} %get-tuple-element.68), channel_id=1, source_target_pairs={{0,8},{4,12},{8,0},{12,4},{1,9},{5,13},{9,1},{13,5},{2,10},{6,14},... | collective-permute-start | bytes 589832 | tf_op jit(solution)/shard_map/gather_tokens_and_weights/ppermute | solution.py:149
  9.4 11.7 %collective-permute-start = (bf16[144,512]{1,0:T(8,128)(2,1)S(1)}, bf16[144,512]{1,0:T(8,128)(2,1)S(1)}, u32[]{:S(2)}, u32[]{:S(2)}) collective-permute-start(bf16[144,512]{1,0:T(8,128)(2,1)S(1)} %get-tuple-element.66.refs_0_), channel_id=1, source_target_pairs={{0,4},{4,0},{8,12},{12,8},{1,5},{5,1},{9,13},{13,9},{2,6},{6,2},{1... | collective-permute-start | bytes 442376 | tf_op jit(solution)/shard_map/gather_tokens_and_weights/ppermute | solution.py:149
  9.8 19.4 %collective-permute-start.1 = (bf16[144,512]{1,0:T(8,128)(2,1)S(1)}, bf16[144,512]{1,0:T(8,128)(2,1)S(1)}, u32[]{:S(2)}, u32[]{:S(2)}) collective-permute-start(bf16[144,512]{1,0:T(8,128)(2,1)S(1)} %get-tuple-element.66.refs_0_), channel_id=1, source_target_pairs={{0,8},{4,12},{8,0},{12,4},{1,9},{5,13},{9,1},{13,5},{2,10},{6,14},... | collective-permute-start | bytes 442376 | tf_op jit(solution)/shard_map/gather_tokens_and_weights/ppermute | solution.py:149
  9.8 19.4 %collective-permute-start.2 = (bf16[144,512]{1,0:T(8,128)(2,1)S(1)}, bf16[144,512]{1,0:T(8,128)(2,1)S(1)}, u32[]{:S(2)}, u32[]{:S(2)}) collective-permute-start(bf16[144,512]{1,0:T(8,128)(2,1)S(1)} %get-tuple-element.66.refs_0_), channel_id=1, source_target_pairs={{0,12},{4,8},{8,4},{12,0},{1,13},{5,9},{9,5},{13,1},{2,14},{6,10},... | collective-permute-start | bytes 442376 | tf_op jit(solution)/shard_map/gather_tokens_and_weights/ppermute | solution.py:149
  13.8 0.7 copy-start.11
  29.2 0.7 copy-start.2
  29.2 0.7 copy-start.4
  29.2 10.7 %copy-start.15 = (bf16[256,384]{1,0:T(8,128)(2,1)}, bf16[256,384]{1,0:T(8,128)(2,1)S(1)}, u32[]{:S(2)}) copy-start(bf16[256,384]{1,0:T(8,128)(2,1)S(1)} %collective-permute-done.3.rest_4_) | copy-start | bytes 589828
  29.2 11.1 %copy-start.16 = (bf16[256,384]{1,0:T(8,128)(2,1)}, bf16[256,384]{1,0:T(8,128)(2,1)S(1)}, u32[]{:S(2)}) copy-start(bf16[256,384]{1,0:T(8,128)(2,1)S(1)} %collective-permute-done.4.rest_5_) | copy-start | bytes 589828
  30.7 11.8 %collective-permute-start.6 = (bf16[3,128,512]{2,1,0:T(8,128)(2,1)}, bf16[3,128,512]{2,1,0:T(8,128)(2,1)}, u32[]{:S(2)}, u32[]{:S(2)}) collective-permute-start(bf16[3,128,512]{2,1,0:T(8,128)(2,1)} %pad_maximum_fusion.rest_0_), channel_id=1, source_target_pairs={{0,2},{1,3},{2,0},{3,1},{4,6},{5,7},{6,4},{7,5},{8,10},{9,11},{10,... | collective-permute-start | bytes 1179656 | tf_op jit(solution)/shard_map/gather_tokens_and_weights/ppermute | solution.py:149
  32.2 7.7 %collective-permute-start.7 = (bf16[256,384]{1,0:T(8,128)(2,1)S(1)}, bf16[256,384]{1,0:T(8,128)(2,1)}, u32[]{:S(2)}, u32[]{:S(2)}) collective-permute-start(bf16[256,384]{1,0:T(8,128)(2,1)S(1)} %get-tuple-element.73), channel_id=1, source_target_pairs={{0,12},{4,8},{8,4},{12,0},{1,13},{5,9},{9,5},{13,1},{2,14},{6,10},... | collective-permute-start | bytes 589832 | tf_op jit(solution)/shard_map/gather_tokens_and_weights/ppermute | solution.py:149
  34.7 5.7 %collective-permute-start.8 = (bf16[256,384]{1,0:T(8,128)(2,1)S(1)}, bf16[256,384]{1,0:T(8,128)(2,1)S(1)}, u32[]{:S(2)}, u32[]{:S(2)}) collective-permute-start(bf16[256,384]{1,0:T(8,128)(2,1)S(1)} %collective-permute-done.3.rest_4_), channel_id=1, source_target_pairs={{0,16},{16,0},{1,17},{17,1},{2,18},{18,2},{3,19},{19,3},{4,20},{20... | collective-permute-start | bytes 589832 | tf_op jit(solution)/shard_map/gather_tokens_and_weights/ppermute | solution.py:149
  36.2 6.3 %collective-permute-start.9 = (bf16[256,384]{1,0:T(8,128)(2,1)S(1)}, bf16[256,384]{1,0:T(8,128)(2,1)S(1)}, u32[]{:S(2)}, u32[]{:S(2)}) collective-permute-start(bf16[256,384]{1,0:T(8,128)(2,1)S(1)} %collective-permute-done.4.rest_5_), channel_id=1, source_target_pairs={{0,16},{16,0},{1,17},{17,1},{2,18},{18,2},{3,19},{19,3},{4,20},{20... | collective-permute-start | bytes 589832 | tf_op jit(solution)/shard_map/gather_tokens_and_weights/ppermute | solution.py:149
  40.4 2.1 %copy-start.17 = (bf16[256,384]{1,0:T(8,128)(2,1)}, bf16[256,384]{1,0:T(8,128)(2,1)S(1)}, u32[]{:S(2)}) copy-start(bf16[256,384]{1,0:T(8,128)(2,1)S(1)} %collective-permute-done.8.rest_7_) | copy-start | bytes 589828
  42.5 0.7 copy-start.18
  43.2 13.9 %collective-permute-start.13 = (bf16[512,512]{1,0:T(8,128)(2,1)}, bf16[512,512]{1,0:T(8,128)(2,1)}, u32[]{:S(2)}, u32[]{:S(2)}) collective-permute-start(bf16[512,512]{1,0:T(8,128)(2,1)} %get-tuple-element.86.refs_0_), channel_id=1, source_target_pairs={{0,2},{1,3},{2,0},{3,1},{4,6},{5,7},{6,4},{7,5},{8,10},{9,11},{10,... | collective-permute-start | bytes 1572872 | tf_op jit(solution)/shard_map/gather_tokens_and_weights/ppermute | solution.py:149
  43.7 6.1 %collective-permute-start.5 = (bf16[3,128,512]{2,1,0:T(8,128)(2,1)}, bf16[3,128,512]{2,1,0:T(8,128)(2,1)}, u32[]{:S(2)}, u32[]{:S(2)}) collective-permute-start(bf16[3,128,512]{2,1,0:T(8,128)(2,1)} %pad_maximum_fusion.rest_0_), channel_id=1, source_target_pairs={{0,1},{1,0},{2,3},{3,2},{4,5},{5,4},{6,7},{7,6},{8,9},{9,8},{10,11... | collective-permute-start | bytes 1179656 | tf_op jit(solution)/shard_map/gather_tokens_and_weights/ppermute | solution.py:149
  43.7 7.6 %collective-permute-start.10 = (bf16[3,128,512]{2,1,0:T(8,128)(2,1)}, bf16[3,128,512]{2,1,0:T(8,128)(2,1)}, u32[]{:S(2)}, u32[]{:S(2)}) collective-permute-start(bf16[3,128,512]{2,1,0:T(8,128)(2,1)} %collective-permute-done.6.rest_2_), channel_id=1, source_target_pairs={{0,1},{1,0},{2,3},{3,2},{4,5},{5,4},{6,7},{7,6},{8,9},{9,8},{10,11... | collective-permute-start | bytes 1179656 | tf_op jit(solution)/shard_map/gather_tokens_and_weights/ppermute | solution.py:149
  44.2 7.1 %collective-permute-start.11 = (bf16[256,384]{1,0:T(8,128)(2,1)}, bf16[256,384]{1,0:T(8,128)(2,1)}, u32[]{:S(2)}, u32[]{:S(2)}) collective-permute-start(bf16[256,384]{1,0:T(8,128)(2,1)} %collective-permute-done.7.rest_6_), channel_id=1, source_target_pairs={{0,16},{16,0},{1,17},{17,1},{2,18},{18,2},{3,19},{19,3},{4,20},{20... | collective-permute-start | bytes 589832 | tf_op jit(solution)/shard_map/gather_tokens_and_weights/ppermute | solution.py:149
  45.7 0.9 copy-start.3
  46.6 0.9 copy-start.5
  47.6 0.9 copy-start.12
  49.8 22.3 %copy-start = (f32[1280,128]{1,0:T(8,128)}, f32[1280,128]{1,0:T(8,128)S(1)}, u32[]{:S(2)}) copy-start(f32[1280,128]{1,0:T(8,128)S(1)} %get-tuple-element.103.weight) | copy-start | bytes 1966084
  57.0 17.0 %collective-permute-start.12 = (bf16[512,512]{1,0:T(8,128)(2,1)}, bf16[512,512]{1,0:T(8,128)(2,1)}, u32[]{:S(2)}, u32[]{:S(2)}) collective-permute-start(bf16[512,512]{1,0:T(8,128)(2,1)} %get-tuple-element.86.refs_0_), channel_id=1, source_target_pairs={{0,1},{1,0},{2,3},{3,2},{4,5},{5,4},{6,7},{7,6},{8,9},{9,8},{10,11... | collective-permute-start | bytes 1572872 | tf_op jit(solution)/shard_map/heads_to_tokens/ppermute | solution.py:149
  57.0 17.0 %collective-permute-start.14 = (bf16[512,512]{1,0:T(8,128)(2,1)}, bf16[512,512]{1,0:T(8,128)(2,1)}, u32[]{:S(2)}, u32[]{:S(2)}) collective-permute-start(bf16[512,512]{1,0:T(8,128)(2,1)} %collective-permute-done.13.refs_2_), channel_id=1, source_target_pairs={{0,1},{1,0},{2,3},{3,2},{4,5},{5,4},{6,7},{7,6},{8,9},{9,8},{10,11... | collective-permute-start | bytes 1572872 | tf_op jit(solution)/shard_map/heads_to_tokens/ppermute | solution.py:149
  57.6 3.5 %collective-permute-start.17 = (bf16[128,128]{1,0:T(8,128)(2,1)S(1)}, bf16[128,128]{1,0:T(8,128)(2,1)S(1)}, u32[]{:S(2)}, u32[]{:S(2)}) collective-permute-start(bf16[128,128]{1,0:T(8,128)(2,1)S(1)} %get-tuple-element.126), channel_id=1, source_target_pairs={{0,3},{1,2},{2,1},{3,0},{4,7},{5,6},{6,5},{7,4},{8,11},{9,10},{10,... | collective-permute-start | bytes 98312 | tf_op jit(solution)/shard_map/heads_to_tokens/ppermute | solution.py:149
  58.8 3.9 %collective-permute-start.16 = (bf16[128,128]{1,0:T(8,128)(2,1)S(1)}, bf16[128,128]{1,0:T(8,128)(2,1)S(1)}, u32[]{:S(2)}, u32[]{:S(2)}) collective-permute-start(bf16[128,128]{1,0:T(8,128)(2,1)S(1)} %get-tuple-element.127), channel_id=1, source_target_pairs={{0,2},{1,3},{2,0},{3,1},{4,6},{5,7},{6,4},{7,5},{8,10},{9,11},{10,... | collective-permute-start | bytes 98312 | tf_op jit(solution)/shard_map/heads_to_tokens/ppermute | solution.py:149
  59.3 3.4 %collective-permute-start.15 = (bf16[128,128]{1,0:T(8,128)(2,1)S(1)}, bf16[128,128]{1,0:T(8,128)(2,1)S(1)}, u32[]{:S(2)}, u32[]{:S(2)}) collective-permute-start(bf16[128,128]{1,0:T(8,128)(2,1)S(1)} %get-tuple-element.128), channel_id=1, source_target_pairs={{0,1},{1,0},{2,3},{3,2},{4,5},{5,4},{6,7},{7,6},{8,9},{9,8},{10,11... | collective-permute-start | bytes 98312 | tf_op jit(solution)/shard_map/heads_to_tokens/ppermute | solution.py:149
  62.7 9.3 %collective-permute-start.19 = (bf16[4,128,128]{2,1,0:T(8,128)(2,1)S(1)}, bf16[4,128,128]{2,1,0:T(8,128)(2,1)S(1)}, u32[]{:S(2)}, u32[]{:S(2)}) collective-permute-start(bf16[4,128,128]{2,1,0:T(8,128)(2,1)S(1)} %pad_maximum_fusion.1.rest_4_), channel_id=1, source_target_pairs={{0,8},{4,12},{8,0},{12,4},{1,9},{5,13},{9,1},{13,5},{2,10},{6,14},... | collective-permute-start | bytes 393224 | tf_op jit(solution)/shard_map/heads_to_tokens/ppermute | solution.py:149
  65.4 10.2 %collective-permute-start.18 = (bf16[4,128,128]{2,1,0:T(8,128)(2,1)S(1)}, bf16[4,128,128]{2,1,0:T(8,128)(2,1)S(1)}, u32[]{:S(2)}, u32[]{:S(2)}) collective-permute-start(bf16[4,128,128]{2,1,0:T(8,128)(2,1)S(1)} %pad_maximum_fusion.1.rest_4_), channel_id=1, source_target_pairs={{0,4},{4,0},{8,12},{12,8},{1,5},{5,1},{9,13},{13,9},{2,6},{6,2},{1... | collective-permute-start | bytes 393224 | tf_op jit(solution)/shard_map/heads_to_tokens/ppermute | solution.py:149
  72.1 5.0 %collective-permute-start.20 = (bf16[4,128,128]{2,1,0:T(8,128)(2,1)S(1)}, bf16[4,128,128]{2,1,0:T(8,128)(2,1)S(1)}, u32[]{:S(2)}, u32[]{:S(2)}) collective-permute-start(bf16[4,128,128]{2,1,0:T(8,128)(2,1)S(1)} %collective-permute-done.19.rest_6_), channel_id=1, source_target_pairs={{0,4},{4,0},{8,12},{12,8},{1,5},{5,1},{9,13},{13,9},{2,6},{6,2},{1... | collective-permute-start | bytes 393224 | tf_op jit(solution)/shard_map/heads_to_tokens/ppermute | solution.py:149
  78.5 17.1 %copy-start.13 = (f32[2048]{0:T(1024)S(1)}, f32[2048]{0:T(1024)}, u32[]{:S(2)}) copy-start(f32[2048]{0:T(1024)} %param.12) | copy-start | bytes 24580
  78.5 5.4 %collective-permute-start.23 = (bf16[128,512]{1,0:T(8,128)(2,1)S(1)}, bf16[128,512]{1,0:T(8,128)(2,1)S(1)}, u32[]{:S(2)}, u32[]{:S(2)}) collective-permute-start(bf16[128,512]{1,0:T(8,128)(2,1)S(1)} %output_projection.1.refs_0_), channel_id=1, source_target_pairs={{0,4},{4,0},{8,12},{12,8},{1,5},{5,1},{9,13},{13,9},{2,6},{6,2},{1... | collective-permute-start | bytes 393224 | tf_op jit(solution)/shard_map/gather_residual/ppermute | solution.py:149
  80.4 7.4 %collective-permute-start.21 = (bf16[128,512]{1,0:T(8,128)(2,1)S(1)}, bf16[128,512]{1,0:T(8,128)(2,1)S(1)}, u32[]{:S(2)}, u32[]{:S(2)}) collective-permute-start(bf16[128,512]{1,0:T(8,128)(2,1)S(1)} %output_projection.1.refs_0_), channel_id=1, source_target_pairs={{0,8},{4,12},{8,0},{12,4},{1,9},{5,13},{9,1},{13,5},{2,10},{6,14},... | collective-permute-start | bytes 393224 | tf_op jit(solution)/shard_map/gather_residual/ppermute | solution.py:149
  81.5 6.4 %collective-permute-start.28 = (bf16[128,512]{1,0:T(8,128)(2,1)S(1)}, bf16[128,512]{1,0:T(8,128)(2,1)S(1)}, u32[]{:S(2)}, u32[]{:S(2)}) collective-permute-start(bf16[128,512]{1,0:T(8,128)(2,1)S(1)} %output_projection.1.refs_0_), channel_id=1, source_target_pairs={{0,2},{1,3},{2,0},{3,1},{4,6},{5,7},{6,4},{7,5},{8,10},{9,11},{10,... | collective-permute-start | bytes 393224 | tf_op jit(solution)/shard_map/gather_residual/ppermute | solution.py:149
  83.9 5.0 %collective-permute-start.30 = (bf16[128,512]{1,0:T(8,128)(2,1)S(1)}, bf16[128,512]{1,0:T(8,128)(2,1)S(1)}, u32[]{:S(2)}, u32[]{:S(2)}) collective-permute-start(bf16[128,512]{1,0:T(8,128)(2,1)S(1)} %collective-permute-done.23.refs_4_), channel_id=1, source_target_pairs={{0,2},{1,3},{2,0},{3,1},{4,6},{5,7},{6,4},{7,5},{8,10},{9,11},{10,... | collective-permute-start | bytes 393224 | tf_op jit(solution)/shard_map/gather_residual/ppermute | solution.py:149
  87.8 5.2 %collective-permute-start.22 = (bf16[128,512]{1,0:T(8,128)(2,1)S(1)}, bf16[128,512]{1,0:T(8,128)(2,1)S(1)}, u32[]{:S(2)}, u32[]{:S(2)}) collective-permute-start(bf16[128,512]{1,0:T(8,128)(2,1)S(1)} %collective-permute-done.21.refs_0_), channel_id=1, source_target_pairs={{0,4},{4,0},{8,12},{12,8},{1,5},{5,1},{9,13},{13,9},{2,6},{6,2},{1... | collective-permute-start | bytes 393224 | tf_op jit(solution)/shard_map/gather_residual/ppermute | solution.py:149
  87.9 5.6 %collective-permute-start.27 = (bf16[128,512]{1,0:T(8,128)(2,1)S(1)}, bf16[128,512]{1,0:T(8,128)(2,1)S(1)}, u32[]{:S(2)}, u32[]{:S(2)}) collective-permute-start(bf16[128,512]{1,0:T(8,128)(2,1)S(1)} %output_projection.1.refs_0_), channel_id=1, source_target_pairs={{0,1},{1,0},{2,3},{3,2},{4,5},{5,4},{6,7},{7,6},{8,9},{9,8},{10,11... | collective-permute-start | bytes 393224 | tf_op jit(solution)/shard_map/gather_residual/ppermute | solution.py:149
  87.9 7.0 %collective-permute-start.29 = (bf16[128,512]{1,0:T(8,128)(2,1)S(1)}, bf16[128,512]{1,0:T(8,128)(2,1)S(1)}, u32[]{:S(2)}, u32[]{:S(2)}) collective-permute-start(bf16[128,512]{1,0:T(8,128)(2,1)S(1)} %collective-permute-done.28.refs_2_), channel_id=1, source_target_pairs={{0,1},{1,0},{2,3},{3,2},{4,5},{5,4},{6,7},{7,6},{8,9},{9,8},{10,11... | collective-permute-start | bytes 393224 | tf_op jit(solution)/shard_map/gather_residual/ppermute | solution.py:149
  88.4 6.5 %collective-permute-start.24 = (bf16[128,512]{1,0:T(8,128)(2,1)S(1)}, bf16[128,512]{1,0:T(8,128)(2,1)S(1)}, u32[]{:S(2)}, u32[]{:S(2)}) collective-permute-start(bf16[128,512]{1,0:T(8,128)(2,1)S(1)} %collective-permute-done.23.refs_4_), channel_id=1, source_target_pairs={{0,1},{1,0},{2,3},{3,2},{4,5},{5,4},{6,7},{7,6},{8,9},{9,8},{10,11... | collective-permute-start | bytes 393224 | tf_op jit(solution)/shard_map/gather_residual/ppermute | solution.py:149
  88.9 6.7 %collective-permute-start.31 = (bf16[128,512]{1,0:T(8,128)(2,1)S(1)}, bf16[128,512]{1,0:T(8,128)(2,1)S(1)}, u32[]{:S(2)}, u32[]{:S(2)}) collective-permute-start(bf16[128,512]{1,0:T(8,128)(2,1)S(1)} %collective-permute-done.30.refs_6_), channel_id=1, source_target_pairs={{0,1},{1,0},{2,3},{3,2},{4,5},{5,4},{6,7},{7,6},{8,9},{9,8},{10,11... | collective-permute-start | bytes 393224 | tf_op jit(solution)/shard_map/gather_residual/ppermute | solution.py:149
  92.9 8.9 %collective-permute-start.33 = (bf16[128,512]{1,0:T(8,128)(2,1)S(1)}, bf16[128,512]{1,0:T(8,128)(2,1)S(1)}, u32[]{:S(2)}, u32[]{:S(2)}) collective-permute-start(bf16[128,512]{1,0:T(8,128)(2,1)S(1)} %collective-permute-done.21.refs_0_), channel_id=1, source_target_pairs={{0,1},{1,0},{2,3},{3,2},{4,5},{5,4},{6,7},{7,6},{8,9},{9,8},{10,11... | collective-permute-start | bytes 393224 | tf_op jit(solution)/shard_map/gather_residual/ppermute | solution.py:149
  93.5 7.3 %collective-permute-start.25 = (bf16[128,512]{1,0:T(8,128)(2,1)S(1)}, bf16[128,512]{1,0:T(8,128)(2,1)S(1)}, u32[]{:S(2)}, u32[]{:S(2)}) collective-permute-start(bf16[128,512]{1,0:T(8,128)(2,1)S(1)} %collective-permute-done.21.refs_0_), channel_id=1, source_target_pairs={{0,2},{1,3},{2,0},{3,1},{4,6},{5,7},{6,4},{7,5},{8,10},{9,11},{10,... | collective-permute-start | bytes 393224 | tf_op jit(solution)/shard_map/gather_residual/ppermute | solution.py:149
  94.9 7.0 %collective-permute-start.35 = (bf16[128,512]{1,0:T(8,128)(2,1)S(1)}, bf16[128,512]{1,0:T(8,128)(2,1)S(1)}, u32[]{:S(2)}, u32[]{:S(2)}) collective-permute-start(bf16[128,512]{1,0:T(8,128)(2,1)S(1)} %collective-permute-done.22.refs_4_), channel_id=1, source_target_pairs={{0,1},{1,0},{2,3},{3,2},{4,5},{5,4},{6,7},{7,6},{8,9},{9,8},{10,11... | collective-permute-start | bytes 393224 | tf_op jit(solution)/shard_map/gather_residual/ppermute | solution.py:149
  94.9 6.9 %collective-permute-start.26 = (bf16[128,512]{1,0:T(8,128)(2,1)S(1)}, bf16[128,512]{1,0:T(8,128)(2,1)S(1)}, u32[]{:S(2)}, u32[]{:S(2)}) collective-permute-start(bf16[128,512]{1,0:T(8,128)(2,1)S(1)} %collective-permute-done.22.refs_4_), channel_id=1, source_target_pairs={{0,2},{1,3},{2,0},{3,1},{4,6},{5,7},{6,4},{7,5},{8,10},{9,11},{10,... | collective-permute-start | bytes 393224 | tf_op jit(solution)/shard_map/gather_residual/ppermute | solution.py:149
  95.6 7.5 %copy-start.1 = (f32[1280,128]{1,0:T(8,128)S(1)}, f32[1280,128]{1,0:T(8,128)}, u32[]{:S(2)}) copy-start(f32[1280,128]{1,0:T(8,128)} %copy-done) | copy-start | bytes 1966084
  100.8 9.0 %copy-start.6 = (bf16[128,512]{1,0:T(8,128)(2,1)}, bf16[128,512]{1,0:T(8,128)(2,1)S(1)}, u32[]{:S(2)}) copy-start(bf16[128,512]{1,0:T(8,128)(2,1)S(1)} %collective-permute-done.25.refs_2_) | copy-start | bytes 393220
  100.8 1.4 collective-permute-start.34
  101.8 1.3 collective-permute-start.32
  103.2 6.6 %copy-start.8 = (bf16[128,512]{1,0:T(8,128)(2,1)}, bf16[128,512]{1,0:T(8,128)(2,1)S(1)}, u32[]{:S(2)}) copy-start(bf16[128,512]{1,0:T(8,128)(2,1)S(1)} %collective-permute-done.32.refs_7_) | copy-start | bytes 393220
  114.1 4.4 %collective-permute-start.36 = (bf16[512,512]{1,0:T(8,128)(2,1)S(1)}, bf16[512,512]{1,0:T(8,128)(2,1)S(1)}, u32[]{:S(2)}, u32[]{:S(2)}) collective-permute-start(bf16[512,512]{1,0:T(8,128)(2,1)S(1)} %get-tuple-element.109), channel_id=1, source_target_pairs={{0,1},{1,0},{2,3},{3,2},{4,5},{5,4},{6,7},{7,6},{8,9},{9,8},{10,11... | collective-permute-start | bytes 1572872 | tf_op jit(solution)/shard_map/sum_over_devices/ppermute | solution.py:149
  114.3 11.6 %collective-permute-start.37 = (bf16[512,512]{1,0:T(8,128)(2,1)}, bf16[512,512]{1,0:T(8,128)(2,1)S(1)}, u32[]{:S(2)}, u32[]{:S(2)}) collective-permute-start(bf16[512,512]{1,0:T(8,128)(2,1)} %get-tuple-element.114), channel_id=1, source_target_pairs={{0,1},{1,0},{2,3},{3,2},{4,5},{5,4},{6,7},{7,6},{8,9},{9,8},{10,11... | collective-permute-start | bytes 1572872 | tf_op jit(solution)/shard_map/sum_over_devices/ppermute | solution.py:149
  119.9 9.4 %collective-permute-start.39 = (bf16[256,512]{1,0:T(8,128)(2,1)}, bf16[256,512]{1,0:T(8,128)(2,1)S(1)}, u32[]{:S(2)}, u32[]{:S(2)}) collective-permute-start(bf16[256,512]{1,0:T(8,128)(2,1)} %get-tuple-element.111), channel_id=1, source_target_pairs={{0,2},{1,3},{2,0},{3,1},{4,6},{5,7},{6,4},{7,5},{8,10},{9,11},{10,... | collective-permute-start | bytes 786440 | tf_op jit(solution)/shard_map/sum_over_devices/ppermute | solution.py:149
  121.2 12.9 %collective-permute-start.38 = (bf16[256,512]{1,0:T(8,128)(2,1)S(1)}, bf16[256,512]{1,0:T(8,128)(2,1)S(1)}, u32[]{:S(2)}, u32[]{:S(2)}) collective-permute-start(bf16[256,512]{1,0:T(8,128)(2,1)S(1)} %get-tuple-element.112), channel_id=1, source_target_pairs={{0,2},{1,3},{2,0},{3,1},{4,6},{5,7},{6,4},{7,5},{8,10},{9,11},{10,... | collective-permute-start | bytes 786440 | tf_op jit(solution)/shard_map/sum_over_devices/ppermute | solution.py:149
  129.9 7.5 %collective-permute-start.41 = (bf16[128,512]{1,0:T(8,128)(2,1)S(1)}, bf16[128,512]{1,0:T(8,128)(2,1)S(1)}, u32[]{:S(2)}, u32[]{:S(2)}) collective-permute-start(bf16[128,512]{1,0:T(8,128)(2,1)S(1)} %get-tuple-element.121), channel_id=1, source_target_pairs={{0,12},{4,8},{8,4},{12,0},{1,13},{5,9},{9,5},{13,1},{2,14},{6,10},... | collective-permute-start | bytes 393224 | tf_op jit(solution)/shard_map/sum_over_devices/ppermute | solution.py:149
  133.1 10.6 %copy-start.7 = (bf16[128,512]{1,0:T(8,128)(2,1)S(1)}, bf16[128,512]{1,0:T(8,128)(2,1)}, u32[]{:S(2)}) copy-start(bf16[128,512]{1,0:T(8,128)(2,1)} %copy-done.6) | copy-start | bytes 393220
  133.1 10.6 %copy-start.9 = (bf16[128,512]{1,0:T(8,128)(2,1)S(1)}, bf16[128,512]{1,0:T(8,128)(2,1)}, u32[]{:S(2)}) copy-start(bf16[128,512]{1,0:T(8,128)(2,1)} %copy-done.8) | copy-start | bytes 393220
  133.1 10.6 %collective-permute-start.40 = (bf16[128,512]{1,0:T(8,128)(2,1)S(1)}, bf16[128,512]{1,0:T(8,128)(2,1)S(1)}, u32[]{:S(2)}, u32[]{:S(2)}) collective-permute-start(bf16[128,512]{1,0:T(8,128)(2,1)S(1)} %get-tuple-element.120), channel_id=1, source_target_pairs={{0,8},{4,12},{8,0},{12,4},{1,9},{5,13},{9,1},{13,5},{2,10},{6,14},... | collective-permute-start | bytes 393224 | tf_op jit(solution)/shard_map/sum_over_devices/ppermute | solution.py:149
  134.7 9.1 %collective-permute-start.42 = (bf16[128,512]{1,0:T(8,128)(2,1)S(1)}, bf16[128,512]{1,0:T(8,128)(2,1)S(1)}, u32[]{:S(2)}, u32[]{:S(2)}) collective-permute-start(bf16[128,512]{1,0:T(8,128)(2,1)S(1)} %get-tuple-element.122), channel_id=1, source_target_pairs={{0,4},{4,0},{8,12},{12,8},{1,5},{5,1},{9,13},{13,9},{2,6},{6,2},{1... | collective-permute-start | bytes 393224 | tf_op jit(solution)/shard_map/sum_over_devices/ppermute | solution.py:149

commit v6 on v5

--- a/solution.py
+++ b/solution.py
@@ -172,7 +172,7 @@
     return lax.optimization_barrier(arrays)
 
 
-def cut_kernel(pos, routes, gates, tokens, weight, x_send, w_own, o_own, *rest):
+def cut_kernel(pos, routes, gates, tokens, weight, x_send, *rest):
     w_sends, (r_here, g_here, sems) = rest[:-3], rest[-3:]
     g, s, h = pos[0], pos[1], pos[2]
     rows, cols, half = tokens.shape[0], x_send.shape[1], w_sends[0].shape[0]
@@ -181,7 +181,6 @@
             tokens.at[:, pl.ds(pl.multiple_of(h * cols, cols), cols)],
             x_send.at[pl.ds(0, rows)],
         ),
-        (weight.at[3], o_own),
         (routes, r_here),
         (gates, g_here),
     ]
@@ -193,12 +192,10 @@
             copies.append(
                 (weight.at[which, own_half, pl.ds(column, HEAD_DIM)], out.at[:, span])
             )
-        column = pl.multiple_of(s * HEAD_DIM, HEAD_DIM)
-        copies.append((weight.at[which, :, pl.ds(column, HEAD_DIM)], w_own.at[:, span]))
     copies = [pltpu.make_async_copy(a, b, sems.at[i]) for i, (a, b) in enumerate(copies)]
     for copy in copies:
         copy.start()
-    for copy in copies[2:4]:
+    for copy in copies[1:3]:
         copy.wait()
     parts, left = [r_here[...].astype(F32)], g_here[...]
     for _ in range(3):
@@ -210,19 +207,19 @@
     if blank.shape[1]:
         lines = jnp.concatenate([lines, blank], axis=1)
     x_send[rows:, :] = lines.astype(BF16)
-    for copy in copies[:2] + copies[4:]:
+    for copy in copies[:1] + copies[3:]:
         copy.wait()
 
 
-def attend_kernel(n, pos, gain, tokens, w_own, *rest):
+def attend_kernel(n, pos, gain, tokens, weight, *rest):
     x_pieces, rest = rest[:n], rest[n:]
     w_near, rest = rest[: n - 1], rest[n - 1 :]
     w_far, rest = rest[: n - 1], rest[n - 1 :]
-    attended, x_share, x_all, w_all, sems = rest
+    attended, (x_share, x_all, w_all, projected, sems) = rest[:n], rest[n:]
     g, s, h = pos[0], pos[1], pos[2]
     rows, width = tokens.shape
     cols = width // n
-    depth, half = w_own.shape[0], w_near[0].shape[0]
+    depth, half = weight.shape[1], w_near[0].shape[0]
     total = n * rows
 
     def at_rows(block, size):
@@ -235,7 +232,9 @@
                 (x_pieces[e].at[d - 1], x_all.at[at_rows(s ^ d, rows), at_rows(h ^ e, cols)])
             )
     n_rows = len(copies)
-    copies.append((w_own, w_all.at[at_rows(s, depth)]))
+    for which in range(3):
+        source = weight.at[which, :, at_rows(s, HEAD_DIM)]
+        copies.append((source, w_all.at[at_rows(s, depth), pl.ds(which * HEAD_DIM, HEAD_DIM)]))
     for d in range(1, n):
         copies.append((w_near[d - 1], w_all.at[at_rows((s ^ d) * 2 + g, half)]))
         copies.append((w_far[d - 1], w_all.at[at_rows((s ^ d) * 2 + (1 - g), half)]))
@@ -256,31 +255,28 @@
     lax.fori_loop(0, n, normalise, 0)
     for copy in copies[n_rows:]:
         copy.wait()
-    projected = [
-        jnp.dot(
-            x_all[block * rows : (block + 1) * rows, :], w_all[...], preferred_element_type=F32
-        ).astype(BF16)
-        for block in range(n)
-    ]
-    whole = jnp.concatenate(projected, axis=0)
-    query, key, value = (whole[:, i * HEAD_DIM : (i + 1) * HEAD_DIM] for i in range(3))
-    for block in range(n):
-        upto = (block + 1) * rows
+    projected[...] = jnp.dot(x_all[...], w_all[...], preferred_element_type=F32).astype(BF16)
+    key, value = projected[:, HEAD_DIM : 2 * HEAD_DIM], projected[:, 2 * HEAD_DIM :]
+    for e in range(n):
+        block = h ^ e
         scores = lax.dot_general(
-            query[block * rows : upto],
-            key[:upto],
+            projected[at_rows(block, rows), :HEAD_DIM],
+            key,
             (((1,), (1,)), ((), ())),
             preferred_element_type=F32,
         )
-        ahead = lax.broadcasted_iota(jnp.int32, scores.shape, 0) + block * rows
-        scores = jnp.where(ahead >= lax.broadcasted_iota(jnp.int32, scores.shape, 1), scores, 0.0)
+        position = lax.broadcasted_iota(jnp.int32, scores.shape, 0) + block * rows
+        scores = jnp.where(
+            position >= lax.broadcasted_iota(jnp.int32, scores.shape, 1), scores, 0.0
+        )
         high = scores.astype(BF16)
         low = (scores - high.astype(F32)).astype(BF16)
-        out = jnp.dot(high, value[:upto], preferred_element_type=F32) + jnp.dot(
-            low, value[:upto], preferred_element_type=F32
+        out = jnp.dot(high, value, preferred_element_type=F32) + jnp.dot(
+            low, value, preferred_element_type=F32
         )
         out = out * lax.rsqrt(jnp.mean(out * out, axis=-1, keepdims=True) + EPS)
-        attended[block] = out.astype(BF16)
+        attended[e][...] = out.astype(BF16)
+
 
 def bring_kernel(*refs):
     count = len(refs) // 2
@@ -374,6 +370,17 @@
     return copies
 
 
+def load_down_kernel(group, distances, pos, w_down, *refs):
+    outs, sems = refs[:-1], refs[-1]
+    copies = []
+    for i in range(outs[0].shape[0] // group):
+        copies += down_copies(pos, distances, i, group, w_down, outs, sems)
+    for copy in copies:
+        copy.start()
+    for copy in copies:
+        copy.wait()
+
+
 def load_kernel(group, distances, pos, w_gate, w_up, g_all, u_all, sems):
     copies = []
     for i in range(g_all.shape[0] // group):
@@ -564,25 +571,49 @@
 
     lines = 2 * TOPK
     with jax.named_scope("cut_pieces"):
-        x_send, w_own, o_own, *w_sends = pl.pallas_call(
+        x_send, *w_sends = pl.pallas_call(
             cut_kernel,
-            out_shape=[
-                sds((rows + lines, cols), BF16),
-                sds((depth, 3 * HEAD_DIM), BF16),
-                sds((depth, cols), BF16),
-            ]
+            out_shape=[sds((rows + lines, cols), BF16)]
             + [sds((half, 3 * HEAD_DIM), BF16)] * (n - 1),
             in_specs=[SMEM] + [ANY] * 4,
-            out_specs=[VMEM] * (n + 2),
+            out_specs=[VMEM] * n,
             scratch_shapes=[
                 pltpu.VMEM((TOPK, rows), jnp.int32),
                 pltpu.VMEM((TOPK, rows), F32),
-                dma((4 + 3 * n,)),
+                dma((3 + 3 * (n - 1),)),
             ],
             compiler_params=room(8),
         )(pos, *map(held, (routes.T, gates.T, tokens, attn_weight)))
     group = experts // 4
     w_gate, w_up, w_down = map(held, (expert_gate, expert_up, expert_down))
+
+    early, late = tuple(range(n // 2)), tuple(range(n // 2, n))
+    wide = n // 2 * cols
+    ahead = experts // 2
+    hidden_cost = cost(pairs * wide * (total + 2 * hidden), 4 * experts * wide * hidden)
+
+    def load(distances, amount, *earlier):
+        return pl.pallas_call(
+            functools.partial(load_kernel, group, distances),
+            out_shape=[pltpu.VMEM((amount, wide, hidden), BF16)] * 2,
+            in_specs=[SMEM] + [ANY] * 2,
+            out_specs=[VMEM] * 2,
+            scratch_shapes=[dma((amount // group, 2 * len(distances)))],
+            compiler_params=room(2),
+            cost_estimate=cost(0, 4 * amount * wide * hidden),
+        )(after(pos, *earlier), w_gate, w_up)
+
+    def load_down(distances, *earlier):
+        count = len(distances)
+        return pl.pallas_call(
+            functools.partial(load_down_kernel, group, distances),
+            out_shape=[pltpu.VMEM((experts, hidden, cols), BF16)] * count,
+            in_specs=[SMEM, ANY],
+            out_specs=[VMEM] * count,
+            scratch_shapes=[dma((experts // group, count))],
+            compiler_params=room(2),
+            cost_estimate=cost(0, 2 * count * experts * cols * hidden),
+        )(after(pos, *earlier), w_down)
 
     with jax.named_scope("gather_tokens_and_weights"):
         x_far = [swap(x_send, "seq", d) for d in range(1, n)]
@@ -593,9 +624,8 @@
         x_pieces[2] = swap(x_pieces[0], "head", 2)
         w_far = [swap(w, "grp", 1) for w in w_near]
         w_near.append(swap(w_last, "seq", n - 1))
-        x_pieces[2], w_near[-1], o_own, *w_far = in_step(x_pieces[2], w_near[-1], o_own, *w_far)
+        x_pieces[2], w_near[-1], *w_far = in_step(x_pieces[2], w_near[-1], *w_far)
         w_far.append(swap(w_near[-1], "grp", 1))
-        o_pieces = {0: o_own, 2: swap(o_own, "head", 2)}
         for e in (0, 2):
             x_pieces[e ^ 1] = swap(x_pieces[e], "head", 1)
     with jax.named_scope("routing"):
@@ -607,41 +637,31 @@
             scratch_shapes=[pltpu.VMEM((2 * TOPK, total), F32)],
             compiler_params=room(16),
         )(pos, x_send, *x_far)
-        w_near[-1] = after(w_near[-1], pick)
+        with jax.named_scope("expert_weights"):
+            late_weights = load(late, ahead, w_near[-1])
+        w_near[-1] = after(w_near[-1], pick, late_weights[0])
+        o_own = after(attn_weight, pick)[3]
+        o_pieces = {0: o_own, 2: swap(o_own, "head", 2)}
 
     with jax.named_scope("attention"):
-        attended, x_share = pl.pallas_call(
+        *attended, x_share = pl.pallas_call(
             functools.partial(attend_kernel, n),
-            out_shape=[sds((n, rows, HEAD_DIM), BF16), sds((rows, cols), BF16)],
+            out_shape=[sds((rows, HEAD_DIM), BF16)] * n + [sds((rows, cols), BF16)],
             in_specs=[SMEM, VMEM] + [ANY] * (2 + n + 2 * (n - 1) - 1) + [VMEM],
-            out_specs=[VMEM] * 2,
+            out_specs=[VMEM] * (n + 1),
             scratch_shapes=[
                 pltpu.VMEM((total, width), BF16),
                 pltpu.VMEM((width, 3 * HEAD_DIM), BF16),
-                dma((2 + n * (n - 1) + 2 * (n - 1),)),
+                pltpu.VMEM((total, 3 * HEAD_DIM), BF16),
+                dma((4 + n * (n - 1) + 2 * (n - 1),)),
             ],
             compiler_params=room(14),
         )(
-            pos, attn_gain.reshape(1, width), held(tokens), held(w_own),
+            pos, attn_gain.reshape(1, width), held(tokens), held(attn_weight),
             *[held(x_pieces[e]) for e in range(n)], *map(held, w_near), *map(held, w_far[:-1]), w_far[-1],
         )
 
-    early, late = tuple(range(n // 2)), tuple(range(n // 2, n))
-    wide = n // 2 * cols
     gain_row = moe_gain.reshape(1, width)
-    ahead = experts // 2
-    hidden_cost = cost(pairs * wide * (total + 2 * hidden), 4 * experts * wide * hidden)
-
-    def load(distances, amount, *earlier):
-        return pl.pallas_call(
-            functools.partial(load_kernel, group, distances),
-            out_shape=[pltpu.VMEM((amount, wide, hidden), BF16)] * 2,
-            in_specs=[SMEM] + [ANY] * 2,
-            out_specs=[VMEM] * 2,
-            scratch_shapes=[dma((amount // group, 2 * len(distances)))],
-            compiler_params=room(2),
-            cost_estimate=cost(0, 4 * amount * wide * hidden),
-        )(after(pos, *earlier), w_gate, w_up)
 
     def first_hidden(pieces, weights):
         return pl.pallas_call(
@@ -673,16 +693,16 @@
 
     with jax.named_scope("heads_to_tokens"):
         for e in (0, 2):
-            o_pieces[e ^ 1] = swap(after(o_pieces[e], attended), "head", 1)
-        by_block = [
-            lax.dynamic_index_in_dim(attended, h ^ e, 0, keepdims=False) for e in range(n)
-        ]
-        arrived = jnp.stack([by_block[0]] + [swap(by_block[e], "head", e) for e in range(1, n)])
+            o_pieces[e ^ 1] = swap(after(o_pieces[e], attended[0]), "head", 1)
+        arrived = jnp.stack([attended[0]] + [swap(attended[e], "head", e) for e in range(1, n)])
         a_pieces = [arrived, swap(arrived, "seq", 1), swap(arrived, "seq", 2)]
         with jax.named_scope("expert_weights"):
             early_weights = load(early, experts, arrived)
         a_pieces[2] = after(a_pieces[2], early_weights[0])
         a_pieces.append(swap(a_pieces[2], "seq", 1))
+        with jax.named_scope("expert_weights"):
+            (d_2,) = load_down((2,), a_pieces[2])
+        x_share = after(x_share, d_2)
 
     with jax.named_scope("bring_out_weights"):
         o_here = pl.pallas_call(
@@ -693,7 +713,7 @@
             scratch_shapes=[dma((n,))],
             compiler_params=room(2),
             cost_estimate=cost(0, 2 * n * depth * cols),
-        )(*[held(o_pieces[e]) for e in range(n)])
+        )(*[o_pieces[e] for e in range(n)])
     with jax.named_scope("output_projection"):
         residual = pl.pallas_call(
             functools.partial(project_kernel, n),
@@ -706,7 +726,6 @@
 
     with jax.named_scope("gather_residual"):
         r_pieces = {0: {0: residual}}
-        late_weights = load(late, ahead, residual)
         for d in (1, 2):
             r_pieces[d] = {0: swap(residual, "seq", d)}
         r_pieces[3] = {0: swap(r_pieces[2][0], "seq", 1)}
@@ -715,7 +734,7 @@
             r_pieces[d][1] = swap(r_pieces[d][0], "head", 1)
         for d in early:
             r_pieces[d][3] = swap(r_pieces[d][2], "head", 1)
-        r_pieces[0][0] = after(residual, late_weights[0], *[r_pieces[d][0] for d in late])
+        r_pieces[0][0] = after(residual, r_pieces[3][0], r_pieces[2][2])
         pieces = [r_pieces[d][e] for d in early for e in range(n)]
         with jax.named_scope("first_hidden_units"):
             state = first_hidden(pieces, early_weights)
@@ -760,7 +779,7 @@
         half_line = n // 2
         out_3, out_1 = down(units, d_3, d_1)
         core_2, core_0 = swap(out_3, "head", 1), swap(out_1, "head", 1)
-        out_2 = self_down(after(units, out_3), 2)
+        (out_2,) = down(after(units, out_3), d_2)
         with jax.named_scope("halves_over_cores"):
             near = pl.pallas_call(
                 halves_kernel,

time: 151 us -> 146 us (0.967)
  local copies, waits for them, and re-layouts: 6.31 us -> 2.7 us
    unnamed x39 -> x23, local copies, waits for them, and re-layouts: 6.27 us -> 1.59 us
    pallas_call x2 -> x1, Pallas kernels: 7.85 us -> 3.93 us  [self_down(): pl.pallas_call(functools.partial(self_down_kernel, slots, group, (distanc...]
    pallas_call x1 -> x2, Pallas kernels: 4.3 us -> 6.4 us  [down(): pl.pallas_call(functools.partial(down_kernel, slots), out_shape=[sds((tot...]
    pallas_call x2 -> x3, Pallas kernels: 8.53 us -> 10.1 us  [the longest x1 5.52 us: square_body(): pl.pallas_call(functools.partial(attend_kernel, n), out_shape=[sds((rows,...]
  transfers between devices with their start and end apart: 43 -> 43, of which waited for: 19 -> 18; matrix products, arithmetic and copies ran while one was open for 0% -> 1% of each run, Pallas kernels for 23% -> 24%
where the time goes in v6:
time: 146 us
  Pallas kernels  48.6 us (33%)
  waiting for transfers between devices  43.8 us (30%)
  starting transfers between devices  43.2 us (30%)
  blocking collectives  6.75 us (5%)
  local copies, waits for them, and re-layouts  2.7 us (2%)
    ppermute x43, waiting for transfers between devices, swap(): return lax.ppermute(array, axis, [(i, i ^ distance) for i in range(size)])  43.8 us
    ppermute x43, starting transfers between devices, swap(): return lax.ppermute(array, axis, [(i, i ^ distance) for i in range(size)])  43.2 us
    pallas_call x2, Pallas kernels, load(): pl.pallas_call(functools.partial(load_kernel, group, distances), out_shap...  10.5 us
    all_gather x1, blocking collectives, square_body(): return lax.all_gather(mixed, 'head', axis=1, tiled=True)  6.75 us
    pallas_call x1, Pallas kernels, last_hidden(): pl.pallas_call(functools.partial(last_hidden_kernel, n, slots, group, lat...  6.63 us
    pallas_call x2, Pallas kernels, down(): pl.pallas_call(functools.partial(down_kernel, slots), out_shape=[sds((tot...  6.4 us
    pallas_call x1, Pallas kernels, square_body(): pl.pallas_call(functools.partial(attend_kernel, n), out_shape=[sds((rows,...  5.52 us
    pallas_call x1, Pallas kernels, first_hidden(): pl.pallas_call(functools.partial(first_hidden_kernel, n, slots, group, ea...  5.17 us
  transfers between devices with their start and end apart: 43, of which 18 were waited for; matrix products, arithmetic and copies ran while one was open for 1% of the time, Pallas kernels for 24%

profile of v6, /device:TPU:0, one launch (start us, length us, event | category | flops | bytes accessed | tf_op | source)
XLA Modules:
  0.0 145.8 jit_solution(13867685068059680280)
XLA Ops:
  0.1 1.8 %cut_pieces.1 = (bf16[144,512]{1,0:T(8,128)(2,1)S(1)}, bf16[256,384]{1,0:T(8,128)(2,1)S(1)}, bf16[256,384]{1,0:T(8,128)(2,1)S(1)}, bf16[256,384]{1,0:T(8,128)(2,1)S(1)}) custom-call(s32[3]{0:T(128)S(1)} %pad_add_fusion.pos, s32[8,128]{1,0:T(8,128)} %bitcast.26, f32[8,128]{1,0:T(8,128)} %bitcast.27, bf16[128,2048]{1,0:T(8,128)(2,1)} %tokens.3, ...), custom_call_target="tpu_custom_call" | custom-call | tf_op jit(solution)/shard_map/cut_pieces/pallas_call | solution.py:574
  1.9 3.1 %collective-permute-start.3 = (bf16[256,384]{1,0:T(8,128)(2,1)S(1)}, bf16[256,384]{1,0:T(8,128)(2,1)S(1)}, u32[]{:S(2)}, u32[]{:S(2)}) collective-permute-start(bf16[256,384]{1,0:T(8,128)(2,1)S(1)} %get-tuple-element.69), channel_id=1, source_target_pairs={{0,4},{4,0},{8,12},{12,8},{1,5},{5,1},{9,13},{13,9},{2,6},{6,2},{1... | collective-permute-start | bytes 589832 | tf_op jit(solution)/shard_map/gather_tokens_and_weights/ppermute | solution.py:149
  5.0 2.6 %collective-permute-start.4 = (bf16[256,384]{1,0:T(8,128)(2,1)S(1)}, bf16[256,384]{1,0:T(8,128)(2,1)S(1)}, u32[]{:S(2)}, u32[]{:S(2)}) collective-permute-start(bf16[256,384]{1,0:T(8,128)(2,1)S(1)} %get-tuple-element.70), channel_id=1, source_target_pairs={{0,8},{4,12},{8,0},{12,4},{1,9},{5,13},{9,1},{13,5},{2,10},{6,14},... | collective-permute-start | bytes 589832 | tf_op jit(solution)/shard_map/gather_tokens_and_weights/ppermute | solution.py:149
  7.6 0.4 collective-permute-start
  8.0 3.9 %collective-permute-start.2 = (bf16[144,512]{1,0:T(8,128)(2,1)S(1)}, bf16[144,512]{1,0:T(8,128)(2,1)S(1)}, u32[]{:S(2)}, u32[]{:S(2)}) collective-permute-start(bf16[144,512]{1,0:T(8,128)(2,1)S(1)} %get-tuple-element.68.refs_0_), channel_id=1, source_target_pairs={{0,12},{4,8},{8,4},{12,0},{1,13},{5,9},{9,5},{13,1},{2,14},{6,10},... | collective-permute-start | bytes 442376 | tf_op jit(solution)/shard_map/gather_tokens_and_weights/ppermute | solution.py:149
  12.0 7.3 %collective-permute-done.refs_1_ = bf16[144,512]{1,0:T(8,128)(2,1)S(1)} collective-permute-done((bf16[144,512]{1,0:T(8,128)(2,1)S(1)}, bf16[144,512]{1,0:T(8,128)(2,1)S(1)}, u32[]{:S(2)}, u32[]{:S(2)}) %collective-permute-start) | collective-permute-done | bytes 147488 | tf_op jit(solution)/shard_map/gather_tokens_and_weights/ppermute | solution.py:149
  19.3 8.1 %collective-permute-done.1.refs_2_ = bf16[144,512]{1,0:T(8,128)(2,1)S(1)} collective-permute-done((bf16[144,512]{1,0:T(8,128)(2,1)S(1)}, bf16[144,512]{1,0:T(8,128)(2,1)S(1)}, u32[]{:S(2)}, u32[]{:S(2)}) %collective-permute-start.1) | collective-permute-done | bytes 147488 | tf_op jit(solution)/shard_map/gather_tokens_and_weights/ppermute | solution.py:149
  27.6 1.6 %collective-permute-start.6 = (bf16[3,128,512]{2,1,0:T(8,128)(2,1)S(1)}, bf16[3,128,512]{2,1,0:T(8,128)(2,1)S(1)}, u32[]{:S(2)}, u32[]{:S(2)}) collective-permute-start(bf16[3,128,512]{2,1,0:T(8,128)(2,1)S(1)} %pad_maximum_fusion.rest_0_), channel_id=1, source_target_pairs={{0,2},{1,3},{2,0},{3,1},{4,6},{5,7},{6,4},{7,5},{8,10},{9,11},{10,... | collective-permute-start | bytes 1179656 | tf_op jit(solution)/shard_map/gather_tokens_and_weights/ppermute | solution.py:149
  29.1 1.3 routing.1
  30.5 2.5 %collective-permute-start.7 = (bf16[256,384]{1,0:T(8,128)(2,1)S(1)}, bf16[256,384]{1,0:T(8,128)(2,1)S(1)}, u32[]{:S(2)}, u32[]{:S(2)}) collective-permute-start(bf16[256,384]{1,0:T(8,128)(2,1)S(1)} %get-tuple-element.75), channel_id=1, source_target_pairs={{0,12},{4,8},{8,4},{12,0},{1,13},{5,9},{9,5},{13,1},{2,14},{6,10},... | collective-permute-start | bytes 589832 | tf_op jit(solution)/shard_map/gather_tokens_and_weights/ppermute | solution.py:149
  33.0 1.5 %collective-permute-start.8 = (bf16[256,384]{1,0:T(8,128)(2,1)S(1)}, bf16[256,384]{1,0:T(8,128)(2,1)S(1)}, u32[]{:S(2)}, u32[]{:S(2)}) collective-permute-start(bf16[256,384]{1,0:T(8,128)(2,1)S(1)} %collective-permute-done.3.rest_4_), channel_id=1, source_target_pairs={{0,16},{16,0},{1,17},{17,1},{2,18},{18,2},{3,19},{19,3},{4,20},{20... | collective-permute-start | bytes 589832 | tf_op jit(solution)/shard_map/gather_tokens_and_weights/ppermute | solution.py:149
  34.5 0.5 collective-permute-start.9
  35.0 1.1 slice_bitcast_fusion.refs_0_
  36.1 0.6 collective-permute-start.17
  36.7 1.4 collective-permute-done.7.rest_6_
  38.1 0.6 collective-permute-done.8.rest_7_
  38.7 2.1 %collective-permute-done.9.rest_8_ = bf16[256,384]{1,0:T(8,128)(2,1)S(1)} collective-permute-done((bf16[256,384]{1,0:T(8,128)(2,1)S(1)}, bf16[256,384]{1,0:T(8,128)(2,1)S(1)}, u32[]{:S(2)}, u32[]{:S(2)}) %collective-permute-start.9) | collective-permute-done | bytes 196640 | tf_op jit(solution)/shard_map/gather_tokens_and_weights/ppermute | solution.py:149
  40.9 1.6 %collective-permute-start.11 = (bf16[256,384]{1,0:T(8,128)(2,1)S(1)}, bf16[256,384]{1,0:T(8,128)(2,1)S(1)}, u32[]{:S(2)}, u32[]{:S(2)}) collective-permute-start(bf16[256,384]{1,0:T(8,128)(2,1)S(1)} %collective-permute-done.7.rest_6_), channel_id=1, source_target_pairs={{0,16},{16,0},{1,17},{17,1},{2,18},{18,2},{3,19},{19,3},{4,20},{20... | collective-permute-start | bytes 589832 | tf_op jit(solution)/shard_map/gather_tokens_and_weights/ppermute | solution.py:149
  42.4 4.0 %expert_weights.3 = (bf16[8,1024,256]{2,1,0:T(8,128)(2,1)S(1)}, bf16[8,1024,256]{2,1,0:T(8,128)(2,1)S(1)}) custom-call(s32[3]{0:T(128)S(1)} %pad_add_fusion.pos, bf16[16,2048,256]{2,1,0:T(8,128)(2,1)} %w_gate.5, bf16[16,2048,256]{2,1,0:T(8,128)(2,1)} %w_up.5), custom_call_target="tpu_custom_call" | custom-call | bytes 8388608 | tf_op jit(solution)/shard_map/routing/expert_weights/pallas_call | solution.py:596
  46.6 1.6 %collective-permute-done.11.rest_9_ = bf16[256,384]{1,0:T(8,128)(2,1)S(1)} collective-permute-done((bf16[256,384]{1,0:T(8,128)(2,1)S(1)}, bf16[256,384]{1,0:T(8,128)(2,1)S(1)}, u32[]{:S(2)}, u32[]{:S(2)}) %collective-permute-start.11) | collective-permute-done | bytes 196640 | tf_op jit(solution)/shard_map/gather_tokens_and_weights/ppermute | solution.py:149
  48.2 0.8 copy-done.5
  49.0 5.5 %attention.1 = (bf16[128,128]{1,0:T(8,128)(2,1)S(1)}, bf16[128,128]{1,0:T(8,128)(2,1)S(1)}, bf16[128,128]{1,0:T(8,128)(2,1)S(1)}, bf16[128,128]{1,0:T(8,128)(2,1)S(1)}, bf16[128,512]{1,0:T(8,128)(2,1)S(1)}) custom-call(s32[3]{0:T(128)S(1)} %pad_add_fusion.pos, f32[1,2048]{1,0:T(1,128)S(1)} %bitcast.22, bf16[128,2048]{1,0:T(8,128)(2,1)} %tokens.3, ...), custom_call_target="tpu_custom_call" | custom-call | tf_op jit(solution)/shard_map/attention/pallas_call | solution.py:647
  54.6 0.5 collective-permute-start.18
  55.3 1.5 %collective-permute-start.13 = (bf16[128,128]{1,0:T(8,128)(2,1)S(1)}, bf16[128,128]{1,0:T(8,128)(2,1)S(1)}, u32[]{:S(2)}, u32[]{:S(2)}) collective-permute-start(bf16[128,128]{1,0:T(8,128)(2,1)S(1)} %get-tuple-element.89), channel_id=1, source_target_pairs={{0,2},{1,3},{2,0},{3,1},{4,6},{5,7},{6,4},{7,5},{8,10},{9,11},{10,... | collective-permute-start | bytes 98312 | tf_op jit(solution)/shard_map/heads_to_tokens/ppermute | solution.py:149
  56.9 1.5 %collective-permute-done.14 = bf16[128,128]{1,0:T(8,128)(2,1)S(1)} collective-permute-done((bf16[128,128]{1,0:T(8,128)(2,1)S(1)}, bf16[128,128]{1,0:T(8,128)(2,1)S(1)}, u32[]{:S(2)}, u32[]{:S(2)}) %collective-permute-start.14) | collective-permute-done | bytes 32800 | tf_op jit(solution)/shard_map/heads_to_tokens/ppermute | solution.py:149
  58.5 1.0 collective-permute-done.13
  59.5 2.9 %collective-permute-start.15 = (bf16[4,128,128]{2,1,0:T(8,128)(2,1)S(1)}, bf16[4,128,128]{2,1,0:T(8,128)(2,1)S(1)}, u32[]{:S(2)}, u32[]{:S(2)}) collective-permute-start(bf16[4,128,128]{2,1,0:T(8,128)(2,1)S(1)} %pad_maximum_fusion.1.rest_4_), channel_id=1, source_target_pairs={{0,8},{4,12},{8,0},{12,4},{1,9},{5,13},{9,1},{13,5},{2,10},{6,14},... | collective-permute-start | bytes 393224 | tf_op jit(solution)/shard_map/heads_to_tokens/ppermute | solution.py:149
  62.4 6.5 %expert_weights.4 = (bf16[16,1024,256]{2,1,0:T(8,128)(2,1)S(1)}, bf16[16,1024,256]{2,1,0:T(8,128)(2,1)S(1)}) custom-call(s32[3]{0:T(128)S(1)} %pad_add_fusion.pos, bf16[16,2048,256]{2,1,0:T(8,128)(2,1)} %w_gate.5, bf16[16,2048,256]{2,1,0:T(8,128)(2,1)} %w_up.5), custom_call_target="tpu_custom_call" | custom-call | bytes 16777216 | tf_op jit(solution)/shard_map/heads_to_tokens/expert_weights/pallas_call | solution.py:596
  68.9 2.1 %collective-permute-start.20 = (bf16[4,128,128]{2,1,0:T(8,128)(2,1)S(1)}, bf16[4,128,128]{2,1,0:T(8,128)(2,1)S(1)}, u32[]{:S(2)}, u32[]{:S(2)}) collective-permute-start(bf16[4,128,128]{2,1,0:T(8,128)(2,1)S(1)} %collective-permute-done.15.rest_6_), channel_id=1, source_target_pairs={{0,4},{4,0},{8,12},{12,8},{1,5},{5,1},{9,13},{13,9},{2,6},{6,2},{1... | collective-permute-start | bytes 393224 | tf_op jit(solution)/shard_map/heads_to_tokens/ppermute | solution.py:149
  70.9 2.8 %expert_weights.5.refs_0_ = bf16[16,256,512]{2,1,0:T(8,128)(2,1)S(1)} custom-call(s32[3]{0:T(128)S(1)} %pad_add_fusion.pos, bf16[16,256,2048]{2,1,0:T(8,128)(2,1)} %w_down.5), custom_call_target="tpu_custom_call" | custom-call | bytes 4194304 | tf_op jit(solution)/shard_map/heads_to_tokens/expert_weights/pallas_call | solution.py:608
  74.0 1.4 output_projection.1.refs_0_
  75.3 2.8 %collective-permute-start.21 = (bf16[128,512]{1,0:T(8,128)(2,1)S(1)}, bf16[128,512]{1,0:T(8,128)(2,1)S(1)}, u32[]{:S(2)}, u32[]{:S(2)}) collective-permute-start(bf16[128,512]{1,0:T(8,128)(2,1)S(1)} %output_projection.1.refs_0_), channel_id=1, source_target_pairs={{0,8},{4,12},{8,0},{12,4},{1,9},{5,13},{9,1},{13,5},{2,10},{6,14},... | collective-permute-start | bytes 393224 | tf_op jit(solution)/shard_map/gather_residual/ppermute | solution.py:149
  78.3 1.2 collective-permute-start.28
  79.5 3.6 %collective-permute-done.21.refs_0_ = bf16[128,512]{1,0:T(8,128)(2,1)S(1)} collective-permute-done((bf16[128,512]{1,0:T(8,128)(2,1)S(1)}, bf16[128,512]{1,0:T(8,128)(2,1)S(1)}, u32[]{:S(2)}, u32[]{:S(2)}) %collective-permute-start.21) | collective-permute-done | bytes 131104 | tf_op jit(solution)/shard_map/gather_residual/ppermute | solution.py:149
  83.3 0.8 collective-permute-done.24.refs_4_
  84.1 1.1 collective-permute-start.30
  85.1 1.0 collective-permute-start.23
  86.1 0.5 collective-permute-start.29
  86.6 1.5 %collective-permute-done.22.refs_4_ = bf16[128,512]{1,0:T(8,128)(2,1)S(1)} collective-permute-done((bf16[128,512]{1,0:T(8,128)(2,1)S(1)}, bf16[128,512]{1,0:T(8,128)(2,1)S(1)}, u32[]{:S(2)}, u32[]{:S(2)}) %collective-permute-start.22) | collective-permute-done | bytes 131104 | tf_op jit(solution)/shard_map/gather_residual/ppermute | solution.py:149
  88.1 1.0 collective-permute-done.30.refs_6_
  89.1 1.4 collective-permute-done.23.refs_2_
  90.5 0.5 collective-permute-start.35
  91.0 1.1 collective-permute-start.26
  92.1 5.2 %first_hidden_units.1 = (f32[1280,512]{1,0:T(8,128)S(1)}, f32[1280,128]{1,0:T(8,128)S(1)}) custom-call(s32[3]{0:T(128)S(1)} %pad_add_fusion.pos, f32[1,2048]{1,0:T(1,128)S(1)} %bitcast.20, bf16[1280,512]{1,0:T(8,128)(2,1)S(1)} %get-tuple-element.80.pick, bf16[16,1024,256]{2,1,0:T(8,128)(2,1)S(1)} %get-tuple-element.92.g_all, ...), custom_call_target="tpu_custom_call" | custom-call | flops 2684354560 | bytes 16777216 | tf_op jit(solution)/shard_map/gather_residual/first_hidden_units/pallas_call | solution.py:667
  97.3 0.5 collective-permute-start.32
  97.8 0.8 collective-permute-done.34.refs_3_
  98.8 6.6 %last_hidden_units.1 = (bf16[1280,256]{1,0:T(8,128)(2,1)S(1)}, bf16[16,256,512]{2,1,0:T(8,128)(2,1)S(1)}, bf16[16,256,512]{2,1,0:T(8,128)(2,1)S(1)}) custom-call(s32[3]{0:T(128)S(1)} %pad_add_fusion.pos, f32[1,2048]{1,0:T(1,128)S(1)} %bitcast.21, bf16[1280,512]{1,0:T(8,128)(2,1)S(1)} %get-tuple-element.80.pick, bf16[16,2048,256]{2,1,0:T(8,128)(2,1)} %w_gate.5, ...), custom_call_target="tpu_custom_call" | custom-call | flops 2684354560 | bytes 16777216 | tf_op jit(solution)/shard_map/gather_residual/last_hidden_units/pallas_call | solution.py:678
  105.5 4.3 %down_products.2 = (bf16[512,512]{1,0:T(8,128)(2,1)S(1)}, bf16[512,512]{1,0:T(8,128)(2,1)}) custom-call(s32[3]{0:T(128)S(1)} %pad_add_fusion.pos, bf16[1280,256]{1,0:T(8,128)(2,1)S(1)} %get-tuple-element.119.hidden, bf16[512,1280]{1,0:T(8,128)(2,1)S(1)} %get-tuple-element.112.place, bf16[16,256,512]{2,1,0:T(8,128)(2,1)S(1)} %get-tuple-element.113.refs_0_, ...), custom_call_target="tpu_custom_call" | custom-call | flops 2013265920 | bytes 8388608 | tf_op jit(solution)/shard_map/sum_over_devices/down_products/pallas_call | solution.py:750
  109.8 0.3 collective-permute-start.36
  110.3 2.1 %down_products.3.base = bf16[512,512]{1,0:T(8,128)(2,1)S(1)} custom-call(s32[3]{0:T(128)S(1)} %pad_add_fusion.pos, bf16[1280,256]{1,0:T(8,128)(2,1)S(1)} %get-tuple-element.119.hidden, bf16[512,1280]{1,0:T(8,128)(2,1)S(1)} %get-tuple-element.112.place, bf16[16,256,512]{2,1,0:T(8,128)(2,1)S(1)} %expert_weights.5.refs_0_), custom_call_target="tpu_custom_call" | custom-call | flops 1006632960 | bytes 4194304 | tf_op jit(solution)/shard_map/sum_over_devices/down_products/pallas_call | solution.py:750
  112.4 1.3 halves_over_cores.1
  113.7 1.0 collective-permute-start.39
  114.7 1.1 collective-permute-start.38
  115.7 3.9 %down_products_alone.1.base = bf16[512,512]{1,0:T(8,128)(2,1)S(1)} custom-call(s32[3]{0:T(128)S(1)} %pad_add_fusion.pos, bf16[1280,256]{1,0:T(8,128)(2,1)S(1)} %get-tuple-element.119.hidden, bf16[512,1280]{1,0:T(8,128)(2,1)S(1)} %get-tuple-element.112.place, bf16[16,256,2048]{2,1,0:T(8,128)(2,1)} %w_down.5), custom_call_target="tpu_custom_call" | custom-call | flops 1006632960 | bytes 4194304 | tf_op jit(solution)/shard_map/sum_over_devices/down_products_alone/pallas_call | solution.py:764
  119.7 3.4 %collective-permute-done.39.part = bf16[256,512]{1,0:T(8,128)(2,1)S(1)} collective-permute-done((bf16[256,512]{1,0:T(8,128)(2,1)}, bf16[256,512]{1,0:T(8,128)(2,1)S(1)}, u32[]{:S(2)}, u32[]{:S(2)}) %collective-permute-start.39) | collective-permute-done | bytes 262176 | tf_op jit(solution)/shard_map/sum_over_devices/ppermute | solution.py:149
  123.0 0.6 far_half_rows.1
  123.7 2.4 %collective-permute-start.41 = (bf16[128,512]{1,0:T(8,128)(2,1)S(1)}, bf16[128,512]{1,0:T(8,128)(2,1)S(1)}, u32[]{:S(2)}, u32[]{:S(2)}) collective-permute-start(bf16[128,512]{1,0:T(8,128)(2,1)S(1)} %get-tuple-element.127), channel_id=1, source_target_pairs={{0,12},{4,8},{8,4},{12,0},{1,13},{5,9},{9,5},{13,1},{2,14},{6,10},... | collective-permute-start | bytes 393224 | tf_op jit(solution)/shard_map/sum_over_devices/ppermute | solution.py:149
  126.1 1.2 collective-permute-start.40
  127.3 0.9 collective-permute-done.38.part
  128.2 1.1 near_half_rows.1
  129.2 2.2 %collective-permute-start.42 = (bf16[128,512]{1,0:T(8,128)(2,1)S(1)}, bf16[128,512]{1,0:T(8,128)(2,1)S(1)}, u32[]{:S(2)}, u32[]{:S(2)}) collective-permute-start(bf16[128,512]{1,0:T(8,128)(2,1)S(1)} %get-tuple-element.128), channel_id=1, source_target_pairs={{0,4},{4,0},{8,12},{12,8},{1,5},{5,1},{9,13},{13,9},{2,6},{6,2},{1... | collective-permute-start | bytes 393224 | tf_op jit(solution)/shard_map/sum_over_devices/ppermute | solution.py:149
  131.4 6.6 %collective-permute-done.40 = bf16[128,512]{1,0:T(8,128)(2,1)S(1)} collective-permute-done((bf16[128,512]{1,0:T(8,128)(2,1)S(1)}, bf16[128,512]{1,0:T(8,128)(2,1)S(1)}, u32[]{:S(2)}, u32[]{:S(2)}) %collective-permute-start.40) | collective-permute-done | bytes 131104 | tf_op jit(solution)/shard_map/sum_over_devices/ppermute | solution.py:149
  138.2 6.8 %all_gather.3 = bf16[128,2048]{1,0:T(8,128)(2,1)S(1)} all-gather(bf16[128,512]{1,0:T(8,128)(2,1)S(1)} %add_convert_fusion), channel_id=1, replica_groups=mesh['grp'=2,'seq'=4,'head'=4] {'head'}, dimensions={1}, use_global_device_ids=true | all-gather | bytes 655360 | tf_op jit(solution)/shard_map/gather_columns/all_gather | solution.py:816
  145.0 0.8 copy.11
  (70 shorter events, 1.9 us)
Async XLA Ops:
  1.9 25.5 %collective-permute-start.3 = (bf16[256,384]{1,0:T(8,128)(2,1)S(1)}, bf16[256,384]{1,0:T(8,128)(2,1)S(1)}, u32[]{:S(2)}, u32[]{:S(2)}) collective-permute-start(bf16[256,384]{1,0:T(8,128)(2,1)S(1)} %get-tuple-element.69), channel_id=1, source_target_pairs={{0,4},{4,0},{8,12},{12,8},{1,5},{5,1},{9,13},{13,9},{2,6},{6,2},{1... | collective-permute-start | bytes 589832 | tf_op jit(solution)/shard_map/gather_tokens_and_weights/ppermute | solution.py:149
  5.0 22.4 %collective-permute-start.4 = (bf16[256,384]{1,0:T(8,128)(2,1)S(1)}, bf16[256,384]{1,0:T(8,128)(2,1)S(1)}, u32[]{:S(2)}, u32[]{:S(2)}) collective-permute-start(bf16[256,384]{1,0:T(8,128)(2,1)S(1)} %get-tuple-element.70), channel_id=1, source_target_pairs={{0,8},{4,12},{8,0},{12,4},{1,9},{5,13},{9,1},{13,5},{2,10},{6,14},... | collective-permute-start | bytes 589832 | tf_op jit(solution)/shard_map/gather_tokens_and_weights/ppermute | solution.py:149
  7.6 11.7 %collective-permute-start = (bf16[144,512]{1,0:T(8,128)(2,1)S(1)}, bf16[144,512]{1,0:T(8,128)(2,1)S(1)}, u32[]{:S(2)}, u32[]{:S(2)}) collective-permute-start(bf16[144,512]{1,0:T(8,128)(2,1)S(1)} %get-tuple-element.68.refs_0_), channel_id=1, source_target_pairs={{0,4},{4,0},{8,12},{12,8},{1,5},{5,1},{9,13},{13,9},{2,6},{6,2},{1... | collective-permute-start | bytes 442376 | tf_op jit(solution)/shard_map/gather_tokens_and_weights/ppermute | solution.py:149
  8.0 19.4 %collective-permute-start.1 = (bf16[144,512]{1,0:T(8,128)(2,1)S(1)}, bf16[144,512]{1,0:T(8,128)(2,1)S(1)}, u32[]{:S(2)}, u32[]{:S(2)}) collective-permute-start(bf16[144,512]{1,0:T(8,128)(2,1)S(1)} %get-tuple-element.68.refs_0_), channel_id=1, source_target_pairs={{0,8},{4,12},{8,0},{12,4},{1,9},{5,13},{9,1},{13,5},{2,10},{6,14},... | collective-permute-start | bytes 442376 | tf_op jit(solution)/shard_map/gather_tokens_and_weights/ppermute | solution.py:149
  8.0 19.4 %collective-permute-start.2 = (bf16[144,512]{1,0:T(8,128)(2,1)S(1)}, bf16[144,512]{1,0:T(8,128)(2,1)S(1)}, u32[]{:S(2)}, u32[]{:S(2)}) collective-permute-start(bf16[144,512]{1,0:T(8,128)(2,1)S(1)} %get-tuple-element.68.refs_0_), channel_id=1, source_target_pairs={{0,12},{4,8},{8,4},{12,0},{1,13},{5,9},{9,5},{13,1},{2,14},{6,10},... | collective-permute-start | bytes 442376 | tf_op jit(solution)/shard_map/gather_tokens_and_weights/ppermute | solution.py:149
  27.4 19.0 %copy-start.6 = (bf16[256,384]{1,0:T(8,128)(2,1)}, bf16[256,384]{1,0:T(8,128)(2,1)S(1)}, u32[]{:S(2)}) copy-start(bf16[256,384]{1,0:T(8,128)(2,1)S(1)} %collective-permute-done.3.rest_4_) | copy-start | bytes 589828
  27.4 19.0 %copy-start.7 = (bf16[256,384]{1,0:T(8,128)(2,1)}, bf16[256,384]{1,0:T(8,128)(2,1)S(1)}, u32[]{:S(2)}) copy-start(bf16[256,384]{1,0:T(8,128)(2,1)S(1)} %collective-permute-done.4.rest_5_) | copy-start | bytes 589828
  27.6 18.9 %copy-start.2 = (bf16[3,128,512]{2,1,0:T(8,128)(2,1)}, bf16[3,128,512]{2,1,0:T(8,128)(2,1)S(1)}, u32[]{:S(2)}) copy-start(bf16[3,128,512]{2,1,0:T(8,128)(2,1)S(1)} %pad_maximum_fusion.rest_0_) | copy-start | bytes 1179652
  27.6 13.2 %collective-permute-start.6 = (bf16[3,128,512]{2,1,0:T(8,128)(2,1)S(1)}, bf16[3,128,512]{2,1,0:T(8,128)(2,1)S(1)}, u32[]{:S(2)}, u32[]{:S(2)}) collective-permute-start(bf16[3,128,512]{2,1,0:T(8,128)(2,1)S(1)} %pad_maximum_fusion.rest_0_), channel_id=1, source_target_pairs={{0,2},{1,3},{2,0},{3,1},{4,6},{5,7},{6,4},{7,5},{8,10},{9,11},{10,... | collective-permute-start | bytes 1179656 | tf_op jit(solution)/shard_map/gather_tokens_and_weights/ppermute | solution.py:149
  30.5 7.6 %collective-permute-start.7 = (bf16[256,384]{1,0:T(8,128)(2,1)S(1)}, bf16[256,384]{1,0:T(8,128)(2,1)S(1)}, u32[]{:S(2)}, u32[]{:S(2)}) collective-permute-start(bf16[256,384]{1,0:T(8,128)(2,1)S(1)} %get-tuple-element.75), channel_id=1, source_target_pairs={{0,12},{4,8},{8,4},{12,0},{1,13},{5,9},{9,5},{13,1},{2,14},{6,10},... | collective-permute-start | bytes 589832 | tf_op jit(solution)/shard_map/gather_tokens_and_weights/ppermute | solution.py:149
  33.0 5.7 %collective-permute-start.8 = (bf16[256,384]{1,0:T(8,128)(2,1)S(1)}, bf16[256,384]{1,0:T(8,128)(2,1)S(1)}, u32[]{:S(2)}, u32[]{:S(2)}) collective-permute-start(bf16[256,384]{1,0:T(8,128)(2,1)S(1)} %collective-permute-done.3.rest_4_), channel_id=1, source_target_pairs={{0,16},{16,0},{1,17},{17,1},{2,18},{18,2},{3,19},{19,3},{4,20},{20... | collective-permute-start | bytes 589832 | tf_op jit(solution)/shard_map/gather_tokens_and_weights/ppermute | solution.py:149
  34.5 6.3 %collective-permute-start.9 = (bf16[256,384]{1,0:T(8,128)(2,1)S(1)}, bf16[256,384]{1,0:T(8,128)(2,1)S(1)}, u32[]{:S(2)}, u32[]{:S(2)}) collective-permute-start(bf16[256,384]{1,0:T(8,128)(2,1)S(1)} %collective-permute-done.4.rest_5_), channel_id=1, source_target_pairs={{0,16},{16,0},{1,17},{17,1},{2,18},{18,2},{3,19},{19,3},{4,20},{20... | collective-permute-start | bytes 589832 | tf_op jit(solution)/shard_map/gather_tokens_and_weights/ppermute | solution.py:149
  36.1 12.8 %copy-start.1 = (f32[2048]{0:T(1024)S(1)}, f32[2048]{0:T(1024)}, u32[]{:S(2)}) copy-start(f32[2048]{0:T(1024)} %param.11) | copy-start | bytes 24580
  36.1 18.4 %collective-permute-start.17 = (bf16[512,512]{1,0:T(8,128)(2,1)S(1)}, bf16[512,512]{1,0:T(8,128)(2,1)S(1)}, u32[]{:S(2)}, u32[]{:S(2)}) collective-permute-start(bf16[512,512]{1,0:T(8,128)(2,1)S(1)} %slice_bitcast_fusion.refs_0_), channel_id=1, source_target_pairs={{0,2},{1,3},{2,0},{3,1},{4,6},{5,7},{6,4},{7,5},{8,10},{9,11},{10,... | collective-permute-start | bytes 1572872 | tf_op jit(solution)/shard_map/routing/ppermute | solution.py:149
  38.1 8.4 %copy-start.8 = (bf16[256,384]{1,0:T(8,128)(2,1)}, bf16[256,384]{1,0:T(8,128)(2,1)S(1)}, u32[]{:S(2)}) copy-start(bf16[256,384]{1,0:T(8,128)(2,1)S(1)} %collective-permute-done.7.rest_6_) | copy-start | bytes 589828
  38.1 8.4 %collective-permute-start.5 = (bf16[3,128,512]{2,1,0:T(8,128)(2,1)S(1)}, bf16[3,128,512]{2,1,0:T(8,128)(2,1)S(1)}, u32[]{:S(2)}, u32[]{:S(2)}) collective-permute-start(bf16[3,128,512]{2,1,0:T(8,128)(2,1)S(1)} %pad_maximum_fusion.rest_0_), channel_id=1, source_target_pairs={{0,1},{1,0},{2,3},{3,2},{4,5},{5,4},{6,7},{7,6},{8,9},{9,8},{10,11... | collective-permute-start | bytes 1179656 | tf_op jit(solution)/shard_map/gather_tokens_and_weights/ppermute | solution.py:149
  38.7 7.8 %copy-start.9 = (bf16[256,384]{1,0:T(8,128)(2,1)}, bf16[256,384]{1,0:T(8,128)(2,1)S(1)}, u32[]{:S(2)}) copy-start(bf16[256,384]{1,0:T(8,128)(2,1)S(1)} %collective-permute-done.8.rest_7_) | copy-start | bytes 589828
  40.8 5.7 %copy-start.10 = (bf16[256,384]{1,0:T(8,128)(2,1)}, bf16[256,384]{1,0:T(8,128)(2,1)S(1)}, u32[]{:S(2)}) copy-start(bf16[256,384]{1,0:T(8,128)(2,1)S(1)} %collective-permute-done.9.rest_8_) | copy-start | bytes 589828
  40.8 5.7 %copy-start.3 = (bf16[3,128,512]{2,1,0:T(8,128)(2,1)}, bf16[3,128,512]{2,1,0:T(8,128)(2,1)S(1)}, u32[]{:S(2)}) copy-start(bf16[3,128,512]{2,1,0:T(8,128)(2,1)S(1)} %collective-permute-done.6.rest_2_) | copy-start | bytes 1179652
  40.8 7.4 %collective-permute-start.10 = (bf16[3,128,512]{2,1,0:T(8,128)(2,1)S(1)}, bf16[3,128,512]{2,1,0:T(8,128)(2,1)S(1)}, u32[]{:S(2)}, u32[]{:S(2)}) collective-permute-start(bf16[3,128,512]{2,1,0:T(8,128)(2,1)S(1)} %collective-permute-done.6.rest_2_), channel_id=1, source_target_pairs={{0,1},{1,0},{2,3},{3,2},{4,5},{5,4},{6,7},{7,6},{8,9},{9,8},{10,11... | collective-permute-start | bytes 1179656 | tf_op jit(solution)/shard_map/gather_tokens_and_weights/ppermute | solution.py:149
  40.9 7.3 %collective-permute-start.11 = (bf16[256,384]{1,0:T(8,128)(2,1)S(1)}, bf16[256,384]{1,0:T(8,128)(2,1)S(1)}, u32[]{:S(2)}, u32[]{:S(2)}) collective-permute-start(bf16[256,384]{1,0:T(8,128)(2,1)S(1)} %collective-permute-done.7.rest_6_), channel_id=1, source_target_pairs={{0,16},{16,0},{1,17},{17,1},{2,18},{18,2},{3,19},{19,3},{4,20},{20... | collective-permute-start | bytes 589832 | tf_op jit(solution)/shard_map/gather_tokens_and_weights/ppermute | solution.py:149
  46.6 1.6 %copy-start.4 = (bf16[3,128,512]{2,1,0:T(8,128)(2,1)}, bf16[3,128,512]{2,1,0:T(8,128)(2,1)S(1)}, u32[]{:S(2)}) copy-start(bf16[3,128,512]{2,1,0:T(8,128)(2,1)S(1)} %collective-permute-done.5.rest_1_) | copy-start | bytes 1179652
  48.2 0.8 copy-start.5
  54.5 19.3 %collective-permute-start.16 = (bf16[512,512]{1,0:T(8,128)(2,1)S(1)}, bf16[512,512]{1,0:T(8,128)(2,1)S(1)}, u32[]{:S(2)}, u32[]{:S(2)}) collective-permute-start(bf16[512,512]{1,0:T(8,128)(2,1)S(1)} %slice_bitcast_fusion.refs_0_), channel_id=1, source_target_pairs={{0,1},{1,0},{2,3},{3,2},{4,5},{5,4},{6,7},{7,6},{8,9},{9,8},{10,11... | collective-permute-start | bytes 1572872 | tf_op jit(solution)/shard_map/heads_to_tokens/ppermute | solution.py:149
  54.6 19.2 %collective-permute-start.18 = (bf16[512,512]{1,0:T(8,128)(2,1)S(1)}, bf16[512,512]{1,0:T(8,128)(2,1)S(1)}, u32[]{:S(2)}, u32[]{:S(2)}) collective-permute-start(bf16[512,512]{1,0:T(8,128)(2,1)S(1)} %collective-permute-done.17.refs_2_), channel_id=1, source_target_pairs={{0,1},{1,0},{2,3},{3,2},{4,5},{5,4},{6,7},{7,6},{8,9},{9,8},{10,11... | collective-permute-start | bytes 1572872 | tf_op jit(solution)/shard_map/heads_to_tokens/ppermute | solution.py:149
  55.1 3.4 %collective-permute-start.14 = (bf16[128,128]{1,0:T(8,128)(2,1)S(1)}, bf16[128,128]{1,0:T(8,128)(2,1)S(1)}, u32[]{:S(2)}, u32[]{:S(2)}) collective-permute-start(bf16[128,128]{1,0:T(8,128)(2,1)S(1)} %get-tuple-element.90), channel_id=1, source_target_pairs={{0,3},{1,2},{2,1},{3,0},{4,7},{5,6},{6,5},{7,4},{8,11},{9,10},{10,... | collective-permute-start | bytes 98312 | tf_op jit(solution)/shard_map/heads_to_tokens/ppermute | solution.py:149
  55.3 4.2 %collective-permute-start.13 = (bf16[128,128]{1,0:T(8,128)(2,1)S(1)}, bf16[128,128]{1,0:T(8,128)(2,1)S(1)}, u32[]{:S(2)}, u32[]{:S(2)}) collective-permute-start(bf16[128,128]{1,0:T(8,128)(2,1)S(1)} %get-tuple-element.89), channel_id=1, source_target_pairs={{0,2},{1,3},{2,0},{3,1},{4,6},{5,7},{6,4},{7,5},{8,10},{9,11},{10,... | collective-permute-start | bytes 98312 | tf_op jit(solution)/shard_map/heads_to_tokens/ppermute | solution.py:149
  56.8 2.7 %collective-permute-start.12 = (bf16[128,128]{1,0:T(8,128)(2,1)S(1)}, bf16[128,128]{1,0:T(8,128)(2,1)S(1)}, u32[]{:S(2)}, u32[]{:S(2)}) collective-permute-start(bf16[128,128]{1,0:T(8,128)(2,1)S(1)} %get-tuple-element.88), channel_id=1, source_target_pairs={{0,1},{1,0},{2,3},{3,2},{4,5},{5,4},{6,7},{7,6},{8,9},{9,8},{10,11... | collective-permute-start | bytes 98312 | tf_op jit(solution)/shard_map/heads_to_tokens/ppermute | solution.py:149
  59.5 9.4 %collective-permute-start.15 = (bf16[4,128,128]{2,1,0:T(8,128)(2,1)S(1)}, bf16[4,128,128]{2,1,0:T(8,128)(2,1)S(1)}, u32[]{:S(2)}, u32[]{:S(2)}) collective-permute-start(bf16[4,128,128]{2,1,0:T(8,128)(2,1)S(1)} %pad_maximum_fusion.1.rest_4_), channel_id=1, source_target_pairs={{0,8},{4,12},{8,0},{12,4},{1,9},{5,13},{9,1},{13,5},{2,10},{6,14},... | collective-permute-start | bytes 393224 | tf_op jit(solution)/shard_map/heads_to_tokens/ppermute | solution.py:149
  62.4 11.6 %collective-permute-start.19 = (bf16[4,128,128]{2,1,0:T(8,128)(2,1)S(1)}, bf16[4,128,128]{2,1,0:T(8,128)(2,1)S(1)}, u32[]{:S(2)}, u32[]{:S(2)}) collective-permute-start(bf16[4,128,128]{2,1,0:T(8,128)(2,1)S(1)} %pad_maximum_fusion.1.rest_4_), channel_id=1, source_target_pairs={{0,4},{4,0},{8,12},{12,8},{1,5},{5,1},{9,13},{13,9},{2,6},{6,2},{1... | collective-permute-start | bytes 393224 | tf_op jit(solution)/shard_map/heads_to_tokens/ppermute | solution.py:149
  68.9 5.1 %collective-permute-start.20 = (bf16[4,128,128]{2,1,0:T(8,128)(2,1)S(1)}, bf16[4,128,128]{2,1,0:T(8,128)(2,1)S(1)}, u32[]{:S(2)}, u32[]{:S(2)}) collective-permute-start(bf16[4,128,128]{2,1,0:T(8,128)(2,1)S(1)} %collective-permute-done.15.rest_6_), channel_id=1, source_target_pairs={{0,4},{4,0},{8,12},{12,8},{1,5},{5,1},{9,13},{13,9},{2,6},{6,2},{1... | collective-permute-start | bytes 393224 | tf_op jit(solution)/shard_map/heads_to_tokens/ppermute | solution.py:149
  73.7 18.3 %copy-start = (f32[2048]{0:T(1024)S(1)}, f32[2048]{0:T(1024)}, u32[]{:S(2)}) copy-start(f32[2048]{0:T(1024)} %param.12) | copy-start | bytes 24580
  75.3 7.8 %collective-permute-start.21 = (bf16[128,512]{1,0:T(8,128)(2,1)S(1)}, bf16[128,512]{1,0:T(8,128)(2,1)S(1)}, u32[]{:S(2)}, u32[]{:S(2)}) collective-permute-start(bf16[128,512]{1,0:T(8,128)(2,1)S(1)} %output_projection.1.refs_0_), channel_id=1, source_target_pairs={{0,8},{4,12},{8,0},{12,4},{1,9},{5,13},{9,1},{13,5},{2,10},{6,14},... | collective-permute-start | bytes 393224 | tf_op jit(solution)/shard_map/gather_residual/ppermute | solution.py:149
  78.2 5.9 %collective-permute-start.24 = (bf16[128,512]{1,0:T(8,128)(2,1)S(1)}, bf16[128,512]{1,0:T(8,128)(2,1)S(1)}, u32[]{:S(2)}, u32[]{:S(2)}) collective-permute-start(bf16[128,512]{1,0:T(8,128)(2,1)S(1)} %output_projection.1.refs_0_), channel_id=1, source_target_pairs={{0,4},{4,0},{8,12},{12,8},{1,5},{5,1},{9,13},{13,9},{2,6},{6,2},{1... | collective-permute-start | bytes 393224 | tf_op jit(solution)/shard_map/gather_residual/ppermute | solution.py:149
  78.3 7.8 %collective-permute-start.28 = (bf16[128,512]{1,0:T(8,128)(2,1)S(1)}, bf16[128,512]{1,0:T(8,128)(2,1)S(1)}, u32[]{:S(2)}, u32[]{:S(2)}) collective-permute-start(bf16[128,512]{1,0:T(8,128)(2,1)S(1)} %output_projection.1.refs_0_), channel_id=1, source_target_pairs={{0,2},{1,3},{2,0},{3,1},{4,6},{5,7},{6,4},{7,5},{8,10},{9,11},{10,... | collective-permute-start | bytes 393224 | tf_op jit(solution)/shard_map/gather_residual/ppermute | solution.py:149
  83.1 5.0 %collective-permute-start.22 = (bf16[128,512]{1,0:T(8,128)(2,1)S(1)}, bf16[128,512]{1,0:T(8,128)(2,1)S(1)}, u32[]{:S(2)}, u32[]{:S(2)}) collective-permute-start(bf16[128,512]{1,0:T(8,128)(2,1)S(1)} %collective-permute-done.21.refs_0_), channel_id=1, source_target_pairs={{0,4},{4,0},{8,12},{12,8},{1,5},{5,1},{9,13},{13,9},{2,6},{6,2},{1... | collective-permute-start | bytes 393224 | tf_op jit(solution)/shard_map/gather_residual/ppermute | solution.py:149
  84.1 5.0 %collective-permute-start.30 = (bf16[128,512]{1,0:T(8,128)(2,1)S(1)}, bf16[128,512]{1,0:T(8,128)(2,1)S(1)}, u32[]{:S(2)}, u32[]{:S(2)}) collective-permute-start(bf16[128,512]{1,0:T(8,128)(2,1)S(1)} %collective-permute-done.24.refs_4_), channel_id=1, source_target_pairs={{0,2},{1,3},{2,0},{3,1},{4,6},{5,7},{6,4},{7,5},{8,10},{9,11},{10,... | collective-permute-start | bytes 393224 | tf_op jit(solution)/shard_map/gather_residual/ppermute | solution.py:149
  85.1 5.3 %collective-permute-start.23 = (bf16[128,512]{1,0:T(8,128)(2,1)S(1)}, bf16[128,512]{1,0:T(8,128)(2,1)S(1)}, u32[]{:S(2)}, u32[]{:S(2)}) collective-permute-start(bf16[128,512]{1,0:T(8,128)(2,1)S(1)} %collective-permute-done.21.refs_0_), channel_id=1, source_target_pairs={{0,2},{1,3},{2,0},{3,1},{4,6},{5,7},{6,4},{7,5},{8,10},{9,11},{10,... | collective-permute-start | bytes 393224 | tf_op jit(solution)/shard_map/gather_residual/ppermute | solution.py:149
  86.1 4.4 %collective-permute-start.27 = (bf16[128,512]{1,0:T(8,128)(2,1)S(1)}, bf16[128,512]{1,0:T(8,128)(2,1)S(1)}, u32[]{:S(2)}, u32[]{:S(2)}) collective-permute-start(bf16[128,512]{1,0:T(8,128)(2,1)S(1)} %output_projection.1.refs_0_), channel_id=1, source_target_pairs={{0,1},{1,0},{2,3},{3,2},{4,5},{5,4},{6,7},{7,6},{8,9},{9,8},{10,11... | collective-permute-start | bytes 393224 | tf_op jit(solution)/shard_map/gather_residual/ppermute | solution.py:149
  86.1 4.9 %collective-permute-start.29 = (bf16[128,512]{1,0:T(8,128)(2,1)S(1)}, bf16[128,512]{1,0:T(8,128)(2,1)S(1)}, u32[]{:S(2)}, u32[]{:S(2)}) collective-permute-start(bf16[128,512]{1,0:T(8,128)(2,1)S(1)} %collective-permute-done.28.refs_2_), channel_id=1, source_target_pairs={{0,1},{1,0},{2,3},{3,2},{4,5},{5,4},{6,7},{7,6},{8,9},{9,8},{10,11... | collective-permute-start | bytes 393224 | tf_op jit(solution)/shard_map/gather_residual/ppermute | solution.py:149
  88.1 4.0 %collective-permute-start.25 = (bf16[128,512]{1,0:T(8,128)(2,1)S(1)}, bf16[128,512]{1,0:T(8,128)(2,1)S(1)}, u32[]{:S(2)}, u32[]{:S(2)}) collective-permute-start(bf16[128,512]{1,0:T(8,128)(2,1)S(1)} %collective-permute-done.24.refs_4_), channel_id=1, source_target_pairs={{0,1},{1,0},{2,3},{3,2},{4,5},{5,4},{6,7},{7,6},{8,9},{9,8},{10,11... | collective-permute-start | bytes 393224 | tf_op jit(solution)/shard_map/gather_residual/ppermute | solution.py:149
  89.1 3.0 %collective-permute-start.31 = (bf16[128,512]{1,0:T(8,128)(2,1)S(1)}, bf16[128,512]{1,0:T(8,128)(2,1)S(1)}, u32[]{:S(2)}, u32[]{:S(2)}) collective-permute-start(bf16[128,512]{1,0:T(8,128)(2,1)S(1)} %collective-permute-done.30.refs_6_), channel_id=1, source_target_pairs={{0,1},{1,0},{2,3},{3,2},{4,5},{5,4},{6,7},{7,6},{8,9},{9,8},{10,11... | collective-permute-start | bytes 393224 | tf_op jit(solution)/shard_map/gather_residual/ppermute | solution.py:149
  90.5 7.3 %collective-permute-start.33 = (bf16[128,512]{1,0:T(8,128)(2,1)S(1)}, bf16[128,512]{1,0:T(8,128)(2,1)S(1)}, u32[]{:S(2)}, u32[]{:S(2)}) collective-permute-start(bf16[128,512]{1,0:T(8,128)(2,1)S(1)} %collective-permute-done.21.refs_0_), channel_id=1, source_target_pairs={{0,1},{1,0},{2,3},{3,2},{4,5},{5,4},{6,7},{7,6},{8,9},{9,8},{10,11... | collective-permute-start | bytes 393224 | tf_op jit(solution)/shard_map/gather_residual/ppermute | solution.py:149
  90.5 7.3 %collective-permute-start.35 = (bf16[128,512]{1,0:T(8,128)(2,1)S(1)}, bf16[128,512]{1,0:T(8,128)(2,1)S(1)}, u32[]{:S(2)}, u32[]{:S(2)}) collective-permute-start(bf16[128,512]{1,0:T(8,128)(2,1)S(1)} %collective-permute-done.22.refs_4_), channel_id=1, source_target_pairs={{0,1},{1,0},{2,3},{3,2},{4,5},{5,4},{6,7},{7,6},{8,9},{9,8},{10,11... | collective-permute-start | bytes 393224 | tf_op jit(solution)/shard_map/gather_residual/ppermute | solution.py:149
  91.0 6.3 %collective-permute-start.26 = (bf16[128,512]{1,0:T(8,128)(2,1)S(1)}, bf16[128,512]{1,0:T(8,128)(2,1)S(1)}, u32[]{:S(2)}, u32[]{:S(2)}) collective-permute-start(bf16[128,512]{1,0:T(8,128)(2,1)S(1)} %collective-permute-done.22.refs_4_), channel_id=1, source_target_pairs={{0,2},{1,3},{2,0},{3,1},{4,6},{5,7},{6,4},{7,5},{8,10},{9,11},{10,... | collective-permute-start | bytes 393224 | tf_op jit(solution)/shard_map/gather_residual/ppermute | solution.py:149
  97.2 1.4 collective-permute-start.34
  97.3 1.5 %collective-permute-start.32 = (bf16[128,512]{1,0:T(8,128)(2,1)S(1)}, bf16[128,512]{1,0:T(8,128)(2,1)S(1)}, u32[]{:S(2)}, u32[]{:S(2)}) collective-permute-start(bf16[128,512]{1,0:T(8,128)(2,1)S(1)} %collective-permute-done.26.refs_6_), channel_id=1, source_target_pairs={{0,1},{1,0},{2,3},{3,2},{4,5},{5,4},{6,7},{7,6},{8,9},{9,8},{10,11... | collective-permute-start | bytes 393224 | tf_op jit(solution)/shard_map/gather_residual/ppermute | solution.py:149
  109.8 2.6 %collective-permute-start.36 = (bf16[512,512]{1,0:T(8,128)(2,1)S(1)}, bf16[512,512]{1,0:T(8,128)(2,1)S(1)}, u32[]{:S(2)}, u32[]{:S(2)}) collective-permute-start(bf16[512,512]{1,0:T(8,128)(2,1)S(1)} %get-tuple-element.115), channel_id=1, source_target_pairs={{0,1},{1,0},{2,3},{3,2},{4,5},{5,4},{6,7},{7,6},{8,9},{9,8},{10,11... | collective-permute-start | bytes 1572872 | tf_op jit(solution)/shard_map/sum_over_devices/ppermute | solution.py:149
  110.1 9.6 %collective-permute-start.37 = (bf16[512,512]{1,0:T(8,128)(2,1)}, bf16[512,512]{1,0:T(8,128)(2,1)S(1)}, u32[]{:S(2)}, u32[]{:S(2)}) collective-permute-start(bf16[512,512]{1,0:T(8,128)(2,1)} %get-tuple-element.120), channel_id=1, source_target_pairs={{0,1},{1,0},{2,3},{3,2},{4,5},{5,4},{6,7},{7,6},{8,9},{9,8},{10,11... | collective-permute-start | bytes 1572872 | tf_op jit(solution)/shard_map/sum_over_devices/ppermute | solution.py:149
  113.7 9.3 %collective-permute-start.39 = (bf16[256,512]{1,0:T(8,128)(2,1)}, bf16[256,512]{1,0:T(8,128)(2,1)S(1)}, u32[]{:S(2)}, u32[]{:S(2)}) collective-permute-start(bf16[256,512]{1,0:T(8,128)(2,1)} %get-tuple-element.117), channel_id=1, source_target_pairs={{0,2},{1,3},{2,0},{3,1},{4,6},{5,7},{6,4},{7,5},{8,10},{9,11},{10,... | collective-permute-start | bytes 786440 | tf_op jit(solution)/shard_map/sum_over_devices/ppermute | solution.py:149
  114.7 13.5 %collective-permute-start.38 = (bf16[256,512]{1,0:T(8,128)(2,1)S(1)}, bf16[256,512]{1,0:T(8,128)(2,1)}, u32[]{:S(2)}, u32[]{:S(2)}) collective-permute-start(bf16[256,512]{1,0:T(8,128)(2,1)S(1)} %get-tuple-element.118), channel_id=1, source_target_pairs={{0,2},{1,3},{2,0},{3,1},{4,6},{5,7},{6,4},{7,5},{8,10},{9,11},{10,... | collective-permute-start | bytes 786440 | tf_op jit(solution)/shard_map/sum_over_devices/ppermute | solution.py:149
  123.7 7.7 %collective-permute-start.41 = (bf16[128,512]{1,0:T(8,128)(2,1)S(1)}, bf16[128,512]{1,0:T(8,128)(2,1)S(1)}, u32[]{:S(2)}, u32[]{:S(2)}) collective-permute-start(bf16[128,512]{1,0:T(8,128)(2,1)S(1)} %get-tuple-element.127), channel_id=1, source_target_pairs={{0,12},{4,8},{8,4},{12,0},{1,13},{5,9},{9,5},{13,1},{2,14},{6,10},... | collective-permute-start | bytes 393224 | tf_op jit(solution)/shard_map/sum_over_devices/ppermute | solution.py:149
  126.1 12.0 %collective-permute-start.40 = (bf16[128,512]{1,0:T(8,128)(2,1)S(1)}, bf16[128,512]{1,0:T(8,128)(2,1)S(1)}, u32[]{:S(2)}, u32[]{:S(2)}) collective-permute-start(bf16[128,512]{1,0:T(8,128)(2,1)S(1)} %get-tuple-element.126), channel_id=1, source_target_pairs={{0,8},{4,12},{8,0},{12,4},{1,9},{5,13},{9,1},{13,5},{2,10},{6,14},... | collective-permute-start | bytes 393224 | tf_op jit(solution)/shard_map/sum_over_devices/ppermute | solution.py:149
  129.2 8.9 %collective-permute-start.42 = (bf16[128,512]{1,0:T(8,128)(2,1)S(1)}, bf16[128,512]{1,0:T(8,128)(2,1)S(1)}, u32[]{:S(2)}, u32[]{:S(2)}) collective-permute-start(bf16[128,512]{1,0:T(8,128)(2,1)S(1)} %get-tuple-element.128), channel_id=1, source_target_pairs={{0,4},{4,0},{8,12},{12,8},{1,5},{5,1},{9,13},{13,9},{2,6},{6,2},{1... | collective-permute-start | bytes 393224 | tf_op jit(solution)/shard_map/sum_over_devices/ppermute | solution.py:149

commit v7 on v6

--- a/solution.py
+++ b/solution.py
@@ -211,56 +211,66 @@
         copy.wait()
 
 
-def attend_kernel(n, pos, gain, tokens, weight, *rest):
-    x_pieces, rest = rest[:n], rest[n:]
-    w_near, rest = rest[: n - 1], rest[n - 1 :]
-    w_far, rest = rest[: n - 1], rest[n - 1 :]
-    attended, (x_share, x_all, w_all, projected, sems) = rest[:n], rest[n:]
+def project_tokens_kernel(n, pos, gain, tokens, weight, *rest):
+    x_pieces, w_near, w_far = rest[:n], rest[n : 2 * n - 1], rest[2 * n - 1 : 3 * n - 3]
+    partial, x_last, x_share, x_all, w_all, x_sems, w_sems = rest[3 * n - 3 :]
     g, s, h = pos[0], pos[1], pos[2]
     rows, width = tokens.shape
     cols = width // n
     depth, half = weight.shape[1], w_near[0].shape[0]
-    total = n * rows
-
-    def at_rows(block, size):
-        return pl.ds(pl.multiple_of(block * size, size), size)
-
-    copies = [(tokens, x_all.at[at_rows(s, rows)])]
+    missing = (s ^ (n - 1)) * 2 + (1 - g)
+    x_copies = [(tokens, x_all.at[span(s, rows)])]
     for d in range(1, n):
         for e in range(n):
-            copies.append(
-                (x_pieces[e].at[d - 1], x_all.at[at_rows(s ^ d, rows), at_rows(h ^ e, cols)])
-            )
-    n_rows = len(copies)
+            target = x_all.at[span(s ^ d, rows), span(h ^ e, cols)]
+            x_copies.append((x_pieces[e].at[d - 1], target))
+    w_copies = []
     for which in range(3):
-        source = weight.at[which, :, at_rows(s, HEAD_DIM)]
-        copies.append((source, w_all.at[at_rows(s, depth), pl.ds(which * HEAD_DIM, HEAD_DIM)]))
+        target = w_all.at[span(s, depth), pl.ds(which * HEAD_DIM, HEAD_DIM)]
+        w_copies.append((weight.at[which, :, span(s, HEAD_DIM)], target))
     for d in range(1, n):
-        copies.append((w_near[d - 1], w_all.at[at_rows((s ^ d) * 2 + g, half)]))
-        copies.append((w_far[d - 1], w_all.at[at_rows((s ^ d) * 2 + (1 - g), half)]))
-    copies = [pltpu.make_async_copy(a, b, sems.at[i]) for i, (a, b) in enumerate(copies)]
-    for copy in copies:
+        w_copies.append((w_near[d - 1], w_all.at[span((s ^ d) * 2 + g, half)]))
+        if d < n - 1:
+            w_copies.append((w_far[d - 1], w_all.at[span((s ^ d) * 2 + (1 - g), half)]))
+    x_copies = [
+        pltpu.make_async_copy(a, b, x_sems.at[i]) for i, (a, b) in enumerate(x_copies)
+    ]
+    w_copies = [
+        pltpu.make_async_copy(a, b, w_sems.at[i]) for i, (a, b) in enumerate(w_copies)
+    ]
+    for copy in x_copies + w_copies:
         copy.start()
-    for copy in copies[:n_rows]:
+    w_all[span(missing, half), :] = jnp.zeros((half, w_all.shape[1]), BF16)
+    for copy in x_copies:
         copy.wait()
-    x_share[...] = x_all[at_rows(h, rows), at_rows(s, cols)]
+    x_share[...] = x_all[span(h, rows), span(s, cols)]
 
     def normalise(block, carry):
-        mine = at_rows(block, rows)
+        mine = span(block, rows)
         wide = x_all[mine, :].astype(F32)
         factor = lax.rsqrt(jnp.mean(wide * wide, axis=-1, keepdims=True) + EPS)
         x_all[mine, :] = (wide * factor * gain[...]).astype(BF16)
         return carry
 
     lax.fori_loop(0, n, normalise, 0)
-    for copy in copies[n_rows:]:
+    x_last[...] = x_all[:, span(missing, half)]
+    for copy in w_copies:
         copy.wait()
-    projected[...] = jnp.dot(x_all[...], w_all[...], preferred_element_type=F32).astype(BF16)
+    partial[...] = jnp.dot(x_all[...], w_all[...], preferred_element_type=F32)
+
+
+def attend_kernel(n, pos, partial, x_last, w_last, *rest):
+    attended, projected = rest[:n], rest[n]
+    h = pos[2]
+    rows = x_last.shape[0] // n
+    projected[...] = (
+        partial[...] + jnp.dot(x_last[...], w_last[...], preferred_element_type=F32)
+    ).astype(BF16)
     key, value = projected[:, HEAD_DIM : 2 * HEAD_DIM], projected[:, 2 * HEAD_DIM :]
     for e in range(n):
         block = h ^ e
         scores = lax.dot_general(
-            projected[at_rows(block, rows), :HEAD_DIM],
+            projected[span(block, rows), :HEAD_DIM],
             key,
             (((1,), (1,)), ((), ())),
             preferred_element_type=F32,
@@ -520,25 +530,36 @@
         out[...] = jnp.dot(place[...], y_slots[...], preferred_element_type=F32).astype(BF16)
 
 
-def add_kernel(distances, pos, base, core, part, *outs):
-    s = pos[1]
+def add_kernel(distances, pos, base, part, *refs):
+    cores, outs = refs[: len(distances)], refs[len(distances) :]
     rows = outs[0].shape[0]
     in_half = part.shape[0] // rows
-    for d, out in zip(distances, outs):
-        block = s ^ d
-        everywhere = pl.ds(pl.multiple_of(block * rows, rows), rows)
-        inside = pl.ds(pl.multiple_of(block % in_half * rows, rows), rows)
-        value = base[everywhere, :].astype(F32) + core[everywhere, :].astype(F32)
-        out[...] = (value + part[inside, :].astype(F32)).astype(out.dtype)
-
-
-def halves_kernel(pos, base, core, far, near):
-    rows = near.shape[0]
-    blocks = base.shape[0] // rows
-    mine = pos[1] // blocks
-    for half, out in ((blocks - 1 - mine, far), (mine, near)):
-        value = base[span(half, rows), :].astype(F32) + core[span(half, rows), :].astype(F32)
-        out[...] = value.astype(out.dtype)
+    for d, core, out in zip(distances, cores, outs):
+        block = pos[1] ^ d
+        value = base[span(block, rows), :].astype(F32) + core[...].astype(F32)
+        out[...] = (value + part[span(block % in_half, rows), :].astype(F32)).astype(out.dtype)
+
+
+def down_blocks_kernel(slots, pos, hidden, place, kept, *refs):
+    outs, (y_slots, whole) = refs[:-2], refs[-2:]
+    rows = outs[0].shape[0]
+    for e in range(kept.shape[0]):
+        mine = slice(e * slots, (e + 1) * slots)
+        product = jnp.dot(hidden[mine, :], kept[e], preferred_element_type=F32)
+        y_slots[mine, :] = product.astype(BF16)
+    whole[...] = jnp.dot(place[...], y_slots[...], preferred_element_type=F32).astype(BF16)
+    for d, out in enumerate(outs):
+        out[...] = whole[span(pos[1] ^ d, rows), :]
+
+
+def cores_kernel(shares, pos, base, core, *outs):
+    rows = outs[0].shape[0] // len(shares[0])
+    for distances, out in zip(shares, outs):
+        for d in distances:
+            block = pos[1] ^ d
+            inside = block % len(distances)
+            value = base[span(block, rows), :].astype(F32) + core[span(block, rows), :].astype(F32)
+            out[span(inside, rows), :] = value.astype(out.dtype)
 
 
 def square_body(
@@ -624,7 +645,10 @@
         x_pieces[2] = swap(x_pieces[0], "head", 2)
         w_far = [swap(w, "grp", 1) for w in w_near]
         w_near.append(swap(w_last, "seq", n - 1))
-        x_pieces[2], w_near[-1], *w_far = in_step(x_pieces[2], w_near[-1], *w_far)
+        late_weights = list(load(late, ahead, w_near[0]))
+        late_weights[0], x_pieces[2], w_near[-1], *w_far = in_step(
+            late_weights[0], x_pieces[2], w_near[-1], *w_far
+        )
         w_far.append(swap(w_near[-1], "grp", 1))
         for e in (0, 2):
             x_pieces[e ^ 1] = swap(x_pieces[e], "head", 1)
@@ -637,29 +661,42 @@
             scratch_shapes=[pltpu.VMEM((2 * TOPK, total), F32)],
             compiler_params=room(16),
         )(pos, x_send, *x_far)
-        with jax.named_scope("expert_weights"):
-            late_weights = load(late, ahead, w_near[-1])
-        w_near[-1] = after(w_near[-1], pick, late_weights[0])
+    with jax.named_scope("gather_out_weights"):
+        w_near[-1] = after(w_near[-1], pick)
         o_own = after(attn_weight, pick)[3]
         o_pieces = {0: o_own, 2: swap(o_own, "head", 2)}
 
-    with jax.named_scope("attention"):
-        *attended, x_share = pl.pallas_call(
-            functools.partial(attend_kernel, n),
-            out_shape=[sds((rows, HEAD_DIM), BF16)] * n + [sds((rows, cols), BF16)],
-            in_specs=[SMEM, VMEM] + [ANY] * (2 + n + 2 * (n - 1) - 1) + [VMEM],
-            out_specs=[VMEM] * (n + 1),
+    with jax.named_scope("projected_tokens"):
+        partial, x_last, x_share = pl.pallas_call(
+            functools.partial(project_tokens_kernel, n),
+            out_shape=[
+                sds((total, 3 * HEAD_DIM), F32),
+                sds((total, half), BF16),
+                sds((rows, cols), BF16),
+            ],
+            in_specs=[SMEM, VMEM] + [ANY] * (2 + n + 2 * (n - 1) - 1),
+            out_specs=[VMEM] * 3,
             scratch_shapes=[
                 pltpu.VMEM((total, width), BF16),
                 pltpu.VMEM((width, 3 * HEAD_DIM), BF16),
-                pltpu.VMEM((total, 3 * HEAD_DIM), BF16),
-                dma((4 + n * (n - 1) + 2 * (n - 1),)),
+                dma((1 + n * (n - 1),)),
+                dma((3 + 2 * (n - 1) - 1,)),
             ],
-            compiler_params=room(14),
+            compiler_params=room(9),
+            cost_estimate=cost(total * width * 3 * HEAD_DIM, 4 * total * width),
         )(
             pos, attn_gain.reshape(1, width), held(tokens), held(attn_weight),
-            *[held(x_pieces[e]) for e in range(n)], *map(held, w_near), *map(held, w_far[:-1]), w_far[-1],
-        )
+            *[held(x_pieces[e]) for e in range(n)], *map(held, w_near), *map(held, w_far[:-1]),
+        )
+    with jax.named_scope("attention"):
+        attended = pl.pallas_call(
+            functools.partial(attend_kernel, n),
+            out_shape=[sds((rows, HEAD_DIM), BF16)] * n,
+            in_specs=[SMEM] + [VMEM] * 3,
+            out_specs=[VMEM] * n,
+            scratch_shapes=[pltpu.VMEM((total, 3 * HEAD_DIM), BF16)],
+            compiler_params=room(6),
+        )(pos, partial, x_last, w_far[-1])
 
     gain_row = moe_gain.reshape(1, width)
 
@@ -694,7 +731,8 @@
     with jax.named_scope("heads_to_tokens"):
         for e in (0, 2):
             o_pieces[e ^ 1] = swap(after(o_pieces[e], attended[0]), "head", 1)
-        arrived = jnp.stack([attended[0]] + [swap(attended[e], "head", e) for e in range(1, n)])
+        arrived = [attended[0]] + [swap(attended[e], "head", e) for e in range(1, n)]
+        arrived = jnp.stack(arrived)
         a_pieces = [arrived, swap(arrived, "seq", 1), swap(arrived, "seq", 2)]
         with jax.named_scope("expert_weights"):
             early_weights = load(early, experts, arrived)
@@ -772,42 +810,52 @@
                     dma((experts // group, 1)),
                 ],
                 compiler_params=room(9),
-                cost_estimate=cost(pairs * cols * (total + hidden), 2 * experts * cols * hidden),
+                cost_estimate=cost(0, 0),
             )(pos, units, place, w_down)
 
     with jax.named_scope("sum_over_devices"):
-        half_line = n // 2
-        out_3, out_1 = down(units, d_3, d_1)
-        core_2, core_0 = swap(out_3, "head", 1), swap(out_1, "head", 1)
+        (out_3,) = down(units, d_3)
+        core_2 = swap(out_3, "head", 1)
         (out_2,) = down(after(units, out_3), d_2)
-        with jax.named_scope("halves_over_cores"):
+        halves = (tuple(range(n // 2, n)), tuple(range(n // 2)))
+        with jax.named_scope("sums_over_cores"):
             near = pl.pallas_call(
-                halves_kernel,
-                out_shape=[sds((half_line * rows, cols), BF16)] * 2,
+                functools.partial(cores_kernel, halves),
+                out_shape=[sds((len(d) * rows, cols), BF16) for d in halves],
                 in_specs=[SMEM] + [VMEM] * 2,
-                out_specs=[VMEM] * 2,
+                out_specs=[VMEM] * len(halves),
                 compiler_params=room(4),
                 cost_estimate=cost(0, 4 * total * cols),
             )(pos, out_2, core_2)
         far = [swap(part, "head", 2) for part in near]
-        out_0 = self_down(after(units, *near), 0)
-
-        def add_parts(scope, distances, part, macs):
-            with jax.named_scope(scope):
+        with jax.named_scope("down_products_by_block"):
+            out_1 = pl.pallas_call(
+                functools.partial(down_blocks_kernel, slots),
+                out_shape=[sds((rows, cols), BF16)] * n,
+                in_specs=[SMEM] + [VMEM] * 3,
+                out_specs=[VMEM] * n,
+                scratch_shapes=[pltpu.VMEM((pairs, cols), BF16), pltpu.VMEM((total, cols), BF16)],
+                compiler_params=room(6),
+                cost_estimate=cost(SLOW, 2 * experts * cols * hidden),
+            )(pos, after(units, *near), place, here(d_1))
+        core_0 = [swap(part, "head", 1) for part in out_1]
+        out_0 = self_down(after(units, out_1[0]), 0)
+
+        def add_parts(distances, part, macs):
+            with jax.named_scope("rows_" + "_".join(map(str, distances))):
                 return pl.pallas_call(
                     functools.partial(add_kernel, distances),
                     out_shape=[sds((rows, cols), BF16 if d else F32) for d in distances],
-                    in_specs=[SMEM] + [VMEM] * 3,
+                    in_specs=[SMEM] + [VMEM] * (2 + len(distances)),
                     out_specs=[VMEM] * len(distances),
                     compiler_params=room(4),
                     cost_estimate=cost(macs, 4 * part.size),
-                )(pos, out_0, core_0, part)
-
-        far_line = tuple(range(half_line, n))
-        near_line = tuple(range(half_line))
-        far_sums = add_parts("far_half_rows", far_line, far[0], 0)
+                )(pos, out_0, part, *[core_0[d] for d in distances])
+
+        far_line, near_line = halves
+        far_sums = add_parts(far_line, far[0], 0)
         from_far = [swap(part, "seq", d) for d, part in zip(far_line, far_sums)]
-        own_sum, *near_sums = add_parts("near_half_rows", near_line, far[1], SLOW)
+        own_sum, *near_sums = add_parts(near_line, far[1], SLOW)
         from_near = [swap(part, "seq", d) for d, part in zip(near_line[1:], near_sums)]
         mixed = plus(lax.select_n(s ^ h, *in_step(*r_choices, own_sum)[:n]), own_sum, *from_far)
         mixed = plus(*in_step(mixed, *from_near))

time: 146 us -> 141 us (0.966)
  waiting for transfers between devices: 43.8 us -> 37.7 us
  Pallas kernels: 48.6 us -> 50.8 us
    pallas_call x1 -> x3, Pallas kernels: 1.32 us -> 9.15 us  [the longest x1 4.94 us: square_body(): pl.pallas_call(functools.partial(project_tokens_kernel, n), out_shape=[sd...]
    ppermute x43 -> x46, waiting for transfers between devices: 43.8 us -> 37.7 us  [swap(): return lax.ppermute(array, axis, [(i, i ^ distance) for i in range(size)])]
    pallas_call x1, Pallas kernels: 5.52 us -> 1.95 us  [square_body(): pl.pallas_call(functools.partial(attend_kernel, n), out_shape=[sds((rows,...]
    pallas_call x2, Pallas kernels: 6.4 us -> 4.2 us  [down(): pl.pallas_call(functools.partial(down_kernel, slots), out_shape=[sds((tot...]
    ppermute x43 -> x46, starting transfers between devices: 43.2 us -> 42.4 us  [swap(): return lax.ppermute(array, axis, [(i, i ^ distance) for i in range(size)])]
  transfers between devices with their start and end apart: 43 -> 46, of which waited for: 18 -> 17; matrix products, arithmetic and copies ran while one was open for 1% -> 1% of each run, Pallas kernels for 24% -> 27%
where the time goes in v7:
time: 141 us
  Pallas kernels  50.8 us (36%)
  starting transfers between devices  42.4 us (30%)
  waiting for transfers between devices  37.7 us (27%)
  blocking collectives  6.51 us (5%)
  local copies, waits for them, and re-layouts  2.7 us (2%)
    ppermute x46, starting transfers between devices, swap(): return lax.ppermute(array, axis, [(i, i ^ distance) for i in range(size)])  42.4 us
    ppermute x46, waiting for transfers between devices, swap(): return lax.ppermute(array, axis, [(i, i ^ distance) for i in range(size)])  37.7 us
    pallas_call x2, Pallas kernels, load(): pl.pallas_call(functools.partial(load_kernel, group, distances), out_shap...  10.5 us
    pallas_call x1, Pallas kernels, last_hidden(): pl.pallas_call(functools.partial(last_hidden_kernel, n, slots, group, lat...  6.67 us
    all_gather x1, blocking collectives, square_body(): return lax.all_gather(mixed, 'head', axis=1, tiled=True)  6.51 us
    pallas_call x1, Pallas kernels, first_hidden(): pl.pallas_call(functools.partial(first_hidden_kernel, n, slots, group, ea...  5.17 us
    pallas_call x1, Pallas kernels, square_body(): pl.pallas_call(functools.partial(project_tokens_kernel, n), out_shape=[sd...  4.94 us
    pallas_call x2, Pallas kernels, down(): pl.pallas_call(functools.partial(down_kernel, slots), out_shape=[sds((tot...  4.2 us
  transfers between devices with their start and end apart: 46, of which 17 were waited for; matrix products, arithmetic and copies ran while one was open for 1% of the time, Pallas kernels for 27%

profile of v7, /device:TPU:0, one launch (start us, length us, event | category | flops | bytes accessed | tf_op | source)
XLA Modules:
  0.0 140.8 jit_solution(2286518713544826353)
XLA Ops:
  0.1 1.8 %cut_pieces.1 = (bf16[144,512]{1,0:T(8,128)(2,1)S(1)}, bf16[256,384]{1,0:T(8,128)(2,1)S(1)}, bf16[256,384]{1,0:T(8,128)(2,1)S(1)}, bf16[256,384]{1,0:T(8,128)(2,1)S(1)}) custom-call(s32[3]{0:T(128)S(1)} %pad_add_fusion.pos, s32[8,128]{1,0:T(8,128)} %bitcast.26, f32[8,128]{1,0:T(8,128)} %bitcast.27, bf16[128,2048]{1,0:T(8,128)(2,1)} %tokens.3, ...), custom_call_target="tpu_custom_call" | custom-call | tf_op jit(solution)/shard_map/cut_pieces/pallas_call | solution.py:595
  1.9 3.1 %collective-permute-start.3 = (bf16[256,384]{1,0:T(8,128)(2,1)S(1)}, bf16[256,384]{1,0:T(8,128)(2,1)S(1)}, u32[]{:S(2)}, u32[]{:S(2)}) collective-permute-start(bf16[256,384]{1,0:T(8,128)(2,1)S(1)} %get-tuple-element.75), channel_id=1, source_target_pairs={{0,4},{4,0},{8,12},{12,8},{1,5},{5,1},{9,13},{13,9},{2,6},{6,2},{1... | collective-permute-start | bytes 589832 | tf_op jit(solution)/shard_map/gather_tokens_and_weights/ppermute | solution.py:149
  5.0 2.6 %collective-permute-start.4 = (bf16[256,384]{1,0:T(8,128)(2,1)S(1)}, bf16[256,384]{1,0:T(8,128)(2,1)S(1)}, u32[]{:S(2)}, u32[]{:S(2)}) collective-permute-start(bf16[256,384]{1,0:T(8,128)(2,1)S(1)} %get-tuple-element.76), channel_id=1, source_target_pairs={{0,8},{4,12},{8,0},{12,4},{1,9},{5,13},{9,1},{13,5},{2,10},{6,14},... | collective-permute-start | bytes 589832 | tf_op jit(solution)/shard_map/gather_tokens_and_weights/ppermute | solution.py:149
  7.6 0.4 collective-permute-start
  8.0 3.9 %collective-permute-start.2 = (bf16[144,512]{1,0:T(8,128)(2,1)S(1)}, bf16[144,512]{1,0:T(8,128)(2,1)S(1)}, u32[]{:S(2)}, u32[]{:S(2)}) collective-permute-start(bf16[144,512]{1,0:T(8,128)(2,1)S(1)} %get-tuple-element.74.refs_0_), channel_id=1, source_target_pairs={{0,12},{4,8},{8,4},{12,0},{1,13},{5,9},{9,5},{13,1},{2,14},{6,10},... | collective-permute-start | bytes 442376 | tf_op jit(solution)/shard_map/gather_tokens_and_weights/ppermute | solution.py:149
  12.0 7.3 %collective-permute-done.refs_1_ = bf16[144,512]{1,0:T(8,128)(2,1)S(1)} collective-permute-done((bf16[144,512]{1,0:T(8,128)(2,1)S(1)}, bf16[144,512]{1,0:T(8,128)(2,1)S(1)}, u32[]{:S(2)}, u32[]{:S(2)}) %collective-permute-start) | collective-permute-done | bytes 147488 | tf_op jit(solution)/shard_map/gather_tokens_and_weights/ppermute | solution.py:149
  19.3 8.1 %collective-permute-done.1.refs_2_ = bf16[144,512]{1,0:T(8,128)(2,1)S(1)} collective-permute-done((bf16[144,512]{1,0:T(8,128)(2,1)S(1)}, bf16[144,512]{1,0:T(8,128)(2,1)S(1)}, u32[]{:S(2)}, u32[]{:S(2)}) %collective-permute-start.1) | collective-permute-done | bytes 147488 | tf_op jit(solution)/shard_map/gather_tokens_and_weights/ppermute | solution.py:149
  27.6 1.6 %collective-permute-start.6 = (bf16[3,128,512]{2,1,0:T(8,128)(2,1)S(1)}, bf16[3,128,512]{2,1,0:T(8,128)(2,1)S(1)}, u32[]{:S(2)}, u32[]{:S(2)}) collective-permute-start(bf16[3,128,512]{2,1,0:T(8,128)(2,1)S(1)} %pad_maximum_fusion.rest_0_), channel_id=1, source_target_pairs={{0,2},{1,3},{2,0},{3,1},{4,6},{5,7},{6,4},{7,5},{8,10},{9,11},{10,... | collective-permute-start | bytes 1179656 | tf_op jit(solution)/shard_map/gather_tokens_and_weights/ppermute | solution.py:149
  29.1 1.3 routing.1
  30.5 2.5 %collective-permute-start.7 = (bf16[256,384]{1,0:T(8,128)(2,1)S(1)}, bf16[256,384]{1,0:T(8,128)(2,1)S(1)}, u32[]{:S(2)}, u32[]{:S(2)}) collective-permute-start(bf16[256,384]{1,0:T(8,128)(2,1)S(1)} %get-tuple-element.84), channel_id=1, source_target_pairs={{0,12},{4,8},{8,4},{12,0},{1,13},{5,9},{9,5},{13,1},{2,14},{6,10},... | collective-permute-start | bytes 589832 | tf_op jit(solution)/shard_map/gather_tokens_and_weights/ppermute | solution.py:149
  33.0 1.5 %collective-permute-start.8 = (bf16[256,384]{1,0:T(8,128)(2,1)S(1)}, bf16[256,384]{1,0:T(8,128)(2,1)S(1)}, u32[]{:S(2)}, u32[]{:S(2)}) collective-permute-start(bf16[256,384]{1,0:T(8,128)(2,1)S(1)} %collective-permute-done.3.rest_4_), channel_id=1, source_target_pairs={{0,16},{16,0},{1,17},{17,1},{2,18},{18,2},{3,19},{19,3},{4,20},{20... | collective-permute-start | bytes 589832 | tf_op jit(solution)/shard_map/gather_tokens_and_weights/ppermute | solution.py:149
  34.5 0.5 collective-permute-start.9
  35.0 1.1 slice_bitcast_fusion.refs_0_
  36.1 0.6 collective-permute-start.17
  36.7 4.0 %gather_tokens_and_weights.1 = (bf16[8,1024,256]{2,1,0:T(8,128)(2,1)S(1)}, bf16[8,1024,256]{2,1,0:T(8,128)(2,1)S(1)}) custom-call(s32[3]{0:T(128)S(1)} %pad_add_fusion.pos, bf16[16,2048,256]{2,1,0:T(8,128)(2,1)} %w_gate.5, bf16[16,2048,256]{2,1,0:T(8,128)(2,1)} %w_up.5), custom_call_target="tpu_custom_call" | custom-call | bytes 8388608 | tf_op jit(solution)/shard_map/gather_tokens_and_weights/pallas_call | solution.py:617
  40.9 0.5 collective-permute-start.10
  41.5 1.5 %collective-permute-start.11 = (bf16[256,384]{1,0:T(8,128)(2,1)S(1)}, bf16[256,384]{1,0:T(8,128)(2,1)S(1)}, u32[]{:S(2)}, u32[]{:S(2)}) collective-permute-start(bf16[256,384]{1,0:T(8,128)(2,1)S(1)} %collective-permute-done.7.rest_6_), channel_id=1, source_target_pairs={{0,16},{16,0},{1,17},{17,1},{2,18},{18,2},{3,19},{19,3},{4,20},{20... | collective-permute-start | bytes 589832 | tf_op jit(solution)/shard_map/gather_tokens_and_weights/ppermute | solution.py:149
  43.2 0.6 copy-done.4
  43.9 4.9 %projected_tokens.1 = (f32[512,384]{1,0:T(8,128)S(1)}, bf16[512,256]{1,0:T(8,128)(2,1)S(1)}, bf16[128,512]{1,0:T(8,128)(2,1)S(1)}) custom-call(s32[3]{0:T(128)S(1)} %pad_add_fusion.pos, f32[1,2048]{1,0:T(1,128)S(1)} %bitcast.22, bf16[128,2048]{1,0:T(8,128)(2,1)} %tokens.3, bf16[4,512,512]{2,1,0:T(8,128)(2,1)} %weight.3, bf16[3,128,512]{2,1,0:T(8,128)(2,1)} %copy-done.2, ...), custom_call_target="tpu_custom_call" | custom-call | flops 805306368 | bytes 4194304 | tf_op jit(solution)/shard_map/projected_tokens/pallas_call | solution.py:670
  48.9 2.0 %attention.1 = (bf16[128,128]{1,0:T(8,128)(2,1)S(1)}, bf16[128,128]{1,0:T(8,128)(2,1)S(1)}, bf16[128,128]{1,0:T(8,128)(2,1)S(1)}, bf16[128,128]{1,0:T(8,128)(2,1)S(1)}) custom-call(s32[3]{0:T(128)S(1)} %pad_add_fusion.pos, f32[512,384]{1,0:T(8,128)S(1)} %get-tuple-element.93.partial, bf16[512,256]{1,0:T(8,128)(2,1)S(1)} %get-tuple-element.94.x_last, ...), custom_call_target="tpu_custom_call" | custom-call | tf_op jit(solution)/shard_map/attention/pallas_call | solution.py:692
  51.0 0.4 collective-permute-start.18
  51.4 1.2 collective-permute-start.14
  52.6 0.5 collective-permute-start.13
  53.3 1.5 %collective-permute-done.14 = bf16[128,128]{1,0:T(8,128)(2,1)S(1)} collective-permute-done((bf16[128,128]{1,0:T(8,128)(2,1)S(1)}, bf16[128,128]{1,0:T(8,128)(2,1)S(1)}, u32[]{:S(2)}, u32[]{:S(2)}) %collective-permute-start.14) | collective-permute-done | bytes 32800 | tf_op jit(solution)/shard_map/heads_to_tokens/ppermute | solution.py:149
  54.8 1.7 %collective-permute-done.13 = bf16[128,128]{1,0:T(8,128)(2,1)S(1)} collective-permute-done((bf16[128,128]{1,0:T(8,128)(2,1)S(1)}, bf16[128,128]{1,0:T(8,128)(2,1)S(1)}, u32[]{:S(2)}, u32[]{:S(2)}) %collective-permute-start.13) | collective-permute-done | bytes 32800 | tf_op jit(solution)/shard_map/heads_to_tokens/ppermute | solution.py:149
  56.6 1.7 %collective-permute-start.15 = (bf16[4,128,128]{2,1,0:T(8,128)(2,1)S(1)}, bf16[4,128,128]{2,1,0:T(8,128)(2,1)S(1)}, u32[]{:S(2)}, u32[]{:S(2)}) collective-permute-start(bf16[4,128,128]{2,1,0:T(8,128)(2,1)S(1)} %pad_maximum_fusion.1.rest_4_), channel_id=1, source_target_pairs={{0,8},{4,12},{8,0},{12,4},{1,9},{5,13},{9,1},{13,5},{2,10},{6,14},... | collective-permute-start | bytes 393224 | tf_op jit(solution)/shard_map/heads_to_tokens/ppermute | solution.py:149
  58.6 6.5 %expert_weights.2 = (bf16[16,1024,256]{2,1,0:T(8,128)(2,1)S(1)}, bf16[16,1024,256]{2,1,0:T(8,128)(2,1)S(1)}) custom-call(s32[3]{0:T(128)S(1)} %pad_add_fusion.pos, bf16[16,2048,256]{2,1,0:T(8,128)(2,1)} %w_gate.5, bf16[16,2048,256]{2,1,0:T(8,128)(2,1)} %w_up.5), custom_call_target="tpu_custom_call" | custom-call | bytes 16777216 | tf_op jit(solution)/shard_map/heads_to_tokens/expert_weights/pallas_call | solution.py:617
  65.1 1.8 %collective-permute-start.20 = (bf16[4,128,128]{2,1,0:T(8,128)(2,1)S(1)}, bf16[4,128,128]{2,1,0:T(8,128)(2,1)S(1)}, u32[]{:S(2)}, u32[]{:S(2)}) collective-permute-start(bf16[4,128,128]{2,1,0:T(8,128)(2,1)S(1)} %collective-permute-done.15.rest_6_), channel_id=1, source_target_pairs={{0,4},{4,0},{8,12},{12,8},{1,5},{5,1},{9,13},{13,9},{2,6},{6,2},{1... | collective-permute-start | bytes 393224 | tf_op jit(solution)/shard_map/heads_to_tokens/ppermute | solution.py:149
  66.9 2.8 %expert_weights.3.refs_0_ = bf16[16,256,512]{2,1,0:T(8,128)(2,1)S(1)} custom-call(s32[3]{0:T(128)S(1)} %pad_add_fusion.pos, bf16[16,256,2048]{2,1,0:T(8,128)(2,1)} %w_down.5), custom_call_target="tpu_custom_call" | custom-call | bytes 4194304 | tf_op jit(solution)/shard_map/heads_to_tokens/expert_weights/pallas_call | solution.py:629
  70.1 1.3 output_projection.1.refs_0_
  71.4 2.6 %collective-permute-start.21 = (bf16[128,512]{1,0:T(8,128)(2,1)S(1)}, bf16[128,512]{1,0:T(8,128)(2,1)S(1)}, u32[]{:S(2)}, u32[]{:S(2)}) collective-permute-start(bf16[128,512]{1,0:T(8,128)(2,1)S(1)} %output_projection.1.refs_0_), channel_id=1, source_target_pairs={{0,8},{4,12},{8,0},{12,4},{1,9},{5,13},{9,1},{13,5},{2,10},{6,14},... | collective-permute-start | bytes 393224 | tf_op jit(solution)/shard_map/gather_residual/ppermute | solution.py:149
  74.0 0.5 collective-permute-start.24
  74.6 0.9 collective-permute-start.28
  75.4 3.5 %collective-permute-done.21.refs_0_ = bf16[128,512]{1,0:T(8,128)(2,1)S(1)} collective-permute-done((bf16[128,512]{1,0:T(8,128)(2,1)S(1)}, bf16[128,512]{1,0:T(8,128)(2,1)S(1)}, u32[]{:S(2)}, u32[]{:S(2)}) %collective-permute-start.21) | collective-permute-done | bytes 131104 | tf_op jit(solution)/shard_map/gather_residual/ppermute | solution.py:149
  79.2 1.0 collective-permute-done.24.refs_4_
  80.2 1.1 collective-permute-start.30
  81.4 0.9 collective-permute-start.23
  82.3 0.5 collective-permute-start.29
  82.8 1.2 collective-permute-done.22.refs_4_
  83.9 1.3 collective-permute-done.30.refs_6_
  85.2 1.4 collective-permute-done.23.refs_2_
  86.6 0.5 collective-permute-start.35
  87.1 1.1 collective-permute-start.26
  88.3 5.2 %first_hidden_units.1 = (f32[1280,512]{1,0:T(8,128)S(1)}, f32[1280,128]{1,0:T(8,128)S(1)}) custom-call(s32[3]{0:T(128)S(1)} %pad_add_fusion.pos, f32[1,2048]{1,0:T(1,128)S(1)} %bitcast.20, bf16[1280,512]{1,0:T(8,128)(2,1)S(1)} %get-tuple-element.88.pick, bf16[16,1024,256]{2,1,0:T(8,128)(2,1)S(1)} %get-tuple-element.100.g_all, ...), custom_call_target="tpu_custom_call" | custom-call | flops 2684354560 | bytes 16777216 | tf_op jit(solution)/shard_map/gather_residual/first_hidden_units/pallas_call | solution.py:704
  93.5 0.5 collective-permute-start.32
  94.0 0.8 collective-permute-done.34.refs_3_
  95.0 6.7 %last_hidden_units.1 = (bf16[1280,256]{1,0:T(8,128)(2,1)S(1)}, bf16[16,256,512]{2,1,0:T(8,128)(2,1)S(1)}, bf16[16,256,512]{2,1,0:T(8,128)(2,1)S(1)}) custom-call(s32[3]{0:T(128)S(1)} %pad_add_fusion.pos, f32[1,2048]{1,0:T(1,128)S(1)} %bitcast.21, bf16[1280,512]{1,0:T(8,128)(2,1)S(1)} %get-tuple-element.88.pick, bf16[16,2048,256]{2,1,0:T(8,128)(2,1)} %w_gate.5, ...), custom_call_target="tpu_custom_call" | custom-call | flops 2684354560 | bytes 16777216 | tf_op jit(solution)/shard_map/gather_residual/last_hidden_units/pallas_call | solution.py:715
  101.7 2.1 %down_products.2 = bf16[512,512]{1,0:T(8,128)(2,1)S(1)} custom-call(s32[3]{0:T(128)S(1)} %pad_add_fusion.pos, bf16[1280,256]{1,0:T(8,128)(2,1)S(1)} %get-tuple-element.129.hidden, bf16[512,1280]{1,0:T(8,128)(2,1)S(1)} %get-tuple-element.121.place, bf16[16,256,512]{2,1,0:T(8,128)(2,1)S(1)} %get-tuple-element.122.refs_0_), custom_call_target="tpu_custom_call" | custom-call | flops 1006632960 | bytes 4194304 | tf_op jit(solution)/shard_map/sum_over_devices/down_products/pallas_call | solution.py:788
  104.2 2.1 %down_products.3.base = bf16[512,512]{1,0:T(8,128)(2,1)S(1)} custom-call(s32[3]{0:T(128)S(1)} %pad_add_fusion.pos, bf16[1280,256]{1,0:T(8,128)(2,1)S(1)} %get-tuple-element.129.hidden, bf16[512,1280]{1,0:T(8,128)(2,1)S(1)} %get-tuple-element.121.place, bf16[16,256,512]{2,1,0:T(8,128)(2,1)S(1)} %expert_weights.3.refs_0_), custom_call_target="tpu_custom_call" | custom-call | flops 1006632960 | bytes 4194304 | tf_op jit(solution)/shard_map/sum_over_devices/down_products/pallas_call | solution.py:788
  106.3 1.3 sums_over_cores.1
  107.6 0.9 collective-permute-start.40
  108.5 2.9 %down_products_by_block.1 = (bf16[128,512]{1,0:T(8,128)(2,1)}, bf16[128,512]{1,0:T(8,128)(2,1)}, bf16[128,512]{1,0:T(8,128)(2,1)S(1)}, bf16[128,512]{1,0:T(8,128)(2,1)}) custom-call(s32[3]{0:T(128)S(1)} %pad_add_fusion.pos, bf16[1280,256]{1,0:T(8,128)(2,1)S(1)} %get-tuple-element.129.hidden, bf16[512,1280]{1,0:T(8,128)(2,1)S(1)} %get-tuple-element.121.place, ...), custom_call_target="tpu_custom_call" | custom-call | flops 20000000000 | bytes 4194304 | tf_op jit(solution)/shard_map/sum_over_devices/down_products_by_block/pallas_call | solution.py:832
  111.4 1.1 collective-permute-start.37
  113.3 3.9 %down_products_alone.1.base = bf16[512,512]{1,0:T(8,128)(2,1)S(1)} custom-call(s32[3]{0:T(128)S(1)} %pad_add_fusion.pos, bf16[1280,256]{1,0:T(8,128)(2,1)S(1)} %get-tuple-element.129.hidden, bf16[512,1280]{1,0:T(8,128)(2,1)S(1)} %get-tuple-element.121.place, bf16[16,256,2048]{2,1,0:T(8,128)(2,1)} %w_down.5), custom_call_target="tpu_custom_call" | custom-call | tf_op jit(solution)/shard_map/sum_over_devices/down_products_alone/pallas_call | solution.py:802
  117.3 0.6 rows_2_3.1
  117.9 1.8 %collective-permute-start.44 = (bf16[128,512]{1,0:T(8,128)(2,1)S(1)}, bf16[128,512]{1,0:T(8,128)(2,1)S(1)}, u32[]{:S(2)}, u32[]{:S(2)}) collective-permute-start(bf16[128,512]{1,0:T(8,128)(2,1)S(1)} %get-tuple-element.139), channel_id=1, source_target_pairs={{0,12},{4,8},{8,4},{12,0},{1,13},{5,9},{9,5},{13,1},{2,14},{6,10},... | collective-permute-start | bytes 393224 | tf_op jit(solution)/shard_map/sum_over_devices/ppermute | solution.py:149
  119.7 1.5 %collective-permute-start.43 = (bf16[128,512]{1,0:T(8,128)(2,1)S(1)}, bf16[128,512]{1,0:T(8,128)(2,1)S(1)}, u32[]{:S(2)}, u32[]{:S(2)}) collective-permute-start(bf16[128,512]{1,0:T(8,128)(2,1)S(1)} %get-tuple-element.138), channel_id=1, source_target_pairs={{0,8},{4,12},{8,0},{12,4},{1,9},{5,13},{9,1},{13,5},{2,10},{6,14},... | collective-permute-start | bytes 393224 | tf_op jit(solution)/shard_map/sum_over_devices/ppermute | solution.py:149
  121.2 0.6 collective-permute-done.37.part
  121.9 1.1 rows_0_1.1
  122.9 1.8 %collective-permute-start.45 = (bf16[128,512]{1,0:T(8,128)(2,1)S(1)}, bf16[128,512]{1,0:T(8,128)(2,1)S(1)}, u32[]{:S(2)}, u32[]{:S(2)}) collective-permute-start(bf16[128,512]{1,0:T(8,128)(2,1)S(1)} %get-tuple-element.140), channel_id=1, source_target_pairs={{0,4},{4,0},{8,12},{12,8},{1,5},{5,1},{9,13},{13,9},{2,6},{6,2},{1... | collective-permute-start | bytes 393224 | tf_op jit(solution)/shard_map/sum_over_devices/ppermute | solution.py:149
  124.8 1.4 %collective-permute-done.44 = bf16[128,512]{1,0:T(8,128)(2,1)S(1)} collective-permute-done((bf16[128,512]{1,0:T(8,128)(2,1)S(1)}, bf16[128,512]{1,0:T(8,128)(2,1)S(1)}, u32[]{:S(2)}, u32[]{:S(2)}) %collective-permute-start.44) | collective-permute-done | bytes 131104 | tf_op jit(solution)/shard_map/sum_over_devices/ppermute | solution.py:149
  126.2 7.1 %collective-permute-done.43 = bf16[128,512]{1,0:T(8,128)(2,1)S(1)} collective-permute-done((bf16[128,512]{1,0:T(8,128)(2,1)S(1)}, bf16[128,512]{1,0:T(8,128)(2,1)S(1)}, u32[]{:S(2)}, u32[]{:S(2)}) %collective-permute-start.43) | collective-permute-done | bytes 131104 | tf_op jit(solution)/shard_map/sum_over_devices/ppermute | solution.py:149
  133.5 6.5 %all_gather.3 = bf16[128,2048]{1,0:T(8,128)(2,1)S(1)} all-gather(bf16[128,512]{1,0:T(8,128)(2,1)S(1)} %add_convert_fusion), channel_id=1, replica_groups=mesh['grp'=2,'seq'=4,'head'=4] {'head'}, dimensions={1}, use_global_device_ids=true | all-gather | bytes 655360 | tf_op jit(solution)/shard_map/gather_columns/all_gather | solution.py:864
  140.0 0.8 copy.11
  (78 shorter events, 3.5 us)
Async XLA Ops:
  1.9 25.5 %collective-permute-start.3 = (bf16[256,384]{1,0:T(8,128)(2,1)S(1)}, bf16[256,384]{1,0:T(8,128)(2,1)S(1)}, u32[]{:S(2)}, u32[]{:S(2)}) collective-permute-start(bf16[256,384]{1,0:T(8,128)(2,1)S(1)} %get-tuple-element.75), channel_id=1, source_target_pairs={{0,4},{4,0},{8,12},{12,8},{1,5},{5,1},{9,13},{13,9},{2,6},{6,2},{1... | collective-permute-start | bytes 589832 | tf_op jit(solution)/shard_map/gather_tokens_and_weights/ppermute | solution.py:149
  5.0 22.4 %collective-permute-start.4 = (bf16[256,384]{1,0:T(8,128)(2,1)S(1)}, bf16[256,384]{1,0:T(8,128)(2,1)S(1)}, u32[]{:S(2)}, u32[]{:S(2)}) collective-permute-start(bf16[256,384]{1,0:T(8,128)(2,1)S(1)} %get-tuple-element.76), channel_id=1, source_target_pairs={{0,8},{4,12},{8,0},{12,4},{1,9},{5,13},{9,1},{13,5},{2,10},{6,14},... | collective-permute-start | bytes 589832 | tf_op jit(solution)/shard_map/gather_tokens_and_weights/ppermute | solution.py:149
  7.6 11.7 %collective-permute-start = (bf16[144,512]{1,0:T(8,128)(2,1)S(1)}, bf16[144,512]{1,0:T(8,128)(2,1)S(1)}, u32[]{:S(2)}, u32[]{:S(2)}) collective-permute-start(bf16[144,512]{1,0:T(8,128)(2,1)S(1)} %get-tuple-element.74.refs_0_), channel_id=1, source_target_pairs={{0,4},{4,0},{8,12},{12,8},{1,5},{5,1},{9,13},{13,9},{2,6},{6,2},{1... | collective-permute-start | bytes 442376 | tf_op jit(solution)/shard_map/gather_tokens_and_weights/ppermute | solution.py:149
  8.0 19.4 %collective-permute-start.1 = (bf16[144,512]{1,0:T(8,128)(2,1)S(1)}, bf16[144,512]{1,0:T(8,128)(2,1)S(1)}, u32[]{:S(2)}, u32[]{:S(2)}) collective-permute-start(bf16[144,512]{1,0:T(8,128)(2,1)S(1)} %get-tuple-element.74.refs_0_), channel_id=1, source_target_pairs={{0,8},{4,12},{8,0},{12,4},{1,9},{5,13},{9,1},{13,5},{2,10},{6,14},... | collective-permute-start | bytes 442376 | tf_op jit(solution)/shard_map/gather_tokens_and_weights/ppermute | solution.py:149
  8.0 19.4 %collective-permute-start.2 = (bf16[144,512]{1,0:T(8,128)(2,1)S(1)}, bf16[144,512]{1,0:T(8,128)(2,1)S(1)}, u32[]{:S(2)}, u32[]{:S(2)}) collective-permute-start(bf16[144,512]{1,0:T(8,128)(2,1)S(1)} %get-tuple-element.74.refs_0_), channel_id=1, source_target_pairs={{0,12},{4,8},{8,4},{12,0},{1,13},{5,9},{9,5},{13,1},{2,14},{6,10},... | collective-permute-start | bytes 442376 | tf_op jit(solution)/shard_map/gather_tokens_and_weights/ppermute | solution.py:149
  27.4 13.3 %copy-start.6 = (bf16[256,384]{1,0:T(8,128)(2,1)}, bf16[256,384]{1,0:T(8,128)(2,1)S(1)}, u32[]{:S(2)}) copy-start(bf16[256,384]{1,0:T(8,128)(2,1)S(1)} %collective-permute-done.3.rest_4_) | copy-start | bytes 589828
  27.4 13.3 %copy-start.7 = (bf16[256,384]{1,0:T(8,128)(2,1)}, bf16[256,384]{1,0:T(8,128)(2,1)S(1)}, u32[]{:S(2)}) copy-start(bf16[256,384]{1,0:T(8,128)(2,1)S(1)} %collective-permute-done.4.rest_5_) | copy-start | bytes 589828
  27.6 13.2 %copy-start.2 = (bf16[3,128,512]{2,1,0:T(8,128)(2,1)}, bf16[3,128,512]{2,1,0:T(8,128)(2,1)S(1)}, u32[]{:S(2)}) copy-start(bf16[3,128,512]{2,1,0:T(8,128)(2,1)S(1)} %pad_maximum_fusion.rest_0_) | copy-start | bytes 1179652
  27.6 13.4 %collective-permute-start.6 = (bf16[3,128,512]{2,1,0:T(8,128)(2,1)S(1)}, bf16[3,128,512]{2,1,0:T(8,128)(2,1)S(1)}, u32[]{:S(2)}, u32[]{:S(2)}) collective-permute-start(bf16[3,128,512]{2,1,0:T(8,128)(2,1)S(1)} %pad_maximum_fusion.rest_0_), channel_id=1, source_target_pairs={{0,2},{1,3},{2,0},{3,1},{4,6},{5,7},{6,4},{7,5},{8,10},{9,11},{10,... | collective-permute-start | bytes 1179656 | tf_op jit(solution)/shard_map/gather_tokens_and_weights/ppermute | solution.py:149
  30.5 10.3 %collective-permute-start.7 = (bf16[256,384]{1,0:T(8,128)(2,1)S(1)}, bf16[256,384]{1,0:T(8,128)(2,1)S(1)}, u32[]{:S(2)}, u32[]{:S(2)}) collective-permute-start(bf16[256,384]{1,0:T(8,128)(2,1)S(1)} %get-tuple-element.84), channel_id=1, source_target_pairs={{0,12},{4,8},{8,4},{12,0},{1,13},{5,9},{9,5},{13,1},{2,14},{6,10},... | collective-permute-start | bytes 589832 | tf_op jit(solution)/shard_map/gather_tokens_and_weights/ppermute | solution.py:149
  33.0 7.9 %collective-permute-start.8 = (bf16[256,384]{1,0:T(8,128)(2,1)S(1)}, bf16[256,384]{1,0:T(8,128)(2,1)S(1)}, u32[]{:S(2)}, u32[]{:S(2)}) collective-permute-start(bf16[256,384]{1,0:T(8,128)(2,1)S(1)} %collective-permute-done.3.rest_4_), channel_id=1, source_target_pairs={{0,16},{16,0},{1,17},{17,1},{2,18},{18,2},{3,19},{19,3},{4,20},{20... | collective-permute-start | bytes 589832 | tf_op jit(solution)/shard_map/gather_tokens_and_weights/ppermute | solution.py:149
  34.5 6.4 %collective-permute-start.9 = (bf16[256,384]{1,0:T(8,128)(2,1)S(1)}, bf16[256,384]{1,0:T(8,128)(2,1)S(1)}, u32[]{:S(2)}, u32[]{:S(2)}) collective-permute-start(bf16[256,384]{1,0:T(8,128)(2,1)S(1)} %collective-permute-done.4.rest_5_), channel_id=1, source_target_pairs={{0,16},{16,0},{1,17},{17,1},{2,18},{18,2},{3,19},{19,3},{4,20},{20... | collective-permute-start | bytes 589832 | tf_op jit(solution)/shard_map/gather_tokens_and_weights/ppermute | solution.py:149
  36.1 7.8 %copy-start.1 = (f32[2048]{0:T(1024)S(1)}, f32[2048]{0:T(1024)}, u32[]{:S(2)}) copy-start(f32[2048]{0:T(1024)} %param.11) | copy-start | bytes 24580
  36.1 14.9 %collective-permute-start.17 = (bf16[512,512]{1,0:T(8,128)(2,1)S(1)}, bf16[512,512]{1,0:T(8,128)(2,1)S(1)}, u32[]{:S(2)}, u32[]{:S(2)}) collective-permute-start(bf16[512,512]{1,0:T(8,128)(2,1)S(1)} %slice_bitcast_fusion.refs_0_), channel_id=1, source_target_pairs={{0,2},{1,3},{2,0},{3,1},{4,6},{5,7},{6,4},{7,5},{8,10},{9,11},{10,... | collective-permute-start | bytes 1572872 | tf_op jit(solution)/shard_map/gather_out_weights/ppermute | solution.py:149
  40.8 2.4 %copy-start.8 = (bf16[256,384]{1,0:T(8,128)(2,1)}, bf16[256,384]{1,0:T(8,128)(2,1)S(1)}, u32[]{:S(2)}) copy-start(bf16[256,384]{1,0:T(8,128)(2,1)S(1)} %collective-permute-done.7.rest_6_) | copy-start | bytes 589828
  40.8 2.2 %collective-permute-start.5 = (bf16[3,128,512]{2,1,0:T(8,128)(2,1)S(1)}, bf16[3,128,512]{2,1,0:T(8,128)(2,1)S(1)}, u32[]{:S(2)}, u32[]{:S(2)}) collective-permute-start(bf16[3,128,512]{2,1,0:T(8,128)(2,1)S(1)} %pad_maximum_fusion.rest_0_), channel_id=1, source_target_pairs={{0,1},{1,0},{2,3},{3,2},{4,5},{5,4},{6,7},{7,6},{8,9},{9,8},{10,11... | collective-permute-start | bytes 1179656 | tf_op jit(solution)/shard_map/gather_tokens_and_weights/ppermute | solution.py:149
  40.9 2.3 %copy-start.9 = (bf16[256,384]{1,0:T(8,128)(2,1)}, bf16[256,384]{1,0:T(8,128)(2,1)S(1)}, u32[]{:S(2)}) copy-start(bf16[256,384]{1,0:T(8,128)(2,1)S(1)} %collective-permute-done.8.rest_7_) | copy-start | bytes 589828
  40.9 2.3 %copy-start.10 = (bf16[256,384]{1,0:T(8,128)(2,1)}, bf16[256,384]{1,0:T(8,128)(2,1)S(1)}, u32[]{:S(2)}) copy-start(bf16[256,384]{1,0:T(8,128)(2,1)S(1)} %collective-permute-done.9.rest_8_) | copy-start | bytes 589828
  40.9 2.2 %copy-start.3 = (bf16[3,128,512]{2,1,0:T(8,128)(2,1)}, bf16[3,128,512]{2,1,0:T(8,128)(2,1)S(1)}, u32[]{:S(2)}) copy-start(bf16[3,128,512]{2,1,0:T(8,128)(2,1)S(1)} %collective-permute-done.6.rest_2_) | copy-start | bytes 1179652
  40.9 2.2 %collective-permute-start.10 = (bf16[3,128,512]{2,1,0:T(8,128)(2,1)S(1)}, bf16[3,128,512]{2,1,0:T(8,128)(2,1)S(1)}, u32[]{:S(2)}, u32[]{:S(2)}) collective-permute-start(bf16[3,128,512]{2,1,0:T(8,128)(2,1)S(1)} %collective-permute-done.6.rest_2_), channel_id=1, source_target_pairs={{0,1},{1,0},{2,3},{3,2},{4,5},{5,4},{6,7},{7,6},{8,9},{9,8},{10,11... | collective-permute-start | bytes 1179656 | tf_op jit(solution)/shard_map/gather_tokens_and_weights/ppermute | solution.py:149
  41.5 7.4 %collective-permute-start.11 = (bf16[256,384]{1,0:T(8,128)(2,1)S(1)}, bf16[256,384]{1,0:T(8,128)(2,1)S(1)}, u32[]{:S(2)}, u32[]{:S(2)}) collective-permute-start(bf16[256,384]{1,0:T(8,128)(2,1)S(1)} %collective-permute-done.7.rest_6_), channel_id=1, source_target_pairs={{0,16},{16,0},{1,17},{17,1},{2,18},{18,2},{3,19},{19,3},{4,20},{20... | collective-permute-start | bytes 589832 | tf_op jit(solution)/shard_map/gather_tokens_and_weights/ppermute | solution.py:149
  43.0 0.8 copy-start.4
  43.2 0.8 copy-start.5
  50.9 18.8 %collective-permute-start.16 = (bf16[512,512]{1,0:T(8,128)(2,1)S(1)}, bf16[512,512]{1,0:T(8,128)(2,1)S(1)}, u32[]{:S(2)}, u32[]{:S(2)}) collective-permute-start(bf16[512,512]{1,0:T(8,128)(2,1)S(1)} %slice_bitcast_fusion.refs_0_), channel_id=1, source_target_pairs={{0,1},{1,0},{2,3},{3,2},{4,5},{5,4},{6,7},{7,6},{8,9},{9,8},{10,11... | collective-permute-start | bytes 1572872 | tf_op jit(solution)/shard_map/heads_to_tokens/ppermute | solution.py:149
  51.0 18.6 %collective-permute-start.18 = (bf16[512,512]{1,0:T(8,128)(2,1)S(1)}, bf16[512,512]{1,0:T(8,128)(2,1)S(1)}, u32[]{:S(2)}, u32[]{:S(2)}) collective-permute-start(bf16[512,512]{1,0:T(8,128)(2,1)S(1)} %collective-permute-done.17.refs_2_), channel_id=1, source_target_pairs={{0,1},{1,0},{2,3},{3,2},{4,5},{5,4},{6,7},{7,6},{8,9},{9,8},{10,11... | collective-permute-start | bytes 1572872 | tf_op jit(solution)/shard_map/heads_to_tokens/ppermute | solution.py:149
  51.4 3.4 %collective-permute-start.14 = (bf16[128,128]{1,0:T(8,128)(2,1)S(1)}, bf16[128,128]{1,0:T(8,128)(2,1)S(1)}, u32[]{:S(2)}, u32[]{:S(2)}) collective-permute-start(bf16[128,128]{1,0:T(8,128)(2,1)S(1)} %get-tuple-element.98), channel_id=1, source_target_pairs={{0,3},{1,2},{2,1},{3,0},{4,7},{5,6},{6,5},{7,4},{8,11},{9,10},{10,... | collective-permute-start | bytes 98312 | tf_op jit(solution)/shard_map/heads_to_tokens/ppermute | solution.py:149
  52.6 3.9 %collective-permute-start.13 = (bf16[128,128]{1,0:T(8,128)(2,1)S(1)}, bf16[128,128]{1,0:T(8,128)(2,1)S(1)}, u32[]{:S(2)}, u32[]{:S(2)}) collective-permute-start(bf16[128,128]{1,0:T(8,128)(2,1)S(1)} %get-tuple-element.97), channel_id=1, source_target_pairs={{0,2},{1,3},{2,0},{3,1},{4,6},{5,7},{6,4},{7,5},{8,10},{9,11},{10,... | collective-permute-start | bytes 98312 | tf_op jit(solution)/shard_map/heads_to_tokens/ppermute | solution.py:149
  53.2 3.4 %collective-permute-start.12 = (bf16[128,128]{1,0:T(8,128)(2,1)S(1)}, bf16[128,128]{1,0:T(8,128)(2,1)S(1)}, u32[]{:S(2)}, u32[]{:S(2)}) collective-permute-start(bf16[128,128]{1,0:T(8,128)(2,1)S(1)} %get-tuple-element.96), channel_id=1, source_target_pairs={{0,1},{1,0},{2,3},{3,2},{4,5},{5,4},{6,7},{7,6},{8,9},{9,8},{10,11... | collective-permute-start | bytes 98312 | tf_op jit(solution)/shard_map/heads_to_tokens/ppermute | solution.py:149
  56.6 8.5 %collective-permute-start.15 = (bf16[4,128,128]{2,1,0:T(8,128)(2,1)S(1)}, bf16[4,128,128]{2,1,0:T(8,128)(2,1)S(1)}, u32[]{:S(2)}, u32[]{:S(2)}) collective-permute-start(bf16[4,128,128]{2,1,0:T(8,128)(2,1)S(1)} %pad_maximum_fusion.1.rest_4_), channel_id=1, source_target_pairs={{0,8},{4,12},{8,0},{12,4},{1,9},{5,13},{9,1},{13,5},{2,10},{6,14},... | collective-permute-start | bytes 393224 | tf_op jit(solution)/shard_map/heads_to_tokens/ppermute | solution.py:149
  58.3 11.6 %collective-permute-start.19 = (bf16[4,128,128]{2,1,0:T(8,128)(2,1)S(1)}, bf16[4,128,128]{2,1,0:T(8,128)(2,1)S(1)}, u32[]{:S(2)}, u32[]{:S(2)}) collective-permute-start(bf16[4,128,128]{2,1,0:T(8,128)(2,1)S(1)} %pad_maximum_fusion.1.rest_4_), channel_id=1, source_target_pairs={{0,4},{4,0},{8,12},{12,8},{1,5},{5,1},{9,13},{13,9},{2,6},{6,2},{1... | collective-permute-start | bytes 393224 | tf_op jit(solution)/shard_map/heads_to_tokens/ppermute | solution.py:149
  65.1 5.0 %collective-permute-start.20 = (bf16[4,128,128]{2,1,0:T(8,128)(2,1)S(1)}, bf16[4,128,128]{2,1,0:T(8,128)(2,1)S(1)}, u32[]{:S(2)}, u32[]{:S(2)}) collective-permute-start(bf16[4,128,128]{2,1,0:T(8,128)(2,1)S(1)} %collective-permute-done.15.rest_6_), channel_id=1, source_target_pairs={{0,4},{4,0},{8,12},{12,8},{1,5},{5,1},{9,13},{13,9},{2,6},{6,2},{1... | collective-permute-start | bytes 393224 | tf_op jit(solution)/shard_map/heads_to_tokens/ppermute | solution.py:149
  69.7 18.6 %copy-start = (f32[2048]{0:T(1024)S(1)}, f32[2048]{0:T(1024)}, u32[]{:S(2)}) copy-start(f32[2048]{0:T(1024)} %param.12) | copy-start | bytes 24580
  71.4 7.5 %collective-permute-start.21 = (bf16[128,512]{1,0:T(8,128)(2,1)S(1)}, bf16[128,512]{1,0:T(8,128)(2,1)S(1)}, u32[]{:S(2)}, u32[]{:S(2)}) collective-permute-start(bf16[128,512]{1,0:T(8,128)(2,1)S(1)} %output_projection.1.refs_0_), channel_id=1, source_target_pairs={{0,8},{4,12},{8,0},{12,4},{1,9},{5,13},{9,1},{13,5},{2,10},{6,14},... | collective-permute-start | bytes 393224 | tf_op jit(solution)/shard_map/gather_residual/ppermute | solution.py:149
  74.0 6.2 %collective-permute-start.24 = (bf16[128,512]{1,0:T(8,128)(2,1)S(1)}, bf16[128,512]{1,0:T(8,128)(2,1)S(1)}, u32[]{:S(2)}, u32[]{:S(2)}) collective-permute-start(bf16[128,512]{1,0:T(8,128)(2,1)S(1)} %output_projection.1.refs_0_), channel_id=1, source_target_pairs={{0,4},{4,0},{8,12},{12,8},{1,5},{5,1},{9,13},{13,9},{2,6},{6,2},{1... | collective-permute-start | bytes 393224 | tf_op jit(solution)/shard_map/gather_residual/ppermute | solution.py:149
  74.6 7.7 %collective-permute-start.28 = (bf16[128,512]{1,0:T(8,128)(2,1)S(1)}, bf16[128,512]{1,0:T(8,128)(2,1)S(1)}, u32[]{:S(2)}, u32[]{:S(2)}) collective-permute-start(bf16[128,512]{1,0:T(8,128)(2,1)S(1)} %output_projection.1.refs_0_), channel_id=1, source_target_pairs={{0,2},{1,3},{2,0},{3,1},{4,6},{5,7},{6,4},{7,5},{8,10},{9,11},{10,... | collective-permute-start | bytes 393224 | tf_op jit(solution)/shard_map/gather_residual/ppermute | solution.py:149
  79.0 5.0 %collective-permute-start.22 = (bf16[128,512]{1,0:T(8,128)(2,1)S(1)}, bf16[128,512]{1,0:T(8,128)(2,1)S(1)}, u32[]{:S(2)}, u32[]{:S(2)}) collective-permute-start(bf16[128,512]{1,0:T(8,128)(2,1)S(1)} %collective-permute-done.21.refs_0_), channel_id=1, source_target_pairs={{0,4},{4,0},{8,12},{12,8},{1,5},{5,1},{9,13},{13,9},{2,6},{6,2},{1... | collective-permute-start | bytes 393224 | tf_op jit(solution)/shard_map/gather_residual/ppermute | solution.py:149
  80.2 5.0 %collective-permute-start.30 = (bf16[128,512]{1,0:T(8,128)(2,1)S(1)}, bf16[128,512]{1,0:T(8,128)(2,1)S(1)}, u32[]{:S(2)}, u32[]{:S(2)}) collective-permute-start(bf16[128,512]{1,0:T(8,128)(2,1)S(1)} %collective-permute-done.24.refs_4_), channel_id=1, source_target_pairs={{0,2},{1,3},{2,0},{3,1},{4,6},{5,7},{6,4},{7,5},{8,10},{9,11},{10,... | collective-permute-start | bytes 393224 | tf_op jit(solution)/shard_map/gather_residual/ppermute | solution.py:149
  81.4 5.2 %collective-permute-start.23 = (bf16[128,512]{1,0:T(8,128)(2,1)S(1)}, bf16[128,512]{1,0:T(8,128)(2,1)S(1)}, u32[]{:S(2)}, u32[]{:S(2)}) collective-permute-start(bf16[128,512]{1,0:T(8,128)(2,1)S(1)} %collective-permute-done.21.refs_0_), channel_id=1, source_target_pairs={{0,2},{1,3},{2,0},{3,1},{4,6},{5,7},{6,4},{7,5},{8,10},{9,11},{10,... | collective-permute-start | bytes 393224 | tf_op jit(solution)/shard_map/gather_residual/ppermute | solution.py:149
  82.2 4.4 %collective-permute-start.27 = (bf16[128,512]{1,0:T(8,128)(2,1)S(1)}, bf16[128,512]{1,0:T(8,128)(2,1)S(1)}, u32[]{:S(2)}, u32[]{:S(2)}) collective-permute-start(bf16[128,512]{1,0:T(8,128)(2,1)S(1)} %output_projection.1.refs_0_), channel_id=1, source_target_pairs={{0,1},{1,0},{2,3},{3,2},{4,5},{5,4},{6,7},{7,6},{8,9},{9,8},{10,11... | collective-permute-start | bytes 393224 | tf_op jit(solution)/shard_map/gather_residual/ppermute | solution.py:149
  82.3 4.9 %collective-permute-start.29 = (bf16[128,512]{1,0:T(8,128)(2,1)S(1)}, bf16[128,512]{1,0:T(8,128)(2,1)S(1)}, u32[]{:S(2)}, u32[]{:S(2)}) collective-permute-start(bf16[128,512]{1,0:T(8,128)(2,1)S(1)} %collective-permute-done.28.refs_2_), channel_id=1, source_target_pairs={{0,1},{1,0},{2,3},{3,2},{4,5},{5,4},{6,7},{7,6},{8,9},{9,8},{10,11... | collective-permute-start | bytes 393224 | tf_op jit(solution)/shard_map/gather_residual/ppermute | solution.py:149
  83.9 4.3 %collective-permute-start.25 = (bf16[128,512]{1,0:T(8,128)(2,1)S(1)}, bf16[128,512]{1,0:T(8,128)(2,1)S(1)}, u32[]{:S(2)}, u32[]{:S(2)}) collective-permute-start(bf16[128,512]{1,0:T(8,128)(2,1)S(1)} %collective-permute-done.24.refs_4_), channel_id=1, source_target_pairs={{0,1},{1,0},{2,3},{3,2},{4,5},{5,4},{6,7},{7,6},{8,9},{9,8},{10,11... | collective-permute-start | bytes 393224 | tf_op jit(solution)/shard_map/gather_residual/ppermute | solution.py:149
  85.2 3.1 %collective-permute-start.31 = (bf16[128,512]{1,0:T(8,128)(2,1)S(1)}, bf16[128,512]{1,0:T(8,128)(2,1)S(1)}, u32[]{:S(2)}, u32[]{:S(2)}) collective-permute-start(bf16[128,512]{1,0:T(8,128)(2,1)S(1)} %collective-permute-done.30.refs_6_), channel_id=1, source_target_pairs={{0,1},{1,0},{2,3},{3,2},{4,5},{5,4},{6,7},{7,6},{8,9},{9,8},{10,11... | collective-permute-start | bytes 393224 | tf_op jit(solution)/shard_map/gather_residual/ppermute | solution.py:149
  86.6 7.4 %collective-permute-start.33 = (bf16[128,512]{1,0:T(8,128)(2,1)S(1)}, bf16[128,512]{1,0:T(8,128)(2,1)S(1)}, u32[]{:S(2)}, u32[]{:S(2)}) collective-permute-start(bf16[128,512]{1,0:T(8,128)(2,1)S(1)} %collective-permute-done.21.refs_0_), channel_id=1, source_target_pairs={{0,1},{1,0},{2,3},{3,2},{4,5},{5,4},{6,7},{7,6},{8,9},{9,8},{10,11... | collective-permute-start | bytes 393224 | tf_op jit(solution)/shard_map/gather_residual/ppermute | solution.py:149
  86.6 7.4 %collective-permute-start.35 = (bf16[128,512]{1,0:T(8,128)(2,1)S(1)}, bf16[128,512]{1,0:T(8,128)(2,1)S(1)}, u32[]{:S(2)}, u32[]{:S(2)}) collective-permute-start(bf16[128,512]{1,0:T(8,128)(2,1)S(1)} %collective-permute-done.22.refs_4_), channel_id=1, source_target_pairs={{0,1},{1,0},{2,3},{3,2},{4,5},{5,4},{6,7},{7,6},{8,9},{9,8},{10,11... | collective-permute-start | bytes 393224 | tf_op jit(solution)/shard_map/gather_residual/ppermute | solution.py:149
  87.1 6.4 %collective-permute-start.26 = (bf16[128,512]{1,0:T(8,128)(2,1)S(1)}, bf16[128,512]{1,0:T(8,128)(2,1)S(1)}, u32[]{:S(2)}, u32[]{:S(2)}) collective-permute-start(bf16[128,512]{1,0:T(8,128)(2,1)S(1)} %collective-permute-done.22.refs_4_), channel_id=1, source_target_pairs={{0,2},{1,3},{2,0},{3,1},{4,6},{5,7},{6,4},{7,5},{8,10},{9,11},{10,... | collective-permute-start | bytes 393224 | tf_op jit(solution)/shard_map/gather_residual/ppermute | solution.py:149
  93.4 1.4 %collective-permute-start.34 = (bf16[128,512]{1,0:T(8,128)(2,1)S(1)}, bf16[128,512]{1,0:T(8,128)(2,1)S(1)}, u32[]{:S(2)}, u32[]{:S(2)}) collective-permute-start(bf16[128,512]{1,0:T(8,128)(2,1)S(1)} %collective-permute-done.23.refs_2_), channel_id=1, source_target_pairs={{0,1},{1,0},{2,3},{3,2},{4,5},{5,4},{6,7},{7,6},{8,9},{9,8},{10,11... | collective-permute-start | bytes 393224 | tf_op jit(solution)/shard_map/gather_residual/ppermute | solution.py:149
  93.5 1.5 %collective-permute-start.32 = (bf16[128,512]{1,0:T(8,128)(2,1)S(1)}, bf16[128,512]{1,0:T(8,128)(2,1)S(1)}, u32[]{:S(2)}, u32[]{:S(2)}) collective-permute-start(bf16[128,512]{1,0:T(8,128)(2,1)S(1)} %collective-permute-done.26.refs_6_), channel_id=1, source_target_pairs={{0,1},{1,0},{2,3},{3,2},{4,5},{5,4},{6,7},{7,6},{8,9},{9,8},{10,11... | collective-permute-start | bytes 393224 | tf_op jit(solution)/shard_map/gather_residual/ppermute | solution.py:149
  103.8 2.5 %collective-permute-start.36 = (bf16[512,512]{1,0:T(8,128)(2,1)S(1)}, bf16[512,512]{1,0:T(8,128)(2,1)S(1)}, u32[]{:S(2)}, u32[]{:S(2)}) collective-permute-start(bf16[512,512]{1,0:T(8,128)(2,1)S(1)} %down_products.2), channel_id=1, source_target_pairs={{0,1},{1,0},{2,3},{3,2},{4,5},{5,4},{6,7},{7,6},{8,9},{9,8},{10,11... | collective-permute-start | bytes 1572872 | tf_op jit(solution)/shard_map/sum_over_devices/ppermute | solution.py:149
  107.6 9.6 %collective-permute-start.40 = (bf16[256,512]{1,0:T(8,128)(2,1)}, bf16[256,512]{1,0:T(8,128)(2,1)S(1)}, u32[]{:S(2)}, u32[]{:S(2)}) collective-permute-start(bf16[256,512]{1,0:T(8,128)(2,1)} %get-tuple-element.124), channel_id=1, source_target_pairs={{0,2},{1,3},{2,0},{3,1},{4,6},{5,7},{6,4},{7,5},{8,10},{9,11},{10,... | collective-permute-start | bytes 786440 | tf_op jit(solution)/shard_map/sum_over_devices/ppermute | solution.py:149
  111.4 1.7 %collective-permute-start.41 = (bf16[128,512]{1,0:T(8,128)(2,1)S(1)}, bf16[128,512]{1,0:T(8,128)(2,1)S(1)}, u32[]{:S(2)}, u32[]{:S(2)}) collective-permute-start(bf16[128,512]{1,0:T(8,128)(2,1)S(1)} %get-tuple-element.136), channel_id=1, source_target_pairs={{0,1},{1,0},{2,3},{3,2},{4,5},{5,4},{6,7},{7,6},{8,9},{9,8},{10,11... | collective-permute-start | bytes 393224 | tf_op jit(solution)/shard_map/sum_over_devices/ppermute | solution.py:149
  111.4 10.4 %collective-permute-start.37 = (bf16[256,512]{1,0:T(8,128)(2,1)S(1)}, bf16[256,512]{1,0:T(8,128)(2,1)S(1)}, u32[]{:S(2)}, u32[]{:S(2)}) collective-permute-start(bf16[256,512]{1,0:T(8,128)(2,1)S(1)} %get-tuple-element.125), channel_id=1, source_target_pairs={{0,2},{1,3},{2,0},{3,1},{4,6},{5,7},{6,4},{7,5},{8,10},{9,11},{10,... | collective-permute-start | bytes 786440 | tf_op jit(solution)/shard_map/sum_over_devices/ppermute | solution.py:149
  112.6 4.7 %collective-permute-start.42 = (bf16[128,512]{1,0:T(8,128)(2,1)}, bf16[128,512]{1,0:T(8,128)(2,1)S(1)}, u32[]{:S(2)}, u32[]{:S(2)}) collective-permute-start(bf16[128,512]{1,0:T(8,128)(2,1)} %get-tuple-element.137), channel_id=1, source_target_pairs={{0,1},{1,0},{2,3},{3,2},{4,5},{5,4},{6,7},{7,6},{8,9},{9,8},{10,11... | collective-permute-start | bytes 393224 | tf_op jit(solution)/shard_map/sum_over_devices/ppermute | solution.py:149
  112.8 8.4 %collective-permute-start.38 = (bf16[128,512]{1,0:T(8,128)(2,1)}, bf16[128,512]{1,0:T(8,128)(2,1)}, u32[]{:S(2)}, u32[]{:S(2)}) collective-permute-start(bf16[128,512]{1,0:T(8,128)(2,1)} %get-tuple-element.128), channel_id=1, source_target_pairs={{0,1},{1,0},{2,3},{3,2},{4,5},{5,4},{6,7},{7,6},{8,9},{9,8},{10,11... | collective-permute-start | bytes 393224 | tf_op jit(solution)/shard_map/sum_over_devices/ppermute | solution.py:149
  113.1 8.1 %collective-permute-start.39 = (bf16[128,512]{1,0:T(8,128)(2,1)}, bf16[128,512]{1,0:T(8,128)(2,1)}, u32[]{:S(2)}, u32[]{:S(2)}) collective-permute-start(bf16[128,512]{1,0:T(8,128)(2,1)} %get-tuple-element.130), channel_id=1, source_target_pairs={{0,1},{1,0},{2,3},{3,2},{4,5},{5,4},{6,7},{7,6},{8,9},{9,8},{10,11... | collective-permute-start | bytes 393224 | tf_op jit(solution)/shard_map/sum_over_devices/ppermute | solution.py:149
  117.9 8.3 %collective-permute-start.44 = (bf16[128,512]{1,0:T(8,128)(2,1)S(1)}, bf16[128,512]{1,0:T(8,128)(2,1)S(1)}, u32[]{:S(2)}, u32[]{:S(2)}) collective-permute-start(bf16[128,512]{1,0:T(8,128)(2,1)S(1)} %get-tuple-element.139), channel_id=1, source_target_pairs={{0,12},{4,8},{8,4},{12,0},{1,13},{5,9},{9,5},{13,1},{2,14},{6,10},... | collective-permute-start | bytes 393224 | tf_op jit(solution)/shard_map/sum_over_devices/ppermute | solution.py:149
  119.7 13.6 %collective-permute-start.43 = (bf16[128,512]{1,0:T(8,128)(2,1)S(1)}, bf16[128,512]{1,0:T(8,128)(2,1)S(1)}, u32[]{:S(2)}, u32[]{:S(2)}) collective-permute-start(bf16[128,512]{1,0:T(8,128)(2,1)S(1)} %get-tuple-element.138), channel_id=1, source_target_pairs={{0,8},{4,12},{8,0},{12,4},{1,9},{5,13},{9,1},{13,5},{2,10},{6,14},... | collective-permute-start | bytes 393224 | tf_op jit(solution)/shard_map/sum_over_devices/ppermute | solution.py:149
  122.9 10.5 %collective-permute-start.45 = (bf16[128,512]{1,0:T(8,128)(2,1)S(1)}, bf16[128,512]{1,0:T(8,128)(2,1)S(1)}, u32[]{:S(2)}, u32[]{:S(2)}) collective-permute-start(bf16[128,512]{1,0:T(8,128)(2,1)S(1)} %get-tuple-element.140), channel_id=1, source_target_pairs={{0,4},{4,0},{8,12},{12,8},{1,5},{5,1},{9,13},{13,9},{2,6},{6,2},{1... | collective-permute-start | bytes 393224 | tf_op jit(solution)/shard_map/sum_over_devices/ppermute | solution.py:149

commit v8 on v7

--- a/solution.py
+++ b/solution.py
@@ -772,7 +772,7 @@
             r_pieces[d][1] = swap(r_pieces[d][0], "head", 1)
         for d in early:
             r_pieces[d][3] = swap(r_pieces[d][2], "head", 1)
-        r_pieces[0][0] = after(residual, r_pieces[3][0], r_pieces[2][2])
+        r_pieces[0][0] = after(residual, r_pieces[3][0])
         pieces = [r_pieces[d][e] for d in early for e in range(n)]
         with jax.named_scope("first_hidden_units"):
             state = first_hidden(pieces, early_weights)
@@ -831,7 +831,7 @@
         with jax.named_scope("down_products_by_block"):
             out_1 = pl.pallas_call(
                 functools.partial(down_blocks_kernel, slots),
-                out_shape=[sds((rows, cols), BF16)] * n,
+                out_shape=[pltpu.VMEM((rows, cols), BF16)] * n,
                 in_specs=[SMEM] + [VMEM] * 3,
                 out_specs=[VMEM] * n,
                 scratch_shapes=[pltpu.VMEM((pairs, cols), BF16), pltpu.VMEM((total, cols), BF16)],

time: 141 us -> 140 us (level)
  starting transfers between devices: 42.4 us -> 38.7 us
  waiting for transfers between devices: 37.7 us -> 40 us
    ppermute x46, starting transfers between devices: 42.4 us -> 38.7 us  [swap(): return lax.ppermute(array, axis, [(i, i ^ distance) for i in range(size)])]
    ppermute x46, waiting for transfers between devices: 37.7 us -> 40 us  [swap(): return lax.ppermute(array, axis, [(i, i ^ distance) for i in range(size)])]
where the time goes in v8:
time: 140 us
  Pallas kernels  50.8 us (36%)
  waiting for transfers between devices  40 us (29%)
  starting transfers between devices  38.7 us (28%)
  blocking collectives  6.94 us (5%)
  local copies, waits for them, and re-layouts  2.7 us (2%)
    ppermute x46, waiting for transfers between devices, swap(): return lax.ppermute(array, axis, [(i, i ^ distance) for i in range(size)])  40 us
    ppermute x46, starting transfers between devices, swap(): return lax.ppermute(array, axis, [(i, i ^ distance) for i in range(size)])  38.7 us
    pallas_call x2, Pallas kernels, load(): pl.pallas_call(functools.partial(load_kernel, group, distances), out_shap...  10.5 us
    all_gather x1, blocking collectives, square_body(): return lax.all_gather(mixed, 'head', axis=1, tiled=True)  6.94 us
    pallas_call x1, Pallas kernels, last_hidden(): pl.pallas_call(functools.partial(last_hidden_kernel, n, slots, group, lat...  6.68 us
    pallas_call x1, Pallas kernels, first_hidden(): pl.pallas_call(functools.partial(first_hidden_kernel, n, slots, group, ea...  5.17 us
    pallas_call x1, Pallas kernels, square_body(): pl.pallas_call(functools.partial(project_tokens_kernel, n), out_shape=[sd...  4.94 us
    pallas_call x2, Pallas kernels, down(): pl.pallas_call(functools.partial(down_kernel, slots), out_shape=[sds((tot...  4.2 us
  transfers between devices with their start and end apart: 46, of which 17 were waited for; matrix products, arithmetic and copies ran while one was open for 1% of the time, Pallas kernels for 27%

profile of v8, /device:TPU:0, one launch (start us, length us, event | category | flops | bytes accessed | tf_op | source)
XLA Modules:
  0.0 139.9 jit_solution(5142650397849278374)
XLA Ops:
  0.1 1.8 %cut_pieces.1 = (bf16[144,512]{1,0:T(8,128)(2,1)S(1)}, bf16[256,384]{1,0:T(8,128)(2,1)S(1)}, bf16[256,384]{1,0:T(8,128)(2,1)S(1)}, bf16[256,384]{1,0:T(8,128)(2,1)S(1)}) custom-call(s32[3]{0:T(128)S(1)} %pad_add_fusion.pos, s32[8,128]{1,0:T(8,128)} %bitcast.26, f32[8,128]{1,0:T(8,128)} %bitcast.27, bf16[128,2048]{1,0:T(8,128)(2,1)} %tokens.3, ...), custom_call_target="tpu_custom_call" | custom-call | tf_op jit(solution)/shard_map/cut_pieces/pallas_call | solution.py:595
  1.9 3.1 %collective-permute-start.3 = (bf16[256,384]{1,0:T(8,128)(2,1)S(1)}, bf16[256,384]{1,0:T(8,128)(2,1)S(1)}, u32[]{:S(2)}, u32[]{:S(2)}) collective-permute-start(bf16[256,384]{1,0:T(8,128)(2,1)S(1)} %get-tuple-element.75), channel_id=1, source_target_pairs={{0,4},{4,0},{8,12},{12,8},{1,5},{5,1},{9,13},{13,9},{2,6},{6,2},{1... | collective-permute-start | bytes 589832 | tf_op jit(solution)/shard_map/gather_tokens_and_weights/ppermute | solution.py:149
  5.0 2.6 %collective-permute-start.4 = (bf16[256,384]{1,0:T(8,128)(2,1)S(1)}, bf16[256,384]{1,0:T(8,128)(2,1)S(1)}, u32[]{:S(2)}, u32[]{:S(2)}) collective-permute-start(bf16[256,384]{1,0:T(8,128)(2,1)S(1)} %get-tuple-element.76), channel_id=1, source_target_pairs={{0,8},{4,12},{8,0},{12,4},{1,9},{5,13},{9,1},{13,5},{2,10},{6,14},... | collective-permute-start | bytes 589832 | tf_op jit(solution)/shard_map/gather_tokens_and_weights/ppermute | solution.py:149
  7.6 0.4 collective-permute-start
  8.0 3.9 %collective-permute-start.2 = (bf16[144,512]{1,0:T(8,128)(2,1)S(1)}, bf16[144,512]{1,0:T(8,128)(2,1)S(1)}, u32[]{:S(2)}, u32[]{:S(2)}) collective-permute-start(bf16[144,512]{1,0:T(8,128)(2,1)S(1)} %get-tuple-element.74.refs_0_), channel_id=1, source_target_pairs={{0,12},{4,8},{8,4},{12,0},{1,13},{5,9},{9,5},{13,1},{2,14},{6,10},... | collective-permute-start | bytes 442376 | tf_op jit(solution)/shard_map/gather_tokens_and_weights/ppermute | solution.py:149
  12.0 7.3 %collective-permute-done.refs_1_ = bf16[144,512]{1,0:T(8,128)(2,1)S(1)} collective-permute-done((bf16[144,512]{1,0:T(8,128)(2,1)S(1)}, bf16[144,512]{1,0:T(8,128)(2,1)S(1)}, u32[]{:S(2)}, u32[]{:S(2)}) %collective-permute-start) | collective-permute-done | bytes 147488 | tf_op jit(solution)/shard_map/gather_tokens_and_weights/ppermute | solution.py:149
  19.3 8.1 %collective-permute-done.1.refs_2_ = bf16[144,512]{1,0:T(8,128)(2,1)S(1)} collective-permute-done((bf16[144,512]{1,0:T(8,128)(2,1)S(1)}, bf16[144,512]{1,0:T(8,128)(2,1)S(1)}, u32[]{:S(2)}, u32[]{:S(2)}) %collective-permute-start.1) | collective-permute-done | bytes 147488 | tf_op jit(solution)/shard_map/gather_tokens_and_weights/ppermute | solution.py:149
  27.6 1.6 %collective-permute-start.6 = (bf16[3,128,512]{2,1,0:T(8,128)(2,1)S(1)}, bf16[3,128,512]{2,1,0:T(8,128)(2,1)S(1)}, u32[]{:S(2)}, u32[]{:S(2)}) collective-permute-start(bf16[3,128,512]{2,1,0:T(8,128)(2,1)S(1)} %pad_maximum_fusion.rest_0_), channel_id=1, source_target_pairs={{0,2},{1,3},{2,0},{3,1},{4,6},{5,7},{6,4},{7,5},{8,10},{9,11},{10,... | collective-permute-start | bytes 1179656 | tf_op jit(solution)/shard_map/gather_tokens_and_weights/ppermute | solution.py:149
  29.1 1.3 routing.1
  30.5 2.5 %collective-permute-start.7 = (bf16[256,384]{1,0:T(8,128)(2,1)S(1)}, bf16[256,384]{1,0:T(8,128)(2,1)S(1)}, u32[]{:S(2)}, u32[]{:S(2)}) collective-permute-start(bf16[256,384]{1,0:T(8,128)(2,1)S(1)} %get-tuple-element.84), channel_id=1, source_target_pairs={{0,12},{4,8},{8,4},{12,0},{1,13},{5,9},{9,5},{13,1},{2,14},{6,10},... | collective-permute-start | bytes 589832 | tf_op jit(solution)/shard_map/gather_tokens_and_weights/ppermute | solution.py:149
  33.0 1.5 %collective-permute-start.8 = (bf16[256,384]{1,0:T(8,128)(2,1)S(1)}, bf16[256,384]{1,0:T(8,128)(2,1)S(1)}, u32[]{:S(2)}, u32[]{:S(2)}) collective-permute-start(bf16[256,384]{1,0:T(8,128)(2,1)S(1)} %collective-permute-done.3.rest_4_), channel_id=1, source_target_pairs={{0,16},{16,0},{1,17},{17,1},{2,18},{18,2},{3,19},{19,3},{4,20},{20... | collective-permute-start | bytes 589832 | tf_op jit(solution)/shard_map/gather_tokens_and_weights/ppermute | solution.py:149
  34.5 0.5 collective-permute-start.9
  35.0 1.1 slice_bitcast_fusion.refs_0_
  36.1 0.6 collective-permute-start.17
  36.7 4.0 %gather_tokens_and_weights.1 = (bf16[8,1024,256]{2,1,0:T(8,128)(2,1)S(1)}, bf16[8,1024,256]{2,1,0:T(8,128)(2,1)S(1)}) custom-call(s32[3]{0:T(128)S(1)} %pad_add_fusion.pos, bf16[16,2048,256]{2,1,0:T(8,128)(2,1)} %w_gate.5, bf16[16,2048,256]{2,1,0:T(8,128)(2,1)} %w_up.5), custom_call_target="tpu_custom_call" | custom-call | bytes 8388608 | tf_op jit(solution)/shard_map/gather_tokens_and_weights/pallas_call | solution.py:617
  40.9 0.5 collective-permute-start.10
  41.5 1.5 %collective-permute-start.11 = (bf16[256,384]{1,0:T(8,128)(2,1)S(1)}, bf16[256,384]{1,0:T(8,128)(2,1)S(1)}, u32[]{:S(2)}, u32[]{:S(2)}) collective-permute-start(bf16[256,384]{1,0:T(8,128)(2,1)S(1)} %collective-permute-done.7.rest_6_), channel_id=1, source_target_pairs={{0,16},{16,0},{1,17},{17,1},{2,18},{18,2},{3,19},{19,3},{4,20},{20... | collective-permute-start | bytes 589832 | tf_op jit(solution)/shard_map/gather_tokens_and_weights/ppermute | solution.py:149
  43.2 0.6 copy-done.4
  43.9 4.9 %projected_tokens.1 = (f32[512,384]{1,0:T(8,128)S(1)}, bf16[512,256]{1,0:T(8,128)(2,1)S(1)}, bf16[128,512]{1,0:T(8,128)(2,1)S(1)}) custom-call(s32[3]{0:T(128)S(1)} %pad_add_fusion.pos, f32[1,2048]{1,0:T(1,128)S(1)} %bitcast.22, bf16[128,2048]{1,0:T(8,128)(2,1)} %tokens.3, bf16[4,512,512]{2,1,0:T(8,128)(2,1)} %weight.3, bf16[3,128,512]{2,1,0:T(8,128)(2,1)} %copy-done.2, ...), custom_call_target="tpu_custom_call" | custom-call | flops 805306368 | bytes 4194304 | tf_op jit(solution)/shard_map/projected_tokens/pallas_call | solution.py:670
  48.9 2.0 %attention.1 = (bf16[128,128]{1,0:T(8,128)(2,1)S(1)}, bf16[128,128]{1,0:T(8,128)(2,1)S(1)}, bf16[128,128]{1,0:T(8,128)(2,1)S(1)}, bf16[128,128]{1,0:T(8,128)(2,1)S(1)}) custom-call(s32[3]{0:T(128)S(1)} %pad_add_fusion.pos, f32[512,384]{1,0:T(8,128)S(1)} %get-tuple-element.93.partial, bf16[512,256]{1,0:T(8,128)(2,1)S(1)} %get-tuple-element.94.x_last, ...), custom_call_target="tpu_custom_call" | custom-call | tf_op jit(solution)/shard_map/attention/pallas_call | solution.py:692
  51.0 0.4 collective-permute-start.18
  51.4 1.2 collective-permute-start.14
  52.6 0.5 collective-permute-start.13
  53.3 1.5 %collective-permute-done.14 = bf16[128,128]{1,0:T(8,128)(2,1)S(1)} collective-permute-done((bf16[128,128]{1,0:T(8,128)(2,1)S(1)}, bf16[128,128]{1,0:T(8,128)(2,1)S(1)}, u32[]{:S(2)}, u32[]{:S(2)}) %collective-permute-start.14) | collective-permute-done | bytes 32800 | tf_op jit(solution)/shard_map/heads_to_tokens/ppermute | solution.py:149
  54.8 1.7 %collective-permute-done.13 = bf16[128,128]{1,0:T(8,128)(2,1)S(1)} collective-permute-done((bf16[128,128]{1,0:T(8,128)(2,1)S(1)}, bf16[128,128]{1,0:T(8,128)(2,1)S(1)}, u32[]{:S(2)}, u32[]{:S(2)}) %collective-permute-start.13) | collective-permute-done | bytes 32800 | tf_op jit(solution)/shard_map/heads_to_tokens/ppermute | solution.py:149
  56.6 1.7 %collective-permute-start.15 = (bf16[4,128,128]{2,1,0:T(8,128)(2,1)S(1)}, bf16[4,128,128]{2,1,0:T(8,128)(2,1)S(1)}, u32[]{:S(2)}, u32[]{:S(2)}) collective-permute-start(bf16[4,128,128]{2,1,0:T(8,128)(2,1)S(1)} %pad_maximum_fusion.1.rest_4_), channel_id=1, source_target_pairs={{0,8},{4,12},{8,0},{12,4},{1,9},{5,13},{9,1},{13,5},{2,10},{6,14},... | collective-permute-start | bytes 393224 | tf_op jit(solution)/shard_map/heads_to_tokens/ppermute | solution.py:149
  58.3 0.3 collective-permute-start.19
  58.6 6.5 %expert_weights.2 = (bf16[16,1024,256]{2,1,0:T(8,128)(2,1)S(1)}, bf16[16,1024,256]{2,1,0:T(8,128)(2,1)S(1)}) custom-call(s32[3]{0:T(128)S(1)} %pad_add_fusion.pos, bf16[16,2048,256]{2,1,0:T(8,128)(2,1)} %w_gate.5, bf16[16,2048,256]{2,1,0:T(8,128)(2,1)} %w_up.5), custom_call_target="tpu_custom_call" | custom-call | bytes 16777216 | tf_op jit(solution)/shard_map/heads_to_tokens/expert_weights/pallas_call | solution.py:617
  65.1 1.8 %collective-permute-start.20 = (bf16[4,128,128]{2,1,0:T(8,128)(2,1)S(1)}, bf16[4,128,128]{2,1,0:T(8,128)(2,1)S(1)}, u32[]{:S(2)}, u32[]{:S(2)}) collective-permute-start(bf16[4,128,128]{2,1,0:T(8,128)(2,1)S(1)} %collective-permute-done.15.rest_6_), channel_id=1, source_target_pairs={{0,4},{4,0},{8,12},{12,8},{1,5},{5,1},{9,13},{13,9},{2,6},{6,2},{1... | collective-permute-start | bytes 393224 | tf_op jit(solution)/shard_map/heads_to_tokens/ppermute | solution.py:149
  66.9 2.8 %expert_weights.3.refs_0_ = bf16[16,256,512]{2,1,0:T(8,128)(2,1)S(1)} custom-call(s32[3]{0:T(128)S(1)} %pad_add_fusion.pos, bf16[16,256,2048]{2,1,0:T(8,128)(2,1)} %w_down.5), custom_call_target="tpu_custom_call" | custom-call | bytes 4194304 | tf_op jit(solution)/shard_map/heads_to_tokens/expert_weights/pallas_call | solution.py:629
  70.1 1.3 output_projection.1.refs_0_
  71.4 1.8 %collective-permute-start.23 = (bf16[128,512]{1,0:T(8,128)(2,1)S(1)}, bf16[128,512]{1,0:T(8,128)(2,1)S(1)}, u32[]{:S(2)}, u32[]{:S(2)}) collective-permute-start(bf16[128,512]{1,0:T(8,128)(2,1)S(1)} %output_projection.1.refs_0_), channel_id=1, source_target_pairs={{0,4},{4,0},{8,12},{12,8},{1,5},{5,1},{9,13},{13,9},{2,6},{6,2},{1... | collective-permute-start | bytes 393224 | tf_op jit(solution)/shard_map/gather_residual/ppermute | solution.py:149
  73.3 1.3 collective-permute-start.21
  74.6 0.9 collective-permute-start.28
  75.4 1.4 collective-permute-done.23.refs_4_
  76.8 1.0 collective-permute-start.30
  77.8 2.7 %collective-permute-done.21.refs_0_ = bf16[128,512]{1,0:T(8,128)(2,1)S(1)} collective-permute-done((bf16[128,512]{1,0:T(8,128)(2,1)S(1)}, bf16[128,512]{1,0:T(8,128)(2,1)S(1)}, u32[]{:S(2)}, u32[]{:S(2)}) %collective-permute-start.21) | collective-permute-done | bytes 131104 | tf_op jit(solution)/shard_map/gather_residual/ppermute | solution.py:149
  80.5 0.5 collective-permute-start.29
  81.1 0.6 collective-permute-done.30.refs_6_
  81.8 3.7 %collective-permute-done.22.refs_4_ = bf16[128,512]{1,0:T(8,128)(2,1)S(1)} collective-permute-done((bf16[128,512]{1,0:T(8,128)(2,1)S(1)}, bf16[128,512]{1,0:T(8,128)(2,1)S(1)}, u32[]{:S(2)}, u32[]{:S(2)}) %collective-permute-start.22) | collective-permute-done | bytes 131104 | tf_op jit(solution)/shard_map/gather_residual/ppermute | solution.py:149
  85.5 1.2 collective-permute-start.25
  86.7 0.2 collective-permute-start.35
  86.9 0.8 collective-permute-start.26
  87.8 5.2 %first_hidden_units.1 = (f32[1280,512]{1,0:T(8,128)S(1)}, f32[1280,128]{1,0:T(8,128)S(1)}) custom-call(s32[3]{0:T(128)S(1)} %pad_add_fusion.pos, f32[1,2048]{1,0:T(1,128)S(1)} %bitcast.20, bf16[1280,512]{1,0:T(8,128)(2,1)S(1)} %get-tuple-element.88.pick, bf16[16,1024,256]{2,1,0:T(8,128)(2,1)S(1)} %get-tuple-element.100.g_all, ...), custom_call_target="tpu_custom_call" | custom-call | flops 2684354560 | bytes 16777216 | tf_op jit(solution)/shard_map/gather_residual/first_hidden_units/pallas_call | solution.py:704
  93.0 1.2 collective-permute-done.26.refs_6_
  94.4 1.2 collective-permute-done.32.refs_7_
  95.6 6.7 %last_hidden_units.1 = (bf16[1280,256]{1,0:T(8,128)(2,1)S(1)}, bf16[16,256,512]{2,1,0:T(8,128)(2,1)S(1)}, bf16[16,256,512]{2,1,0:T(8,128)(2,1)S(1)}) custom-call(s32[3]{0:T(128)S(1)} %pad_add_fusion.pos, f32[1,2048]{1,0:T(1,128)S(1)} %bitcast.21, bf16[1280,512]{1,0:T(8,128)(2,1)S(1)} %get-tuple-element.88.pick, bf16[16,2048,256]{2,1,0:T(8,128)(2,1)} %w_gate.5, ...), custom_call_target="tpu_custom_call" | custom-call | flops 2684354560 | bytes 16777216 | tf_op jit(solution)/shard_map/gather_residual/last_hidden_units/pallas_call | solution.py:715
  102.3 2.1 %down_products.2 = bf16[512,512]{1,0:T(8,128)(2,1)S(1)} custom-call(s32[3]{0:T(128)S(1)} %pad_add_fusion.pos, bf16[1280,256]{1,0:T(8,128)(2,1)S(1)} %get-tuple-element.129.hidden, bf16[512,1280]{1,0:T(8,128)(2,1)S(1)} %get-tuple-element.121.place, bf16[16,256,512]{2,1,0:T(8,128)(2,1)S(1)} %get-tuple-element.122.refs_0_), custom_call_target="tpu_custom_call" | custom-call | flops 1006632960 | bytes 4194304 | tf_op jit(solution)/shard_map/sum_over_devices/down_products/pallas_call | solution.py:788
  104.6 2.1 %down_products.3.base = bf16[512,512]{1,0:T(8,128)(2,1)S(1)} custom-call(s32[3]{0:T(128)S(1)} %pad_add_fusion.pos, bf16[1280,256]{1,0:T(8,128)(2,1)S(1)} %get-tuple-element.129.hidden, bf16[512,1280]{1,0:T(8,128)(2,1)S(1)} %get-tuple-element.121.place, bf16[16,256,512]{2,1,0:T(8,128)(2,1)S(1)} %expert_weights.3.refs_0_), custom_call_target="tpu_custom_call" | custom-call | flops 1006632960 | bytes 4194304 | tf_op jit(solution)/shard_map/sum_over_devices/down_products/pallas_call | solution.py:788
  106.7 1.3 sums_over_cores.1
  108.0 1.2 collective-permute-start.40
  109.2 2.9 %down_products_by_block.1 = (bf16[128,512]{1,0:T(8,128)(2,1)}, bf16[128,512]{1,0:T(8,128)(2,1)}, bf16[128,512]{1,0:T(8,128)(2,1)S(1)}, bf16[128,512]{1,0:T(8,128)(2,1)}) custom-call(s32[3]{0:T(128)S(1)} %pad_add_fusion.pos, bf16[1280,256]{1,0:T(8,128)(2,1)S(1)} %get-tuple-element.129.hidden, bf16[512,1280]{1,0:T(8,128)(2,1)S(1)} %get-tuple-element.121.place, ...), custom_call_target="tpu_custom_call" | custom-call | flops 20000000000 | bytes 4194304 | tf_op jit(solution)/shard_map/sum_over_devices/down_products_by_block/pallas_call | solution.py:832
  112.1 0.9 collective-permute-start.37
  113.2 0.3 collective-permute-start.38
  113.7 3.9 %down_products_alone.1.base = bf16[512,512]{1,0:T(8,128)(2,1)S(1)} custom-call(s32[3]{0:T(128)S(1)} %pad_add_fusion.pos, bf16[1280,256]{1,0:T(8,128)(2,1)S(1)} %get-tuple-element.129.hidden, bf16[512,1280]{1,0:T(8,128)(2,1)S(1)} %get-tuple-element.121.place, bf16[16,256,2048]{2,1,0:T(8,128)(2,1)} %w_down.5), custom_call_target="tpu_custom_call" | custom-call | tf_op jit(solution)/shard_map/sum_over_devices/down_products_alone/pallas_call | solution.py:802
  117.6 0.6 rows_2_3.1
  118.3 2.3 %collective-permute-start.44 = (bf16[128,512]{1,0:T(8,128)(2,1)S(1)}, bf16[128,512]{1,0:T(8,128)(2,1)S(1)}, u32[]{:S(2)}, u32[]{:S(2)}) collective-permute-start(bf16[128,512]{1,0:T(8,128)(2,1)S(1)} %get-tuple-element.139), channel_id=1, source_target_pairs={{0,12},{4,8},{8,4},{12,0},{1,13},{5,9},{9,5},{13,1},{2,14},{6,10},... | collective-permute-start | bytes 393224 | tf_op jit(solution)/shard_map/sum_over_devices/ppermute | solution.py:149
  120.6 1.8 %collective-permute-done.37.part = bf16[256,512]{1,0:T(8,128)(2,1)S(1)} collective-permute-done((bf16[256,512]{1,0:T(8,128)(2,1)S(1)}, bf16[256,512]{1,0:T(8,128)(2,1)S(1)}, u32[]{:S(2)}, u32[]{:S(2)}) %collective-permute-start.37) | collective-permute-done | bytes 262176 | tf_op jit(solution)/shard_map/sum_over_devices/ppermute | solution.py:149
  122.4 1.1 rows_0_1.1
  123.5 0.4 collective-permute-start.45
  123.9 2.7 %collective-permute-done.44 = bf16[128,512]{1,0:T(8,128)(2,1)S(1)} collective-permute-done((bf16[128,512]{1,0:T(8,128)(2,1)S(1)}, bf16[128,512]{1,0:T(8,128)(2,1)S(1)}, u32[]{:S(2)}, u32[]{:S(2)}) %collective-permute-start.44) | collective-permute-done | bytes 131104 | tf_op jit(solution)/shard_map/sum_over_devices/ppermute | solution.py:149
  126.6 5.4 %collective-permute-done.43 = bf16[128,512]{1,0:T(8,128)(2,1)S(1)} collective-permute-done((bf16[128,512]{1,0:T(8,128)(2,1)S(1)}, bf16[128,512]{1,0:T(8,128)(2,1)S(1)}, u32[]{:S(2)}, u32[]{:S(2)}) %collective-permute-start.43) | collective-permute-done | bytes 131104 | tf_op jit(solution)/shard_map/sum_over_devices/ppermute | solution.py:149
  132.2 6.9 %all_gather.3 = bf16[128,2048]{1,0:T(8,128)(2,1)S(1)} all-gather(bf16[128,512]{1,0:T(8,128)(2,1)S(1)} %add_convert_fusion), channel_id=1, replica_groups=mesh['grp'=2,'seq'=4,'head'=4] {'head'}, dimensions={1}, use_global_device_ids=true | all-gather | bytes 655360 | tf_op jit(solution)/shard_map/gather_columns/all_gather | solution.py:864
  139.1 0.8 copy.11
  (78 shorter events, 2.5 us)
Async XLA Ops:
  1.9 25.5 %collective-permute-start.3 = (bf16[256,384]{1,0:T(8,128)(2,1)S(1)}, bf16[256,384]{1,0:T(8,128)(2,1)S(1)}, u32[]{:S(2)}, u32[]{:S(2)}) collective-permute-start(bf16[256,384]{1,0:T(8,128)(2,1)S(1)} %get-tuple-element.75), channel_id=1, source_target_pairs={{0,4},{4,0},{8,12},{12,8},{1,5},{5,1},{9,13},{13,9},{2,6},{6,2},{1... | collective-permute-start | bytes 589832 | tf_op jit(solution)/shard_map/gather_tokens_and_weights/ppermute | solution.py:149
  5.0 22.4 %collective-permute-start.4 = (bf16[256,384]{1,0:T(8,128)(2,1)S(1)}, bf16[256,384]{1,0:T(8,128)(2,1)S(1)}, u32[]{:S(2)}, u32[]{:S(2)}) collective-permute-start(bf16[256,384]{1,0:T(8,128)(2,1)S(1)} %get-tuple-element.76), channel_id=1, source_target_pairs={{0,8},{4,12},{8,0},{12,4},{1,9},{5,13},{9,1},{13,5},{2,10},{6,14},... | collective-permute-start | bytes 589832 | tf_op jit(solution)/shard_map/gather_tokens_and_weights/ppermute | solution.py:149
  7.6 11.7 %collective-permute-start = (bf16[144,512]{1,0:T(8,128)(2,1)S(1)}, bf16[144,512]{1,0:T(8,128)(2,1)S(1)}, u32[]{:S(2)}, u32[]{:S(2)}) collective-permute-start(bf16[144,512]{1,0:T(8,128)(2,1)S(1)} %get-tuple-element.74.refs_0_), channel_id=1, source_target_pairs={{0,4},{4,0},{8,12},{12,8},{1,5},{5,1},{9,13},{13,9},{2,6},{6,2},{1... | collective-permute-start | bytes 442376 | tf_op jit(solution)/shard_map/gather_tokens_and_weights/ppermute | solution.py:149
  8.0 19.4 %collective-permute-start.1 = (bf16[144,512]{1,0:T(8,128)(2,1)S(1)}, bf16[144,512]{1,0:T(8,128)(2,1)S(1)}, u32[]{:S(2)}, u32[]{:S(2)}) collective-permute-start(bf16[144,512]{1,0:T(8,128)(2,1)S(1)} %get-tuple-element.74.refs_0_), channel_id=1, source_target_pairs={{0,8},{4,12},{8,0},{12,4},{1,9},{5,13},{9,1},{13,5},{2,10},{6,14},... | collective-permute-start | bytes 442376 | tf_op jit(solution)/shard_map/gather_tokens_and_weights/ppermute | solution.py:149
  8.0 19.4 %collective-permute-start.2 = (bf16[144,512]{1,0:T(8,128)(2,1)S(1)}, bf16[144,512]{1,0:T(8,128)(2,1)S(1)}, u32[]{:S(2)}, u32[]{:S(2)}) collective-permute-start(bf16[144,512]{1,0:T(8,128)(2,1)S(1)} %get-tuple-element.74.refs_0_), channel_id=1, source_target_pairs={{0,12},{4,8},{8,4},{12,0},{1,13},{5,9},{9,5},{13,1},{2,14},{6,10},... | collective-permute-start | bytes 442376 | tf_op jit(solution)/shard_map/gather_tokens_and_weights/ppermute | solution.py:149
  27.4 13.3 %copy-start.6 = (bf16[256,384]{1,0:T(8,128)(2,1)}, bf16[256,384]{1,0:T(8,128)(2,1)S(1)}, u32[]{:S(2)}) copy-start(bf16[256,384]{1,0:T(8,128)(2,1)S(1)} %collective-permute-done.3.rest_4_) | copy-start | bytes 589828
  27.4 13.3 %copy-start.7 = (bf16[256,384]{1,0:T(8,128)(2,1)}, bf16[256,384]{1,0:T(8,128)(2,1)S(1)}, u32[]{:S(2)}) copy-start(bf16[256,384]{1,0:T(8,128)(2,1)S(1)} %collective-permute-done.4.rest_5_) | copy-start | bytes 589828
  27.6 13.2 %copy-start.2 = (bf16[3,128,512]{2,1,0:T(8,128)(2,1)}, bf16[3,128,512]{2,1,0:T(8,128)(2,1)S(1)}, u32[]{:S(2)}) copy-start(bf16[3,128,512]{2,1,0:T(8,128)(2,1)S(1)} %pad_maximum_fusion.rest_0_) | copy-start | bytes 1179652
  27.6 13.4 %collective-permute-start.6 = (bf16[3,128,512]{2,1,0:T(8,128)(2,1)S(1)}, bf16[3,128,512]{2,1,0:T(8,128)(2,1)S(1)}, u32[]{:S(2)}, u32[]{:S(2)}) collective-permute-start(bf16[3,128,512]{2,1,0:T(8,128)(2,1)S(1)} %pad_maximum_fusion.rest_0_), channel_id=1, source_target_pairs={{0,2},{1,3},{2,0},{3,1},{4,6},{5,7},{6,4},{7,5},{8,10},{9,11},{10,... | collective-permute-start | bytes 1179656 | tf_op jit(solution)/shard_map/gather_tokens_and_weights/ppermute | solution.py:149
  30.5 10.3 %collective-permute-start.7 = (bf16[256,384]{1,0:T(8,128)(2,1)S(1)}, bf16[256,384]{1,0:T(8,128)(2,1)S(1)}, u32[]{:S(2)}, u32[]{:S(2)}) collective-permute-start(bf16[256,384]{1,0:T(8,128)(2,1)S(1)} %get-tuple-element.84), channel_id=1, source_target_pairs={{0,12},{4,8},{8,4},{12,0},{1,13},{5,9},{9,5},{13,1},{2,14},{6,10},... | collective-permute-start | bytes 589832 | tf_op jit(solution)/shard_map/gather_tokens_and_weights/ppermute | solution.py:149
  33.0 7.9 %collective-permute-start.8 = (bf16[256,384]{1,0:T(8,128)(2,1)S(1)}, bf16[256,384]{1,0:T(8,128)(2,1)S(1)}, u32[]{:S(2)}, u32[]{:S(2)}) collective-permute-start(bf16[256,384]{1,0:T(8,128)(2,1)S(1)} %collective-permute-done.3.rest_4_), channel_id=1, source_target_pairs={{0,16},{16,0},{1,17},{17,1},{2,18},{18,2},{3,19},{19,3},{4,20},{20... | collective-permute-start | bytes 589832 | tf_op jit(solution)/shard_map/gather_tokens_and_weights/ppermute | solution.py:149
  34.5 6.4 %collective-permute-start.9 = (bf16[256,384]{1,0:T(8,128)(2,1)S(1)}, bf16[256,384]{1,0:T(8,128)(2,1)S(1)}, u32[]{:S(2)}, u32[]{:S(2)}) collective-permute-start(bf16[256,384]{1,0:T(8,128)(2,1)S(1)} %collective-permute-done.4.rest_5_), channel_id=1, source_target_pairs={{0,16},{16,0},{1,17},{17,1},{2,18},{18,2},{3,19},{19,3},{4,20},{20... | collective-permute-start | bytes 589832 | tf_op jit(solution)/shard_map/gather_tokens_and_weights/ppermute | solution.py:149
  36.1 7.8 %copy-start.1 = (f32[2048]{0:T(1024)S(1)}, f32[2048]{0:T(1024)}, u32[]{:S(2)}) copy-start(f32[2048]{0:T(1024)} %param.11) | copy-start | bytes 24580
  36.1 14.9 %collective-permute-start.17 = (bf16[512,512]{1,0:T(8,128)(2,1)S(1)}, bf16[512,512]{1,0:T(8,128)(2,1)S(1)}, u32[]{:S(2)}, u32[]{:S(2)}) collective-permute-start(bf16[512,512]{1,0:T(8,128)(2,1)S(1)} %slice_bitcast_fusion.refs_0_), channel_id=1, source_target_pairs={{0,2},{1,3},{2,0},{3,1},{4,6},{5,7},{6,4},{7,5},{8,10},{9,11},{10,... | collective-permute-start | bytes 1572872 | tf_op jit(solution)/shard_map/gather_out_weights/ppermute | solution.py:149
  40.8 2.4 %copy-start.8 = (bf16[256,384]{1,0:T(8,128)(2,1)}, bf16[256,384]{1,0:T(8,128)(2,1)S(1)}, u32[]{:S(2)}) copy-start(bf16[256,384]{1,0:T(8,128)(2,1)S(1)} %collective-permute-done.7.rest_6_) | copy-start | bytes 589828
  40.8 2.2 %collective-permute-start.5 = (bf16[3,128,512]{2,1,0:T(8,128)(2,1)S(1)}, bf16[3,128,512]{2,1,0:T(8,128)(2,1)S(1)}, u32[]{:S(2)}, u32[]{:S(2)}) collective-permute-start(bf16[3,128,512]{2,1,0:T(8,128)(2,1)S(1)} %pad_maximum_fusion.rest_0_), channel_id=1, source_target_pairs={{0,1},{1,0},{2,3},{3,2},{4,5},{5,4},{6,7},{7,6},{8,9},{9,8},{10,11... | collective-permute-start | bytes 1179656 | tf_op jit(solution)/shard_map/gather_tokens_and_weights/ppermute | solution.py:149
  40.9 2.3 %copy-start.9 = (bf16[256,384]{1,0:T(8,128)(2,1)}, bf16[256,384]{1,0:T(8,128)(2,1)S(1)}, u32[]{:S(2)}) copy-start(bf16[256,384]{1,0:T(8,128)(2,1)S(1)} %collective-permute-done.8.rest_7_) | copy-start | bytes 589828
  40.9 2.3 %copy-start.10 = (bf16[256,384]{1,0:T(8,128)(2,1)}, bf16[256,384]{1,0:T(8,128)(2,1)S(1)}, u32[]{:S(2)}) copy-start(bf16[256,384]{1,0:T(8,128)(2,1)S(1)} %collective-permute-done.9.rest_8_) | copy-start | bytes 589828
  40.9 2.2 %copy-start.3 = (bf16[3,128,512]{2,1,0:T(8,128)(2,1)}, bf16[3,128,512]{2,1,0:T(8,128)(2,1)S(1)}, u32[]{:S(2)}) copy-start(bf16[3,128,512]{2,1,0:T(8,128)(2,1)S(1)} %collective-permute-done.6.rest_2_) | copy-start | bytes 1179652
  40.9 2.2 %collective-permute-start.10 = (bf16[3,128,512]{2,1,0:T(8,128)(2,1)S(1)}, bf16[3,128,512]{2,1,0:T(8,128)(2,1)S(1)}, u32[]{:S(2)}, u32[]{:S(2)}) collective-permute-start(bf16[3,128,512]{2,1,0:T(8,128)(2,1)S(1)} %collective-permute-done.6.rest_2_), channel_id=1, source_target_pairs={{0,1},{1,0},{2,3},{3,2},{4,5},{5,4},{6,7},{7,6},{8,9},{9,8},{10,11... | collective-permute-start | bytes 1179656 | tf_op jit(solution)/shard_map/gather_tokens_and_weights/ppermute | solution.py:149
  41.5 7.4 %collective-permute-start.11 = (bf16[256,384]{1,0:T(8,128)(2,1)S(1)}, bf16[256,384]{1,0:T(8,128)(2,1)S(1)}, u32[]{:S(2)}, u32[]{:S(2)}) collective-permute-start(bf16[256,384]{1,0:T(8,128)(2,1)S(1)} %collective-permute-done.7.rest_6_), channel_id=1, source_target_pairs={{0,16},{16,0},{1,17},{17,1},{2,18},{18,2},{3,19},{19,3},{4,20},{20... | collective-permute-start | bytes 589832 | tf_op jit(solution)/shard_map/gather_tokens_and_weights/ppermute | solution.py:149
  43.0 0.8 copy-start.4
  43.2 0.8 copy-start.5
  50.9 18.8 %collective-permute-start.16 = (bf16[512,512]{1,0:T(8,128)(2,1)S(1)}, bf16[512,512]{1,0:T(8,128)(2,1)S(1)}, u32[]{:S(2)}, u32[]{:S(2)}) collective-permute-start(bf16[512,512]{1,0:T(8,128)(2,1)S(1)} %slice_bitcast_fusion.refs_0_), channel_id=1, source_target_pairs={{0,1},{1,0},{2,3},{3,2},{4,5},{5,4},{6,7},{7,6},{8,9},{9,8},{10,11... | collective-permute-start | bytes 1572872 | tf_op jit(solution)/shard_map/heads_to_tokens/ppermute | solution.py:149
  51.0 18.6 %collective-permute-start.18 = (bf16[512,512]{1,0:T(8,128)(2,1)S(1)}, bf16[512,512]{1,0:T(8,128)(2,1)S(1)}, u32[]{:S(2)}, u32[]{:S(2)}) collective-permute-start(bf16[512,512]{1,0:T(8,128)(2,1)S(1)} %collective-permute-done.17.refs_2_), channel_id=1, source_target_pairs={{0,1},{1,0},{2,3},{3,2},{4,5},{5,4},{6,7},{7,6},{8,9},{9,8},{10,11... | collective-permute-start | bytes 1572872 | tf_op jit(solution)/shard_map/heads_to_tokens/ppermute | solution.py:149
  51.4 3.4 %collective-permute-start.14 = (bf16[128,128]{1,0:T(8,128)(2,1)S(1)}, bf16[128,128]{1,0:T(8,128)(2,1)S(1)}, u32[]{:S(2)}, u32[]{:S(2)}) collective-permute-start(bf16[128,128]{1,0:T(8,128)(2,1)S(1)} %get-tuple-element.98), channel_id=1, source_target_pairs={{0,3},{1,2},{2,1},{3,0},{4,7},{5,6},{6,5},{7,4},{8,11},{9,10},{10,... | collective-permute-start | bytes 98312 | tf_op jit(solution)/shard_map/heads_to_tokens/ppermute | solution.py:149
  52.6 3.9 %collective-permute-start.13 = (bf16[128,128]{1,0:T(8,128)(2,1)S(1)}, bf16[128,128]{1,0:T(8,128)(2,1)S(1)}, u32[]{:S(2)}, u32[]{:S(2)}) collective-permute-start(bf16[128,128]{1,0:T(8,128)(2,1)S(1)} %get-tuple-element.97), channel_id=1, source_target_pairs={{0,2},{1,3},{2,0},{3,1},{4,6},{5,7},{6,4},{7,5},{8,10},{9,11},{10,... | collective-permute-start | bytes 98312 | tf_op jit(solution)/shard_map/heads_to_tokens/ppermute | solution.py:149
  53.2 3.4 %collective-permute-start.12 = (bf16[128,128]{1,0:T(8,128)(2,1)S(1)}, bf16[128,128]{1,0:T(8,128)(2,1)S(1)}, u32[]{:S(2)}, u32[]{:S(2)}) collective-permute-start(bf16[128,128]{1,0:T(8,128)(2,1)S(1)} %get-tuple-element.96), channel_id=1, source_target_pairs={{0,1},{1,0},{2,3},{3,2},{4,5},{5,4},{6,7},{7,6},{8,9},{9,8},{10,11... | collective-permute-start | bytes 98312 | tf_op jit(solution)/shard_map/heads_to_tokens/ppermute | solution.py:149
  56.6 8.5 %collective-permute-start.15 = (bf16[4,128,128]{2,1,0:T(8,128)(2,1)S(1)}, bf16[4,128,128]{2,1,0:T(8,128)(2,1)S(1)}, u32[]{:S(2)}, u32[]{:S(2)}) collective-permute-start(bf16[4,128,128]{2,1,0:T(8,128)(2,1)S(1)} %pad_maximum_fusion.1.rest_4_), channel_id=1, source_target_pairs={{0,8},{4,12},{8,0},{12,4},{1,9},{5,13},{9,1},{13,5},{2,10},{6,14},... | collective-permute-start | bytes 393224 | tf_op jit(solution)/shard_map/heads_to_tokens/ppermute | solution.py:149
  58.3 11.6 %collective-permute-start.19 = (bf16[4,128,128]{2,1,0:T(8,128)(2,1)S(1)}, bf16[4,128,128]{2,1,0:T(8,128)(2,1)S(1)}, u32[]{:S(2)}, u32[]{:S(2)}) collective-permute-start(bf16[4,128,128]{2,1,0:T(8,128)(2,1)S(1)} %pad_maximum_fusion.1.rest_4_), channel_id=1, source_target_pairs={{0,4},{4,0},{8,12},{12,8},{1,5},{5,1},{9,13},{13,9},{2,6},{6,2},{1... | collective-permute-start | bytes 393224 | tf_op jit(solution)/shard_map/heads_to_tokens/ppermute | solution.py:149
  65.1 5.0 %collective-permute-start.20 = (bf16[4,128,128]{2,1,0:T(8,128)(2,1)S(1)}, bf16[4,128,128]{2,1,0:T(8,128)(2,1)S(1)}, u32[]{:S(2)}, u32[]{:S(2)}) collective-permute-start(bf16[4,128,128]{2,1,0:T(8,128)(2,1)S(1)} %collective-permute-done.15.rest_6_), channel_id=1, source_target_pairs={{0,4},{4,0},{8,12},{12,8},{1,5},{5,1},{9,13},{13,9},{2,6},{6,2},{1... | collective-permute-start | bytes 393224 | tf_op jit(solution)/shard_map/heads_to_tokens/ppermute | solution.py:149
  69.7 18.1 %copy-start = (f32[2048]{0:T(1024)S(1)}, f32[2048]{0:T(1024)}, u32[]{:S(2)}) copy-start(f32[2048]{0:T(1024)} %param.12) | copy-start | bytes 24580
  71.4 5.3 %collective-permute-start.23 = (bf16[128,512]{1,0:T(8,128)(2,1)S(1)}, bf16[128,512]{1,0:T(8,128)(2,1)S(1)}, u32[]{:S(2)}, u32[]{:S(2)}) collective-permute-start(bf16[128,512]{1,0:T(8,128)(2,1)S(1)} %output_projection.1.refs_0_), channel_id=1, source_target_pairs={{0,4},{4,0},{8,12},{12,8},{1,5},{5,1},{9,13},{13,9},{2,6},{6,2},{1... | collective-permute-start | bytes 393224 | tf_op jit(solution)/shard_map/gather_residual/ppermute | solution.py:149
  73.3 7.3 %collective-permute-start.21 = (bf16[128,512]{1,0:T(8,128)(2,1)S(1)}, bf16[128,512]{1,0:T(8,128)(2,1)S(1)}, u32[]{:S(2)}, u32[]{:S(2)}) collective-permute-start(bf16[128,512]{1,0:T(8,128)(2,1)S(1)} %output_projection.1.refs_0_), channel_id=1, source_target_pairs={{0,8},{4,12},{8,0},{12,4},{1,9},{5,13},{9,1},{13,5},{2,10},{6,14},... | collective-permute-start | bytes 393224 | tf_op jit(solution)/shard_map/gather_residual/ppermute | solution.py:149
  74.6 6.0 %collective-permute-start.28 = (bf16[128,512]{1,0:T(8,128)(2,1)S(1)}, bf16[128,512]{1,0:T(8,128)(2,1)S(1)}, u32[]{:S(2)}, u32[]{:S(2)}) collective-permute-start(bf16[128,512]{1,0:T(8,128)(2,1)S(1)} %output_projection.1.refs_0_), channel_id=1, source_target_pairs={{0,2},{1,3},{2,0},{3,1},{4,6},{5,7},{6,4},{7,5},{8,10},{9,11},{10,... | collective-permute-start | bytes 393224 | tf_op jit(solution)/shard_map/gather_residual/ppermute | solution.py:149
  76.8 5.0 %collective-permute-start.30 = (bf16[128,512]{1,0:T(8,128)(2,1)S(1)}, bf16[128,512]{1,0:T(8,128)(2,1)S(1)}, u32[]{:S(2)}, u32[]{:S(2)}) collective-permute-start(bf16[128,512]{1,0:T(8,128)(2,1)S(1)} %collective-permute-done.23.refs_4_), channel_id=1, source_target_pairs={{0,2},{1,3},{2,0},{3,1},{4,6},{5,7},{6,4},{7,5},{8,10},{9,11},{10,... | collective-permute-start | bytes 393224 | tf_op jit(solution)/shard_map/gather_residual/ppermute | solution.py:149
  80.5 5.0 %collective-permute-start.22 = (bf16[128,512]{1,0:T(8,128)(2,1)S(1)}, bf16[128,512]{1,0:T(8,128)(2,1)S(1)}, u32[]{:S(2)}, u32[]{:S(2)}) collective-permute-start(bf16[128,512]{1,0:T(8,128)(2,1)S(1)} %collective-permute-done.21.refs_0_), channel_id=1, source_target_pairs={{0,4},{4,0},{8,12},{12,8},{1,5},{5,1},{9,13},{13,9},{2,6},{6,2},{1... | collective-permute-start | bytes 393224 | tf_op jit(solution)/shard_map/gather_residual/ppermute | solution.py:149
  80.5 5.0 %collective-permute-start.27 = (bf16[128,512]{1,0:T(8,128)(2,1)S(1)}, bf16[128,512]{1,0:T(8,128)(2,1)S(1)}, u32[]{:S(2)}, u32[]{:S(2)}) collective-permute-start(bf16[128,512]{1,0:T(8,128)(2,1)S(1)} %output_projection.1.refs_0_), channel_id=1, source_target_pairs={{0,1},{1,0},{2,3},{3,2},{4,5},{5,4},{6,7},{7,6},{8,9},{9,8},{10,11... | collective-permute-start | bytes 393224 | tf_op jit(solution)/shard_map/gather_residual/ppermute | solution.py:149
  80.5 6.1 %collective-permute-start.29 = (bf16[128,512]{1,0:T(8,128)(2,1)S(1)}, bf16[128,512]{1,0:T(8,128)(2,1)S(1)}, u32[]{:S(2)}, u32[]{:S(2)}) collective-permute-start(bf16[128,512]{1,0:T(8,128)(2,1)S(1)} %collective-permute-done.28.refs_2_), channel_id=1, source_target_pairs={{0,1},{1,0},{2,3},{3,2},{4,5},{5,4},{6,7},{7,6},{8,9},{9,8},{10,11... | collective-permute-start | bytes 393224 | tf_op jit(solution)/shard_map/gather_residual/ppermute | solution.py:149
  81.0 5.9 %collective-permute-start.24 = (bf16[128,512]{1,0:T(8,128)(2,1)S(1)}, bf16[128,512]{1,0:T(8,128)(2,1)S(1)}, u32[]{:S(2)}, u32[]{:S(2)}) collective-permute-start(bf16[128,512]{1,0:T(8,128)(2,1)S(1)} %collective-permute-done.23.refs_4_), channel_id=1, source_target_pairs={{0,1},{1,0},{2,3},{3,2},{4,5},{5,4},{6,7},{7,6},{8,9},{9,8},{10,11... | collective-permute-start | bytes 393224 | tf_op jit(solution)/shard_map/gather_residual/ppermute | solution.py:149
  81.8 6.0 %collective-permute-start.31 = (bf16[128,512]{1,0:T(8,128)(2,1)S(1)}, bf16[128,512]{1,0:T(8,128)(2,1)S(1)}, u32[]{:S(2)}, u32[]{:S(2)}) collective-permute-start(bf16[128,512]{1,0:T(8,128)(2,1)S(1)} %collective-permute-done.30.refs_6_), channel_id=1, source_target_pairs={{0,1},{1,0},{2,3},{3,2},{4,5},{5,4},{6,7},{7,6},{8,9},{9,8},{10,11... | collective-permute-start | bytes 393224 | tf_op jit(solution)/shard_map/gather_residual/ppermute | solution.py:149
  85.5 8.7 %collective-permute-start.33 = (bf16[128,512]{1,0:T(8,128)(2,1)S(1)}, bf16[128,512]{1,0:T(8,128)(2,1)S(1)}, u32[]{:S(2)}, u32[]{:S(2)}) collective-permute-start(bf16[128,512]{1,0:T(8,128)(2,1)S(1)} %collective-permute-done.21.refs_0_), channel_id=1, source_target_pairs={{0,1},{1,0},{2,3},{3,2},{4,5},{5,4},{6,7},{7,6},{8,9},{9,8},{10,11... | collective-permute-start | bytes 393224 | tf_op jit(solution)/shard_map/gather_residual/ppermute | solution.py:149
  85.5 7.4 %collective-permute-start.25 = (bf16[128,512]{1,0:T(8,128)(2,1)S(1)}, bf16[128,512]{1,0:T(8,128)(2,1)S(1)}, u32[]{:S(2)}, u32[]{:S(2)}) collective-permute-start(bf16[128,512]{1,0:T(8,128)(2,1)S(1)} %collective-permute-done.21.refs_0_), channel_id=1, source_target_pairs={{0,2},{1,3},{2,0},{3,1},{4,6},{5,7},{6,4},{7,5},{8,10},{9,11},{10,... | collective-permute-start | bytes 393224 | tf_op jit(solution)/shard_map/gather_residual/ppermute | solution.py:149
  86.7 7.5 %collective-permute-start.35 = (bf16[128,512]{1,0:T(8,128)(2,1)S(1)}, bf16[128,512]{1,0:T(8,128)(2,1)S(1)}, u32[]{:S(2)}, u32[]{:S(2)}) collective-permute-start(bf16[128,512]{1,0:T(8,128)(2,1)S(1)} %collective-permute-done.22.refs_4_), channel_id=1, source_target_pairs={{0,1},{1,0},{2,3},{3,2},{4,5},{5,4},{6,7},{7,6},{8,9},{9,8},{10,11... | collective-permute-start | bytes 393224 | tf_op jit(solution)/shard_map/gather_residual/ppermute | solution.py:149
  86.9 7.3 %collective-permute-start.26 = (bf16[128,512]{1,0:T(8,128)(2,1)S(1)}, bf16[128,512]{1,0:T(8,128)(2,1)S(1)}, u32[]{:S(2)}, u32[]{:S(2)}) collective-permute-start(bf16[128,512]{1,0:T(8,128)(2,1)S(1)} %collective-permute-done.22.refs_4_), channel_id=1, source_target_pairs={{0,2},{1,3},{2,0},{3,1},{4,6},{5,7},{6,4},{7,5},{8,10},{9,11},{10,... | collective-permute-start | bytes 393224 | tf_op jit(solution)/shard_map/gather_residual/ppermute | solution.py:149
  92.9 1.4 %collective-permute-start.34 = (bf16[128,512]{1,0:T(8,128)(2,1)S(1)}, bf16[128,512]{1,0:T(8,128)(2,1)S(1)}, u32[]{:S(2)}, u32[]{:S(2)}) collective-permute-start(bf16[128,512]{1,0:T(8,128)(2,1)S(1)} %collective-permute-done.25.refs_2_), channel_id=1, source_target_pairs={{0,1},{1,0},{2,3},{3,2},{4,5},{5,4},{6,7},{7,6},{8,9},{9,8},{10,11... | collective-permute-start | bytes 393224 | tf_op jit(solution)/shard_map/gather_residual/ppermute | solution.py:149
  94.2 1.3 collective-permute-start.32
  104.4 2.3 %collective-permute-start.36 = (bf16[512,512]{1,0:T(8,128)(2,1)S(1)}, bf16[512,512]{1,0:T(8,128)(2,1)S(1)}, u32[]{:S(2)}, u32[]{:S(2)}) collective-permute-start(bf16[512,512]{1,0:T(8,128)(2,1)S(1)} %down_products.2), channel_id=1, source_target_pairs={{0,1},{1,0},{2,3},{3,2},{4,5},{5,4},{6,7},{7,6},{8,9},{9,8},{10,11... | collective-permute-start | bytes 1572872 | tf_op jit(solution)/shard_map/sum_over_devices/ppermute | solution.py:149
  108.0 9.6 %collective-permute-start.40 = (bf16[256,512]{1,0:T(8,128)(2,1)}, bf16[256,512]{1,0:T(8,128)(2,1)S(1)}, u32[]{:S(2)}, u32[]{:S(2)}) collective-permute-start(bf16[256,512]{1,0:T(8,128)(2,1)} %get-tuple-element.124), channel_id=1, source_target_pairs={{0,2},{1,3},{2,0},{3,1},{4,6},{5,7},{6,4},{7,5},{8,10},{9,11},{10,... | collective-permute-start | bytes 786440 | tf_op jit(solution)/shard_map/sum_over_devices/ppermute | solution.py:149
  112.1 1.4 %collective-permute-start.41 = (bf16[128,512]{1,0:T(8,128)(2,1)S(1)}, bf16[128,512]{1,0:T(8,128)(2,1)S(1)}, u32[]{:S(2)}, u32[]{:S(2)}) collective-permute-start(bf16[128,512]{1,0:T(8,128)(2,1)S(1)} %get-tuple-element.136), channel_id=1, source_target_pairs={{0,1},{1,0},{2,3},{3,2},{4,5},{5,4},{6,7},{7,6},{8,9},{9,8},{10,11... | collective-permute-start | bytes 393224 | tf_op jit(solution)/shard_map/sum_over_devices/ppermute | solution.py:149
  112.1 10.3 %collective-permute-start.37 = (bf16[256,512]{1,0:T(8,128)(2,1)S(1)}, bf16[256,512]{1,0:T(8,128)(2,1)S(1)}, u32[]{:S(2)}, u32[]{:S(2)}) collective-permute-start(bf16[256,512]{1,0:T(8,128)(2,1)S(1)} %get-tuple-element.125), channel_id=1, source_target_pairs={{0,2},{1,3},{2,0},{3,1},{4,6},{5,7},{6,4},{7,5},{8,10},{9,11},{10,... | collective-permute-start | bytes 786440 | tf_op jit(solution)/shard_map/sum_over_devices/ppermute | solution.py:149
  113.0 4.6 %collective-permute-start.42 = (bf16[128,512]{1,0:T(8,128)(2,1)}, bf16[128,512]{1,0:T(8,128)(2,1)S(1)}, u32[]{:S(2)}, u32[]{:S(2)}) collective-permute-start(bf16[128,512]{1,0:T(8,128)(2,1)} %get-tuple-element.137), channel_id=1, source_target_pairs={{0,1},{1,0},{2,3},{3,2},{4,5},{5,4},{6,7},{7,6},{8,9},{9,8},{10,11... | collective-permute-start | bytes 393224 | tf_op jit(solution)/shard_map/sum_over_devices/ppermute | solution.py:149
  113.2 7.5 %collective-permute-start.38 = (bf16[128,512]{1,0:T(8,128)(2,1)}, bf16[128,512]{1,0:T(8,128)(2,1)}, u32[]{:S(2)}, u32[]{:S(2)}) collective-permute-start(bf16[128,512]{1,0:T(8,128)(2,1)} %get-tuple-element.128), channel_id=1, source_target_pairs={{0,1},{1,0},{2,3},{3,2},{4,5},{5,4},{6,7},{7,6},{8,9},{9,8},{10,11... | collective-permute-start | bytes 393224 | tf_op jit(solution)/shard_map/sum_over_devices/ppermute | solution.py:149
  113.5 7.1 %collective-permute-start.39 = (bf16[128,512]{1,0:T(8,128)(2,1)}, bf16[128,512]{1,0:T(8,128)(2,1)}, u32[]{:S(2)}, u32[]{:S(2)}) collective-permute-start(bf16[128,512]{1,0:T(8,128)(2,1)} %get-tuple-element.130), channel_id=1, source_target_pairs={{0,1},{1,0},{2,3},{3,2},{4,5},{5,4},{6,7},{7,6},{8,9},{9,8},{10,11... | collective-permute-start | bytes 393224 | tf_op jit(solution)/shard_map/sum_over_devices/ppermute | solution.py:149
  118.3 8.3 %collective-permute-start.44 = (bf16[128,512]{1,0:T(8,128)(2,1)S(1)}, bf16[128,512]{1,0:T(8,128)(2,1)S(1)}, u32[]{:S(2)}, u32[]{:S(2)}) collective-permute-start(bf16[128,512]{1,0:T(8,128)(2,1)S(1)} %get-tuple-element.139), channel_id=1, source_target_pairs={{0,12},{4,8},{8,4},{12,0},{1,13},{5,9},{9,5},{13,1},{2,14},{6,10},... | collective-permute-start | bytes 393224 | tf_op jit(solution)/shard_map/sum_over_devices/ppermute | solution.py:149
  120.6 11.4 %collective-permute-start.43 = (bf16[128,512]{1,0:T(8,128)(2,1)S(1)}, bf16[128,512]{1,0:T(8,128)(2,1)S(1)}, u32[]{:S(2)}, u32[]{:S(2)}) collective-permute-start(bf16[128,512]{1,0:T(8,128)(2,1)S(1)} %get-tuple-element.138), channel_id=1, source_target_pairs={{0,8},{4,12},{8,0},{12,4},{1,9},{5,13},{9,1},{13,5},{2,10},{6,14},... | collective-permute-start | bytes 393224 | tf_op jit(solution)/shard_map/sum_over_devices/ppermute | solution.py:149
  123.5 8.6 %collective-permute-start.45 = (bf16[128,512]{1,0:T(8,128)(2,1)S(1)}, bf16[128,512]{1,0:T(8,128)(2,1)S(1)}, u32[]{:S(2)}, u32[]{:S(2)}) collective-permute-start(bf16[128,512]{1,0:T(8,128)(2,1)S(1)} %get-tuple-element.140), channel_id=1, source_target_pairs={{0,4},{4,0},{8,12},{12,8},{1,5},{5,1},{9,13},{13,9},{2,6},{6,2},{1... | collective-permute-start | bytes 393224 | tf_op jit(solution)/shard_map/sum_over_devices/ppermute | solution.py:149

commit v9 on v8

--- a/solution.py
+++ b/solution.py
@@ -439,11 +439,13 @@
 
 def last_hidden_kernel(
     n, slots, group, distances, downs, pos, gain, pick, w_gate, w_up, w_down, g_some, u_some,
-    total_in, square_in, weight, *refs,
+    total_in, square_in, weight, place, *refs,
 ):
     pieces = [refs[k * n : (k + 1) * n] for k in range(len(distances))]
-    hidden_out, *refs = refs[n * len(distances) :]
-    d_outs, (r_all, x_slots, g_all, u_all, sems, d_sems) = refs[: len(downs)], refs[len(downs) :]
+    hidden_out, out, d_next, r_all, x_slots, g_all, u_all, d_here, y_slots, sems, d_sems = refs[
+        n * len(distances) :
+    ]
+    d_outs = (d_here, d_next)
     some, wide, hidden = g_some.shape
     ready, parts = some // group, (some + g_all.shape[0]) // group
     width = n * wide // len(distances)
@@ -497,6 +499,11 @@
     for i in range(parts):
         for copy in d_copies(i):
             copy.wait()
+    for e in range(d_here.shape[0]):
+        mine = slice(e * slots, (e + 1) * slots)
+        product = jnp.dot(hidden_out[mine, :], d_here[e], preferred_element_type=F32)
+        y_slots[mine, :] = product.astype(BF16)
+    out[...] = jnp.dot(place[...], y_slots[...], preferred_element_type=F32).astype(BF16)
 
 
 def self_down_kernel(slots, group, distances, pos, hidden, place, w_down, out, kept, y_slots, sems):
@@ -714,18 +721,23 @@
     def last_hidden(pieces, weights, state, downs):
         return pl.pallas_call(
             functools.partial(last_hidden_kernel, n, slots, group, late, downs),
-            out_shape=[sds((pairs, hidden), BF16)]
-            + [pltpu.VMEM((experts, hidden, cols), BF16)] * len(downs),
-            in_specs=[SMEM] + [VMEM] * 2 + [ANY] * 3 + [VMEM] * (5 + n * len(late)),
-            out_specs=[VMEM] * (1 + len(downs)),
+            out_shape=[
+                sds((pairs, hidden), BF16),
+                sds((total, cols), BF16),
+                pltpu.VMEM((experts, hidden, cols), BF16),
+            ],
+            in_specs=[SMEM] + [VMEM] * 2 + [ANY] * 3 + [VMEM] * (6 + n * len(late)),
+            out_specs=[VMEM] * 3,
             scratch_shapes=[pltpu.VMEM((total, wide), BF16), pltpu.VMEM((group * slots, wide), BF16)]
             + [pltpu.VMEM((experts - ahead, wide, hidden), BF16)] * 2
+            + [pltpu.VMEM((experts, hidden, cols), BF16), pltpu.VMEM((pairs, cols), BF16)]
             + [dma(((experts - ahead) // group, 2 * len(late)))]
             + [dma((experts // group, len(downs)))],
-            compiler_params=room(16),
+            compiler_params=room(21),
             cost_estimate=hidden_cost,
         )(
-            pos, gain_row, pick, w_gate, w_up, w_down, *map(here, weights), *state, weight, *pieces
+            pos, gain_row, pick, w_gate, w_up, w_down, *map(here, weights), *state,
+            weight, place, *pieces,
         )
 
     with jax.named_scope("heads_to_tokens"):
@@ -780,7 +792,7 @@
             r_pieces[d][3] = swap(after(r_pieces[d][2], state[1]), "head", 1)
         pieces = [r_pieces[d][e] for d in late for e in range(n)]
         with jax.named_scope("last_hidden_units"):
-            units, d_3, d_1 = last_hidden(pieces, late_weights, state, (3, 1))
+            units, out_3, d_1 = last_hidden(pieces, late_weights, state, (3, 1))
         r_choices = [r_pieces[d][d] for d in range(n)]
     def down(units, *weights):
         count = len(weights)
@@ -814,7 +826,6 @@
             )(pos, units, place, w_down)
 
     with jax.named_scope("sum_over_devices"):
-        (out_3,) = down(units, d_3)
         core_2 = swap(out_3, "head", 1)
         (out_2,) = down(after(units, out_3), d_2)
         halves = (tuple(range(n // 2, n)), tuple(range(n // 2)))

time: 140 us -> 140 us (level)
    pallas_call x2 -> x1, Pallas kernels: 4.2 us -> 2.1 us  [down(): pl.pallas_call(functools.partial(down_kernel, slots), out_shape=[sds((tot...]
    pallas_call x1, Pallas kernels: 6.68 us -> 8.25 us  [last_hidden(): pl.pallas_call(functools.partial(last_hidden_kernel, n, slots, group, lat...]
where the time goes in v9:
time: 140 us; the launch traced here: 139 us
  Pallas kernels  50.3 us (36%)
  waiting for transfers between devices  40 us (29%)
  starting transfers between devices  38.7 us (28%)
  blocking collectives  6.94 us (5%)
  local copies, waits for them, and re-layouts  2.7 us (2%)
    ppermute x46, waiting for transfers between devices, swap(): return lax.ppermute(array, axis, [(i, i ^ distance) for i in range(size)])  40 us
    ppermute x46, starting transfers between devices, swap(): return lax.ppermute(array, axis, [(i, i ^ distance) for i in range(size)])  38.7 us
    pallas_call x2, Pallas kernels, load(): pl.pallas_call(functools.partial(load_kernel, group, distances), out_shap...  10.5 us
    pallas_call x1, Pallas kernels, last_hidden(): pl.pallas_call(functools.partial(last_hidden_kernel, n, slots, group, lat...  8.25 us
    all_gather x1, blocking collectives, square_body(): return lax.all_gather(mixed, 'head', axis=1, tiled=True)  6.94 us
    pallas_call x1, Pallas kernels, first_hidden(): pl.pallas_call(functools.partial(first_hidden_kernel, n, slots, group, ea...  5.22 us
    pallas_call x1, Pallas kernels, square_body(): pl.pallas_call(functools.partial(project_tokens_kernel, n), out_shape=[sd...  4.94 us
    pallas_call x1, Pallas kernels, self_down(): pl.pallas_call(functools.partial(self_down_kernel, slots, group, (distanc...  3.93 us
  transfers between devices with their start and end apart: 46, of which 17 were waited for; matrix products, arithmetic and copies ran while one was open for 1% of the time, Pallas kernels for 27%

profile of v9, /device:TPU:0, one launch (start us, length us, event | category | flops | bytes accessed | tf_op | source)
XLA Modules:
  0.0 139.4 jit_solution(18415780690181133171)
XLA Ops:
  0.1 1.8 %cut_pieces.1 = (bf16[144,512]{1,0:T(8,128)(2,1)S(1)}, bf16[256,384]{1,0:T(8,128)(2,1)S(1)}, bf16[256,384]{1,0:T(8,128)(2,1)S(1)}, bf16[256,384]{1,0:T(8,128)(2,1)S(1)}) custom-call(s32[3]{0:T(128)S(1)} %pad_add_fusion.pos, s32[8,128]{1,0:T(8,128)} %bitcast.26, f32[8,128]{1,0:T(8,128)} %bitcast.27, bf16[128,2048]{1,0:T(8,128)(2,1)} %tokens.3, ...), custom_call_target="tpu_custom_call" | custom-call | tf_op jit(solution)/shard_map/cut_pieces/pallas_call | solution.py:602
  1.9 3.1 %collective-permute-start.3 = (bf16[256,384]{1,0:T(8,128)(2,1)S(1)}, bf16[256,384]{1,0:T(8,128)(2,1)S(1)}, u32[]{:S(2)}, u32[]{:S(2)}) collective-permute-start(bf16[256,384]{1,0:T(8,128)(2,1)S(1)} %get-tuple-element.75), channel_id=1, source_target_pairs={{0,4},{4,0},{8,12},{12,8},{1,5},{5,1},{9,13},{13,9},{2,6},{6,2},{1... | collective-permute-start | bytes 589832 | tf_op jit(solution)/shard_map/gather_tokens_and_weights/ppermute | solution.py:149
  5.0 2.6 %collective-permute-start.4 = (bf16[256,384]{1,0:T(8,128)(2,1)S(1)}, bf16[256,384]{1,0:T(8,128)(2,1)S(1)}, u32[]{:S(2)}, u32[]{:S(2)}) collective-permute-start(bf16[256,384]{1,0:T(8,128)(2,1)S(1)} %get-tuple-element.76), channel_id=1, source_target_pairs={{0,8},{4,12},{8,0},{12,4},{1,9},{5,13},{9,1},{13,5},{2,10},{6,14},... | collective-permute-start | bytes 589832 | tf_op jit(solution)/shard_map/gather_tokens_and_weights/ppermute | solution.py:149
  7.6 0.4 collective-permute-start
  8.0 3.9 %collective-permute-start.2 = (bf16[144,512]{1,0:T(8,128)(2,1)S(1)}, bf16[144,512]{1,0:T(8,128)(2,1)S(1)}, u32[]{:S(2)}, u32[]{:S(2)}) collective-permute-start(bf16[144,512]{1,0:T(8,128)(2,1)S(1)} %get-tuple-element.74.refs_0_), channel_id=1, source_target_pairs={{0,12},{4,8},{8,4},{12,0},{1,13},{5,9},{9,5},{13,1},{2,14},{6,10},... | collective-permute-start | bytes 442376 | tf_op jit(solution)/shard_map/gather_tokens_and_weights/ppermute | solution.py:149
  12.0 7.3 %collective-permute-done.refs_1_ = bf16[144,512]{1,0:T(8,128)(2,1)S(1)} collective-permute-done((bf16[144,512]{1,0:T(8,128)(2,1)S(1)}, bf16[144,512]{1,0:T(8,128)(2,1)S(1)}, u32[]{:S(2)}, u32[]{:S(2)}) %collective-permute-start) | collective-permute-done | bytes 147488 | tf_op jit(solution)/shard_map/gather_tokens_and_weights/ppermute | solution.py:149
  19.3 8.1 %collective-permute-done.1.refs_2_ = bf16[144,512]{1,0:T(8,128)(2,1)S(1)} collective-permute-done((bf16[144,512]{1,0:T(8,128)(2,1)S(1)}, bf16[144,512]{1,0:T(8,128)(2,1)S(1)}, u32[]{:S(2)}, u32[]{:S(2)}) %collective-permute-start.1) | collective-permute-done | bytes 147488 | tf_op jit(solution)/shard_map/gather_tokens_and_weights/ppermute | solution.py:149
  27.6 1.6 %collective-permute-start.6 = (bf16[3,128,512]{2,1,0:T(8,128)(2,1)S(1)}, bf16[3,128,512]{2,1,0:T(8,128)(2,1)S(1)}, u32[]{:S(2)}, u32[]{:S(2)}) collective-permute-start(bf16[3,128,512]{2,1,0:T(8,128)(2,1)S(1)} %pad_maximum_fusion.rest_0_), channel_id=1, source_target_pairs={{0,2},{1,3},{2,0},{3,1},{4,6},{5,7},{6,4},{7,5},{8,10},{9,11},{10,... | collective-permute-start | bytes 1179656 | tf_op jit(solution)/shard_map/gather_tokens_and_weights/ppermute | solution.py:149
  29.1 1.3 routing.1
  30.5 2.5 %collective-permute-start.7 = (bf16[256,384]{1,0:T(8,128)(2,1)S(1)}, bf16[256,384]{1,0:T(8,128)(2,1)S(1)}, u32[]{:S(2)}, u32[]{:S(2)}) collective-permute-start(bf16[256,384]{1,0:T(8,128)(2,1)S(1)} %get-tuple-element.84), channel_id=1, source_target_pairs={{0,12},{4,8},{8,4},{12,0},{1,13},{5,9},{9,5},{13,1},{2,14},{6,10},... | collective-permute-start | bytes 589832 | tf_op jit(solution)/shard_map/gather_tokens_and_weights/ppermute | solution.py:149
  33.0 1.5 %collective-permute-start.8 = (bf16[256,384]{1,0:T(8,128)(2,1)S(1)}, bf16[256,384]{1,0:T(8,128)(2,1)S(1)}, u32[]{:S(2)}, u32[]{:S(2)}) collective-permute-start(bf16[256,384]{1,0:T(8,128)(2,1)S(1)} %collective-permute-done.3.rest_4_), channel_id=1, source_target_pairs={{0,16},{16,0},{1,17},{17,1},{2,18},{18,2},{3,19},{19,3},{4,20},{20... | collective-permute-start | bytes 589832 | tf_op jit(solution)/shard_map/gather_tokens_and_weights/ppermute | solution.py:149
  34.5 0.5 collective-permute-start.9
  35.0 1.1 slice_bitcast_fusion.refs_0_
  36.1 0.6 collective-permute-start.17
  36.7 4.0 %gather_tokens_and_weights.1 = (bf16[8,1024,256]{2,1,0:T(8,128)(2,1)S(1)}, bf16[8,1024,256]{2,1,0:T(8,128)(2,1)S(1)}) custom-call(s32[3]{0:T(128)S(1)} %pad_add_fusion.pos, bf16[16,2048,256]{2,1,0:T(8,128)(2,1)} %w_gate.5, bf16[16,2048,256]{2,1,0:T(8,128)(2,1)} %w_up.5), custom_call_target="tpu_custom_call" | custom-call | bytes 8388608 | tf_op jit(solution)/shard_map/gather_tokens_and_weights/pallas_call | solution.py:624
  40.9 0.5 collective-permute-start.10
  41.5 1.5 %collective-permute-start.11 = (bf16[256,384]{1,0:T(8,128)(2,1)S(1)}, bf16[256,384]{1,0:T(8,128)(2,1)S(1)}, u32[]{:S(2)}, u32[]{:S(2)}) collective-permute-start(bf16[256,384]{1,0:T(8,128)(2,1)S(1)} %collective-permute-done.7.rest_6_), channel_id=1, source_target_pairs={{0,16},{16,0},{1,17},{17,1},{2,18},{18,2},{3,19},{19,3},{4,20},{20... | collective-permute-start | bytes 589832 | tf_op jit(solution)/shard_map/gather_tokens_and_weights/ppermute | solution.py:149
  43.2 0.6 copy-done.4
  43.9 4.9 %projected_tokens.1 = (f32[512,384]{1,0:T(8,128)S(1)}, bf16[512,256]{1,0:T(8,128)(2,1)S(1)}, bf16[128,512]{1,0:T(8,128)(2,1)S(1)}) custom-call(s32[3]{0:T(128)S(1)} %pad_add_fusion.pos, f32[1,2048]{1,0:T(1,128)S(1)} %bitcast.22, bf16[128,2048]{1,0:T(8,128)(2,1)} %tokens.3, bf16[4,512,512]{2,1,0:T(8,128)(2,1)} %weight.3, bf16[3,128,512]{2,1,0:T(8,128)(2,1)} %copy-done.2, ...), custom_call_target="tpu_custom_call" | custom-call | flops 805306368 | bytes 4194304 | tf_op jit(solution)/shard_map/projected_tokens/pallas_call | solution.py:677
  48.9 2.0 %attention.1 = (bf16[128,128]{1,0:T(8,128)(2,1)S(1)}, bf16[128,128]{1,0:T(8,128)(2,1)S(1)}, bf16[128,128]{1,0:T(8,128)(2,1)S(1)}, bf16[128,128]{1,0:T(8,128)(2,1)S(1)}) custom-call(s32[3]{0:T(128)S(1)} %pad_add_fusion.pos, f32[512,384]{1,0:T(8,128)S(1)} %get-tuple-element.93.partial, bf16[512,256]{1,0:T(8,128)(2,1)S(1)} %get-tuple-element.94.x_last, ...), custom_call_target="tpu_custom_call" | custom-call | tf_op jit(solution)/shard_map/attention/pallas_call | solution.py:699
  51.0 0.4 collective-permute-start.18
  51.4 1.2 collective-permute-start.14
  52.7 0.5 collective-permute-start.13
  53.3 1.5 %collective-permute-done.14 = bf16[128,128]{1,0:T(8,128)(2,1)S(1)} collective-permute-done((bf16[128,128]{1,0:T(8,128)(2,1)S(1)}, bf16[128,128]{1,0:T(8,128)(2,1)S(1)}, u32[]{:S(2)}, u32[]{:S(2)}) %collective-permute-start.14) | collective-permute-done | bytes 32800 | tf_op jit(solution)/shard_map/heads_to_tokens/ppermute | solution.py:149
  54.8 1.7 %collective-permute-done.13 = bf16[128,128]{1,0:T(8,128)(2,1)S(1)} collective-permute-done((bf16[128,128]{1,0:T(8,128)(2,1)S(1)}, bf16[128,128]{1,0:T(8,128)(2,1)S(1)}, u32[]{:S(2)}, u32[]{:S(2)}) %collective-permute-start.13) | collective-permute-done | bytes 32800 | tf_op jit(solution)/shard_map/heads_to_tokens/ppermute | solution.py:149
  56.6 1.7 %collective-permute-start.15 = (bf16[4,128,128]{2,1,0:T(8,128)(2,1)S(1)}, bf16[4,128,128]{2,1,0:T(8,128)(2,1)S(1)}, u32[]{:S(2)}, u32[]{:S(2)}) collective-permute-start(bf16[4,128,128]{2,1,0:T(8,128)(2,1)S(1)} %pad_maximum_fusion.1.rest_4_), channel_id=1, source_target_pairs={{0,8},{4,12},{8,0},{12,4},{1,9},{5,13},{9,1},{13,5},{2,10},{6,14},... | collective-permute-start | bytes 393224 | tf_op jit(solution)/shard_map/heads_to_tokens/ppermute | solution.py:149
  58.3 0.3 collective-permute-start.19
  58.6 6.5 %expert_weights.2 = (bf16[16,1024,256]{2,1,0:T(8,128)(2,1)S(1)}, bf16[16,1024,256]{2,1,0:T(8,128)(2,1)S(1)}) custom-call(s32[3]{0:T(128)S(1)} %pad_add_fusion.pos, bf16[16,2048,256]{2,1,0:T(8,128)(2,1)} %w_gate.5, bf16[16,2048,256]{2,1,0:T(8,128)(2,1)} %w_up.5), custom_call_target="tpu_custom_call" | custom-call | bytes 16777216 | tf_op jit(solution)/shard_map/heads_to_tokens/expert_weights/pallas_call | solution.py:624
  65.1 1.8 %collective-permute-start.20 = (bf16[4,128,128]{2,1,0:T(8,128)(2,1)S(1)}, bf16[4,128,128]{2,1,0:T(8,128)(2,1)S(1)}, u32[]{:S(2)}, u32[]{:S(2)}) collective-permute-start(bf16[4,128,128]{2,1,0:T(8,128)(2,1)S(1)} %collective-permute-done.15.rest_6_), channel_id=1, source_target_pairs={{0,4},{4,0},{8,12},{12,8},{1,5},{5,1},{9,13},{13,9},{2,6},{6,2},{1... | collective-permute-start | bytes 393224 | tf_op jit(solution)/shard_map/heads_to_tokens/ppermute | solution.py:149
  66.9 2.8 %expert_weights.3.refs_0_ = bf16[16,256,512]{2,1,0:T(8,128)(2,1)S(1)} custom-call(s32[3]{0:T(128)S(1)} %pad_add_fusion.pos, bf16[16,256,2048]{2,1,0:T(8,128)(2,1)} %w_down.5), custom_call_target="tpu_custom_call" | custom-call | bytes 4194304 | tf_op jit(solution)/shard_map/heads_to_tokens/expert_weights/pallas_call | solution.py:636
  70.1 1.4 output_projection.1.refs_0_
  71.5 1.8 %collective-permute-start.23 = (bf16[128,512]{1,0:T(8,128)(2,1)S(1)}, bf16[128,512]{1,0:T(8,128)(2,1)S(1)}, u32[]{:S(2)}, u32[]{:S(2)}) collective-permute-start(bf16[128,512]{1,0:T(8,128)(2,1)S(1)} %output_projection.1.refs_0_), channel_id=1, source_target_pairs={{0,4},{4,0},{8,12},{12,8},{1,5},{5,1},{9,13},{13,9},{2,6},{6,2},{1... | collective-permute-start | bytes 393224 | tf_op jit(solution)/shard_map/gather_residual/ppermute | solution.py:149
  73.3 1.3 collective-permute-start.21
  74.6 0.9 collective-permute-start.28
  75.4 1.4 collective-permute-done.23.refs_4_
  76.8 1.0 collective-permute-start.30
  77.8 2.8 %collective-permute-done.21.refs_0_ = bf16[128,512]{1,0:T(8,128)(2,1)S(1)} collective-permute-done((bf16[128,512]{1,0:T(8,128)(2,1)S(1)}, bf16[128,512]{1,0:T(8,128)(2,1)S(1)}, u32[]{:S(2)}, u32[]{:S(2)}) %collective-permute-start.21) | collective-permute-done | bytes 131104 | tf_op jit(solution)/shard_map/gather_residual/ppermute | solution.py:149
  80.5 0.5 collective-permute-start.29
  81.1 0.6 collective-permute-done.30.refs_6_
  81.8 3.7 %collective-permute-done.22.refs_4_ = bf16[128,512]{1,0:T(8,128)(2,1)S(1)} collective-permute-done((bf16[128,512]{1,0:T(8,128)(2,1)S(1)}, bf16[128,512]{1,0:T(8,128)(2,1)S(1)}, u32[]{:S(2)}, u32[]{:S(2)}) %collective-permute-start.22) | collective-permute-done | bytes 131104 | tf_op jit(solution)/shard_map/gather_residual/ppermute | solution.py:149
  85.5 1.2 collective-permute-start.25
  86.7 0.2 collective-permute-start.35
  86.9 0.9 collective-permute-start.26
  87.8 5.2 %first_hidden_units.1 = (f32[1280,512]{1,0:T(8,128)S(1)}, f32[1280,128]{1,0:T(8,128)S(1)}) custom-call(s32[3]{0:T(128)S(1)} %pad_add_fusion.pos, f32[1,2048]{1,0:T(1,128)S(1)} %bitcast.20, bf16[1280,512]{1,0:T(8,128)(2,1)S(1)} %get-tuple-element.88.pick, bf16[16,1024,256]{2,1,0:T(8,128)(2,1)S(1)} %get-tuple-element.100.g_all, ...), custom_call_target="tpu_custom_call" | custom-call | flops 2684354560 | bytes 16777216 | tf_op jit(solution)/shard_map/gather_residual/first_hidden_units/pallas_call | solution.py:711
  93.1 1.1 collective-permute-done.26.refs_6_
  94.4 1.2 collective-permute-done.32.refs_7_
  95.6 8.2 %last_hidden_units.1 = (bf16[1280,256]{1,0:T(8,128)(2,1)S(1)}, bf16[512,512]{1,0:T(8,128)(2,1)S(1)}, bf16[16,256,512]{2,1,0:T(8,128)(2,1)S(1)}) custom-call(s32[3]{0:T(128)S(1)} %pad_add_fusion.pos, f32[1,2048]{1,0:T(1,128)S(1)} %bitcast.21, bf16[1280,512]{1,0:T(8,128)(2,1)S(1)} %get-tuple-element.88.pick, bf16[16,2048,256]{2,1,0:T(8,128)(2,1)} %w_gate.5, ...), custom_call_target="tpu_custom_call" | custom-call | flops 2684354560 | bytes 16777216 | tf_op jit(solution)/shard_map/gather_residual/last_hidden_units/pallas_call | solution.py:722
  103.8 0.2 collective-permute-start.36
  104.0 2.1 %down_products.1.base = bf16[512,512]{1,0:T(8,128)(2,1)S(1)} custom-call(s32[3]{0:T(128)S(1)} %pad_add_fusion.pos, bf16[1280,256]{1,0:T(8,128)(2,1)S(1)} %get-tuple-element.129.hidden, bf16[512,1280]{1,0:T(8,128)(2,1)S(1)} %get-tuple-element.119.place, bf16[16,256,512]{2,1,0:T(8,128)(2,1)S(1)} %expert_weights.3.refs_0_), custom_call_target="tpu_custom_call" | custom-call | flops 1006632960 | bytes 4194304 | tf_op jit(solution)/shard_map/sum_over_devices/down_products/pallas_call | solution.py:800
  106.2 1.3 sums_over_cores.1
  107.5 1.2 collective-permute-start.40
  108.7 2.9 %down_products_by_block.1 = (bf16[128,512]{1,0:T(8,128)(2,1)}, bf16[128,512]{1,0:T(8,128)(2,1)}, bf16[128,512]{1,0:T(8,128)(2,1)S(1)}, bf16[128,512]{1,0:T(8,128)(2,1)}) custom-call(s32[3]{0:T(128)S(1)} %pad_add_fusion.pos, bf16[1280,256]{1,0:T(8,128)(2,1)S(1)} %get-tuple-element.129.hidden, bf16[512,1280]{1,0:T(8,128)(2,1)S(1)} %get-tuple-element.119.place, ...), custom_call_target="tpu_custom_call" | custom-call | flops 20000000000 | bytes 4194304 | tf_op jit(solution)/shard_map/sum_over_devices/down_products_by_block/pallas_call | solution.py:843
  111.6 0.8 collective-permute-start.37
  112.6 0.3 collective-permute-start.38
  113.2 3.9 %down_products_alone.1.base = bf16[512,512]{1,0:T(8,128)(2,1)S(1)} custom-call(s32[3]{0:T(128)S(1)} %pad_add_fusion.pos, bf16[1280,256]{1,0:T(8,128)(2,1)S(1)} %get-tuple-element.129.hidden, bf16[512,1280]{1,0:T(8,128)(2,1)S(1)} %get-tuple-element.119.place, bf16[16,256,2048]{2,1,0:T(8,128)(2,1)} %w_down.5), custom_call_target="tpu_custom_call" | custom-call | tf_op jit(solution)/shard_map/sum_over_devices/down_products_alone/pallas_call | solution.py:814
  117.1 0.6 rows_2_3.1
  117.8 2.3 %collective-permute-start.44 = (bf16[128,512]{1,0:T(8,128)(2,1)S(1)}, bf16[128,512]{1,0:T(8,128)(2,1)S(1)}, u32[]{:S(2)}, u32[]{:S(2)}) collective-permute-start(bf16[128,512]{1,0:T(8,128)(2,1)S(1)} %get-tuple-element.139), channel_id=1, source_target_pairs={{0,12},{4,8},{8,4},{12,0},{1,13},{5,9},{9,5},{13,1},{2,14},{6,10},... | collective-permute-start | bytes 393224 | tf_op jit(solution)/shard_map/sum_over_devices/ppermute | solution.py:149
  120.1 1.8 %collective-permute-done.37.part = bf16[256,512]{1,0:T(8,128)(2,1)S(1)} collective-permute-done((bf16[256,512]{1,0:T(8,128)(2,1)S(1)}, bf16[256,512]{1,0:T(8,128)(2,1)S(1)}, u32[]{:S(2)}, u32[]{:S(2)}) %collective-permute-start.37) | collective-permute-done | bytes 262176 | tf_op jit(solution)/shard_map/sum_over_devices/ppermute | solution.py:149
  121.9 1.1 rows_0_1.1
  123.0 0.4 collective-permute-start.45
  123.4 2.7 %collective-permute-done.44 = bf16[128,512]{1,0:T(8,128)(2,1)S(1)} collective-permute-done((bf16[128,512]{1,0:T(8,128)(2,1)S(1)}, bf16[128,512]{1,0:T(8,128)(2,1)S(1)}, u32[]{:S(2)}, u32[]{:S(2)}) %collective-permute-start.44) | collective-permute-done | bytes 131104 | tf_op jit(solution)/shard_map/sum_over_devices/ppermute | solution.py:149
  126.0 5.4 %collective-permute-done.43 = bf16[128,512]{1,0:T(8,128)(2,1)S(1)} collective-permute-done((bf16[128,512]{1,0:T(8,128)(2,1)S(1)}, bf16[128,512]{1,0:T(8,128)(2,1)S(1)}, u32[]{:S(2)}, u32[]{:S(2)}) %collective-permute-start.43) | collective-permute-done | bytes 131104 | tf_op jit(solution)/shard_map/sum_over_devices/ppermute | solution.py:149
  131.6 6.9 %all_gather.3 = bf16[128,2048]{1,0:T(8,128)(2,1)S(1)} all-gather(bf16[128,512]{1,0:T(8,128)(2,1)S(1)} %add_convert_fusion), channel_id=1, replica_groups=mesh['grp'=2,'seq'=4,'head'=4] {'head'}, dimensions={1}, use_global_device_ids=true | all-gather | bytes 655360 | tf_op jit(solution)/shard_map/gather_columns/all_gather | solution.py:875
  138.6 0.8 copy.11
  (77 shorter events, 2.3 us)
Async XLA Ops:
  1.9 25.5 %collective-permute-start.3 = (bf16[256,384]{1,0:T(8,128)(2,1)S(1)}, bf16[256,384]{1,0:T(8,128)(2,1)S(1)}, u32[]{:S(2)}, u32[]{:S(2)}) collective-permute-start(bf16[256,384]{1,0:T(8,128)(2,1)S(1)} %get-tuple-element.75), channel_id=1, source_target_pairs={{0,4},{4,0},{8,12},{12,8},{1,5},{5,1},{9,13},{13,9},{2,6},{6,2},{1... | collective-permute-start | bytes 589832 | tf_op jit(solution)/shard_map/gather_tokens_and_weights/ppermute | solution.py:149
  5.0 22.4 %collective-permute-start.4 = (bf16[256,384]{1,0:T(8,128)(2,1)S(1)}, bf16[256,384]{1,0:T(8,128)(2,1)S(1)}, u32[]{:S(2)}, u32[]{:S(2)}) collective-permute-start(bf16[256,384]{1,0:T(8,128)(2,1)S(1)} %get-tuple-element.76), channel_id=1, source_target_pairs={{0,8},{4,12},{8,0},{12,4},{1,9},{5,13},{9,1},{13,5},{2,10},{6,14},... | collective-permute-start | bytes 589832 | tf_op jit(solution)/shard_map/gather_tokens_and_weights/ppermute | solution.py:149
  7.6 11.7 %collective-permute-start = (bf16[144,512]{1,0:T(8,128)(2,1)S(1)}, bf16[144,512]{1,0:T(8,128)(2,1)S(1)}, u32[]{:S(2)}, u32[]{:S(2)}) collective-permute-start(bf16[144,512]{1,0:T(8,128)(2,1)S(1)} %get-tuple-element.74.refs_0_), channel_id=1, source_target_pairs={{0,4},{4,0},{8,12},{12,8},{1,5},{5,1},{9,13},{13,9},{2,6},{6,2},{1... | collective-permute-start | bytes 442376 | tf_op jit(solution)/shard_map/gather_tokens_and_weights/ppermute | solution.py:149
  8.0 19.4 %collective-permute-start.1 = (bf16[144,512]{1,0:T(8,128)(2,1)S(1)}, bf16[144,512]{1,0:T(8,128)(2,1)S(1)}, u32[]{:S(2)}, u32[]{:S(2)}) collective-permute-start(bf16[144,512]{1,0:T(8,128)(2,1)S(1)} %get-tuple-element.74.refs_0_), channel_id=1, source_target_pairs={{0,8},{4,12},{8,0},{12,4},{1,9},{5,13},{9,1},{13,5},{2,10},{6,14},... | collective-permute-start | bytes 442376 | tf_op jit(solution)/shard_map/gather_tokens_and_weights/ppermute | solution.py:149
  8.0 19.4 %collective-permute-start.2 = (bf16[144,512]{1,0:T(8,128)(2,1)S(1)}, bf16[144,512]{1,0:T(8,128)(2,1)S(1)}, u32[]{:S(2)}, u32[]{:S(2)}) collective-permute-start(bf16[144,512]{1,0:T(8,128)(2,1)S(1)} %get-tuple-element.74.refs_0_), channel_id=1, source_target_pairs={{0,12},{4,8},{8,4},{12,0},{1,13},{5,9},{9,5},{13,1},{2,14},{6,10},... | collective-permute-start | bytes 442376 | tf_op jit(solution)/shard_map/gather_tokens_and_weights/ppermute | solution.py:149
  27.4 13.3 %copy-start.6 = (bf16[256,384]{1,0:T(8,128)(2,1)}, bf16[256,384]{1,0:T(8,128)(2,1)S(1)}, u32[]{:S(2)}) copy-start(bf16[256,384]{1,0:T(8,128)(2,1)S(1)} %collective-permute-done.3.rest_4_) | copy-start | bytes 589828
  27.4 13.3 %copy-start.7 = (bf16[256,384]{1,0:T(8,128)(2,1)}, bf16[256,384]{1,0:T(8,128)(2,1)S(1)}, u32[]{:S(2)}) copy-start(bf16[256,384]{1,0:T(8,128)(2,1)S(1)} %collective-permute-done.4.rest_5_) | copy-start | bytes 589828
  27.6 13.2 %copy-start.2 = (bf16[3,128,512]{2,1,0:T(8,128)(2,1)}, bf16[3,128,512]{2,1,0:T(8,128)(2,1)S(1)}, u32[]{:S(2)}) copy-start(bf16[3,128,512]{2,1,0:T(8,128)(2,1)S(1)} %pad_maximum_fusion.rest_0_) | copy-start | bytes 1179652
  27.6 13.4 %collective-permute-start.6 = (bf16[3,128,512]{2,1,0:T(8,128)(2,1)S(1)}, bf16[3,128,512]{2,1,0:T(8,128)(2,1)S(1)}, u32[]{:S(2)}, u32[]{:S(2)}) collective-permute-start(bf16[3,128,512]{2,1,0:T(8,128)(2,1)S(1)} %pad_maximum_fusion.rest_0_), channel_id=1, source_target_pairs={{0,2},{1,3},{2,0},{3,1},{4,6},{5,7},{6,4},{7,5},{8,10},{9,11},{10,... | collective-permute-start | bytes 1179656 | tf_op jit(solution)/shard_map/gather_tokens_and_weights/ppermute | solution.py:149
  30.5 10.3 %collective-permute-start.7 = (bf16[256,384]{1,0:T(8,128)(2,1)S(1)}, bf16[256,384]{1,0:T(8,128)(2,1)S(1)}, u32[]{:S(2)}, u32[]{:S(2)}) collective-permute-start(bf16[256,384]{1,0:T(8,128)(2,1)S(1)} %get-tuple-element.84), channel_id=1, source_target_pairs={{0,12},{4,8},{8,4},{12,0},{1,13},{5,9},{9,5},{13,1},{2,14},{6,10},... | collective-permute-start | bytes 589832 | tf_op jit(solution)/shard_map/gather_tokens_and_weights/ppermute | solution.py:149
  33.0 7.9 %collective-permute-start.8 = (bf16[256,384]{1,0:T(8,128)(2,1)S(1)}, bf16[256,384]{1,0:T(8,128)(2,1)S(1)}, u32[]{:S(2)}, u32[]{:S(2)}) collective-permute-start(bf16[256,384]{1,0:T(8,128)(2,1)S(1)} %collective-permute-done.3.rest_4_), channel_id=1, source_target_pairs={{0,16},{16,0},{1,17},{17,1},{2,18},{18,2},{3,19},{19,3},{4,20},{20... | collective-permute-start | bytes 589832 | tf_op jit(solution)/shard_map/gather_tokens_and_weights/ppermute | solution.py:149
  34.5 6.4 %collective-permute-start.9 = (bf16[256,384]{1,0:T(8,128)(2,1)S(1)}, bf16[256,384]{1,0:T(8,128)(2,1)S(1)}, u32[]{:S(2)}, u32[]{:S(2)}) collective-permute-start(bf16[256,384]{1,0:T(8,128)(2,1)S(1)} %collective-permute-done.4.rest_5_), channel_id=1, source_target_pairs={{0,16},{16,0},{1,17},{17,1},{2,18},{18,2},{3,19},{19,3},{4,20},{20... | collective-permute-start | bytes 589832 | tf_op jit(solution)/shard_map/gather_tokens_and_weights/ppermute | solution.py:149
  36.1 7.8 %copy-start.1 = (f32[2048]{0:T(1024)S(1)}, f32[2048]{0:T(1024)}, u32[]{:S(2)}) copy-start(f32[2048]{0:T(1024)} %param.11) | copy-start | bytes 24580
  36.1 14.9 %collective-permute-start.17 = (bf16[512,512]{1,0:T(8,128)(2,1)S(1)}, bf16[512,512]{1,0:T(8,128)(2,1)S(1)}, u32[]{:S(2)}, u32[]{:S(2)}) collective-permute-start(bf16[512,512]{1,0:T(8,128)(2,1)S(1)} %slice_bitcast_fusion.refs_0_), channel_id=1, source_target_pairs={{0,2},{1,3},{2,0},{3,1},{4,6},{5,7},{6,4},{7,5},{8,10},{9,11},{10,... | collective-permute-start | bytes 1572872 | tf_op jit(solution)/shard_map/gather_out_weights/ppermute | solution.py:149
  40.8 2.4 %copy-start.8 = (bf16[256,384]{1,0:T(8,128)(2,1)}, bf16[256,384]{1,0:T(8,128)(2,1)S(1)}, u32[]{:S(2)}) copy-start(bf16[256,384]{1,0:T(8,128)(2,1)S(1)} %collective-permute-done.7.rest_6_) | copy-start | bytes 589828
  40.8 2.2 %collective-permute-start.5 = (bf16[3,128,512]{2,1,0:T(8,128)(2,1)S(1)}, bf16[3,128,512]{2,1,0:T(8,128)(2,1)S(1)}, u32[]{:S(2)}, u32[]{:S(2)}) collective-permute-start(bf16[3,128,512]{2,1,0:T(8,128)(2,1)S(1)} %pad_maximum_fusion.rest_0_), channel_id=1, source_target_pairs={{0,1},{1,0},{2,3},{3,2},{4,5},{5,4},{6,7},{7,6},{8,9},{9,8},{10,11... | collective-permute-start | bytes 1179656 | tf_op jit(solution)/shard_map/gather_tokens_and_weights/ppermute | solution.py:149
  40.9 2.3 %copy-start.9 = (bf16[256,384]{1,0:T(8,128)(2,1)}, bf16[256,384]{1,0:T(8,128)(2,1)S(1)}, u32[]{:S(2)}) copy-start(bf16[256,384]{1,0:T(8,128)(2,1)S(1)} %collective-permute-done.8.rest_7_) | copy-start | bytes 589828
  40.9 2.3 %copy-start.10 = (bf16[256,384]{1,0:T(8,128)(2,1)}, bf16[256,384]{1,0:T(8,128)(2,1)S(1)}, u32[]{:S(2)}) copy-start(bf16[256,384]{1,0:T(8,128)(2,1)S(1)} %collective-permute-done.9.rest_8_) | copy-start | bytes 589828
  40.9 2.2 %copy-start.3 = (bf16[3,128,512]{2,1,0:T(8,128)(2,1)}, bf16[3,128,512]{2,1,0:T(8,128)(2,1)S(1)}, u32[]{:S(2)}) copy-start(bf16[3,128,512]{2,1,0:T(8,128)(2,1)S(1)} %collective-permute-done.6.rest_2_) | copy-start | bytes 1179652
  40.9 2.2 %collective-permute-start.10 = (bf16[3,128,512]{2,1,0:T(8,128)(2,1)S(1)}, bf16[3,128,512]{2,1,0:T(8,128)(2,1)S(1)}, u32[]{:S(2)}, u32[]{:S(2)}) collective-permute-start(bf16[3,128,512]{2,1,0:T(8,128)(2,1)S(1)} %collective-permute-done.6.rest_2_), channel_id=1, source_target_pairs={{0,1},{1,0},{2,3},{3,2},{4,5},{5,4},{6,7},{7,6},{8,9},{9,8},{10,11... | collective-permute-start | bytes 1179656 | tf_op jit(solution)/shard_map/gather_tokens_and_weights/ppermute | solution.py:149
  41.5 7.4 %collective-permute-start.11 = (bf16[256,384]{1,0:T(8,128)(2,1)S(1)}, bf16[256,384]{1,0:T(8,128)(2,1)S(1)}, u32[]{:S(2)}, u32[]{:S(2)}) collective-permute-start(bf16[256,384]{1,0:T(8,128)(2,1)S(1)} %collective-permute-done.7.rest_6_), channel_id=1, source_target_pairs={{0,16},{16,0},{1,17},{17,1},{2,18},{18,2},{3,19},{19,3},{4,20},{20... | collective-permute-start | bytes 589832 | tf_op jit(solution)/shard_map/gather_tokens_and_weights/ppermute | solution.py:149
  43.0 0.8 copy-start.4
  43.2 0.8 copy-start.5
  50.9 18.8 %collective-permute-start.16 = (bf16[512,512]{1,0:T(8,128)(2,1)S(1)}, bf16[512,512]{1,0:T(8,128)(2,1)S(1)}, u32[]{:S(2)}, u32[]{:S(2)}) collective-permute-start(bf16[512,512]{1,0:T(8,128)(2,1)S(1)} %slice_bitcast_fusion.refs_0_), channel_id=1, source_target_pairs={{0,1},{1,0},{2,3},{3,2},{4,5},{5,4},{6,7},{7,6},{8,9},{9,8},{10,11... | collective-permute-start | bytes 1572872 | tf_op jit(solution)/shard_map/heads_to_tokens/ppermute | solution.py:149
  51.0 18.6 %collective-permute-start.18 = (bf16[512,512]{1,0:T(8,128)(2,1)S(1)}, bf16[512,512]{1,0:T(8,128)(2,1)S(1)}, u32[]{:S(2)}, u32[]{:S(2)}) collective-permute-start(bf16[512,512]{1,0:T(8,128)(2,1)S(1)} %collective-permute-done.17.refs_2_), channel_id=1, source_target_pairs={{0,1},{1,0},{2,3},{3,2},{4,5},{5,4},{6,7},{7,6},{8,9},{9,8},{10,11... | collective-permute-start | bytes 1572872 | tf_op jit(solution)/shard_map/heads_to_tokens/ppermute | solution.py:149
  51.4 3.4 %collective-permute-start.14 = (bf16[128,128]{1,0:T(8,128)(2,1)S(1)}, bf16[128,128]{1,0:T(8,128)(2,1)S(1)}, u32[]{:S(2)}, u32[]{:S(2)}) collective-permute-start(bf16[128,128]{1,0:T(8,128)(2,1)S(1)} %get-tuple-element.98), channel_id=1, source_target_pairs={{0,3},{1,2},{2,1},{3,0},{4,7},{5,6},{6,5},{7,4},{8,11},{9,10},{10,... | collective-permute-start | bytes 98312 | tf_op jit(solution)/shard_map/heads_to_tokens/ppermute | solution.py:149
  52.7 3.9 %collective-permute-start.13 = (bf16[128,128]{1,0:T(8,128)(2,1)S(1)}, bf16[128,128]{1,0:T(8,128)(2,1)S(1)}, u32[]{:S(2)}, u32[]{:S(2)}) collective-permute-start(bf16[128,128]{1,0:T(8,128)(2,1)S(1)} %get-tuple-element.97), channel_id=1, source_target_pairs={{0,2},{1,3},{2,0},{3,1},{4,6},{5,7},{6,4},{7,5},{8,10},{9,11},{10,... | collective-permute-start | bytes 98312 | tf_op jit(solution)/shard_map/heads_to_tokens/ppermute | solution.py:149
  53.2 3.4 %collective-permute-start.12 = (bf16[128,128]{1,0:T(8,128)(2,1)S(1)}, bf16[128,128]{1,0:T(8,128)(2,1)S(1)}, u32[]{:S(2)}, u32[]{:S(2)}) collective-permute-start(bf16[128,128]{1,0:T(8,128)(2,1)S(1)} %get-tuple-element.96), channel_id=1, source_target_pairs={{0,1},{1,0},{2,3},{3,2},{4,5},{5,4},{6,7},{7,6},{8,9},{9,8},{10,11... | collective-permute-start | bytes 98312 | tf_op jit(solution)/shard_map/heads_to_tokens/ppermute | solution.py:149
  56.6 8.5 %collective-permute-start.15 = (bf16[4,128,128]{2,1,0:T(8,128)(2,1)S(1)}, bf16[4,128,128]{2,1,0:T(8,128)(2,1)S(1)}, u32[]{:S(2)}, u32[]{:S(2)}) collective-permute-start(bf16[4,128,128]{2,1,0:T(8,128)(2,1)S(1)} %pad_maximum_fusion.1.rest_4_), channel_id=1, source_target_pairs={{0,8},{4,12},{8,0},{12,4},{1,9},{5,13},{9,1},{13,5},{2,10},{6,14},... | collective-permute-start | bytes 393224 | tf_op jit(solution)/shard_map/heads_to_tokens/ppermute | solution.py:149
  58.3 11.6 %collective-permute-start.19 = (bf16[4,128,128]{2,1,0:T(8,128)(2,1)S(1)}, bf16[4,128,128]{2,1,0:T(8,128)(2,1)S(1)}, u32[]{:S(2)}, u32[]{:S(2)}) collective-permute-start(bf16[4,128,128]{2,1,0:T(8,128)(2,1)S(1)} %pad_maximum_fusion.1.rest_4_), channel_id=1, source_target_pairs={{0,4},{4,0},{8,12},{12,8},{1,5},{5,1},{9,13},{13,9},{2,6},{6,2},{1... | collective-permute-start | bytes 393224 | tf_op jit(solution)/shard_map/heads_to_tokens/ppermute | solution.py:149
  65.1 5.0 %collective-permute-start.20 = (bf16[4,128,128]{2,1,0:T(8,128)(2,1)S(1)}, bf16[4,128,128]{2,1,0:T(8,128)(2,1)S(1)}, u32[]{:S(2)}, u32[]{:S(2)}) collective-permute-start(bf16[4,128,128]{2,1,0:T(8,128)(2,1)S(1)} %collective-permute-done.15.rest_6_), channel_id=1, source_target_pairs={{0,4},{4,0},{8,12},{12,8},{1,5},{5,1},{9,13},{13,9},{2,6},{6,2},{1... | collective-permute-start | bytes 393224 | tf_op jit(solution)/shard_map/heads_to_tokens/ppermute | solution.py:149
  69.6 18.1 %copy-start = (f32[2048]{0:T(1024)S(1)}, f32[2048]{0:T(1024)}, u32[]{:S(2)}) copy-start(f32[2048]{0:T(1024)} %param.12) | copy-start | bytes 24580
  71.5 5.3 %collective-permute-start.23 = (bf16[128,512]{1,0:T(8,128)(2,1)S(1)}, bf16[128,512]{1,0:T(8,128)(2,1)S(1)}, u32[]{:S(2)}, u32[]{:S(2)}) collective-permute-start(bf16[128,512]{1,0:T(8,128)(2,1)S(1)} %output_projection.1.refs_0_), channel_id=1, source_target_pairs={{0,4},{4,0},{8,12},{12,8},{1,5},{5,1},{9,13},{13,9},{2,6},{6,2},{1... | collective-permute-start | bytes 393224 | tf_op jit(solution)/shard_map/gather_residual/ppermute | solution.py:149
  73.3 7.3 %collective-permute-start.21 = (bf16[128,512]{1,0:T(8,128)(2,1)S(1)}, bf16[128,512]{1,0:T(8,128)(2,1)S(1)}, u32[]{:S(2)}, u32[]{:S(2)}) collective-permute-start(bf16[128,512]{1,0:T(8,128)(2,1)S(1)} %output_projection.1.refs_0_), channel_id=1, source_target_pairs={{0,8},{4,12},{8,0},{12,4},{1,9},{5,13},{9,1},{13,5},{2,10},{6,14},... | collective-permute-start | bytes 393224 | tf_op jit(solution)/shard_map/gather_residual/ppermute | solution.py:149
  74.6 6.0 %collective-permute-start.28 = (bf16[128,512]{1,0:T(8,128)(2,1)S(1)}, bf16[128,512]{1,0:T(8,128)(2,1)S(1)}, u32[]{:S(2)}, u32[]{:S(2)}) collective-permute-start(bf16[128,512]{1,0:T(8,128)(2,1)S(1)} %output_projection.1.refs_0_), channel_id=1, source_target_pairs={{0,2},{1,3},{2,0},{3,1},{4,6},{5,7},{6,4},{7,5},{8,10},{9,11},{10,... | collective-permute-start | bytes 393224 | tf_op jit(solution)/shard_map/gather_residual/ppermute | solution.py:149
  76.8 5.0 %collective-permute-start.30 = (bf16[128,512]{1,0:T(8,128)(2,1)S(1)}, bf16[128,512]{1,0:T(8,128)(2,1)S(1)}, u32[]{:S(2)}, u32[]{:S(2)}) collective-permute-start(bf16[128,512]{1,0:T(8,128)(2,1)S(1)} %collective-permute-done.23.refs_4_), channel_id=1, source_target_pairs={{0,2},{1,3},{2,0},{3,1},{4,6},{5,7},{6,4},{7,5},{8,10},{9,11},{10,... | collective-permute-start | bytes 393224 | tf_op jit(solution)/shard_map/gather_residual/ppermute | solution.py:149
  80.5 5.0 %collective-permute-start.22 = (bf16[128,512]{1,0:T(8,128)(2,1)S(1)}, bf16[128,512]{1,0:T(8,128)(2,1)S(1)}, u32[]{:S(2)}, u32[]{:S(2)}) collective-permute-start(bf16[128,512]{1,0:T(8,128)(2,1)S(1)} %collective-permute-done.21.refs_0_), channel_id=1, source_target_pairs={{0,4},{4,0},{8,12},{12,8},{1,5},{5,1},{9,13},{13,9},{2,6},{6,2},{1... | collective-permute-start | bytes 393224 | tf_op jit(solution)/shard_map/gather_residual/ppermute | solution.py:149
  80.5 5.0 %collective-permute-start.27 = (bf16[128,512]{1,0:T(8,128)(2,1)S(1)}, bf16[128,512]{1,0:T(8,128)(2,1)S(1)}, u32[]{:S(2)}, u32[]{:S(2)}) collective-permute-start(bf16[128,512]{1,0:T(8,128)(2,1)S(1)} %output_projection.1.refs_0_), channel_id=1, source_target_pairs={{0,1},{1,0},{2,3},{3,2},{4,5},{5,4},{6,7},{7,6},{8,9},{9,8},{10,11... | collective-permute-start | bytes 393224 | tf_op jit(solution)/shard_map/gather_residual/ppermute | solution.py:149
  80.5 6.1 %collective-permute-start.29 = (bf16[128,512]{1,0:T(8,128)(2,1)S(1)}, bf16[128,512]{1,0:T(8,128)(2,1)S(1)}, u32[]{:S(2)}, u32[]{:S(2)}) collective-permute-start(bf16[128,512]{1,0:T(8,128)(2,1)S(1)} %collective-permute-done.28.refs_2_), channel_id=1, source_target_pairs={{0,1},{1,0},{2,3},{3,2},{4,5},{5,4},{6,7},{7,6},{8,9},{9,8},{10,11... | collective-permute-start | bytes 393224 | tf_op jit(solution)/shard_map/gather_residual/ppermute | solution.py:149
  81.1 5.9 %collective-permute-start.24 = (bf16[128,512]{1,0:T(8,128)(2,1)S(1)}, bf16[128,512]{1,0:T(8,128)(2,1)S(1)}, u32[]{:S(2)}, u32[]{:S(2)}) collective-permute-start(bf16[128,512]{1,0:T(8,128)(2,1)S(1)} %collective-permute-done.23.refs_4_), channel_id=1, source_target_pairs={{0,1},{1,0},{2,3},{3,2},{4,5},{5,4},{6,7},{7,6},{8,9},{9,8},{10,11... | collective-permute-start | bytes 393224 | tf_op jit(solution)/shard_map/gather_residual/ppermute | solution.py:149
  81.8 6.0 %collective-permute-start.31 = (bf16[128,512]{1,0:T(8,128)(2,1)S(1)}, bf16[128,512]{1,0:T(8,128)(2,1)S(1)}, u32[]{:S(2)}, u32[]{:S(2)}) collective-permute-start(bf16[128,512]{1,0:T(8,128)(2,1)S(1)} %collective-permute-done.30.refs_6_), channel_id=1, source_target_pairs={{0,1},{1,0},{2,3},{3,2},{4,5},{5,4},{6,7},{7,6},{8,9},{9,8},{10,11... | collective-permute-start | bytes 393224 | tf_op jit(solution)/shard_map/gather_residual/ppermute | solution.py:149
  85.5 8.7 %collective-permute-start.33 = (bf16[128,512]{1,0:T(8,128)(2,1)S(1)}, bf16[128,512]{1,0:T(8,128)(2,1)S(1)}, u32[]{:S(2)}, u32[]{:S(2)}) collective-permute-start(bf16[128,512]{1,0:T(8,128)(2,1)S(1)} %collective-permute-done.21.refs_0_), channel_id=1, source_target_pairs={{0,1},{1,0},{2,3},{3,2},{4,5},{5,4},{6,7},{7,6},{8,9},{9,8},{10,11... | collective-permute-start | bytes 393224 | tf_op jit(solution)/shard_map/gather_residual/ppermute | solution.py:149
  85.5 7.5 %collective-permute-start.25 = (bf16[128,512]{1,0:T(8,128)(2,1)S(1)}, bf16[128,512]{1,0:T(8,128)(2,1)S(1)}, u32[]{:S(2)}, u32[]{:S(2)}) collective-permute-start(bf16[128,512]{1,0:T(8,128)(2,1)S(1)} %collective-permute-done.21.refs_0_), channel_id=1, source_target_pairs={{0,2},{1,3},{2,0},{3,1},{4,6},{5,7},{6,4},{7,5},{8,10},{9,11},{10,... | collective-permute-start | bytes 393224 | tf_op jit(solution)/shard_map/gather_residual/ppermute | solution.py:149
  86.7 7.5 %collective-permute-start.35 = (bf16[128,512]{1,0:T(8,128)(2,1)S(1)}, bf16[128,512]{1,0:T(8,128)(2,1)S(1)}, u32[]{:S(2)}, u32[]{:S(2)}) collective-permute-start(bf16[128,512]{1,0:T(8,128)(2,1)S(1)} %collective-permute-done.22.refs_4_), channel_id=1, source_target_pairs={{0,1},{1,0},{2,3},{3,2},{4,5},{5,4},{6,7},{7,6},{8,9},{9,8},{10,11... | collective-permute-start | bytes 393224 | tf_op jit(solution)/shard_map/gather_residual/ppermute | solution.py:149
  86.9 7.3 %collective-permute-start.26 = (bf16[128,512]{1,0:T(8,128)(2,1)S(1)}, bf16[128,512]{1,0:T(8,128)(2,1)S(1)}, u32[]{:S(2)}, u32[]{:S(2)}) collective-permute-start(bf16[128,512]{1,0:T(8,128)(2,1)S(1)} %collective-permute-done.22.refs_4_), channel_id=1, source_target_pairs={{0,2},{1,3},{2,0},{3,1},{4,6},{5,7},{6,4},{7,5},{8,10},{9,11},{10,... | collective-permute-start | bytes 393224 | tf_op jit(solution)/shard_map/gather_residual/ppermute | solution.py:149
  93.0 1.4 %collective-permute-start.34 = (bf16[128,512]{1,0:T(8,128)(2,1)S(1)}, bf16[128,512]{1,0:T(8,128)(2,1)S(1)}, u32[]{:S(2)}, u32[]{:S(2)}) collective-permute-start(bf16[128,512]{1,0:T(8,128)(2,1)S(1)} %collective-permute-done.25.refs_2_), channel_id=1, source_target_pairs={{0,1},{1,0},{2,3},{3,2},{4,5},{5,4},{6,7},{7,6},{8,9},{9,8},{10,11... | collective-permute-start | bytes 393224 | tf_op jit(solution)/shard_map/gather_residual/ppermute | solution.py:149
  94.2 1.3 collective-permute-start.32
  103.8 2.3 %collective-permute-start.36 = (bf16[512,512]{1,0:T(8,128)(2,1)S(1)}, bf16[512,512]{1,0:T(8,128)(2,1)S(1)}, u32[]{:S(2)}, u32[]{:S(2)}) collective-permute-start(bf16[512,512]{1,0:T(8,128)(2,1)S(1)} %get-tuple-element.122), channel_id=1, source_target_pairs={{0,1},{1,0},{2,3},{3,2},{4,5},{5,4},{6,7},{7,6},{8,9},{9,8},{10,11... | collective-permute-start | bytes 1572872 | tf_op jit(solution)/shard_map/sum_over_devices/ppermute | solution.py:149
  107.5 9.6 %collective-permute-start.40 = (bf16[256,512]{1,0:T(8,128)(2,1)}, bf16[256,512]{1,0:T(8,128)(2,1)S(1)}, u32[]{:S(2)}, u32[]{:S(2)}) collective-permute-start(bf16[256,512]{1,0:T(8,128)(2,1)} %get-tuple-element.124), channel_id=1, source_target_pairs={{0,2},{1,3},{2,0},{3,1},{4,6},{5,7},{6,4},{7,5},{8,10},{9,11},{10,... | collective-permute-start | bytes 786440 | tf_op jit(solution)/shard_map/sum_over_devices/ppermute | solution.py:149
  111.6 1.4 %collective-permute-start.41 = (bf16[128,512]{1,0:T(8,128)(2,1)S(1)}, bf16[128,512]{1,0:T(8,128)(2,1)S(1)}, u32[]{:S(2)}, u32[]{:S(2)}) collective-permute-start(bf16[128,512]{1,0:T(8,128)(2,1)S(1)} %get-tuple-element.136), channel_id=1, source_target_pairs={{0,1},{1,0},{2,3},{3,2},{4,5},{5,4},{6,7},{7,6},{8,9},{9,8},{10,11... | collective-permute-start | bytes 393224 | tf_op jit(solution)/shard_map/sum_over_devices/ppermute | solution.py:149
  111.6 10.2 %collective-permute-start.37 = (bf16[256,512]{1,0:T(8,128)(2,1)S(1)}, bf16[256,512]{1,0:T(8,128)(2,1)S(1)}, u32[]{:S(2)}, u32[]{:S(2)}) collective-permute-start(bf16[256,512]{1,0:T(8,128)(2,1)S(1)} %get-tuple-element.125), channel_id=1, source_target_pairs={{0,2},{1,3},{2,0},{3,1},{4,6},{5,7},{6,4},{7,5},{8,10},{9,11},{10,... | collective-permute-start | bytes 786440 | tf_op jit(solution)/shard_map/sum_over_devices/ppermute | solution.py:149
  112.5 4.6 %collective-permute-start.42 = (bf16[128,512]{1,0:T(8,128)(2,1)}, bf16[128,512]{1,0:T(8,128)(2,1)S(1)}, u32[]{:S(2)}, u32[]{:S(2)}) collective-permute-start(bf16[128,512]{1,0:T(8,128)(2,1)} %get-tuple-element.137), channel_id=1, source_target_pairs={{0,1},{1,0},{2,3},{3,2},{4,5},{5,4},{6,7},{7,6},{8,9},{9,8},{10,11... | collective-permute-start | bytes 393224 | tf_op jit(solution)/shard_map/sum_over_devices/ppermute | solution.py:149
  112.6 7.4 %collective-permute-start.38 = (bf16[128,512]{1,0:T(8,128)(2,1)}, bf16[128,512]{1,0:T(8,128)(2,1)}, u32[]{:S(2)}, u32[]{:S(2)}) collective-permute-start(bf16[128,512]{1,0:T(8,128)(2,1)} %get-tuple-element.128), channel_id=1, source_target_pairs={{0,1},{1,0},{2,3},{3,2},{4,5},{5,4},{6,7},{7,6},{8,9},{9,8},{10,11... | collective-permute-start | bytes 393224 | tf_op jit(solution)/shard_map/sum_over_devices/ppermute | solution.py:149
  113.0 7.1 %collective-permute-start.39 = (bf16[128,512]{1,0:T(8,128)(2,1)}, bf16[128,512]{1,0:T(8,128)(2,1)}, u32[]{:S(2)}, u32[]{:S(2)}) collective-permute-start(bf16[128,512]{1,0:T(8,128)(2,1)} %get-tuple-element.130), channel_id=1, source_target_pairs={{0,1},{1,0},{2,3},{3,2},{4,5},{5,4},{6,7},{7,6},{8,9},{9,8},{10,11... | collective-permute-start | bytes 393224 | tf_op jit(solution)/shard_map/sum_over_devices/ppermute | solution.py:149
  117.8 8.3 %collective-permute-start.44 = (bf16[128,512]{1,0:T(8,128)(2,1)S(1)}, bf16[128,512]{1,0:T(8,128)(2,1)S(1)}, u32[]{:S(2)}, u32[]{:S(2)}) collective-permute-start(bf16[128,512]{1,0:T(8,128)(2,1)S(1)} %get-tuple-element.139), channel_id=1, source_target_pairs={{0,12},{4,8},{8,4},{12,0},{1,13},{5,9},{9,5},{13,1},{2,14},{6,10},... | collective-permute-start | bytes 393224 | tf_op jit(solution)/shard_map/sum_over_devices/ppermute | solution.py:149
  120.1 11.4 %collective-permute-start.43 = (bf16[128,512]{1,0:T(8,128)(2,1)S(1)}, bf16[128,512]{1,0:T(8,128)(2,1)S(1)}, u32[]{:S(2)}, u32[]{:S(2)}) collective-permute-start(bf16[128,512]{1,0:T(8,128)(2,1)S(1)} %get-tuple-element.138), channel_id=1, source_target_pairs={{0,8},{4,12},{8,0},{12,4},{1,9},{5,13},{9,1},{13,5},{2,10},{6,14},... | collective-permute-start | bytes 393224 | tf_op jit(solution)/shard_map/sum_over_devices/ppermute | solution.py:149
  123.0 8.6 %collective-permute-start.45 = (bf16[128,512]{1,0:T(8,128)(2,1)S(1)}, bf16[128,512]{1,0:T(8,128)(2,1)S(1)}, u32[]{:S(2)}, u32[]{:S(2)}) collective-permute-start(bf16[128,512]{1,0:T(8,128)(2,1)S(1)} %get-tuple-element.140), channel_id=1, source_target_pairs={{0,4},{4,0},{8,12},{12,8},{1,5},{5,1},{9,13},{13,9},{2,6},{6,2},{1... | collective-permute-start | bytes 393224 | tf_op jit(solution)/shard_map/sum_over_devices/ppermute | solution.py:149

commit v10 on v9

--- a/solution.py
+++ b/solution.py
@@ -460,12 +460,11 @@
             copy.start()
         return carry
 
-    def d_copies(i):
-        return down_copies(pos, downs, i, group, w_down, d_outs, d_sems)
-
-    def start_down(i, carry):
-        for copy in d_copies(i):
-            copy.start()
+    def d_copy(k, i):
+        return down_copies(pos, downs, i, group, w_down, d_outs, d_sems)[k]
+
+    def start_down(k, i, carry):
+        d_copy(k, i).start()
         return carry
 
     def step(g_from, u_from, skipped, i, carry):
@@ -492,18 +491,20 @@
         return carry
 
     lax.fori_loop(0, parts - ready, start, 0)
-    lax.fori_loop(0, parts, start_down, 0)
+    for k in range(len(downs)):
+        lax.fori_loop(0, parts, functools.partial(start_down, k), 0)
     place_rows(n, distances, pos, pieces, r_all)
     lax.fori_loop(0, ready, functools.partial(step, g_some, u_some, 0), 0)
     lax.fori_loop(ready, parts, functools.partial(step, g_all, u_all, ready), 0)
     for i in range(parts):
-        for copy in d_copies(i):
-            copy.wait()
+        d_copy(0, i).wait()
     for e in range(d_here.shape[0]):
         mine = slice(e * slots, (e + 1) * slots)
         product = jnp.dot(hidden_out[mine, :], d_here[e], preferred_element_type=F32)
         y_slots[mine, :] = product.astype(BF16)
     out[...] = jnp.dot(place[...], y_slots[...], preferred_element_type=F32).astype(BF16)
+    for i in range(parts):
+        d_copy(1, i).wait()
 
 
 def self_down_kernel(slots, group, distances, pos, hidden, place, w_down, out, kept, y_slots, sems):

time: 140 us -> 140 us (level)
  no operation moved by 1% of the time
where the time goes in v10:
time: 140 us; the launch traced here: 139 us
  Pallas kernels  50.3 us (36%)
  waiting for transfers between devices  40 us (29%)
  starting transfers between devices  38.7 us (28%)
  blocking collectives  6.94 us (5%)
  local copies, waits for them, and re-layouts  2.7 us (2%)
    ppermute x46, waiting for transfers between devices, swap(): return lax.ppermute(array, axis, [(i, i ^ distance) for i in range(size)])  40 us
    ppermute x46, starting transfers between devices, swap(): return lax.ppermute(array, axis, [(i, i ^ distance) for i in range(size)])  38.7 us
    pallas_call x2, Pallas kernels, load(): pl.pallas_call(functools.partial(load_kernel, group, distances), out_shap...  10.5 us
    pallas_call x1, Pallas kernels, last_hidden(): pl.pallas_call(functools.partial(last_hidden_kernel, n, slots, group, lat...  8.27 us
    all_gather x1, blocking collectives, square_body(): return lax.all_gather(mixed, 'head', axis=1, tiled=True)  6.94 us
    pallas_call x1, Pallas kernels, first_hidden(): pl.pallas_call(functools.partial(first_hidden_kernel, n, slots, group, ea...  5.22 us
    pallas_call x1, Pallas kernels, square_body(): pl.pallas_call(functools.partial(project_tokens_kernel, n), out_shape=[sd...  4.94 us
    pallas_call x1, Pallas kernels, self_down(): pl.pallas_call(functools.partial(self_down_kernel, slots, group, (distanc...  3.93 us
  transfers between devices with their start and end apart: 46, of which 17 were waited for; matrix products, arithmetic and copies ran while one was open for 1% of the time, Pallas kernels for 27%

profile of v10, /device:TPU:0, one launch (start us, length us, event | category | flops | bytes accessed | tf_op | source)
XLA Modules:
  0.0 139.4 jit_solution(8807561224155793315)
XLA Ops:
  0.1 1.8 %cut_pieces.1 = (bf16[144,512]{1,0:T(8,128)(2,1)S(1)}, bf16[256,384]{1,0:T(8,128)(2,1)S(1)}, bf16[256,384]{1,0:T(8,128)(2,1)S(1)}, bf16[256,384]{1,0:T(8,128)(2,1)S(1)}) custom-call(s32[3]{0:T(128)S(1)} %pad_add_fusion.pos, s32[8,128]{1,0:T(8,128)} %bitcast.26, f32[8,128]{1,0:T(8,128)} %bitcast.27, bf16[128,2048]{1,0:T(8,128)(2,1)} %tokens.3, ...), custom_call_target="tpu_custom_call" | custom-call | tf_op jit(solution)/shard_map/cut_pieces/pallas_call | solution.py:603
  1.9 3.1 %collective-permute-start.3 = (bf16[256,384]{1,0:T(8,128)(2,1)S(1)}, bf16[256,384]{1,0:T(8,128)(2,1)S(1)}, u32[]{:S(2)}, u32[]{:S(2)}) collective-permute-start(bf16[256,384]{1,0:T(8,128)(2,1)S(1)} %get-tuple-element.75), channel_id=1, source_target_pairs={{0,4},{4,0},{8,12},{12,8},{1,5},{5,1},{9,13},{13,9},{2,6},{6,2},{1... | collective-permute-start | bytes 589832 | tf_op jit(solution)/shard_map/gather_tokens_and_weights/ppermute | solution.py:149
  5.0 2.6 %collective-permute-start.4 = (bf16[256,384]{1,0:T(8,128)(2,1)S(1)}, bf16[256,384]{1,0:T(8,128)(2,1)S(1)}, u32[]{:S(2)}, u32[]{:S(2)}) collective-permute-start(bf16[256,384]{1,0:T(8,128)(2,1)S(1)} %get-tuple-element.76), channel_id=1, source_target_pairs={{0,8},{4,12},{8,0},{12,4},{1,9},{5,13},{9,1},{13,5},{2,10},{6,14},... | collective-permute-start | bytes 589832 | tf_op jit(solution)/shard_map/gather_tokens_and_weights/ppermute | solution.py:149
  7.6 0.4 collective-permute-start
  8.0 3.9 %collective-permute-start.2 = (bf16[144,512]{1,0:T(8,128)(2,1)S(1)}, bf16[144,512]{1,0:T(8,128)(2,1)S(1)}, u32[]{:S(2)}, u32[]{:S(2)}) collective-permute-start(bf16[144,512]{1,0:T(8,128)(2,1)S(1)} %get-tuple-element.74.refs_0_), channel_id=1, source_target_pairs={{0,12},{4,8},{8,4},{12,0},{1,13},{5,9},{9,5},{13,1},{2,14},{6,10},... | collective-permute-start | bytes 442376 | tf_op jit(solution)/shard_map/gather_tokens_and_weights/ppermute | solution.py:149
  12.0 7.3 %collective-permute-done.refs_1_ = bf16[144,512]{1,0:T(8,128)(2,1)S(1)} collective-permute-done((bf16[144,512]{1,0:T(8,128)(2,1)S(1)}, bf16[144,512]{1,0:T(8,128)(2,1)S(1)}, u32[]{:S(2)}, u32[]{:S(2)}) %collective-permute-start) | collective-permute-done | bytes 147488 | tf_op jit(solution)/shard_map/gather_tokens_and_weights/ppermute | solution.py:149
  19.3 8.1 %collective-permute-done.1.refs_2_ = bf16[144,512]{1,0:T(8,128)(2,1)S(1)} collective-permute-done((bf16[144,512]{1,0:T(8,128)(2,1)S(1)}, bf16[144,512]{1,0:T(8,128)(2,1)S(1)}, u32[]{:S(2)}, u32[]{:S(2)}) %collective-permute-start.1) | collective-permute-done | bytes 147488 | tf_op jit(solution)/shard_map/gather_tokens_and_weights/ppermute | solution.py:149
  27.6 1.6 %collective-permute-start.6 = (bf16[3,128,512]{2,1,0:T(8,128)(2,1)S(1)}, bf16[3,128,512]{2,1,0:T(8,128)(2,1)S(1)}, u32[]{:S(2)}, u32[]{:S(2)}) collective-permute-start(bf16[3,128,512]{2,1,0:T(8,128)(2,1)S(1)} %pad_maximum_fusion.rest_0_), channel_id=1, source_target_pairs={{0,2},{1,3},{2,0},{3,1},{4,6},{5,7},{6,4},{7,5},{8,10},{9,11},{10,... | collective-permute-start | bytes 1179656 | tf_op jit(solution)/shard_map/gather_tokens_and_weights/ppermute | solution.py:149
  29.1 1.3 routing.1
  30.5 2.5 %collective-permute-start.7 = (bf16[256,384]{1,0:T(8,128)(2,1)S(1)}, bf16[256,384]{1,0:T(8,128)(2,1)S(1)}, u32[]{:S(2)}, u32[]{:S(2)}) collective-permute-start(bf16[256,384]{1,0:T(8,128)(2,1)S(1)} %get-tuple-element.84), channel_id=1, source_target_pairs={{0,12},{4,8},{8,4},{12,0},{1,13},{5,9},{9,5},{13,1},{2,14},{6,10},... | collective-permute-start | bytes 589832 | tf_op jit(solution)/shard_map/gather_tokens_and_weights/ppermute | solution.py:149
  33.0 1.5 %collective-permute-start.8 = (bf16[256,384]{1,0:T(8,128)(2,1)S(1)}, bf16[256,384]{1,0:T(8,128)(2,1)S(1)}, u32[]{:S(2)}, u32[]{:S(2)}) collective-permute-start(bf16[256,384]{1,0:T(8,128)(2,1)S(1)} %collective-permute-done.3.rest_4_), channel_id=1, source_target_pairs={{0,16},{16,0},{1,17},{17,1},{2,18},{18,2},{3,19},{19,3},{4,20},{20... | collective-permute-start | bytes 589832 | tf_op jit(solution)/shard_map/gather_tokens_and_weights/ppermute | solution.py:149
  34.5 0.5 collective-permute-start.9
  35.0 1.1 slice_bitcast_fusion.refs_0_
  36.1 0.6 collective-permute-start.17
  36.7 4.0 %gather_tokens_and_weights.1 = (bf16[8,1024,256]{2,1,0:T(8,128)(2,1)S(1)}, bf16[8,1024,256]{2,1,0:T(8,128)(2,1)S(1)}) custom-call(s32[3]{0:T(128)S(1)} %pad_add_fusion.pos, bf16[16,2048,256]{2,1,0:T(8,128)(2,1)} %w_gate.5, bf16[16,2048,256]{2,1,0:T(8,128)(2,1)} %w_up.5), custom_call_target="tpu_custom_call" | custom-call | bytes 8388608 | tf_op jit(solution)/shard_map/gather_tokens_and_weights/pallas_call | solution.py:625
  40.9 0.5 collective-permute-start.10
  41.5 1.5 %collective-permute-start.11 = (bf16[256,384]{1,0:T(8,128)(2,1)S(1)}, bf16[256,384]{1,0:T(8,128)(2,1)S(1)}, u32[]{:S(2)}, u32[]{:S(2)}) collective-permute-start(bf16[256,384]{1,0:T(8,128)(2,1)S(1)} %collective-permute-done.7.rest_6_), channel_id=1, source_target_pairs={{0,16},{16,0},{1,17},{17,1},{2,18},{18,2},{3,19},{19,3},{4,20},{20... | collective-permute-start | bytes 589832 | tf_op jit(solution)/shard_map/gather_tokens_and_weights/ppermute | solution.py:149
  43.2 0.6 copy-done.4
  43.9 4.9 %projected_tokens.1 = (f32[512,384]{1,0:T(8,128)S(1)}, bf16[512,256]{1,0:T(8,128)(2,1)S(1)}, bf16[128,512]{1,0:T(8,128)(2,1)S(1)}) custom-call(s32[3]{0:T(128)S(1)} %pad_add_fusion.pos, f32[1,2048]{1,0:T(1,128)S(1)} %bitcast.22, bf16[128,2048]{1,0:T(8,128)(2,1)} %tokens.3, bf16[4,512,512]{2,1,0:T(8,128)(2,1)} %weight.3, bf16[3,128,512]{2,1,0:T(8,128)(2,1)} %copy-done.2, ...), custom_call_target="tpu_custom_call" | custom-call | flops 805306368 | bytes 4194304 | tf_op jit(solution)/shard_map/projected_tokens/pallas_call | solution.py:678
  48.9 2.0 %attention.1 = (bf16[128,128]{1,0:T(8,128)(2,1)S(1)}, bf16[128,128]{1,0:T(8,128)(2,1)S(1)}, bf16[128,128]{1,0:T(8,128)(2,1)S(1)}, bf16[128,128]{1,0:T(8,128)(2,1)S(1)}) custom-call(s32[3]{0:T(128)S(1)} %pad_add_fusion.pos, f32[512,384]{1,0:T(8,128)S(1)} %get-tuple-element.93.partial, bf16[512,256]{1,0:T(8,128)(2,1)S(1)} %get-tuple-element.94.x_last, ...), custom_call_target="tpu_custom_call" | custom-call | tf_op jit(solution)/shard_map/attention/pallas_call | solution.py:700
  51.0 0.4 collective-permute-start.18
  51.4 1.2 collective-permute-start.14
  52.7 0.5 collective-permute-start.13
  53.3 1.5 %collective-permute-done.14 = bf16[128,128]{1,0:T(8,128)(2,1)S(1)} collective-permute-done((bf16[128,128]{1,0:T(8,128)(2,1)S(1)}, bf16[128,128]{1,0:T(8,128)(2,1)S(1)}, u32[]{:S(2)}, u32[]{:S(2)}) %collective-permute-start.14) | collective-permute-done | bytes 32800 | tf_op jit(solution)/shard_map/heads_to_tokens/ppermute | solution.py:149
  54.8 1.7 %collective-permute-done.13 = bf16[128,128]{1,0:T(8,128)(2,1)S(1)} collective-permute-done((bf16[128,128]{1,0:T(8,128)(2,1)S(1)}, bf16[128,128]{1,0:T(8,128)(2,1)S(1)}, u32[]{:S(2)}, u32[]{:S(2)}) %collective-permute-start.13) | collective-permute-done | bytes 32800 | tf_op jit(solution)/shard_map/heads_to_tokens/ppermute | solution.py:149
  56.6 1.7 %collective-permute-start.15 = (bf16[4,128,128]{2,1,0:T(8,128)(2,1)S(1)}, bf16[4,128,128]{2,1,0:T(8,128)(2,1)S(1)}, u32[]{:S(2)}, u32[]{:S(2)}) collective-permute-start(bf16[4,128,128]{2,1,0:T(8,128)(2,1)S(1)} %pad_maximum_fusion.1.rest_4_), channel_id=1, source_target_pairs={{0,8},{4,12},{8,0},{12,4},{1,9},{5,13},{9,1},{13,5},{2,10},{6,14},... | collective-permute-start | bytes 393224 | tf_op jit(solution)/shard_map/heads_to_tokens/ppermute | solution.py:149
  58.3 0.3 collective-permute-start.19
  58.6 6.5 %expert_weights.2 = (bf16[16,1024,256]{2,1,0:T(8,128)(2,1)S(1)}, bf16[16,1024,256]{2,1,0:T(8,128)(2,1)S(1)}) custom-call(s32[3]{0:T(128)S(1)} %pad_add_fusion.pos, bf16[16,2048,256]{2,1,0:T(8,128)(2,1)} %w_gate.5, bf16[16,2048,256]{2,1,0:T(8,128)(2,1)} %w_up.5), custom_call_target="tpu_custom_call" | custom-call | bytes 16777216 | tf_op jit(solution)/shard_map/heads_to_tokens/expert_weights/pallas_call | solution.py:625
  65.1 1.8 %collective-permute-start.20 = (bf16[4,128,128]{2,1,0:T(8,128)(2,1)S(1)}, bf16[4,128,128]{2,1,0:T(8,128)(2,1)S(1)}, u32[]{:S(2)}, u32[]{:S(2)}) collective-permute-start(bf16[4,128,128]{2,1,0:T(8,128)(2,1)S(1)} %collective-permute-done.15.rest_6_), channel_id=1, source_target_pairs={{0,4},{4,0},{8,12},{12,8},{1,5},{5,1},{9,13},{13,9},{2,6},{6,2},{1... | collective-permute-start | bytes 393224 | tf_op jit(solution)/shard_map/heads_to_tokens/ppermute | solution.py:149
  66.9 2.8 %expert_weights.3.refs_0_ = bf16[16,256,512]{2,1,0:T(8,128)(2,1)S(1)} custom-call(s32[3]{0:T(128)S(1)} %pad_add_fusion.pos, bf16[16,256,2048]{2,1,0:T(8,128)(2,1)} %w_down.5), custom_call_target="tpu_custom_call" | custom-call | bytes 4194304 | tf_op jit(solution)/shard_map/heads_to_tokens/expert_weights/pallas_call | solution.py:637
  70.1 1.4 output_projection.1.refs_0_
  71.5 1.8 %collective-permute-start.23 = (bf16[128,512]{1,0:T(8,128)(2,1)S(1)}, bf16[128,512]{1,0:T(8,128)(2,1)S(1)}, u32[]{:S(2)}, u32[]{:S(2)}) collective-permute-start(bf16[128,512]{1,0:T(8,128)(2,1)S(1)} %output_projection.1.refs_0_), channel_id=1, source_target_pairs={{0,4},{4,0},{8,12},{12,8},{1,5},{5,1},{9,13},{13,9},{2,6},{6,2},{1... | collective-permute-start | bytes 393224 | tf_op jit(solution)/shard_map/gather_residual/ppermute | solution.py:149
  73.3 1.3 collective-permute-start.21
  74.6 0.9 collective-permute-start.28
  75.4 1.4 collective-permute-done.23.refs_4_
  76.8 1.0 collective-permute-start.30
  77.8 2.8 %collective-permute-done.21.refs_0_ = bf16[128,512]{1,0:T(8,128)(2,1)S(1)} collective-permute-done((bf16[128,512]{1,0:T(8,128)(2,1)S(1)}, bf16[128,512]{1,0:T(8,128)(2,1)S(1)}, u32[]{:S(2)}, u32[]{:S(2)}) %collective-permute-start.21) | collective-permute-done | bytes 131104 | tf_op jit(solution)/shard_map/gather_residual/ppermute | solution.py:149
  80.5 0.5 collective-permute-start.29
  81.1 0.6 collective-permute-done.30.refs_6_
  81.8 3.7 %collective-permute-done.22.refs_4_ = bf16[128,512]{1,0:T(8,128)(2,1)S(1)} collective-permute-done((bf16[128,512]{1,0:T(8,128)(2,1)S(1)}, bf16[128,512]{1,0:T(8,128)(2,1)S(1)}, u32[]{:S(2)}, u32[]{:S(2)}) %collective-permute-start.22) | collective-permute-done | bytes 131104 | tf_op jit(solution)/shard_map/gather_residual/ppermute | solution.py:149
  85.5 1.2 collective-permute-start.25
  86.7 0.2 collective-permute-start.35
  86.9 0.9 collective-permute-start.26
  87.8 5.2 %first_hidden_units.1 = (f32[1280,512]{1,0:T(8,128)S(1)}, f32[1280,128]{1,0:T(8,128)S(1)}) custom-call(s32[3]{0:T(128)S(1)} %pad_add_fusion.pos, f32[1,2048]{1,0:T(1,128)S(1)} %bitcast.20, bf16[1280,512]{1,0:T(8,128)(2,1)S(1)} %get-tuple-element.88.pick, bf16[16,1024,256]{2,1,0:T(8,128)(2,1)S(1)} %get-tuple-element.100.g_all, ...), custom_call_target="tpu_custom_call" | custom-call | flops 2684354560 | bytes 16777216 | tf_op jit(solution)/shard_map/gather_residual/first_hidden_units/pallas_call | solution.py:712
  93.1 1.1 collective-permute-done.26.refs_6_
  94.4 1.2 collective-permute-done.32.refs_7_
  95.6 8.3 %last_hidden_units.1 = (bf16[1280,256]{1,0:T(8,128)(2,1)S(1)}, bf16[512,512]{1,0:T(8,128)(2,1)S(1)}, bf16[16,256,512]{2,1,0:T(8,128)(2,1)S(1)}) custom-call(s32[3]{0:T(128)S(1)} %pad_add_fusion.pos, f32[1,2048]{1,0:T(1,128)S(1)} %bitcast.21, bf16[1280,512]{1,0:T(8,128)(2,1)S(1)} %get-tuple-element.88.pick, bf16[16,2048,256]{2,1,0:T(8,128)(2,1)} %w_gate.5, ...), custom_call_target="tpu_custom_call" | custom-call | flops 2684354560 | bytes 16777216 | tf_op jit(solution)/shard_map/gather_residual/last_hidden_units/pallas_call | solution.py:723
  103.9 0.2 collective-permute-start.36
  104.1 2.1 %down_products.1.base = bf16[512,512]{1,0:T(8,128)(2,1)S(1)} custom-call(s32[3]{0:T(128)S(1)} %pad_add_fusion.pos, bf16[1280,256]{1,0:T(8,128)(2,1)S(1)} %get-tuple-element.129.hidden, bf16[512,1280]{1,0:T(8,128)(2,1)S(1)} %get-tuple-element.119.place, bf16[16,256,512]{2,1,0:T(8,128)(2,1)S(1)} %expert_weights.3.refs_0_), custom_call_target="tpu_custom_call" | custom-call | flops 1006632960 | bytes 4194304 | tf_op jit(solution)/shard_map/sum_over_devices/down_products/pallas_call | solution.py:801
  106.2 1.3 sums_over_cores.1
  107.5 1.2 collective-permute-start.40
  108.7 2.9 %down_products_by_block.1 = (bf16[128,512]{1,0:T(8,128)(2,1)}, bf16[128,512]{1,0:T(8,128)(2,1)}, bf16[128,512]{1,0:T(8,128)(2,1)S(1)}, bf16[128,512]{1,0:T(8,128)(2,1)}) custom-call(s32[3]{0:T(128)S(1)} %pad_add_fusion.pos, bf16[1280,256]{1,0:T(8,128)(2,1)S(1)} %get-tuple-element.129.hidden, bf16[512,1280]{1,0:T(8,128)(2,1)S(1)} %get-tuple-element.119.place, ...), custom_call_target="tpu_custom_call" | custom-call | flops 20000000000 | bytes 4194304 | tf_op jit(solution)/shard_map/sum_over_devices/down_products_by_block/pallas_call | solution.py:844
  111.6 0.9 collective-permute-start.37
  112.7 0.3 collective-permute-start.38
  113.2 3.9 %down_products_alone.1.base = bf16[512,512]{1,0:T(8,128)(2,1)S(1)} custom-call(s32[3]{0:T(128)S(1)} %pad_add_fusion.pos, bf16[1280,256]{1,0:T(8,128)(2,1)S(1)} %get-tuple-element.129.hidden, bf16[512,1280]{1,0:T(8,128)(2,1)S(1)} %get-tuple-element.119.place, bf16[16,256,2048]{2,1,0:T(8,128)(2,1)} %w_down.5), custom_call_target="tpu_custom_call" | custom-call | tf_op jit(solution)/shard_map/sum_over_devices/down_products_alone/pallas_call | solution.py:815
  117.1 0.6 rows_2_3.1
  117.8 2.3 %collective-permute-start.44 = (bf16[128,512]{1,0:T(8,128)(2,1)S(1)}, bf16[128,512]{1,0:T(8,128)(2,1)S(1)}, u32[]{:S(2)}, u32[]{:S(2)}) collective-permute-start(bf16[128,512]{1,0:T(8,128)(2,1)S(1)} %get-tuple-element.139), channel_id=1, source_target_pairs={{0,12},{4,8},{8,4},{12,0},{1,13},{5,9},{9,5},{13,1},{2,14},{6,10},... | collective-permute-start | bytes 393224 | tf_op jit(solution)/shard_map/sum_over_devices/ppermute | solution.py:149
  120.1 1.8 %collective-permute-done.37.part = bf16[256,512]{1,0:T(8,128)(2,1)S(1)} collective-permute-done((bf16[256,512]{1,0:T(8,128)(2,1)S(1)}, bf16[256,512]{1,0:T(8,128)(2,1)S(1)}, u32[]{:S(2)}, u32[]{:S(2)}) %collective-permute-start.37) | collective-permute-done | bytes 262176 | tf_op jit(solution)/shard_map/sum_over_devices/ppermute | solution.py:149
  121.9 1.1 rows_0_1.1
  123.0 0.4 collective-permute-start.45
  123.4 2.7 %collective-permute-done.44 = bf16[128,512]{1,0:T(8,128)(2,1)S(1)} collective-permute-done((bf16[128,512]{1,0:T(8,128)(2,1)S(1)}, bf16[128,512]{1,0:T(8,128)(2,1)S(1)}, u32[]{:S(2)}, u32[]{:S(2)}) %collective-permute-start.44) | collective-permute-done | bytes 131104 | tf_op jit(solution)/shard_map/sum_over_devices/ppermute | solution.py:149
  126.1 5.4 %collective-permute-done.43 = bf16[128,512]{1,0:T(8,128)(2,1)S(1)} collective-permute-done((bf16[128,512]{1,0:T(8,128)(2,1)S(1)}, bf16[128,512]{1,0:T(8,128)(2,1)S(1)}, u32[]{:S(2)}, u32[]{:S(2)}) %collective-permute-start.43) | collective-permute-done | bytes 131104 | tf_op jit(solution)/shard_map/sum_over_devices/ppermute | solution.py:149
  131.6 6.9 %all_gather.3 = bf16[128,2048]{1,0:T(8,128)(2,1)S(1)} all-gather(bf16[128,512]{1,0:T(8,128)(2,1)S(1)} %add_convert_fusion), channel_id=1, replica_groups=mesh['grp'=2,'seq'=4,'head'=4] {'head'}, dimensions={1}, use_global_device_ids=true | all-gather | bytes 655360 | tf_op jit(solution)/shard_map/gather_columns/all_gather | solution.py:876
  138.6 0.8 copy.11
  (77 shorter events, 2.3 us)
Async XLA Ops:
  1.9 25.5 %collective-permute-start.3 = (bf16[256,384]{1,0:T(8,128)(2,1)S(1)}, bf16[256,384]{1,0:T(8,128)(2,1)S(1)}, u32[]{:S(2)}, u32[]{:S(2)}) collective-permute-start(bf16[256,384]{1,0:T(8,128)(2,1)S(1)} %get-tuple-element.75), channel_id=1, source_target_pairs={{0,4},{4,0},{8,12},{12,8},{1,5},{5,1},{9,13},{13,9},{2,6},{6,2},{1... | collective-permute-start | bytes 589832 | tf_op jit(solution)/shard_map/gather_tokens_and_weights/ppermute | solution.py:149
  5.0 22.4 %collective-permute-start.4 = (bf16[256,384]{1,0:T(8,128)(2,1)S(1)}, bf16[256,384]{1,0:T(8,128)(2,1)S(1)}, u32[]{:S(2)}, u32[]{:S(2)}) collective-permute-start(bf16[256,384]{1,0:T(8,128)(2,1)S(1)} %get-tuple-element.76), channel_id=1, source_target_pairs={{0,8},{4,12},{8,0},{12,4},{1,9},{5,13},{9,1},{13,5},{2,10},{6,14},... | collective-permute-start | bytes 589832 | tf_op jit(solution)/shard_map/gather_tokens_and_weights/ppermute | solution.py:149
  7.6 11.7 %collective-permute-start = (bf16[144,512]{1,0:T(8,128)(2,1)S(1)}, bf16[144,512]{1,0:T(8,128)(2,1)S(1)}, u32[]{:S(2)}, u32[]{:S(2)}) collective-permute-start(bf16[144,512]{1,0:T(8,128)(2,1)S(1)} %get-tuple-element.74.refs_0_), channel_id=1, source_target_pairs={{0,4},{4,0},{8,12},{12,8},{1,5},{5,1},{9,13},{13,9},{2,6},{6,2},{1... | collective-permute-start | bytes 442376 | tf_op jit(solution)/shard_map/gather_tokens_and_weights/ppermute | solution.py:149
  8.0 19.4 %collective-permute-start.1 = (bf16[144,512]{1,0:T(8,128)(2,1)S(1)}, bf16[144,512]{1,0:T(8,128)(2,1)S(1)}, u32[]{:S(2)}, u32[]{:S(2)}) collective-permute-start(bf16[144,512]{1,0:T(8,128)(2,1)S(1)} %get-tuple-element.74.refs_0_), channel_id=1, source_target_pairs={{0,8},{4,12},{8,0},{12,4},{1,9},{5,13},{9,1},{13,5},{2,10},{6,14},... | collective-permute-start | bytes 442376 | tf_op jit(solution)/shard_map/gather_tokens_and_weights/ppermute | solution.py:149
  8.0 19.4 %collective-permute-start.2 = (bf16[144,512]{1,0:T(8,128)(2,1)S(1)}, bf16[144,512]{1,0:T(8,128)(2,1)S(1)}, u32[]{:S(2)}, u32[]{:S(2)}) collective-permute-start(bf16[144,512]{1,0:T(8,128)(2,1)S(1)} %get-tuple-element.74.refs_0_), channel_id=1, source_target_pairs={{0,12},{4,8},{8,4},{12,0},{1,13},{5,9},{9,5},{13,1},{2,14},{6,10},... | collective-permute-start | bytes 442376 | tf_op jit(solution)/shard_map/gather_tokens_and_weights/ppermute | solution.py:149
  27.4 13.3 %copy-start.6 = (bf16[256,384]{1,0:T(8,128)(2,1)}, bf16[256,384]{1,0:T(8,128)(2,1)S(1)}, u32[]{:S(2)}) copy-start(bf16[256,384]{1,0:T(8,128)(2,1)S(1)} %collective-permute-done.3.rest_4_) | copy-start | bytes 589828
  27.4 13.3 %copy-start.7 = (bf16[256,384]{1,0:T(8,128)(2,1)}, bf16[256,384]{1,0:T(8,128)(2,1)S(1)}, u32[]{:S(2)}) copy-start(bf16[256,384]{1,0:T(8,128)(2,1)S(1)} %collective-permute-done.4.rest_5_) | copy-start | bytes 589828
  27.6 13.2 %copy-start.2 = (bf16[3,128,512]{2,1,0:T(8,128)(2,1)}, bf16[3,128,512]{2,1,0:T(8,128)(2,1)S(1)}, u32[]{:S(2)}) copy-start(bf16[3,128,512]{2,1,0:T(8,128)(2,1)S(1)} %pad_maximum_fusion.rest_0_) | copy-start | bytes 1179652
  27.6 13.4 %collective-permute-start.6 = (bf16[3,128,512]{2,1,0:T(8,128)(2,1)S(1)}, bf16[3,128,512]{2,1,0:T(8,128)(2,1)S(1)}, u32[]{:S(2)}, u32[]{:S(2)}) collective-permute-start(bf16[3,128,512]{2,1,0:T(8,128)(2,1)S(1)} %pad_maximum_fusion.rest_0_), channel_id=1, source_target_pairs={{0,2},{1,3},{2,0},{3,1},{4,6},{5,7},{6,4},{7,5},{8,10},{9,11},{10,... | collective-permute-start | bytes 1179656 | tf_op jit(solution)/shard_map/gather_tokens_and_weights/ppermute | solution.py:149
  30.5 10.3 %collective-permute-start.7 = (bf16[256,384]{1,0:T(8,128)(2,1)S(1)}, bf16[256,384]{1,0:T(8,128)(2,1)S(1)}, u32[]{:S(2)}, u32[]{:S(2)}) collective-permute-start(bf16[256,384]{1,0:T(8,128)(2,1)S(1)} %get-tuple-element.84), channel_id=1, source_target_pairs={{0,12},{4,8},{8,4},{12,0},{1,13},{5,9},{9,5},{13,1},{2,14},{6,10},... | collective-permute-start | bytes 589832 | tf_op jit(solution)/shard_map/gather_tokens_and_weights/ppermute | solution.py:149
  33.0 7.9 %collective-permute-start.8 = (bf16[256,384]{1,0:T(8,128)(2,1)S(1)}, bf16[256,384]{1,0:T(8,128)(2,1)S(1)}, u32[]{:S(2)}, u32[]{:S(2)}) collective-permute-start(bf16[256,384]{1,0:T(8,128)(2,1)S(1)} %collective-permute-done.3.rest_4_), channel_id=1, source_target_pairs={{0,16},{16,0},{1,17},{17,1},{2,18},{18,2},{3,19},{19,3},{4,20},{20... | collective-permute-start | bytes 589832 | tf_op jit(solution)/shard_map/gather_tokens_and_weights/ppermute | solution.py:149
  34.5 6.4 %collective-permute-start.9 = (bf16[256,384]{1,0:T(8,128)(2,1)S(1)}, bf16[256,384]{1,0:T(8,128)(2,1)S(1)}, u32[]{:S(2)}, u32[]{:S(2)}) collective-permute-start(bf16[256,384]{1,0:T(8,128)(2,1)S(1)} %collective-permute-done.4.rest_5_), channel_id=1, source_target_pairs={{0,16},{16,0},{1,17},{17,1},{2,18},{18,2},{3,19},{19,3},{4,20},{20... | collective-permute-start | bytes 589832 | tf_op jit(solution)/shard_map/gather_tokens_and_weights/ppermute | solution.py:149
  36.1 7.8 %copy-start.1 = (f32[2048]{0:T(1024)S(1)}, f32[2048]{0:T(1024)}, u32[]{:S(2)}) copy-start(f32[2048]{0:T(1024)} %param.11) | copy-start | bytes 24580
  36.1 14.9 %collective-permute-start.17 = (bf16[512,512]{1,0:T(8,128)(2,1)S(1)}, bf16[512,512]{1,0:T(8,128)(2,1)S(1)}, u32[]{:S(2)}, u32[]{:S(2)}) collective-permute-start(bf16[512,512]{1,0:T(8,128)(2,1)S(1)} %slice_bitcast_fusion.refs_0_), channel_id=1, source_target_pairs={{0,2},{1,3},{2,0},{3,1},{4,6},{5,7},{6,4},{7,5},{8,10},{9,11},{10,... | collective-permute-start | bytes 1572872 | tf_op jit(solution)/shard_map/gather_out_weights/ppermute | solution.py:149
  40.8 2.4 %copy-start.8 = (bf16[256,384]{1,0:T(8,128)(2,1)}, bf16[256,384]{1,0:T(8,128)(2,1)S(1)}, u32[]{:S(2)}) copy-start(bf16[256,384]{1,0:T(8,128)(2,1)S(1)} %collective-permute-done.7.rest_6_) | copy-start | bytes 589828
  40.8 2.2 %collective-permute-start.5 = (bf16[3,128,512]{2,1,0:T(8,128)(2,1)S(1)}, bf16[3,128,512]{2,1,0:T(8,128)(2,1)S(1)}, u32[]{:S(2)}, u32[]{:S(2)}) collective-permute-start(bf16[3,128,512]{2,1,0:T(8,128)(2,1)S(1)} %pad_maximum_fusion.rest_0_), channel_id=1, source_target_pairs={{0,1},{1,0},{2,3},{3,2},{4,5},{5,4},{6,7},{7,6},{8,9},{9,8},{10,11... | collective-permute-start | bytes 1179656 | tf_op jit(solution)/shard_map/gather_tokens_and_weights/ppermute | solution.py:149
  40.9 2.3 %copy-start.9 = (bf16[256,384]{1,0:T(8,128)(2,1)}, bf16[256,384]{1,0:T(8,128)(2,1)S(1)}, u32[]{:S(2)}) copy-start(bf16[256,384]{1,0:T(8,128)(2,1)S(1)} %collective-permute-done.8.rest_7_) | copy-start | bytes 589828
  40.9 2.3 %copy-start.10 = (bf16[256,384]{1,0:T(8,128)(2,1)}, bf16[256,384]{1,0:T(8,128)(2,1)S(1)}, u32[]{:S(2)}) copy-start(bf16[256,384]{1,0:T(8,128)(2,1)S(1)} %collective-permute-done.9.rest_8_) | copy-start | bytes 589828
  40.9 2.2 %copy-start.3 = (bf16[3,128,512]{2,1,0:T(8,128)(2,1)}, bf16[3,128,512]{2,1,0:T(8,128)(2,1)S(1)}, u32[]{:S(2)}) copy-start(bf16[3,128,512]{2,1,0:T(8,128)(2,1)S(1)} %collective-permute-done.6.rest_2_) | copy-start | bytes 1179652
  40.9 2.2 %collective-permute-start.10 = (bf16[3,128,512]{2,1,0:T(8,128)(2,1)S(1)}, bf16[3,128,512]{2,1,0:T(8,128)(2,1)S(1)}, u32[]{:S(2)}, u32[]{:S(2)}) collective-permute-start(bf16[3,128,512]{2,1,0:T(8,128)(2,1)S(1)} %collective-permute-done.6.rest_2_), channel_id=1, source_target_pairs={{0,1},{1,0},{2,3},{3,2},{4,5},{5,4},{6,7},{7,6},{8,9},{9,8},{10,11... | collective-permute-start | bytes 1179656 | tf_op jit(solution)/shard_map/gather_tokens_and_weights/ppermute | solution.py:149
  41.5 7.4 %collective-permute-start.11 = (bf16[256,384]{1,0:T(8,128)(2,1)S(1)}, bf16[256,384]{1,0:T(8,128)(2,1)S(1)}, u32[]{:S(2)}, u32[]{:S(2)}) collective-permute-start(bf16[256,384]{1,0:T(8,128)(2,1)S(1)} %collective-permute-done.7.rest_6_), channel_id=1, source_target_pairs={{0,16},{16,0},{1,17},{17,1},{2,18},{18,2},{3,19},{19,3},{4,20},{20... | collective-permute-start | bytes 589832 | tf_op jit(solution)/shard_map/gather_tokens_and_weights/ppermute | solution.py:149
  43.0 0.8 copy-start.4
  43.2 0.8 copy-start.5
  50.9 18.8 %collective-permute-start.16 = (bf16[512,512]{1,0:T(8,128)(2,1)S(1)}, bf16[512,512]{1,0:T(8,128)(2,1)S(1)}, u32[]{:S(2)}, u32[]{:S(2)}) collective-permute-start(bf16[512,512]{1,0:T(8,128)(2,1)S(1)} %slice_bitcast_fusion.refs_0_), channel_id=1, source_target_pairs={{0,1},{1,0},{2,3},{3,2},{4,5},{5,4},{6,7},{7,6},{8,9},{9,8},{10,11... | collective-permute-start | bytes 1572872 | tf_op jit(solution)/shard_map/heads_to_tokens/ppermute | solution.py:149
  51.0 18.6 %collective-permute-start.18 = (bf16[512,512]{1,0:T(8,128)(2,1)S(1)}, bf16[512,512]{1,0:T(8,128)(2,1)S(1)}, u32[]{:S(2)}, u32[]{:S(2)}) collective-permute-start(bf16[512,512]{1,0:T(8,128)(2,1)S(1)} %collective-permute-done.17.refs_2_), channel_id=1, source_target_pairs={{0,1},{1,0},{2,3},{3,2},{4,5},{5,4},{6,7},{7,6},{8,9},{9,8},{10,11... | collective-permute-start | bytes 1572872 | tf_op jit(solution)/shard_map/heads_to_tokens/ppermute | solution.py:149
  51.4 3.4 %collective-permute-start.14 = (bf16[128,128]{1,0:T(8,128)(2,1)S(1)}, bf16[128,128]{1,0:T(8,128)(2,1)S(1)}, u32[]{:S(2)}, u32[]{:S(2)}) collective-permute-start(bf16[128,128]{1,0:T(8,128)(2,1)S(1)} %get-tuple-element.98), channel_id=1, source_target_pairs={{0,3},{1,2},{2,1},{3,0},{4,7},{5,6},{6,5},{7,4},{8,11},{9,10},{10,... | collective-permute-start | bytes 98312 | tf_op jit(solution)/shard_map/heads_to_tokens/ppermute | solution.py:149
  52.7 3.9 %collective-permute-start.13 = (bf16[128,128]{1,0:T(8,128)(2,1)S(1)}, bf16[128,128]{1,0:T(8,128)(2,1)S(1)}, u32[]{:S(2)}, u32[]{:S(2)}) collective-permute-start(bf16[128,128]{1,0:T(8,128)(2,1)S(1)} %get-tuple-element.97), channel_id=1, source_target_pairs={{0,2},{1,3},{2,0},{3,1},{4,6},{5,7},{6,4},{7,5},{8,10},{9,11},{10,... | collective-permute-start | bytes 98312 | tf_op jit(solution)/shard_map/heads_to_tokens/ppermute | solution.py:149
  53.2 3.4 %collective-permute-start.12 = (bf16[128,128]{1,0:T(8,128)(2,1)S(1)}, bf16[128,128]{1,0:T(8,128)(2,1)S(1)}, u32[]{:S(2)}, u32[]{:S(2)}) collective-permute-start(bf16[128,128]{1,0:T(8,128)(2,1)S(1)} %get-tuple-element.96), channel_id=1, source_target_pairs={{0,1},{1,0},{2,3},{3,2},{4,5},{5,4},{6,7},{7,6},{8,9},{9,8},{10,11... | collective-permute-start | bytes 98312 | tf_op jit(solution)/shard_map/heads_to_tokens/ppermute | solution.py:149
  56.6 8.5 %collective-permute-start.15 = (bf16[4,128,128]{2,1,0:T(8,128)(2,1)S(1)}, bf16[4,128,128]{2,1,0:T(8,128)(2,1)S(1)}, u32[]{:S(2)}, u32[]{:S(2)}) collective-permute-start(bf16[4,128,128]{2,1,0:T(8,128)(2,1)S(1)} %pad_maximum_fusion.1.rest_4_), channel_id=1, source_target_pairs={{0,8},{4,12},{8,0},{12,4},{1,9},{5,13},{9,1},{13,5},{2,10},{6,14},... | collective-permute-start | bytes 393224 | tf_op jit(solution)/shard_map/heads_to_tokens/ppermute | solution.py:149
  58.3 11.6 %collective-permute-start.19 = (bf16[4,128,128]{2,1,0:T(8,128)(2,1)S(1)}, bf16[4,128,128]{2,1,0:T(8,128)(2,1)S(1)}, u32[]{:S(2)}, u32[]{:S(2)}) collective-permute-start(bf16[4,128,128]{2,1,0:T(8,128)(2,1)S(1)} %pad_maximum_fusion.1.rest_4_), channel_id=1, source_target_pairs={{0,4},{4,0},{8,12},{12,8},{1,5},{5,1},{9,13},{13,9},{2,6},{6,2},{1... | collective-permute-start | bytes 393224 | tf_op jit(solution)/shard_map/heads_to_tokens/ppermute | solution.py:149
  65.1 5.0 %collective-permute-start.20 = (bf16[4,128,128]{2,1,0:T(8,128)(2,1)S(1)}, bf16[4,128,128]{2,1,0:T(8,128)(2,1)S(1)}, u32[]{:S(2)}, u32[]{:S(2)}) collective-permute-start(bf16[4,128,128]{2,1,0:T(8,128)(2,1)S(1)} %collective-permute-done.15.rest_6_), channel_id=1, source_target_pairs={{0,4},{4,0},{8,12},{12,8},{1,5},{5,1},{9,13},{13,9},{2,6},{6,2},{1... | collective-permute-start | bytes 393224 | tf_op jit(solution)/shard_map/heads_to_tokens/ppermute | solution.py:149
  69.6 18.1 %copy-start = (f32[2048]{0:T(1024)S(1)}, f32[2048]{0:T(1024)}, u32[]{:S(2)}) copy-start(f32[2048]{0:T(1024)} %param.12) | copy-start | bytes 24580
  71.5 5.3 %collective-permute-start.23 = (bf16[128,512]{1,0:T(8,128)(2,1)S(1)}, bf16[128,512]{1,0:T(8,128)(2,1)S(1)}, u32[]{:S(2)}, u32[]{:S(2)}) collective-permute-start(bf16[128,512]{1,0:T(8,128)(2,1)S(1)} %output_projection.1.refs_0_), channel_id=1, source_target_pairs={{0,4},{4,0},{8,12},{12,8},{1,5},{5,1},{9,13},{13,9},{2,6},{6,2},{1... | collective-permute-start | bytes 393224 | tf_op jit(solution)/shard_map/gather_residual/ppermute | solution.py:149
  73.3 7.3 %collective-permute-start.21 = (bf16[128,512]{1,0:T(8,128)(2,1)S(1)}, bf16[128,512]{1,0:T(8,128)(2,1)S(1)}, u32[]{:S(2)}, u32[]{:S(2)}) collective-permute-start(bf16[128,512]{1,0:T(8,128)(2,1)S(1)} %output_projection.1.refs_0_), channel_id=1, source_target_pairs={{0,8},{4,12},{8,0},{12,4},{1,9},{5,13},{9,1},{13,5},{2,10},{6,14},... | collective-permute-start | bytes 393224 | tf_op jit(solution)/shard_map/gather_residual/ppermute | solution.py:149
  74.6 6.0 %collective-permute-start.28 = (bf16[128,512]{1,0:T(8,128)(2,1)S(1)}, bf16[128,512]{1,0:T(8,128)(2,1)S(1)}, u32[]{:S(2)}, u32[]{:S(2)}) collective-permute-start(bf16[128,512]{1,0:T(8,128)(2,1)S(1)} %output_projection.1.refs_0_), channel_id=1, source_target_pairs={{0,2},{1,3},{2,0},{3,1},{4,6},{5,7},{6,4},{7,5},{8,10},{9,11},{10,... | collective-permute-start | bytes 393224 | tf_op jit(solution)/shard_map/gather_residual/ppermute | solution.py:149
  76.8 5.0 %collective-permute-start.30 = (bf16[128,512]{1,0:T(8,128)(2,1)S(1)}, bf16[128,512]{1,0:T(8,128)(2,1)S(1)}, u32[]{:S(2)}, u32[]{:S(2)}) collective-permute-start(bf16[128,512]{1,0:T(8,128)(2,1)S(1)} %collective-permute-done.23.refs_4_), channel_id=1, source_target_pairs={{0,2},{1,3},{2,0},{3,1},{4,6},{5,7},{6,4},{7,5},{8,10},{9,11},{10,... | collective-permute-start | bytes 393224 | tf_op jit(solution)/shard_map/gather_residual/ppermute | solution.py:149
  80.5 5.0 %collective-permute-start.22 = (bf16[128,512]{1,0:T(8,128)(2,1)S(1)}, bf16[128,512]{1,0:T(8,128)(2,1)S(1)}, u32[]{:S(2)}, u32[]{:S(2)}) collective-permute-start(bf16[128,512]{1,0:T(8,128)(2,1)S(1)} %collective-permute-done.21.refs_0_), channel_id=1, source_target_pairs={{0,4},{4,0},{8,12},{12,8},{1,5},{5,1},{9,13},{13,9},{2,6},{6,2},{1... | collective-permute-start | bytes 393224 | tf_op jit(solution)/shard_map/gather_residual/ppermute | solution.py:149
  80.5 5.0 %collective-permute-start.27 = (bf16[128,512]{1,0:T(8,128)(2,1)S(1)}, bf16[128,512]{1,0:T(8,128)(2,1)S(1)}, u32[]{:S(2)}, u32[]{:S(2)}) collective-permute-start(bf16[128,512]{1,0:T(8,128)(2,1)S(1)} %output_projection.1.refs_0_), channel_id=1, source_target_pairs={{0,1},{1,0},{2,3},{3,2},{4,5},{5,4},{6,7},{7,6},{8,9},{9,8},{10,11... | collective-permute-start | bytes 393224 | tf_op jit(solution)/shard_map/gather_residual/ppermute | solution.py:149
  80.5 6.1 %collective-permute-start.29 = (bf16[128,512]{1,0:T(8,128)(2,1)S(1)}, bf16[128,512]{1,0:T(8,128)(2,1)S(1)}, u32[]{:S(2)}, u32[]{:S(2)}) collective-permute-start(bf16[128,512]{1,0:T(8,128)(2,1)S(1)} %collective-permute-done.28.refs_2_), channel_id=1, source_target_pairs={{0,1},{1,0},{2,3},{3,2},{4,5},{5,4},{6,7},{7,6},{8,9},{9,8},{10,11... | collective-permute-start | bytes 393224 | tf_op jit(solution)/shard_map/gather_residual/ppermute | solution.py:149
  81.1 5.9 %collective-permute-start.24 = (bf16[128,512]{1,0:T(8,128)(2,1)S(1)}, bf16[128,512]{1,0:T(8,128)(2,1)S(1)}, u32[]{:S(2)}, u32[]{:S(2)}) collective-permute-start(bf16[128,512]{1,0:T(8,128)(2,1)S(1)} %collective-permute-done.23.refs_4_), channel_id=1, source_target_pairs={{0,1},{1,0},{2,3},{3,2},{4,5},{5,4},{6,7},{7,6},{8,9},{9,8},{10,11... | collective-permute-start | bytes 393224 | tf_op jit(solution)/shard_map/gather_residual/ppermute | solution.py:149
  81.8 6.0 %collective-permute-start.31 = (bf16[128,512]{1,0:T(8,128)(2,1)S(1)}, bf16[128,512]{1,0:T(8,128)(2,1)S(1)}, u32[]{:S(2)}, u32[]{:S(2)}) collective-permute-start(bf16[128,512]{1,0:T(8,128)(2,1)S(1)} %collective-permute-done.30.refs_6_), channel_id=1, source_target_pairs={{0,1},{1,0},{2,3},{3,2},{4,5},{5,4},{6,7},{7,6},{8,9},{9,8},{10,11... | collective-permute-start | bytes 393224 | tf_op jit(solution)/shard_map/gather_residual/ppermute | solution.py:149
  85.5 8.7 %collective-permute-start.33 = (bf16[128,512]{1,0:T(8,128)(2,1)S(1)}, bf16[128,512]{1,0:T(8,128)(2,1)S(1)}, u32[]{:S(2)}, u32[]{:S(2)}) collective-permute-start(bf16[128,512]{1,0:T(8,128)(2,1)S(1)} %collective-permute-done.21.refs_0_), channel_id=1, source_target_pairs={{0,1},{1,0},{2,3},{3,2},{4,5},{5,4},{6,7},{7,6},{8,9},{9,8},{10,11... | collective-permute-start | bytes 393224 | tf_op jit(solution)/shard_map/gather_residual/ppermute | solution.py:149
  85.5 7.5 %collective-permute-start.25 = (bf16[128,512]{1,0:T(8,128)(2,1)S(1)}, bf16[128,512]{1,0:T(8,128)(2,1)S(1)}, u32[]{:S(2)}, u32[]{:S(2)}) collective-permute-start(bf16[128,512]{1,0:T(8,128)(2,1)S(1)} %collective-permute-done.21.refs_0_), channel_id=1, source_target_pairs={{0,2},{1,3},{2,0},{3,1},{4,6},{5,7},{6,4},{7,5},{8,10},{9,11},{10,... | collective-permute-start | bytes 393224 | tf_op jit(solution)/shard_map/gather_residual/ppermute | solution.py:149
  86.7 7.5 %collective-permute-start.35 = (bf16[128,512]{1,0:T(8,128)(2,1)S(1)}, bf16[128,512]{1,0:T(8,128)(2,1)S(1)}, u32[]{:S(2)}, u32[]{:S(2)}) collective-permute-start(bf16[128,512]{1,0:T(8,128)(2,1)S(1)} %collective-permute-done.22.refs_4_), channel_id=1, source_target_pairs={{0,1},{1,0},{2,3},{3,2},{4,5},{5,4},{6,7},{7,6},{8,9},{9,8},{10,11... | collective-permute-start | bytes 393224 | tf_op jit(solution)/shard_map/gather_residual/ppermute | solution.py:149
  86.9 7.3 %collective-permute-start.26 = (bf16[128,512]{1,0:T(8,128)(2,1)S(1)}, bf16[128,512]{1,0:T(8,128)(2,1)S(1)}, u32[]{:S(2)}, u32[]{:S(2)}) collective-permute-start(bf16[128,512]{1,0:T(8,128)(2,1)S(1)} %collective-permute-done.22.refs_4_), channel_id=1, source_target_pairs={{0,2},{1,3},{2,0},{3,1},{4,6},{5,7},{6,4},{7,5},{8,10},{9,11},{10,... | collective-permute-start | bytes 393224 | tf_op jit(solution)/shard_map/gather_residual/ppermute | solution.py:149
  93.0 1.4 %collective-permute-start.34 = (bf16[128,512]{1,0:T(8,128)(2,1)S(1)}, bf16[128,512]{1,0:T(8,128)(2,1)S(1)}, u32[]{:S(2)}, u32[]{:S(2)}) collective-permute-start(bf16[128,512]{1,0:T(8,128)(2,1)S(1)} %collective-permute-done.25.refs_2_), channel_id=1, source_target_pairs={{0,1},{1,0},{2,3},{3,2},{4,5},{5,4},{6,7},{7,6},{8,9},{9,8},{10,11... | collective-permute-start | bytes 393224 | tf_op jit(solution)/shard_map/gather_residual/ppermute | solution.py:149
  94.2 1.3 collective-permute-start.32
  103.9 2.3 %collective-permute-start.36 = (bf16[512,512]{1,0:T(8,128)(2,1)S(1)}, bf16[512,512]{1,0:T(8,128)(2,1)S(1)}, u32[]{:S(2)}, u32[]{:S(2)}) collective-permute-start(bf16[512,512]{1,0:T(8,128)(2,1)S(1)} %get-tuple-element.122), channel_id=1, source_target_pairs={{0,1},{1,0},{2,3},{3,2},{4,5},{5,4},{6,7},{7,6},{8,9},{9,8},{10,11... | collective-permute-start | bytes 1572872 | tf_op jit(solution)/shard_map/sum_over_devices/ppermute | solution.py:149
  107.5 9.6 %collective-permute-start.40 = (bf16[256,512]{1,0:T(8,128)(2,1)}, bf16[256,512]{1,0:T(8,128)(2,1)S(1)}, u32[]{:S(2)}, u32[]{:S(2)}) collective-permute-start(bf16[256,512]{1,0:T(8,128)(2,1)} %get-tuple-element.124), channel_id=1, source_target_pairs={{0,2},{1,3},{2,0},{3,1},{4,6},{5,7},{6,4},{7,5},{8,10},{9,11},{10,... | collective-permute-start | bytes 786440 | tf_op jit(solution)/shard_map/sum_over_devices/ppermute | solution.py:149
  111.6 1.4 %collective-permute-start.41 = (bf16[128,512]{1,0:T(8,128)(2,1)S(1)}, bf16[128,512]{1,0:T(8,128)(2,1)S(1)}, u32[]{:S(2)}, u32[]{:S(2)}) collective-permute-start(bf16[128,512]{1,0:T(8,128)(2,1)S(1)} %get-tuple-element.136), channel_id=1, source_target_pairs={{0,1},{1,0},{2,3},{3,2},{4,5},{5,4},{6,7},{7,6},{8,9},{9,8},{10,11... | collective-permute-start | bytes 393224 | tf_op jit(solution)/shard_map/sum_over_devices/ppermute | solution.py:149
  111.6 10.3 %collective-permute-start.37 = (bf16[256,512]{1,0:T(8,128)(2,1)S(1)}, bf16[256,512]{1,0:T(8,128)(2,1)S(1)}, u32[]{:S(2)}, u32[]{:S(2)}) collective-permute-start(bf16[256,512]{1,0:T(8,128)(2,1)S(1)} %get-tuple-element.125), channel_id=1, source_target_pairs={{0,2},{1,3},{2,0},{3,1},{4,6},{5,7},{6,4},{7,5},{8,10},{9,11},{10,... | collective-permute-start | bytes 786440 | tf_op jit(solution)/shard_map/sum_over_devices/ppermute | solution.py:149
  112.5 4.6 %collective-permute-start.42 = (bf16[128,512]{1,0:T(8,128)(2,1)}, bf16[128,512]{1,0:T(8,128)(2,1)S(1)}, u32[]{:S(2)}, u32[]{:S(2)}) collective-permute-start(bf16[128,512]{1,0:T(8,128)(2,1)} %get-tuple-element.137), channel_id=1, source_target_pairs={{0,1},{1,0},{2,3},{3,2},{4,5},{5,4},{6,7},{7,6},{8,9},{9,8},{10,11... | collective-permute-start | bytes 393224 | tf_op jit(solution)/shard_map/sum_over_devices/ppermute | solution.py:149
  112.7 7.4 %collective-permute-start.38 = (bf16[128,512]{1,0:T(8,128)(2,1)}, bf16[128,512]{1,0:T(8,128)(2,1)}, u32[]{:S(2)}, u32[]{:S(2)}) collective-permute-start(bf16[128,512]{1,0:T(8,128)(2,1)} %get-tuple-element.128), channel_id=1, source_target_pairs={{0,1},{1,0},{2,3},{3,2},{4,5},{5,4},{6,7},{7,6},{8,9},{9,8},{10,11... | collective-permute-start | bytes 393224 | tf_op jit(solution)/shard_map/sum_over_devices/ppermute | solution.py:149
  113.0 7.1 %collective-permute-start.39 = (bf16[128,512]{1,0:T(8,128)(2,1)}, bf16[128,512]{1,0:T(8,128)(2,1)}, u32[]{:S(2)}, u32[]{:S(2)}) collective-permute-start(bf16[128,512]{1,0:T(8,128)(2,1)} %get-tuple-element.130), channel_id=1, source_target_pairs={{0,1},{1,0},{2,3},{3,2},{4,5},{5,4},{6,7},{7,6},{8,9},{9,8},{10,11... | collective-permute-start | bytes 393224 | tf_op jit(solution)/shard_map/sum_over_devices/ppermute | solution.py:149
  117.8 8.3 %collective-permute-start.44 = (bf16[128,512]{1,0:T(8,128)(2,1)S(1)}, bf16[128,512]{1,0:T(8,128)(2,1)S(1)}, u32[]{:S(2)}, u32[]{:S(2)}) collective-permute-start(bf16[128,512]{1,0:T(8,128)(2,1)S(1)} %get-tuple-element.139), channel_id=1, source_target_pairs={{0,12},{4,8},{8,4},{12,0},{1,13},{5,9},{9,5},{13,1},{2,14},{6,10},... | collective-permute-start | bytes 393224 | tf_op jit(solution)/shard_map/sum_over_devices/ppermute | solution.py:149
  120.1 11.4 %collective-permute-start.43 = (bf16[128,512]{1,0:T(8,128)(2,1)S(1)}, bf16[128,512]{1,0:T(8,128)(2,1)S(1)}, u32[]{:S(2)}, u32[]{:S(2)}) collective-permute-start(bf16[128,512]{1,0:T(8,128)(2,1)S(1)} %get-tuple-element.138), channel_id=1, source_target_pairs={{0,8},{4,12},{8,0},{12,4},{1,9},{5,13},{9,1},{13,5},{2,10},{6,14},... | collective-permute-start | bytes 393224 | tf_op jit(solution)/shard_map/sum_over_devices/ppermute | solution.py:149
  123.0 8.6 %collective-permute-start.45 = (bf16[128,512]{1,0:T(8,128)(2,1)S(1)}, bf16[128,512]{1,0:T(8,128)(2,1)S(1)}, u32[]{:S(2)}, u32[]{:S(2)}) collective-permute-start(bf16[128,512]{1,0:T(8,128)(2,1)S(1)} %get-tuple-element.140), channel_id=1, source_target_pairs={{0,4},{4,0},{8,12},{12,8},{1,5},{5,1},{9,13},{13,9},{2,6},{6,2},{1... | collective-permute-start | bytes 393224 | tf_op jit(solution)/shard_map/sum_over_devices/ppermute | solution.py:149
